TPU v7x, 32 devices: a whole 2x2x4 slice. The times are simulated.
32 devices in a mesh: dp: 8 (over z, y), tensor: 4 (over x, core).
Axes of the slice: x: 2, y: 2, z: 4, core: 2. Of those that a mesh axis runs over, the one named last changes fastest.
Arguments:
- frames_in: bfloat16 [8192, 1024], P(('dp', 'tensor')), may hold values from -6 to 6
- code_emb: bfloat16 [8192, 3, 1024], P(('dp', 'tensor')), may hold values from -6 to 6
- cotangent: bfloat16 [8192, 3, 1024], P(('dp', 'tensor')), may hold values from -6 to 6
- lengths: int32 [8], P('dp'), may hold values from 204 to 1024, as said below
- owner_list: int32 [8], replicated, may hold values from 0 to 7, each once
- master: float32 [2, 1024, 12288], P(None, 'dp', 'tensor'), may hold values from -2 to 2
- first_moment: float32 [2, 1024, 12288], P(None, 'dp', 'tensor'), may hold values from -300 to 300
- second_moment: float32 [2, 1024, 12288], P(None, 'dp', 'tensor'), may hold values from 100 to 100000
- ema: float32 [2, 1024, 12288], P(None, 'dp', 'tensor'), may hold values from -0.2 to 0.2
- left_basis: float32 [2, 1024, 512], P(None, 'dp', 'tensor'), may hold values from -1 to 1
- right_basis: float32 [2, 192, 128, 512], P(None, 'dp', None, 'tensor'), may hold values from -1 to 1
- gains: float32 [4, 1024], replicated, may hold values from 0.5 to 1.5
- gain_first: float32 [4, 1024], replicated, may hold values from -300 to 300
- gain_second: float32 [4, 1024], replicated, may hold values from 100 to 100000
Outputs:
- local_out: bfloat16 [8192, 3, 1024], P(('dp', 'tensor'))
- input_grad: float32 [8192, 1024], P(('dp', 'tensor'))
- weight_grads: float32 [2, 1024, 12288], P(None, 'dp', 'tensor')
- gain_grads: float32 [4, 1024], replicated
- new_master: float32 [2, 1024, 12288], P(None, 'dp', 'tensor')
- new_first: float32 [2, 1024, 12288], P(None, 'dp', 'tensor')
- new_second: float32 [2, 1024, 12288], P(None, 'dp', 'tensor')
- new_ema: float32 [2, 1024, 12288], P(None, 'dp', 'tensor')
- new_gains: float32 [4, 1024], replicated
- new_gain_first: float32 [4, 1024], replicated
- new_gain_second: float32 [4, 1024], replicated
Inputs may be any that keep to these rules, and one draw needn't show every extreme that they name: lengths[i] counts the valid frames of item i, at least 204; in every draw some item has exactly 1024. owner_list is a permutation of 0 to 7.
All inputs are finite; a program needn't handle non-finite values.
Results may differ from a plain program's by a relative error of at most 0.035.
Values may be sent and summed in bfloat16 or wider, within the bound.
A program may use at most 320 MiB of HBM per device.

v0:
```python
import math

import jax
import jax.numpy as jnp
from jax import lax
from jax.sharding import PartitionSpec as P

D = 1024
HD = 64
FF = 4096
CB = 3
LMAX = 1024


norm_eps = 1e-06
beta_first = 0.5
beta_second = 0.5
adam_eps = 1e-08
step_rate = 0.05
gain_rate = 0.4
ema_decay = 0.9
masked_fill = -1e30
highest = lax.Precision.HIGHEST


def dot_rows(left, right):
    return jnp.dot(left, right, preferred_element_type=jnp.float32)


def dot_transposed(left, right):
    return lax.dot_general(
        left, right, (((1,), (1,)), ((), ())), preferred_element_type=jnp.float32
    )


def dot_over_rows(left, right):
    return lax.dot_general(
        left, right, (((0,), (0,)), ((), ())), preferred_element_type=jnp.float32
    )


def keep_rows(values):
    return values


def row_term(operand, weight):
    return dot_transposed(operand, weight)


def rms_forward(rows_in, gain):
    return (
        rows_in * lax.rsqrt(jnp.mean(rows_in * rows_in, axis=-1, keepdims=True) + norm_eps) * gain
    )


def rms_backward(rows_in, gain, grad_out):
    width = rows_in.shape[-1]
    scale_rows = lax.rsqrt(jnp.mean(rows_in * rows_in, axis=-1, keepdims=True) + norm_eps)
    scaled_grad = grad_out * gain
    inner_total = jnp.sum(scaled_grad * rows_in, axis=-1, keepdims=True)
    grad_in = (
        scale_rows * scaled_grad
        - rows_in * (scale_rows * scale_rows * scale_rows) * inner_total / width
    )
    gain_grad = jnp.sum(grad_out * rows_in * scale_rows, axis=0)
    return (grad_in, gain_grad)


def gelu_slope(upper):
    normal_cdf = 0.5 * (1.0 + lax.erf(upper * (1.0 / math.sqrt(2.0))))
    density = jnp.exp(-0.5 * upper * upper) * (1.0 / math.sqrt(2.0 * math.pi))
    return normal_cdf + upper * density


def split_layer(layer_cols, groups, head_cols, ff_cols):
    width = layer_cols.shape[0]
    grouped = layer_cols.reshape(width, groups, -1)

    def columns(begin, extent):
        return grouped[:, :, begin : begin + extent].reshape(width, groups * extent)

    w_qkv = jnp.concatenate(
        [columns(0, head_cols), columns(head_cols, head_cols), columns(2 * head_cols, head_cols)],
        axis=1,
    )
    return (
        w_qkv,
        columns(3 * head_cols, head_cols),
        columns(4 * head_cols, ff_cols),
        columns(4 * head_cols + ff_cols, ff_cols),
    )


def join_layer(grad_parts, groups):
    grad_qkv, grad_out, grad_up, grad_down = grad_parts
    width = grad_qkv.shape[0]
    head_width = grad_qkv.shape[1] // 3
    pieces = [
        grad_qkv[:, 0:head_width],
        grad_qkv[:, head_width : 2 * head_width],
        grad_qkv[:, 2 * head_width :],
        grad_out,
        grad_up,
        grad_down,
    ]
    return jnp.concatenate([piece.reshape(width, groups, -1) for piece in pieces], axis=2).reshape(
        width, -1
    )


def global_scores(queries, key_rows, length):
    span = queries.shape[0]
    heads = queries.shape[1] // HD
    scores = jnp.einsum(
        "qhd,khd->hqk",
        queries.reshape(span, heads, HD),
        key_rows.reshape(span, heads, HD),
        preferred_element_type=jnp.float32,
    ) * HD ** (-0.5)
    rows_at = lax.broadcasted_iota(jnp.int32, (span, span), 0)
    cols_at = lax.broadcasted_iota(jnp.int32, (span, span), 1)
    allowed = (cols_at <= rows_at) & (cols_at < length)
    return jnp.where(allowed[None], scores, masked_fill)


def global_attend(queries, key_rows, value_rows, lengths):
    items = lengths.shape[0]
    span = queries.shape[0] // items
    heads = queries.shape[1] // HD

    def one_item(packed):
        item_query, item_key, item_value, length = packed
        scores = global_scores(item_query, item_key, length)
        row_max = jnp.max(scores, axis=-1, keepdims=True)
        expanded = jnp.exp(scores - row_max)
        row_total = jnp.sum(expanded, axis=-1, keepdims=True)
        probability = (expanded / row_total).astype(jnp.bfloat16)
        mixed = jnp.einsum(
            "hqk,khd->qhd",
            probability,
            item_value.reshape(span, heads, HD),
            preferred_element_type=jnp.float32,
        )
        return (
            mixed.reshape(span, -1).astype(jnp.bfloat16),
            (row_max + jnp.log(row_total))[..., 0],
        )

    mixed, log_total = lax.map(
        one_item,
        (
            queries.reshape(items, span, -1),
            key_rows.reshape(items, span, -1),
            value_rows.reshape(items, span, -1),
            lengths,
        ),
    )
    return (mixed.reshape(items * span, -1), log_total)


def global_attend_back(queries, key_rows, value_rows, lengths, log_total, grad_mixed):
    items = lengths.shape[0]
    span = queries.shape[0] // items
    heads = queries.shape[1] // HD
    scale_score = HD ** (-0.5)

    def one_item(packed):
        item_query, item_key, item_value, length, item_lse, item_grad = packed
        scores = global_scores(item_query, item_key, length)
        probability = jnp.exp(scores - item_lse[..., None])
        grad_heads = item_grad.reshape(span, heads, HD)
        query_heads = item_query.reshape(span, heads, HD)
        key_heads = item_key.reshape(span, heads, HD)
        value_heads = item_value.reshape(span, heads, HD)
        grad_value = jnp.einsum(
            "hqk,qhd->khd",
            probability.astype(jnp.bfloat16),
            grad_heads,
            preferred_element_type=jnp.float32,
        )
        grad_prob = jnp.einsum(
            "qhd,khd->hqk", grad_heads, value_heads, preferred_element_type=jnp.float32
        )
        center = jnp.sum(probability * grad_prob, axis=-1, keepdims=True)
        grad_scores = (probability * (grad_prob - center)).astype(jnp.bfloat16)
        grad_query = (
            jnp.einsum("hqk,khd->qhd", grad_scores, key_heads, preferred_element_type=jnp.float32)
            * scale_score
        )
        grad_key = (
            jnp.einsum("hqk,qhd->khd", grad_scores, query_heads, preferred_element_type=jnp.float32)
            * scale_score
        )
        return jnp.concatenate(
            [
                grad_query.reshape(span, -1),
                grad_key.reshape(span, -1),
                grad_value.reshape(span, -1),
            ],
            axis=1,
        ).astype(jnp.bfloat16)

    grads = lax.map(
        one_item,
        (
            queries.reshape(items, span, -1),
            key_rows.reshape(items, span, -1),
            value_rows.reshape(items, span, -1),
            lengths,
            log_total,
            grad_mixed.reshape(items, span, -1),
        ),
    )
    return grads.reshape(items * span, -1)


def local_probability(queries, key_rows):
    frame_count = queries.shape[0] // CB
    heads = queries.shape[1] // HD
    scores = jnp.einsum(
        "fqhd,fkhd->fhqk",
        queries.reshape(frame_count, CB, heads, HD),
        key_rows.reshape(frame_count, CB, heads, HD),
        preferred_element_type=jnp.float32,
    ) * HD ** (-0.5)
    rows_at = lax.broadcasted_iota(jnp.int32, (CB, CB), 0)
    cols_at = lax.broadcasted_iota(jnp.int32, (CB, CB), 1)
    scores = jnp.where(cols_at <= rows_at, scores, masked_fill)
    row_max = jnp.max(scores, axis=-1, keepdims=True)
    expanded = jnp.exp(scores - row_max)
    return expanded / jnp.sum(expanded, axis=-1, keepdims=True)


def local_attend(queries, key_rows, value_rows):
    frame_count = queries.shape[0] // CB
    heads = queries.shape[1] // HD
    probability = local_probability(queries, key_rows).astype(jnp.bfloat16)
    mixed = jnp.einsum(
        "fhqk,fkhd->fqhd",
        probability,
        value_rows.reshape(frame_count, CB, heads, HD),
        preferred_element_type=jnp.float32,
    )
    return (mixed.reshape(queries.shape[0], -1).astype(jnp.bfloat16), jnp.zeros((), jnp.float32))


def local_attend_back(queries, key_rows, value_rows, saved, grad_mixed):
    frame_count = queries.shape[0] // CB
    heads = queries.shape[1] // HD
    scale_score = HD ** (-0.5)
    probability = local_probability(queries, key_rows)
    grad_heads = grad_mixed.reshape(frame_count, CB, heads, HD)
    query_heads = queries.reshape(frame_count, CB, heads, HD)
    key_heads = key_rows.reshape(frame_count, CB, heads, HD)
    value_heads = value_rows.reshape(frame_count, CB, heads, HD)
    grad_value = jnp.einsum(
        "fhqk,fqhd->fkhd",
        probability.astype(jnp.bfloat16),
        grad_heads,
        preferred_element_type=jnp.float32,
    )
    grad_prob = jnp.einsum(
        "fqhd,fkhd->fhqk", grad_heads, value_heads, preferred_element_type=jnp.float32
    )
    center = jnp.sum(probability * grad_prob, axis=-1, keepdims=True)
    grad_scores = (probability * (grad_prob - center)).astype(jnp.bfloat16)
    grad_query = (
        jnp.einsum("fhqk,fkhd->fqhd", grad_scores, key_heads, preferred_element_type=jnp.float32)
        * scale_score
    )
    grad_key = (
        jnp.einsum("fhqk,fqhd->fkhd", grad_scores, query_heads, preferred_element_type=jnp.float32)
        * scale_score
    )
    total_rows = queries.shape[0]
    return jnp.concatenate(
        [
            grad_query.reshape(total_rows, -1),
            grad_key.reshape(total_rows, -1),
            grad_value.reshape(total_rows, -1),
        ],
        axis=1,
    ).astype(jnp.bfloat16)


def block_forward(rows_in, matrices, gain_a, gain_b, path, attend):
    gather_rows, sum_rows = (path[0], path[1])
    w_qkv, w_out, w_up, w_down = matrices
    normed_a = gather_rows(rms_forward(rows_in, gain_a).astype(jnp.bfloat16))
    projected = dot_rows(normed_a, w_qkv).astype(jnp.bfloat16)
    head_width = projected.shape[1] // 3
    mixed, saved = attend(
        projected[:, :head_width],
        projected[:, head_width : 2 * head_width],
        projected[:, 2 * head_width :],
    )
    middle = rows_in + sum_rows(mixed, w_out)
    normed_b = gather_rows(rms_forward(middle, gain_b).astype(jnp.bfloat16))
    upper = dot_rows(normed_b, w_up)
    active = jax.nn.gelu(upper, approximate=False).astype(jnp.bfloat16)
    result = middle + sum_rows(active, w_down)
    return (result, (rows_in, normed_a, projected, mixed, saved, middle, normed_b, upper, active))


def block_backward(grad_result, kept, matrices, gain_a, gain_b, path, attend_back):
    gather_grads, sum_back = (path[2], path[3])
    rows_in, normed_a, projected, mixed, saved, middle, normed_b, upper, active = kept
    w_qkv, w_out, w_up, w_down = matrices
    grad_branch = gather_grads(grad_result.astype(jnp.bfloat16))
    grad_down = dot_over_rows(grad_branch, active)
    grad_active = dot_rows(grad_branch, w_down)
    grad_upper = (grad_active * gelu_slope(upper)).astype(jnp.bfloat16)
    grad_up = dot_over_rows(normed_b, grad_upper)
    grad_normed_b = sum_back(grad_upper, w_up)
    grad_middle_part, gain_b_grad = rms_backward(middle, gain_b, grad_normed_b)
    grad_middle = grad_result + grad_middle_part
    grad_attn = gather_grads(grad_middle.astype(jnp.bfloat16))
    grad_out = dot_over_rows(grad_attn, mixed)
    grad_mixed = dot_rows(grad_attn, w_out).astype(jnp.bfloat16)
    head_width = projected.shape[1] // 3
    grad_qkv = attend_back(
        projected[:, :head_width],
        projected[:, head_width : 2 * head_width],
        projected[:, 2 * head_width :],
        saved,
        grad_mixed,
    )
    grad_weight_qkv = dot_over_rows(normed_a, grad_qkv)
    grad_normed_a = sum_back(grad_qkv, w_qkv)
    grad_rows_part, gain_a_grad = rms_backward(rows_in, gain_a, grad_normed_a)
    return (
        grad_middle + grad_rows_part,
        (grad_weight_qkv, grad_out, grad_up, grad_down),
        gain_a_grad,
        gain_b_grad,
    )


def shards(
    frames_in,
    code_emb,
    cotangent,
    lengths,
    owner_list,
    master,
    first_moment,
    second_moment,
    ema,
    left_basis,
    right_basis,
    gains,
    gain_first,
    gain_second,
):
    tensor_count = lax.axis_size("tensor")
    group_count = lax.axis_size("dp")
    head_cols = D // tensor_count
    ff_cols = FF // tensor_count
    share = frames_in.shape[0]
    owned_rows = master.shape[1]
    gathered = lax.all_gather(master.astype(jnp.bfloat16), "dp", axis=1, tiled=True)
    layers = jnp.take(gathered.reshape(2, group_count, owned_rows, -1), owner_list, axis=1).reshape(
        2, group_count * owned_rows, -1
    )

    def gather_rows(values):
        return lax.all_gather(values, "tensor", axis=0, tiled=True)

    def gather_grads(values):
        return lax.all_gather(values, "tensor", axis=0, tiled=True)

    def sum_rows(operand, weight):
        return lax.psum_scatter(
            row_term(operand, weight).astype(jnp.bfloat16),
            "tensor",
            scatter_dimension=0,
            tiled=True,
        ).astype(jnp.float32)

    def sum_back(operand, weight):
        return lax.psum_scatter(
            row_term(operand, weight).astype(jnp.bfloat16),
            "tensor",
            scatter_dimension=0,
            tiled=True,
        ).astype(jnp.float32)

    heads_path = (gather_rows, sum_rows, gather_grads, sum_back)
    rows_path = (keep_rows, dot_transposed, keep_rows, dot_transposed)

    def attend_global(queries, key_rows, value_rows):
        return global_attend(queries, key_rows, value_rows, lengths)

    def attend_global_back(queries, key_rows, value_rows, saved, grad_mixed):
        return global_attend_back(queries, key_rows, value_rows, lengths, saved, grad_mixed)

    global_matrices = split_layer(layers[0], 1, head_cols, ff_cols)
    global_out, global_kept = block_forward(
        frames_in.astype(jnp.float32),
        global_matrices,
        gains[0],
        gains[1],
        heads_path,
        attend_global,
    )
    local_in = (global_out[:, None, :] + code_emb.astype(jnp.float32)).reshape(share * CB, -1)
    local_layer = lax.all_gather(layers[1], "tensor", axis=1, tiled=True)
    local_matrices = split_layer(local_layer, tensor_count, head_cols, ff_cols)
    local_result, local_kept = block_forward(
        local_in, local_matrices, gains[2], gains[3], rows_path, local_attend
    )
    local_out = local_result.reshape(share, CB, -1).astype(jnp.bfloat16)
    frame_at = lax.axis_index("tensor") * share + jnp.arange(share, dtype=jnp.int32)
    item_at = frame_at // LMAX
    item_slots = jnp.arange(lengths.shape[0], dtype=jnp.int32)
    item_length = jnp.sum(
        jnp.where(item_at[:, None] == item_slots[None, :], lengths[None, :], 0), axis=1
    )
    valid = (frame_at % LMAX < item_length).astype(jnp.float32)
    grad_local = (cotangent.astype(jnp.float32) * valid[:, None, None]).reshape(share * CB, -1)
    grad_local_in, local_weight_grads, gain_c_grad, gain_d_grad = block_backward(
        grad_local, local_kept, local_matrices, gains[2], gains[3], rows_path, local_attend_back
    )
    grad_global_out = jnp.sum(grad_local_in.reshape(share, CB, -1), axis=1)
    input_grad, global_weight_grads, gain_a_grad, gain_b_grad = block_backward(
        grad_global_out,
        global_kept,
        global_matrices,
        gains[0],
        gains[1],
        heads_path,
        attend_global_back,
    )
    local_grads = join_layer(local_weight_grads, tensor_count)
    local_grads = lax.psum_scatter(
        local_grads.astype(jnp.bfloat16), "tensor", scatter_dimension=1, tiled=True
    ).astype(jnp.float32)
    layer_grads = jnp.stack([join_layer(global_weight_grads, 1), local_grads])
    slots = jnp.arange(group_count, dtype=jnp.int32)
    inverse = jnp.sum(jnp.where(owner_list[None, :] == slots[:, None], slots[None, :], 0), axis=1)
    ordered = jnp.take(
        layer_grads.reshape(2, group_count, owned_rows, -1), inverse, axis=1
    ).reshape(2, group_count * owned_rows, -1)
    weight_grads = lax.psum_scatter(
        ordered.astype(jnp.bfloat16), "dp", scatter_dimension=1, tiled=True
    ).astype(jnp.float32)
    gain_grads = lax.psum(
        jnp.stack([gain_a_grad, gain_b_grad, gain_c_grad, gain_d_grad]), ("dp", "tensor")
    )
    tile_count = right_basis.shape[1]
    turned_left = jnp.einsum("lab,lac->lbc", left_basis, weight_grads, precision=highest)
    rotated = jnp.einsum(
        "lbkc,lkce->lbke",
        turned_left.reshape(2, owned_rows, tile_count, -1),
        right_basis,
        precision=highest,
    ).reshape(weight_grads.shape)
    new_first = beta_first * first_moment + (1.0 - beta_first) * rotated
    new_second = beta_second * second_moment + (1.0 - beta_second) * rotated * rotated
    turned = new_first / (jnp.sqrt(new_second) + adam_eps)
    back_right = jnp.einsum(
        "lbke,lkce->lbkc",
        turned.reshape(2, owned_rows, tile_count, -1),
        right_basis,
        precision=highest,
    )
    back_full = jnp.einsum(
        "lab,lbc->lac", left_basis, back_right.reshape(weight_grads.shape), precision=highest
    )
    new_master = master - step_rate * back_full
    new_ema = ema_decay * ema + (1.0 - ema_decay) * new_master
    new_gain_first = beta_first * gain_first + (1.0 - beta_first) * gain_grads
    new_gain_second = beta_second * gain_second + (1.0 - beta_second) * gain_grads * gain_grads
    new_gains = gains - gain_rate * new_gain_first / (jnp.sqrt(new_gain_second) + adam_eps)
    return (
        local_out,
        input_grad,
        weight_grads,
        gain_grads,
        new_master,
        new_first,
        new_second,
        new_ema,
        new_gains,
        new_gain_first,
        new_gain_second,
    )


def solution(mesh):
    return jax.shard_map(
        shards,
        mesh=mesh,
        in_specs=(
            P(("dp", "tensor"), None),
            P(("dp", "tensor"), None, None),
            P(("dp", "tensor"), None, None),
            P("dp"),
            P(),
            P(None, "dp", "tensor"),
            P(None, "dp", "tensor"),
            P(None, "dp", "tensor"),
            P(None, "dp", "tensor"),
            P(None, "dp", "tensor"),
            P(None, "dp", None, "tensor"),
            P(),
            P(),
            P(),
        ),
        out_specs=(
            P(("dp", "tensor"), None, None),
            P(("dp", "tensor"), None),
            P(None, "dp", "tensor"),
            P(),
            P(None, "dp", "tensor"),
            P(None, "dp", "tensor"),
            P(None, "dp", "tensor"),
            P(None, "dp", "tensor"),
            P(),
            P(),
            P(),
        ),
        check_vma=False,
    )
```

profile of v0, /device:TPU:0, one launch (start us, length us, event | category | flops | bytes accessed | tf_op | source)
XLA Modules:
  0.0 1495.2 jit_solution(8466006288778699804)
XLA Ops:
  17.9 172.1 %all-gather.9.cloned.1.call-done = bf16[2,1024,3072]{2,1,0:T(8,128)(2,1)} async-done(((bf16[2,128,3072]{2,1,0:T(8,128)(2,1)}), bf16[2,1024,3072]{2,1,0:T(8,128)(2,1)}) %all-gather.9.cloned.1.call-update) | async-done | bytes 12582928 | tf_op jit(solution)/shard_map/all_gather | solution.py:361
  190.0 11.2 gather_fusion
  201.2 6.5 select_bitcast_fusion
  219.5 7.5 fusion.167
  227.0 8.0 fusion.2
  235.1 7.4 fusion.95
  246.5 29.7 %reduce-scatter.7.cloned.1.call-done = bf16[256,1024]{1,0:T(8,128)(2,1)} async-done(((bf16[1024,1024]{1,0:T(8,128)(2,1)}), bf16[256,1024]{1,0:T(8,128)(2,1)}) %reduce-scatter.7.cloned.1.call-update) | async-done | bytes 524304 | tf_op jit(solution)/shard_map/reduce_scatter | solution.py:373
  281.3 22.5 %all-gather.11.cloned.1.call-done = bf16[1024,1024]{1,0:T(8,128)(2,1)} async-done(((bf16[256,1024]{1,0:T(8,128)(2,1)}), bf16[1024,1024]{1,0:T(8,128)(2,1)}) %all-gather.11.cloned.1.call-update) | async-done | bytes 2097168 | tf_op jit(solution)/shard_map/all_gather | solution.py:367
  303.8 14.1 fusion.45
  348.1 8.1 reduce-scatter.9.cloned.1.call-done
  363.9 6.7 reshape.437
  371.5 140.9 %all-gather.13.cloned.1.call-done = bf16[1024,12288]{1,0:T(8,128)(2,1)} async-done(((bf16[1024,3072]{1,0:T(8,128)(2,1)}), bf16[1024,12288]{1,0:T(8,128)(2,1)}) %all-gather.13.cloned.1.call-update) | async-done | bytes 25165840 | tf_op jit(solution)/shard_map/all_gather | solution.py:407
  512.4 49.2 %reshape.438 = bf16[1024,4,3072]{2,1,0:T(4,128)(2,1)} reshape(bf16[1024,12288]{1,0:T(8,128)(2,1)} %all-gather.13.cloned.1.call-done) | data formatting | bytes 50331648 | tf_op jit(solution)/shard_map/reshape | solution.py:77
  567.7 15.8 %fusion.159 = (bf16[1024,4,1024]{2,1,0:T(4,128)(2,1)}, bf16[1024,4,1024]{2,1,0:T(4,128)(2,1)}) fusion(bf16[1024,4,3072]{2,1,0:T(4,128)(2,1)} %reshape.438), kind=kLoop, calls=%fused_computation.298 | loop fusion | bytes 33554432 | tf_op jit(solution)/shard_map/slice | solution.py:80
  612.2 18.6 %fusion.168 = (f32[256,16,3]{2,1,0:T(8,128)}, f32[256,16,3,3]{2,3,1,0:T(4,128)}) fusion(pred[3,3]{0,1:T(4,128)(4,1)S(1)} %iota_compare_fusion.3, bf16[256,3,16,64]{3,2,1,0:T(8,128)(2,1)} %reshape.444, bf16[256,3,16,64]{3,2,1,0:T(8,128)(2,1)} %reshape.443), kind=kOutput, calls=%fused_computation.307 | convolution fusion | flops 4866050 | bytes 3342345 | tf_op jit(solution)/shard_map/sub | solution.py:230
  630.9 8.3 fusion.65
  650.8 12.2 copy.213
  663.0 12.5 copy.212
  680.3 36.8 %fusion.15 = (bf16[4096,768]{0,1:T(8,128)(2,1)}, f32[768,4096]{1,0:T(8,128)}) fusion(bf16[1024,4096]{1,0:T(8,128)(2,1)S(1)} %bitcast.266, f32[768,1024]{1,0:T(8,128)S(1)} %get-tuple-element.158, f32[1024]{0:T(1024)S(1)} %bitcast.317, f32[768]{0:T(1024)S(1)} %get-tuple-element.146), kind=kOutput, calls=%fused_computation.28 | convolution fusion | flops 6649282560 | bytes 30415872 | tf_op jit(solution)/shard_map/dot_general | solution.py:27
  717.2 14.3 fusion.12
  731.4 11.8 multiply_reduce_fusion.2
  756.1 15.3 %multiply_reduce_fusion.1 = (f32[256,16,3]{2,1,0:T(8,128)S(1)}, f32[256,16,3,3]{2,3,1,0:T(4,128)}) fusion(f32[256,16,3,3]{2,3,1,0:T(4,128)} %get-tuple-element.156, f32[256,16,3]{2,1,0:T(8,128)} %get-tuple-element.155, bf16[256,3,16,64]{3,2,1,0:T(8,128)(2,1)} %reshape.442, bf16[256,3,16,64]{3,2,1,0:T(8,128)(2,1)} %reshape.449), kind=kOutput, calls=%fused_computation.68 | convolution fusion | flops 4816896 | bytes 3538944 | tf_op jit(solution)/shard_map/fqhd,fkhd->fhqk/dot_general | solution.py:262
  771.4 8.5 multiply_convert_fusion.3
  780.0 7.1 fusion.67
  793.1 8.9 fusion.66
  840.4 10.0 multiply_reduce_fusion.3
  866.6 22.7 %all-gather.15.cloned.1.call-done = bf16[1024,1024]{1,0:T(8,128)(2,1)} async-done(((bf16[256,1024]{1,0:T(8,128)(2,1)}), bf16[1024,1024]{1,0:T(8,128)(2,1)}) %all-gather.15.cloned.1.call-update) | async-done | bytes 2097168 | tf_op jit(solution)/shard_map/all_gather | solution.py:370
  907.4 12.9 convolution_convert_fusion
  920.3 9.6 convolution_convert_fusion.1
  959.7 12.0 copy.205
  971.7 8.6 copy.206
  990.7 7.8 constant_dynamic-update-slice_fusion.11
  998.5 11.7 convert_dynamic-update-slice_fusion
  1019.6 19.1 %multiply_reduce_fusion = (f32[4,1024]{1,0:T(4,128)S(1)}, f32[4,1024,1024]{1,2,0:T(8,128)}) fusion(f32[4,1024,1024]{1,2,0:T(8,128)} %get-tuple-element.152, f32[4,1024]{1,0:T(4,128)S(1)} %log_add_fusion, bf16[1024,4,64]{0,2,1:T(8,128)(2,1)S(1)} %bitcast.284, bf16[1024,4,64]{0,2,1:T(8,128)(2,1)} %bitcast.287), kind=kOutput, calls=%fused_computation.10 | convolution fusion | flops 549449728 | bytes 34635776 | tf_op jit(solution)/shard_map/while/body/eval_jaxpr/qhd,khd->hqk/dot_general | solution.py:181
  1038.8 17.9 %multiply_convert_fusion = bf16[4,1024,1024]{1,2,0:T(8,128)(2,1)} fusion(f32[4,1024,1024]{1,2,0:T(8,128)} %get-tuple-element.164, f32[4,1024,1024]{1,2,0:T(8,128)} %get-tuple-element.152, f32[4,1024]{1,0:T(4,128)S(1)} %get-tuple-element.163, f32[4,1024]{1,0:T(4,128)S(1)} %log_add_fusion), kind=kLoop, calls=%fused_computation.9 | loop fusion | flops 16777216 | bytes 41975808 | tf_op jit(solution)/shard_map/while/body/eval_jaxpr/convert_element_type | solution.py:185
  1056.7 7.0 fusion.94
  1100.1 90.7 %reduce-scatter.15.cloned.1.call-done = bf16[1024,3072]{0,1:T(8,128)(2,1)} async-done(((bf16[1024,12288]{0,1:T(8,128)(2,1)}), bf16[1024,3072]{0,1:T(8,128)(2,1)}) %reduce-scatter.15.cloned.1.call-update) | async-done | bytes 6291472 | tf_op jit(solution)/shard_map/reduce_scatter | solution.py:435
  1190.8 8.6 copy.176
  1199.4 10.7 pad_maximum_fusion
  1210.1 11.4 gather_fusion.1
  1221.5 6.5 copy.177
  1228.1 7.3 fusion.1
  1242.5 38.5 %add_convert_fusion = bf16[768,1024]{1,0:T(8,128)(2,1)} fusion(f32[768,1024]{1,0:T(8,128)} %copy-done.23, bf16[1024,4096]{1,0:T(8,128)(2,1)} %bitcast.262, f32[768,4096]{1,0:T(8,128)} %get-tuple-element.166), kind=kOutput, calls=%fused_computation.143 | convolution fusion | flops 6648496128 | bytes 25690112 | tf_op jit(solution)/shard_map/dot_general | solution.py:31
  1291.6 44.1 %psum.7 = f32[4,1024]{1,0:T(4,128)S(1)} all-reduce(f32[4,1024]{1,0:T(4,128)S(1)} %pad_maximum_fusion.7), channel_id=1, replica_groups=mesh['dp'=8,'tensor'=4] {'dp','tensor'}, use_global_device_ids=true, to_apply=%region_26.27 | all-reduce | flops 4096 | bytes 32768 | tf_op jit(solution)/shard_map/psum | solution.py:447
  1339.9 104.3 %reduce-scatter.17.cloned.1.call-done = bf16[2,128,3072]{2,1,0:T(8,128)(2,1)} async-done(((bf16[2,1024,3072]{2,1,0:T(8,128)(2,1)}), bf16[2,128,3072]{2,1,0:T(8,128)(2,1)}) %reduce-scatter.17.cloned.1.call-update) | async-done | bytes 1572880 | tf_op jit(solution)/shard_map/reduce_scatter | solution.py:444
  1447.3 6.8 fusion.180
  1457.8 8.3 divide_bitcast_fusion
  1466.2 6.6 fusion.80
  (316 shorter events, 341.8 us)
Async XLA Ops:
  7.2 1440.1 %copy-start = (f32[2,24,128,128]{3,2,1,0:T(8,128)S(1)}, f32[2,24,128,128]{3,2,1,0:T(8,128)}, u32[]{:S(2)}) copy-start(f32[2,24,128,128]{3,2,1,0:T(8,128)} %param.24) | copy-start | bytes 9437188
  7.2 182.8 %all-gather.9.cloned.1.call-start = ((), (), s32[]{:S(2)}) async-start(), calls=%async_computation.7 | async-start | bytes 14155776 | tf_op jit(solution)/shard_map/all_gather | solution.py:361
  10.7 204.7 %all-gather.7.cloned.1.call-start = ((), (), s32[]{:S(2)}) async-start(), calls=%async_computation.6 | async-start | bytes 2621440 | tf_op jit(solution)/shard_map/all_gather | solution.py:367
  12.6 188.6 %copy-start.66 = (f32[256]{0:T(256)}, f32[256]{0:T(256)S(1)}, u32[]{:S(2)}) copy-start(f32[256]{0:T(256)S(1)} %get-tuple-element.148) | copy-start | bytes 3076
  13.2 265.1 %copy-start.40 = (f32[1,1024]{1,0:T(1,128)}, f32[1,1024]{1,0:T(1,128)S(1)}, u32[]{:S(2)}) copy-start(f32[1,1024]{1,0:T(1,128)S(1)} %get-tuple-element.143) | copy-start | bytes 12292
  13.2 572.4 %copy-start.59 = (f32[1,1024]{1,0:T(1,128)}, f32[1,1024]{1,0:T(1,128)S(1)}, u32[]{:S(2)}) copy-start(f32[1,1024]{1,0:T(1,128)S(1)} %get-tuple-element.142) | copy-start | bytes 12292
  15.8 260.4 %reduce-scatter.7.cloned.1.call-start = ((), (), s32[]{:S(2)}) async-start(), calls=%async_computation.8 | async-start | bytes 2621440 | tf_op jit(solution)/shard_map/reduce_scatter | solution.py:373
  219.5 15.6 %copy-start.25 = (bf16[1024,256]{0,1:T(8,128)(2,1)}, bf16[1024,256]{0,1:T(8,128)(2,1)S(1)}, u32[]{:S(2)}) copy-start(bf16[1024,256]{0,1:T(8,128)(2,1)S(1)} %get-tuple-element.140) | copy-start | bytes 1572868
  246.4 57.4 %all-gather.11.cloned.1.call-start = ((), (), s32[]{:S(2)}) async-start(), calls=%async_computation.9 | async-start | bytes 2621440 | tf_op jit(solution)/shard_map/all_gather | solution.py:367
  281.1 75.1 %reduce-scatter.9.cloned.1.call-start = ((), (), s32[]{:S(2)}) async-start(), calls=%async_computation.10 | async-start | bytes 2621440 | tf_op jit(solution)/shard_map/reduce_scatter | solution.py:373
  324.6 187.8 %all-gather.13.cloned.1.call-start = ((), (), s32[]{:S(2)}) async-start(), calls=%async_computation.11 | async-start | bytes 31457280 | tf_op jit(solution)/shard_map/all_gather | solution.py:407
  325.2 564.1 %all-gather.15.cloned.1.call-start = ((), (), s32[]{:S(2)}) async-start(), calls=%async_computation.12 | async-start | bytes 2621440 | tf_op jit(solution)/shard_map/all_gather | solution.py:370
  370.9 214.6 %copy-start.50 = (f32[768]{0:T(1024)}, f32[768]{0:T(1024)S(1)}, u32[]{:S(2)}) copy-start(f32[768]{0:T(1024)S(1)} %rsqrt.54) | copy-start | bytes 9220
  663.0 12.6 copy-start.2
  675.5 41.6 %slice-start.4 = ((s8[8388608]{0:T(1024)(128)(4,1)}), s8[4194304]{0:T(1024)(128)(4,1)S(1)}, s32[]{:S(2)}) async-start(s8[8388608]{0:T(1024)(128)(4,1)} %bitcast.263), calls=%async_computation.22 | async-start | bytes 8388608
  679.7 37.4 %copy-start.23 = (f32[768,1024]{1,0:T(8,128)}, f32[768,1024]{1,0:T(8,128)S(1)}, u32[]{:S(2)}) copy-start(f32[768,1024]{1,0:T(8,128)S(1)} %get-tuple-element.158) | copy-start | bytes 9437188
  680.3 63.0 %copy-start.55 = (f32[768]{0:T(1024)}, f32[768]{0:T(1024)S(1)}, u32[]{:S(2)}) copy-start(f32[768]{0:T(1024)S(1)} %get-tuple-element.146) | copy-start | bytes 9220
  680.3 36.8 %slice-start.5 = ((s8[8388608]{0:T(1024)(128)(4,1)}), s8[4194304]{0:T(1024)(128)(4,1)S(1)}, s32[]{:S(2)}) async-start(s8[8388608]{0:T(1024)(128)(4,1)} %bitcast.263), calls=%async_computation.23 | async-start | bytes 8388608
  717.1 14.3 copy-start.14
  717.1 14.3 copy-start.24
  731.4 11.9 copy-start.5
  731.4 11.9 copy-start.57
  756.1 15.3 %copy-start.26 = (f32[256,16,3]{2,1,0:T(8,128)S(1)}, f32[256,16,3]{2,1,0:T(8,128)}, u32[]{:S(2)}) copy-start(f32[256,16,3]{2,1,0:T(8,128)} %get-tuple-element.155) | copy-start | bytes 147460
  866.6 67.2 %reduce-scatter.11.cloned.1.call-start = ((), (), s32[]{:S(2)}) async-start(), calls=%async_computation.13 | async-start | bytes 2621440 | tf_op jit(solution)/shard_map/reduce_scatter | solution.py:381
  902.1 114.9 %all-gather.17.cloned.1.call-start = ((), (), s32[]{:S(2)}) async-start(), calls=%async_computation.14 | async-start | bytes 2621440 | tf_op jit(solution)/shard_map/all_gather | solution.py:370
  907.4 12.9 copy-start.4
  920.3 13.4 copy-start.41
  920.3 13.4 copy-start.53
  920.3 15.8 %copy-start.70 = (f32[256]{0:T(256)S(1)}, f32[256]{0:T(256)}, u32[]{:S(2)}) copy-start(f32[256]{0:T(256)} %get-tuple-element.149) | copy-start | bytes 3076
  939.0 251.8 %reduce-scatter.15.cloned.1.call-start = ((), (), s32[]{:S(2)}) async-start(), calls=%async_computation.16 | async-start | bytes 31457280 | tf_op jit(solution)/shard_map/reduce_scatter | solution.py:435
  1010.2 279.6 %reduce-scatter.13.cloned.1.call-start = ((), (), s32[]{:S(2)}) async-start(), calls=%async_computation.15 | async-start | bytes 2621440 | tf_op jit(solution)/shard_map/reduce_scatter | solution.py:381
  1038.8 17.9 %copy-start.20 = (bf16[1024,256]{0,1:T(8,128)(2,1)S(1)}, bf16[1024,256]{0,1:T(8,128)(2,1)}, u32[]{:S(2)}) copy-start(bf16[1024,256]{0,1:T(8,128)(2,1)} %copy-done.19) | copy-start | bytes 1572868
  1038.8 31.2 %slice-start = ((s8[16777216]{0:T(1024)(128)(4,1)}), s8[4194304]{0:T(1024)(128)(4,1)S(1)}, s32[]{:S(2)}) async-start(s8[16777216]{0:T(1024)(128)(4,1)} %bitcast.243), calls=%async_computation.18 | async-start | bytes 8388608
  1038.8 31.2 %slice-start.1 = ((s8[16777216]{0:T(1024)(128)(4,1)}), s8[4194304]{0:T(1024)(128)(4,1)S(1)}, s32[]{:S(2)}) async-start(s8[16777216]{0:T(1024)(128)(4,1)} %bitcast.243), calls=%async_computation.19 | async-start | bytes 8388608
  1038.8 31.2 %slice-start.2 = ((s8[16777216]{0:T(1024)(128)(4,1)}), s8[4194304]{0:T(1024)(128)(4,1)S(1)}, s32[]{:S(2)}) async-start(s8[16777216]{0:T(1024)(128)(4,1)} %bitcast.243), calls=%async_computation.20 | async-start | bytes 8388608
  1056.7 13.3 slice-start.3
  1078.5 365.7 %reduce-scatter.17.cloned.1.call-start = ((), (), s32[]{:S(2)}) async-start(), calls=%async_computation.17 | async-start | bytes 14155776 | tf_op jit(solution)/shard_map/reduce_scatter | solution.py:444
  1281.0 10.6 copy-start.63
  1281.0 54.7 %copy-start.46 = (f32[4,1024]{1,0:T(4,128)S(1)}, f32[4,1024]{1,0:T(4,128)}, u32[]{:S(2)}) copy-start(f32[4,1024]{1,0:T(4,128)} %param.25) | copy-start | bytes 49156
  1281.0 54.7 %copy-start.64 = (f32[4,1024]{1,0:T(4,128)S(1)}, f32[4,1024]{1,0:T(4,128)}, u32[]{:S(2)}) copy-start(f32[4,1024]{1,0:T(4,128)} %param.26) | copy-start | bytes 49156
  1281.0 54.6 %copy-start.65 = (f32[4,1024]{1,0:T(4,128)S(1)}, f32[4,1024]{1,0:T(4,128)}, u32[]{:S(2)}) copy-start(f32[4,1024]{1,0:T(4,128)} %param.27) | copy-start | bytes 49156
  1281.0 55.3 %copy-start.42 = (f32[1,1024]{1,0:T(1,128)S(1)}, f32[1,1024]{1,0:T(1,128)}, u32[]{:S(2)}) copy-start(f32[1,1024]{1,0:T(1,128)} %copy-done.40) | copy-start | bytes 12292
  1281.1 55.3 %copy-start.54 = (f32[256]{0:T(256)S(1)}, f32[256]{0:T(256)}, u32[]{:S(2)}) copy-start(f32[256]{0:T(256)} %copy-done.52) | copy-start | bytes 3076
  1281.1 55.3 %copy-start.69 = (f32[256]{0:T(256)S(1)}, f32[256]{0:T(256)}, u32[]{:S(2)}) copy-start(f32[256]{0:T(256)} %copy-done.68) | copy-start | bytes 3076
  1281.1 55.3 %copy-start.71 = (f32[256]{0:T(256)S(1)}, f32[256]{0:T(256)}, u32[]{:S(2)}) copy-start(f32[256]{0:T(256)} %get-tuple-element.149) | copy-start | bytes 3076
  1281.1 55.3 %copy-start.72 = (f32[256]{0:T(256)S(1)}, f32[256]{0:T(256)}, u32[]{:S(2)}) copy-start(f32[256]{0:T(256)} %get-tuple-element.147) | copy-start | bytes 3076
  1286.4 157.8 %copy-start.34 = (f32[2,128,128]{2,1,0:T(8,128)S(1)}, f32[2,128,128]{2,1,0:T(8,128)}, u32[]{:S(2)}) copy-start(f32[2,128,128]{2,1,0:T(8,128)} %param.23) | copy-start | bytes 393220
  1335.7 111.6 %copy-start.47 = (f32[4,1024]{1,0:T(4,128)}, f32[4,1024]{1,0:T(4,128)S(1)}, u32[]{:S(2)}) copy-start(f32[4,1024]{1,0:T(4,128)S(1)} %psum.7) | copy-start | bytes 49156
  (49 other events, 263.1 us)
Sparse Core Ops, SparseCore 0:
  10.8 179.1 all-gather.8
  192.1 20.7 all-gather.6
  246.6 29.6 reduce-scatter.6
  281.2 22.5 all-gather.10
  324.7 31.4 reduce-scatter.8
  357.6 154.7 all-gather.12
  866.7 22.5 all-gather.14
  902.2 31.4 reduce-scatter.10
  939.1 22.5 all-gather.16
  1010.3 180.4 reduce-scatter.14
  1193.9 31.4 reduce-scatter.12
  1235.5 208.6 reduce-scatter.16
where the time goes:
time: 1510 us; the launch traced here: 1500 us
  waiting for transfers between devices  596 us (39%)
  local copies, waits for them, and re-layouts  362 us (24%)
  matrix products  361 us (24%)
  other arithmetic  116 us (8%)
  blocking collectives  44.1 us (3%)
  between operations  16 us (1%)
    all_gather x1, waiting for transfers between devices, shards(): lax.all_gather(master.astype(jnp.bfloat16), 'dp', axis=1, tiled=True)  172 us
    all_gather x1, waiting for transfers between devices, shards(): local_layer = lax.all_gather(layers[1], 'tensor', axis=1, tiled=True)  141 us
    reduce_scatter x1, waiting for transfers between devices, shards(): lax.psum_scatter(ordered.astype(jnp.bfloat16), 'dp', scatter_dimension=1,...  104 us
    reduce_scatter x1, waiting for transfers between devices, shards(): lax.psum_scatter(local_grads.astype(jnp.bfloat16), 'tensor', scatter_dime...  90.7 us
    dot_general x8, matrix products, dot_rows(): return jnp.dot(left, right, preferred_element_type=jnp.float32)  86.6 us
    unnamed x193, local copies, waits for them, and re-layouts  85 us
    dot_general x8, matrix products, dot_transposed(): lax.dot_general(left, right, (((1,), (1,)), ((), ())), preferred_element_...  83.1 us
    dot_general x8, matrix products, dot_over_rows(): lax.dot_general(left, right, (((0,), (0,)), ((), ())), preferred_element_...  55 us
  transfers between devices with their start and end apart: 12, of which 9 were waited for; matrix products, arithmetic and copies ran while one was open for 24% of the time, Pallas kernels for 0%

commit v1 on v0

--- a/solution.py
+++ b/solution.py
@@ -3,6 +3,8 @@
 import jax
 import jax.numpy as jnp
 from jax import lax
+from jax.experimental import pallas as pl
+from jax.experimental.pallas import tpu as pltpu
 from jax.sharding import PartitionSpec as P
 
 D = 1024
@@ -336,7 +338,7 @@
     )
 
 
-def shards(
+def shards_any(
     frames_in,
     code_emb,
     cotangent,
@@ -487,9 +489,1412 @@
     )
 
 
+MIB = 1024 * 1024
+VMEM_WHOLE = pl.BlockSpec(memory_space=pltpu.VMEM)
+IN_SMEM = pl.BlockSpec(memory_space=pltpu.SMEM)
+IN_HBM = pl.BlockSpec(memory_space=pl.ANY)
+
+
+def shaped(shape, kind):
+    return jax.ShapeDtypeStruct(shape, kind)
+
+
+def cost(flops, moved, exps=0):
+    return pl.CostEstimate(flops=int(flops), bytes_accessed=int(moved), transcendentals=int(exps))
+
+
+def settings(limit=48):
+    return pltpu.CompilerParams(vmem_limit_bytes=limit * MIB)
+
+class Line:
+    def __init__(self):
+        self.token = None
+
+    def run(self, body, args, in_specs, out_specs, out_shape, aliases=None, **rest):
+        lead = 0 if self.token is None else 1
+        inputs, outputs = lead + len(args), len(out_shape)
+
+        def inner(*refs):
+            body(*refs[lead:inputs], *refs[inputs : inputs + outputs], *refs[inputs + outputs + 1 :])
+
+        found = pl.pallas_call(
+            inner,
+            in_specs=[IN_HBM] * lead + list(in_specs),
+            out_specs=list(out_specs) + [IN_HBM],
+            out_shape=list(out_shape) + [shaped((8, 128), jnp.float32)],
+            input_output_aliases={lead + at: to for at, to in (aliases or {}).items()},
+            cost_estimate=cost(1000, 1000),
+            **rest,
+        )(*([self.token] * lead), *args)
+        self.token = found[-1]
+        return list(found[:-1])
+
+
+def lanes_of(source_ref, at, width):
+    return pl.ds(pl.multiple_of(source_ref[at] * width, width), width)
+
+
+def norm_rows(rows, gain):
+    scale = lax.rsqrt(jnp.mean(rows * rows, axis=-1, keepdims=True) + norm_eps)
+    return rows * scale * gain
+
+
+def norm_rows_back(rows, gain, grad):
+    scale = lax.rsqrt(jnp.mean(rows * rows, axis=-1, keepdims=True) + norm_eps)
+    scaled = grad * gain
+    inner = jnp.sum(scaled * rows, axis=-1, keepdims=True)
+    grad_in = scale * scaled - rows * (scale * scale * scale) * inner / rows.shape[-1]
+    return grad_in, jnp.sum(grad * rows * scale, axis=0, keepdims=True)
+
+
+def gelu_both(upper):
+    size = jnp.abs(upper)
+    base = 1.0 + (0.3275911 / math.sqrt(2.0)) * size
+    guess = pl.reciprocal(base, approx=True)
+    ratio = guess * (2.0 - base * guess)
+    bell = jnp.exp(-0.5 * upper * upper)
+    series = ratio * (
+        0.5 * 0.254829592
+        + ratio
+        * (
+            -0.5 * 0.284496736
+            + ratio * (0.5 * 1.421413741 + ratio * (-0.5 * 1.453152027 + ratio * (0.5 * 1.061405429)))
+        )
+    )
+    tail = series * bell
+    cdf = jnp.where(upper >= 0.0, 1.0 - tail, tail)
+    density = bell * (1.0 / math.sqrt(2.0 * math.pi))
+    return (upper * cdf).astype(jnp.bfloat16), (cdf + upper * density).astype(jnp.bfloat16)
+
+
+def both(rows, near, far):
+    depth = near.shape[0]
+    return dot_rows(rows[:, :depth], near) + dot_rows(rows[:, depth:], far)
+
+
+def prep_body(source_ref, frames_ref, gains_ref, rows_ref, gains_out_ref, normed_ref):
+    owned = frames_ref.shape[1] // source_ref.shape[0]
+    for at in range(source_ref.shape[0]):
+        here = slice(at * owned, (at + 1) * owned)
+        rows_ref[:, here] = frames_ref[:, lanes_of(source_ref, at, owned)]
+        gains_out_ref[:, here] = gains_ref[:, lanes_of(source_ref, at, owned)]
+    normed_ref[...] = norm_rows(rows_ref[...].astype(jnp.float32), gains_out_ref[0:1, :]).astype(
+        jnp.bfloat16
+    )
+
+
+def prep(line, source, frames, gains):
+    return line.run(
+        prep_body,
+        (source, frames, gains,),
+        in_specs=[IN_SMEM, VMEM_WHOLE, VMEM_WHOLE],
+        out_specs=[VMEM_WHOLE] * 3,
+        out_shape=[
+            shaped(frames.shape, jnp.bfloat16),
+            shaped(gains.shape, jnp.float32),
+            shaped(frames.shape, jnp.bfloat16),
+        ],
+        compiler_params=settings(16),
+        name="prep_rows",
+    )
+
+
+def merge_body(which, base_ref, one_ref, two_ref, three_ref, gains_ref, middle_ref, normed_ref=None):
+    total = base_ref[...].astype(jnp.float32)
+    for ref in (one_ref, two_ref, three_ref):
+        total = total + ref[...].astype(jnp.float32)
+    middle_ref[...] = total
+    if normed_ref is not None:
+        normed_ref[...] = norm_rows(total, gains_ref[which : which + 1, :]).astype(jnp.bfloat16)
+
+
+def merge(line, base, terms, gains, which, normed=True):
+    outs = [shaped(base.shape, jnp.float32)]
+    if normed:
+        outs.append(shaped(base.shape, jnp.bfloat16))
+    return line.run(
+        lambda *refs: merge_body(which, *refs),
+        (base, *terms, gains,),
+        in_specs=[VMEM_WHOLE] * 5,
+        out_specs=[VMEM_WHOLE] * len(outs),
+        out_shape=outs,
+        compiler_params=settings(16),
+        name="merge_rows",
+    )
+
+
+def merge_back_body(
+    which, rows_ref, one_ref, two_ref, three_ref, grad_ref, gains_ref, total_ref, small_ref, gain_ref
+):
+    grad = one_ref[...].astype(jnp.float32)
+    for ref in (two_ref, three_ref):
+        grad = grad + ref[...].astype(jnp.float32)
+    part, gain_grad = norm_rows_back(
+        rows_ref[...].astype(jnp.float32), gains_ref[which : which + 1, :], grad
+    )
+    total = grad_ref[...] + part
+    total_ref[...] = total
+    small_ref[...] = total.astype(jnp.bfloat16)
+    gain_ref[...] = gain_grad
+
+
+def merge_back(line, rows, terms, grad, gains, which):
+    return line.run(
+        lambda *refs: merge_back_body(which, *refs),
+        (rows, *terms, grad, gains,),
+        in_specs=[VMEM_WHOLE] * 6,
+        out_specs=[VMEM_WHOLE] * 3,
+        out_shape=[
+            shaped(rows.shape, jnp.float32),
+            shaped(rows.shape, jnp.bfloat16),
+            shaped((1, rows.shape[1]), jnp.float32),
+        ],
+        compiler_params=settings(16),
+        name="merge_rows_back",
+    )
+
+
+def finish_body(
+    source_ref, rows_ref, one_ref, two_ref, three_ref, grad_ref, gains_ref, gb_ref, gc_ref, gd_ref,
+    out_ref, gain_ref,
+):
+    grad = one_ref[...].astype(jnp.float32)
+    for ref in (two_ref, three_ref):
+        grad = grad + ref[...].astype(jnp.float32)
+    part, gain_grad = norm_rows_back(rows_ref[...].astype(jnp.float32), gains_ref[0:1, :], grad)
+    total = grad_ref[...] + part
+    owned = out_ref.shape[1] // source_ref.shape[0]
+    for at in range(source_ref.shape[0]):
+        here = slice(at * owned, (at + 1) * owned)
+        there = lanes_of(source_ref, at, owned)
+        out_ref[:, there] = total[:, here]
+        gain_ref[0:1, there] = gain_grad[:, here]
+        gain_ref[1:2, there] = gb_ref[:, here]
+        gain_ref[2:3, there] = gc_ref[:, here]
+        gain_ref[3:4, there] = gd_ref[:, here]
+
+
+def finish(line, source, rows, terms, grad, gains, others):
+    return line.run(
+        finish_body,
+        (source, rows, *terms, grad, gains, *others,),
+        in_specs=[IN_SMEM] + [VMEM_WHOLE] * 9,
+        out_specs=[VMEM_WHOLE] * 2,
+        out_shape=[shaped(rows.shape, jnp.float32), shaped((4, rows.shape[1]), jnp.float32)],
+        compiler_params=settings(16),
+        name="input_grad",
+    )
+
+
+def global_heads_body(
+    info_ref, x0, x1, x2, x3, near_ref, far_ref, qkv_ref, mixed_ref, lse_ref, p0, p1, p2, p3, acc, lse_wide
+):
+    share = x0.shape[0]
+    span = 4 * share
+    width = mixed_ref.shape[1]
+    mine, length = info_ref[0], info_ref[1]
+    scale = HD ** (-0.5)
+    for rel, x_ref in enumerate((x0, x1, x2, x3)):
+        at = pl.ds(pl.multiple_of((mine ^ rel) * share, share), share)
+        full = both(x_ref[...], near_ref[:, : 3 * width], far_ref[:, : 3 * width])
+        qkv_ref[at, :] = full.astype(jnp.bfloat16)
+    acc[...] = jnp.zeros_like(acc)
+    lse_wide[...] = jnp.zeros_like(lse_wide)
+    head_of = lax.broadcasted_iota(jnp.int32, (1, width), 1) // HD
+    lane = lax.broadcasted_iota(jnp.int32, (1, 128), 1)
+
+    @pl.loop(0, width // HD)
+    def per_head(head):
+        own = head_of == head
+        for block in range(4):
+            rows = slice(block * share, (block + 1) * share)
+            reach = (block + 1) * share
+            query = jnp.where(own, qkv_ref[rows, :width] * scale, 0.0).astype(jnp.bfloat16)
+            scores = dot_transposed(query, qkv_ref[:reach, width : 2 * width])
+            row_at = block * share + lax.broadcasted_iota(jnp.int32, scores.shape, 0)
+            col_at = lax.broadcasted_iota(jnp.int32, scores.shape, 1)
+            scores = jnp.where((col_at <= row_at) & (col_at < length), scores, masked_fill)
+            top = jnp.max(scores, axis=-1, keepdims=True)
+            expanded = jnp.exp(scores - top)
+            total = jnp.sum(expanded, axis=-1, keepdims=True)
+            prob = (expanded * (1.0 / total)).astype(jnp.bfloat16)
+            value = jnp.where(own, qkv_ref[:reach, 2 * width :], 0.0).astype(jnp.bfloat16)
+            acc[rows, :] += dot_rows(prob, value)
+            lse_wide[rows, :] = jnp.where(lane == head, top + jnp.log(total), lse_wide[rows, :])
+
+    mixed_ref[...] = acc[...].astype(jnp.bfloat16)
+    lse_ref[...] = jnp.transpose(lse_wide[...])[: lse_ref.shape[0], :]
+    half = near_ref.shape[0]
+    for rel, p_ref in enumerate((p0, p1, p2, p3)):
+        at = pl.ds(pl.multiple_of((mine ^ rel) * share, share), share)
+        rows = mixed_ref[at, :]
+        p_ref[:, :half] = dot_transposed(rows, near_ref[:, 3 * width :]).astype(jnp.bfloat16)
+        p_ref[:, half:] = dot_transposed(rows, far_ref[:, 3 * width :]).astype(jnp.bfloat16)
+
+
+def global_heads(line, info, rows, halves):
+    share, width = rows[0].shape[0], halves[0].shape[1] // 4
+    span = 4 * share
+    return line.run(
+        global_heads_body,
+        (info, *rows, *halves,),
+        in_specs=[IN_SMEM] + [VMEM_WHOLE] * 6,
+        out_specs=[VMEM_WHOLE] * 7,
+        out_shape=[
+            shaped((span, 3 * width), jnp.bfloat16),
+            shaped((span, width), jnp.bfloat16),
+            shaped((8, span), jnp.float32),
+        ]
+        + [shaped((share, D), jnp.bfloat16)] * 4,
+        scratch_shapes=[pltpu.VMEM((span, width), jnp.float32), pltpu.VMEM((span, 128), jnp.float32)],
+        compiler_params=settings(40),
+        name="global_heads",
+    )
+
+
+def global_heads_back_body(
+    info_ref, g0, g1, g2, g3, near_ref, far_ref, qkv_ref, mixed_ref, lse_ref, dqkv_ref, p0, p1, p2, p3,
+    dmix, dq_t, dk_acc, dv_acc, center, k_t,
+):
+    share = g0.shape[0]
+    width = mixed_ref.shape[1]
+    heads = width // HD
+    mine, length = info_ref[0], info_ref[1]
+    scale = HD ** (-0.5)
+    for rel, g_ref in enumerate((g0, g1, g2, g3)):
+        at = pl.ds(pl.multiple_of((mine ^ rel) * share, share), share)
+        full = both(g_ref[...], near_ref[:, 3 * width :], far_ref[:, 3 * width :])
+        dmix[at, :] = full.astype(jnp.bfloat16)
+    head_of = lax.broadcasted_iota(jnp.int32, (1, width), 1) // HD
+    pick = (
+        lax.broadcasted_iota(jnp.int32, (8, width), 1) // HD
+        == lax.broadcasted_iota(jnp.int32, (8, width), 0)
+    ).astype(jnp.bfloat16)
+    product = dmix[...].astype(jnp.float32) * mixed_ref[...].astype(jnp.float32)
+    high = product.astype(jnp.bfloat16)
+    low = (product - high.astype(jnp.float32)).astype(jnp.bfloat16)
+    center[...] = dot_transposed(pick, high) + dot_transposed(pick, low)
+    k_t[...] = jnp.transpose(qkv_ref[:, width : 2 * width])
+    dq_t[...] = jnp.zeros_like(dq_t)
+    dk_acc[...] = jnp.zeros_like(dk_acc)
+    dv_acc[...] = jnp.zeros_like(dv_acc)
+    for head in range(heads):
+        own = head_of == head
+        for block in range(4):
+            rows = slice(block * share, (block + 1) * share)
+            reach = (block + 1) * share
+            query = jnp.where(own, qkv_ref[rows, :width] * scale, 0.0).astype(jnp.bfloat16)
+            grad = jnp.where(own, dmix[rows, :], 0.0).astype(jnp.bfloat16)
+            scores = dot_transposed(qkv_ref[:reach, width : 2 * width], query)
+            key_at = lax.broadcasted_iota(jnp.int32, scores.shape, 0)
+            row_at = block * share + lax.broadcasted_iota(jnp.int32, scores.shape, 1)
+            prob = jnp.where(
+                (key_at <= row_at) & (key_at < length),
+                jnp.exp(scores - lse_ref[head : head + 1, rows]),
+                0.0,
+            )
+            dprob = dot_transposed(qkv_ref[:reach, 2 * width :], grad)
+            dscore = (prob * (dprob - center[head : head + 1, rows])).astype(jnp.bfloat16)
+            dv_acc[:reach, :] += dot_rows(prob.astype(jnp.bfloat16), grad)
+            dk_acc[:reach, :] += dot_rows(dscore, query)
+            lanes = slice(head * HD, (head + 1) * HD)
+            dq_t[lanes, rows] += dot_rows(k_t[lanes, :reach], dscore)
+    dqkv_ref[:, :width] = (jnp.transpose(dq_t[...]) * scale).astype(jnp.bfloat16)
+    dqkv_ref[:, width : 2 * width] = dk_acc[...].astype(jnp.bfloat16)
+    dqkv_ref[:, 2 * width :] = dv_acc[...].astype(jnp.bfloat16)
+    half = near_ref.shape[0]
+    for rel, p_ref in enumerate((p0, p1, p2, p3)):
+        at = pl.ds(pl.multiple_of((mine ^ rel) * share, share), share)
+        rows = dqkv_ref[at, :]
+        p_ref[:, :half] = dot_transposed(rows, near_ref[:, : 3 * width]).astype(jnp.bfloat16)
+        p_ref[:, half:] = dot_transposed(rows, far_ref[:, : 3 * width]).astype(jnp.bfloat16)
+
+
+def global_heads_back(line, info, grads, halves, qkv, mixed, lse):
+    share, width = grads[0].shape[0], mixed.shape[1]
+    span = 4 * share
+    return line.run(
+        global_heads_back_body,
+        (info, *grads, *halves, qkv, mixed, lse,),
+        in_specs=[IN_SMEM] + [VMEM_WHOLE] * 9,
+        out_specs=[VMEM_WHOLE] * 5,
+        out_shape=[shaped((span, 3 * width), jnp.bfloat16)]
+        + [shaped((share, D), jnp.bfloat16)] * 4,
+        scratch_shapes=[
+            pltpu.VMEM((span, width), jnp.bfloat16),
+            pltpu.VMEM((width, span), jnp.float32),
+            pltpu.VMEM((span, width), jnp.float32),
+            pltpu.VMEM((span, width), jnp.float32),
+            pltpu.VMEM((8, span), jnp.float32),
+            pltpu.VMEM((width, span), jnp.bfloat16),
+        ],
+        compiler_params=settings(40),
+        name="global_heads_back",
+    )
+
+
+def global_grads_heads_body(
+    info_ref, a0, a1, a2, a3, g0, g1, g2, g3, dqkv_ref, mixed_ref, near_ref, far_ref, a_t, g_t
+):
+    share = a0.shape[0]
+    width = mixed_ref.shape[1]
+    mine = info_ref[0]
+    for rel in range(4):
+        at = pl.ds(pl.multiple_of((mine ^ rel) * share, share), share)
+        a_t[:, at] = jnp.transpose((a0, a1, a2, a3)[rel][...])
+        g_t[:, at] = jnp.transpose((g0, g1, g2, g3)[rel][...])
+
+    for at in range(D // 256):
+        rows = slice(at * 256, (at + 1) * 256)
+        out_ref, begin = (near_ref, 0) if at * 256 < D // 2 else (far_ref, D // 2)
+        there = slice(at * 256 - begin, at * 256 - begin + 256)
+        out_ref[there, : 3 * width] = dot_rows(a_t[rows, :], dqkv_ref[...]).astype(jnp.bfloat16)
+        out_ref[there, 3 * width :] = dot_rows(g_t[rows, :], mixed_ref[...]).astype(jnp.bfloat16)
+
+
+def global_grads_heads(line, info, normed, grads, dqkv, mixed):
+    span, width = mixed.shape
+    return line.run(
+        global_grads_heads_body,
+        (info, *normed, *grads, dqkv, mixed,),
+        in_specs=[IN_SMEM] + [VMEM_WHOLE] * 10,
+        out_specs=[VMEM_WHOLE] * 2,
+        out_shape=[shaped((D // 2, 4 * width), jnp.bfloat16)] * 2,
+        scratch_shapes=[pltpu.VMEM((D, span), jnp.bfloat16)] * 2,
+        compiler_params=settings(40),
+        name="global_heads_grads",
+    )
+
+
+def global_ff_body(x0, x1, x2, x3, up0, up1, down0, down1, active_ref, slope_ref, p0, p1, p2, p3, acc):
+    step = pl.program_id(0)
+    share = x0.shape[0]
+    half = up0.shape[0]
+
+    @pl.when(step == 0)
+    def _():
+        acc[...] = jnp.zeros_like(acc)
+
+    for rel, x_ref in enumerate((x0, x1, x2, x3)):
+        rows = slice(rel * share, (rel + 1) * share)
+        active, slope = gelu_both(both(x_ref[...], up0[...], up1[...]))
+        active_ref[rows, :] = active
+        slope_ref[rows, :] = slope
+        for at, down in enumerate((down0, down1)):
+            lanes = slice(at * half, (at + 1) * half)
+            acc[rows, lanes] += dot_transposed(active, down[...])
+
+    @pl.when(step == pl.num_programs(0) - 1)
+    def _():
+        for rel, p_ref in enumerate((p0, p1, p2, p3)):
+            p_ref[...] = acc[rel * share : (rel + 1) * share, :].astype(jnp.bfloat16)
+
+
+def held(shape):
+    return pl.BlockSpec(shape, lambda step: (0,) * len(shape), pipeline_mode=pl.Buffered(1))
+
+
+def by_cols(shape):
+    return pl.BlockSpec(shape, lambda step: (0, step))
+
+
+def global_ff(line, rows, up, down, tile=256):
+    share = rows[0].shape[0]
+    span, hidden, half = 4 * share, up[0].shape[1], up[0].shape[0]
+    return line.run(
+        global_ff_body,
+        (*rows, *up, *down,),
+        grid=(hidden // tile,),
+        in_specs=[held((share, D))] * 4 + [by_cols((half, tile))] * 4,
+        out_specs=[by_cols((span, tile))] * 2 + [held((share, D))] * 4,
+        out_shape=[shaped((span, hidden), jnp.bfloat16)] * 2
+        + [shaped((share, D), jnp.bfloat16)] * 4,
+        scratch_shapes=[pltpu.VMEM((span, D), jnp.float32)],
+        compiler_params=settings(40),
+        name="global_ff",
+    )
+
+
+def global_ff_back_body(g0, g1, g2, g3, slope_ref, up0, up1, down0, down1, dup_ref, p0, p1, p2, p3, acc):
+    step = pl.program_id(0)
+    share = g0.shape[0]
+    half = up0.shape[0]
+
+    @pl.when(step == 0)
+    def _():
+        acc[...] = jnp.zeros_like(acc)
+
+    for rel, g_ref in enumerate((g0, g1, g2, g3)):
+        rows = slice(rel * share, (rel + 1) * share)
+        grad = both(g_ref[...], down0[...], down1[...])
+        dup = (grad * slope_ref[rows, :].astype(jnp.float32)).astype(jnp.bfloat16)
+        dup_ref[rows, :] = dup
+        for at, up in enumerate((up0, up1)):
+            lanes = slice(at * half, (at + 1) * half)
+            acc[rows, lanes] += dot_transposed(dup, up[...])
+
+    @pl.when(step == pl.num_programs(0) - 1)
+    def _():
+        for rel, p_ref in enumerate((p0, p1, p2, p3)):
+            p_ref[...] = acc[rel * share : (rel + 1) * share, :].astype(jnp.bfloat16)
+
+
+def global_ff_back(line, grads, slope, up, down, tile=256):
+    share = grads[0].shape[0]
+    span, hidden, half = 4 * share, up[0].shape[1], up[0].shape[0]
+    return line.run(
+        global_ff_back_body,
+        (*grads, slope, *up, *down,),
+        grid=(hidden // tile,),
+        in_specs=[held((share, D))] * 4 + [by_cols((span, tile))] + [by_cols((half, tile))] * 4,
+        out_specs=[by_cols((span, tile))] + [held((share, D))] * 4,
+        out_shape=[shaped((span, hidden), jnp.bfloat16)] + [shaped((share, D), jnp.bfloat16)] * 4,
+        scratch_shapes=[pltpu.VMEM((span, D), jnp.float32)],
+        compiler_params=settings(40),
+        name="global_ff_back",
+    )
+
+
+def outer_body(r0, r1, r2, r3, right_ref, near_ref, far_ref, left_t):
+    share = r0.shape[0]
+
+    @pl.when(pl.program_id(0) == 0)
+    def _():
+        for rel, ref in enumerate((r0, r1, r2, r3)):
+            left_t[:, rel * share : (rel + 1) * share] = jnp.transpose(ref[...])
+
+    for at in range(D // 256):
+        rows = slice(at * 256, (at + 1) * 256)
+        out_ref, begin = (near_ref, 0) if at * 256 < D // 2 else (far_ref, D // 2)
+        out_ref[at * 256 - begin : at * 256 - begin + 256, :] = dot_rows(
+            left_t[rows, :], right_ref[...]
+        ).astype(jnp.bfloat16)
+
+
+def global_outer(line, rows, right, tile=256):
+    share = rows[0].shape[0]
+    span, hidden = right.shape
+    return line.run(
+        outer_body,
+        (*rows, right,),
+        grid=(hidden // tile,),
+        in_specs=[held((share, D))] * 4 + [by_cols((span, tile))],
+        out_specs=[by_cols((D // 2, tile))] * 2,
+        out_shape=[shaped((D // 2, hidden), jnp.bfloat16)] * 2,
+        scratch_shapes=[pltpu.VMEM((D, span), jnp.bfloat16)],
+        compiler_params=settings(32),
+        name="global_ff_grads",
+    )
+
+
+def head_sums(width):
+    row_at = lax.broadcasted_iota(jnp.int32, (width, width), 0) // HD
+    col_at = lax.broadcasted_iota(jnp.int32, (width, width), 1) // HD
+    return (row_at == col_at).astype(jnp.bfloat16)
+
+
+def over_heads(product, ones):
+    high = product.astype(jnp.bfloat16)
+    low = (product - high.astype(jnp.float32)).astype(jnp.bfloat16)
+    return dot_rows(high, ones) + dot_rows(low, ones)
+
+
+def frame_probs(queries, keys, ones):
+    found = []
+    for at in range(CB):
+        scores = [over_heads(queries[at] * keys[c2], ones) * HD ** (-0.5) for c2 in range(at + 1)]
+        top = scores[0]
+        for one in scores[1:]:
+            top = jnp.maximum(top, one)
+        expanded = [jnp.exp(one - top) for one in scores]
+        total = expanded[0]
+        for one in expanded[1:]:
+            total = total + one
+        inverse = 1.0 / total
+        found.append([one * inverse for one in expanded])
+    return found
+
+
+def rounded_f32(values):
+    return values.astype(jnp.bfloat16).astype(jnp.float32)
+
+
+def start_weights(parts, buffer, sems):
+    for at, pair in enumerate(parts):
+        for half, ref in enumerate(pair):
+            pltpu.make_async_copy(ref, buffer.at[at, half], sems.at[at, half]).start()
+
+
+def wait_weights(parts, buffer, sems, at):
+    for half in range(2):
+        pltpu.make_async_copy(parts[0][half], buffer.at[at, half], sems.at[at, half]).wait()
+
+
+def local_heads_body(
+    source_ref, out_ref_in, code_ref, gains_ref, *refs
+):
+    count = 4
+    parts = [refs[2 * at : 2 * at + 2] for at in range(count)]
+    qkv_ref, mixed_ref, middle_ref, normed_b_ref, a_t_ref, normed_a, local_in, buffer, sems = refs[2 * count :]
+    step = pl.program_id(0)
+    frames = out_ref_in.shape[0]
+    width = mixed_ref.shape[2]
+    half = D // 2
+
+    @pl.when(step == 0)
+    def _():
+        start_weights(parts, buffer, sems)
+        owned = D // source_ref.shape[0]
+        for c in range(CB):
+            rows = slice(c * frames, (c + 1) * frames)
+            for at in range(source_ref.shape[0]):
+                here = slice(at * owned, (at + 1) * owned)
+                local_in[rows, here] = out_ref_in[:, here] + code_ref[
+                    c, :, lanes_of(source_ref, at, owned)
+                ].astype(jnp.float32)
+            normed = norm_rows(local_in[rows, :], gains_ref[2:3, :]).astype(jnp.bfloat16)
+            normed_a[rows, :] = normed
+            a_t_ref[:, rows] = jnp.transpose(normed)
+        middle_ref[...] = local_in[...]
+
+    wait_weights(parts, buffer, sems, step)
+    ones = head_sums(width)
+    queries, keys, values = ([], [], [])
+    for c in range(CB):
+        rows = slice(c * frames, (c + 1) * frames)
+        qkv = (
+            dot_rows(normed_a[rows, :half], buffer[step, 0, :, : 3 * width])
+            + dot_rows(normed_a[rows, half:], buffer[step, 1, :, : 3 * width])
+        ).astype(jnp.bfloat16)
+        qkv_ref[0, rows, :] = qkv
+        queries.append(qkv[:, :width].astype(jnp.float32))
+        keys.append(qkv[:, width : 2 * width].astype(jnp.float32))
+        values.append(qkv[:, 2 * width :].astype(jnp.float32))
+    prob = frame_probs(queries, keys, ones)
+    for c in range(CB):
+        rows = slice(c * frames, (c + 1) * frames)
+        mix = rounded_f32(prob[c][0]) * values[0]
+        for c2 in range(1, c + 1):
+            mix = mix + rounded_f32(prob[c][c2]) * values[c2]
+        mix = mix.astype(jnp.bfloat16)
+        mixed_ref[0, rows, :] = mix
+        for at in range(2):
+            lanes = slice(at * half, (at + 1) * half)
+            middle_ref[rows, lanes] += dot_transposed(mix, buffer[step, at, :, 3 * width :])
+
+    @pl.when(step == count - 1)
+    def _():
+        for c in range(CB):
+            rows = slice(c * frames, (c + 1) * frames)
+            normed_b_ref[rows, :] = norm_rows(middle_ref[rows, :], gains_ref[3:4, :]).astype(
+                jnp.bfloat16
+            )
+
+
+def local_heads(line, source, global_out, codes, gains, parts):
+    frames = global_out.shape[0]
+    rows = CB * frames
+    width = parts[0][0].shape[1] // 4
+    half = D // 2
+    flat = [ref for pair in parts for ref in pair]
+    return line.run(
+        local_heads_body,
+        (source, global_out, codes, gains, *flat,),
+        grid=(4,),
+        in_specs=[IN_SMEM, held((frames, D)), held((CB, frames, D)), held((4, D))] + [IN_HBM] * 8,
+        out_specs=[
+            pl.BlockSpec((1, rows, 3 * width), lambda step: (step, 0, 0)),
+            pl.BlockSpec((1, rows, width), lambda step: (step, 0, 0)),
+            held((rows, D)),
+            held((rows, D)),
+            held((D, rows)),
+        ],
+        out_shape=[
+            shaped((4, rows, 3 * width), jnp.bfloat16),
+            shaped((4, rows, width), jnp.bfloat16),
+            shaped((rows, D), jnp.float32),
+            shaped((rows, D), jnp.bfloat16),
+            shaped((D, rows), jnp.bfloat16),
+        ],
+        scratch_shapes=[
+            pltpu.VMEM((rows, D), jnp.bfloat16),
+            pltpu.VMEM((rows, D), jnp.float32),
+            pltpu.VMEM((4, 2, half, 4 * width), jnp.bfloat16),
+            pltpu.SemaphoreType.DMA((4, 2)),
+        ],
+        compiler_params=settings(52),
+        name="local_heads",
+    )
+
+
+def local_ff_body(source_ref, normed_ref, middle_ref, *refs):
+    count = 4
+    ups = [refs[2 * at : 2 * at + 2] for at in range(count)]
+    downs = [refs[2 * count + 2 * at : 2 * count + 2 * at + 2] for at in range(count)]
+    active_ref, slope_ref, out_ref, b_t_ref, acc, up_buf, down_buf, up_sems, down_sems = refs[4 * count :]
+    step = pl.program_id(0)
+    rows_all = normed_ref.shape[0]
+    frames = rows_all // CB
+    half = D // 2
+    tile = active_ref.shape[2]
+    per = up_buf.shape[3] // tile
+    group = step // per
+    cols_at = pl.ds(pl.multiple_of((step % per) * tile, tile), tile)
+
+    @pl.when(step == 0)
+    def _():
+        for at in range(count):
+            start_weights_at(ups, up_buf, up_sems, at)
+            start_weights_at(downs, down_buf, down_sems, at)
+        b_t_ref[...] = jnp.transpose(normed_ref[...])
+        acc[...] = middle_ref[...]
+
+    @pl.when(step % per == 0)
+    def _():
+        wait_weights(ups, up_buf, up_sems, group)
+        wait_weights(downs, down_buf, down_sems, group)
+
+    for c in range(CB):
+        rows = slice(c * frames, (c + 1) * frames)
+        upper = dot_rows(normed_ref[rows, :half], up_buf[group, 0, :, cols_at]) + dot_rows(
+            normed_ref[rows, half:], up_buf[group, 1, :, cols_at]
+        )
+        active, slope = gelu_both(upper)
+        active_ref[0, rows, :] = active
+        slope_ref[0, rows, :] = slope
+        for at in range(2):
+            lanes = slice(at * half, (at + 1) * half)
+            acc[rows, lanes] += dot_transposed(active, down_buf[group, at, :, cols_at])
+
+    @pl.when(step == pl.num_programs(0) - 1)
+    def _():
+        owned = D // source_ref.shape[0]
+        for c in range(CB):
+            rows = slice(c * frames, (c + 1) * frames)
+            for at in range(source_ref.shape[0]):
+                here = slice(at * owned, (at + 1) * owned)
+                out_ref[c, :, lanes_of(source_ref, at, owned)] = acc[rows, here].astype(jnp.bfloat16)
+
+
+def start_weights_at(parts, buffer, sems, at):
+    for half in range(2):
+        pltpu.make_async_copy(parts[at][half], buffer.at[at, half], sems.at[at, half]).start()
+
+
+def local_ff(line, source, normed, middle, ups, downs, tile=512):
+    rows = normed.shape[0]
+    hidden = ups[0][0].shape[1]
+    half = D // 2
+    per = hidden // tile
+    flat = [ref for pair in ups for ref in pair] + [ref for pair in downs for ref in pair]
+    hidden_block = pl.BlockSpec((1, rows, tile), lambda step: (step // per, 0, step % per))
+    return line.run(
+        local_ff_body,
+        (source, normed, middle, *flat,),
+        grid=(4 * per,),
+        in_specs=[IN_SMEM, held((rows, D)), held((rows, D))] + [IN_HBM] * 16,
+        out_specs=[hidden_block, hidden_block, held((CB, rows // CB, D)), held((D, rows))],
+        out_shape=[
+            shaped((4, rows, hidden), jnp.bfloat16),
+            shaped((4, rows, hidden), jnp.bfloat16),
+            shaped((CB, rows // CB, D), jnp.bfloat16),
+            shaped((D, rows), jnp.bfloat16),
+        ],
+        scratch_shapes=[
+            pltpu.VMEM((rows, D), jnp.float32),
+            pltpu.VMEM((4, 2, half, hidden), jnp.bfloat16),
+            pltpu.VMEM((4, 2, half, hidden), jnp.bfloat16),
+            pltpu.SemaphoreType.DMA((4, 2)),
+            pltpu.SemaphoreType.DMA((4, 2)),
+        ],
+        compiler_params=settings(56),
+        name="local_ff",
+    )
+
+
+def seed_body(source_ref, count_ref, cot_ref, grad_ref, grad_t_ref):
+    frames = cot_ref.shape[1]
+    owned = D // source_ref.shape[0]
+    keep = lax.broadcasted_iota(jnp.int32, (frames, 1), 0) < count_ref[0]
+    for c in range(CB):
+        rows = slice(c * frames, (c + 1) * frames)
+        for at in range(source_ref.shape[0]):
+            here = slice(at * owned, (at + 1) * owned)
+            values = cot_ref[c, :, lanes_of(source_ref, at, owned)].astype(jnp.float32)
+            grad_ref[rows, here] = jnp.where(keep, values, 0.0).astype(jnp.bfloat16)
+        grad_t_ref[:, rows] = jnp.transpose(grad_ref[rows, :])
+
+
+def seed(line, source, count, cot):
+    frames = cot.shape[1]
+    rows = CB * frames
+    return line.run(
+        seed_body,
+        (source, count, cot,),
+        in_specs=[IN_SMEM, IN_SMEM, VMEM_WHOLE],
+        out_specs=[VMEM_WHOLE] * 2,
+        out_shape=[shaped((rows, D), jnp.bfloat16), shaped((D, rows), jnp.bfloat16)],
+        compiler_params=settings(24),
+        name="seed_grads",
+    )
+
+
+def local_ff_back_body(last, summed, first, grad_ref, grad_t_ref, b_t_ref, active_ref, slope_ref, up0, up1, down0, down1, *refs):
+    if summed:
+        met_ref, refs = refs[0], refs[1:]
+    so_far_ref, refs = (None, refs) if first else (refs[0], refs[1:])
+    if last:
+        middle_ref, gains_ref, refs = refs[0], refs[1], refs[2:]
+    if summed:
+        down_near, down_far, g_up, refs = refs[0], refs[1], refs[2], refs[3:]
+    else:
+        both_ref, refs = refs[0], refs[1:]
+    outs, (acc, dup) = refs[:-2], refs[-2:]
+    step = pl.program_id(0)
+    frames = grad_ref.shape[0] // CB
+    half = D // 2
+
+    @pl.when(step == 0)
+    def _():
+        if so_far_ref is not None:
+            acc[...] = so_far_ref[...]
+        else:
+            acc[...] = jnp.zeros_like(acc)
+
+    for c in range(CB):
+        rows = slice(c * frames, (c + 1) * frames)
+        grad = dot_rows(grad_ref[rows, :half], down0[...]) + dot_rows(grad_ref[rows, half:], down1[...])
+        one = (grad * slope_ref[0, rows, :].astype(jnp.float32)).astype(jnp.bfloat16)
+        dup[rows, :] = one
+        for at, up in enumerate((up0, up1)):
+            lanes = slice(at * half, (at + 1) * half)
+            acc[rows, lanes] += dot_transposed(one, up[...])
+    for at in range(D // 256):
+        rows = slice(at * 256, (at + 1) * 256)
+        down = dot_rows(grad_t_ref[rows, :], active_ref[0])
+        up = dot_rows(b_t_ref[rows, :], dup[...])
+        if summed:
+            down = (down + met_ref[0, rows, :].astype(jnp.float32)).astype(jnp.bfloat16)
+            if at * 256 < half:
+                down_near[rows, :] = down
+            else:
+                down_far[at * 256 - half : at * 256 - half + 256, :] = down
+            g_up[rows, :] = (up + met_ref[1, rows, :].astype(jnp.float32)).astype(jnp.bfloat16)
+        else:
+            both_ref[0, rows, :] = down.astype(jnp.bfloat16)
+            both_ref[1, rows, :] = up.astype(jnp.bfloat16)
+
+    @pl.when(step == pl.num_programs(0) - 1)
+    def _():
+        if last:
+            grad_mid_ref, small_ref, small_t_ref, gain_ref = outs
+            total_gain = jnp.zeros((1, D), jnp.float32)
+            for c in range(CB):
+                rows = slice(c * frames, (c + 1) * frames)
+                part, gain_grad = norm_rows_back(middle_ref[rows, :], gains_ref[3:4, :], acc[rows, :])
+                total = grad_ref[rows, :].astype(jnp.float32) + part
+                grad_mid_ref[rows, :] = total
+                small = total.astype(jnp.bfloat16)
+                small_ref[rows, :] = small
+                small_t_ref[:, rows] = jnp.transpose(small)
+                total_gain = total_gain + gain_grad
+            gain_ref[...] = total_gain
+        else:
+            outs[0][...] = acc[...]
+
+
+def local_ff_back(line, rel, grad, grad_t, b_t, active, slope, up, down, met=None, so_far=None, tail=None, tile=512):
+    rows = grad.shape[0]
+    hidden = active.shape[2]
+    half = D // 2
+    last, summed = tail is not None, met is not None
+    hidden_block = pl.BlockSpec((1, rows, tile), lambda step: (rel, 0, step))
+    pair_block = pl.BlockSpec((2, D, tile), lambda step: (0, 0, step))
+    extra_args, extra = ([], [])
+    if summed:
+        extra_args.append(met)
+        extra.append(pair_block)
+    if so_far is not None:
+        extra_args.append(so_far)
+        extra.append(held((rows, D)))
+    first = so_far is None
+    if last:
+        extra_args += list(tail)
+        extra += [held((rows, D)), held((4, D))]
+        outs = [
+            shaped((rows, D), jnp.float32),
+            shaped((rows, D), jnp.bfloat16),
+            shaped((D, rows), jnp.bfloat16),
+            shaped((1, D), jnp.float32),
+        ]
+    else:
+        outs = [shaped((rows, D), jnp.float32)]
+    if summed:
+        grad_specs = [by_cols((half, tile)), by_cols((half, tile)), by_cols((D, tile))]
+        grad_shapes = [shaped((half, hidden), jnp.bfloat16)] * 2 + [shaped((D, hidden), jnp.bfloat16)]
+    else:
+        grad_specs = [pair_block]
+        grad_shapes = [shaped((2, D, hidden), jnp.bfloat16)]
+
+    def body(*refs):
+        local_ff_back_body(last, summed, first, *refs)
+
+    found = line.run(
+        body,
+        (grad, grad_t, b_t, active, slope, *up, *down, *extra_args),
+        grid=(hidden // tile,),
+        in_specs=[held((rows, D)), held((D, rows)), held((D, rows)), hidden_block, hidden_block]
+        + [by_cols((half, tile))] * 4
+        + extra,
+        out_specs=grad_specs + [held(one.shape) for one in outs],
+        out_shape=grad_shapes + outs,
+        scratch_shapes=[pltpu.VMEM((rows, D), jnp.float32), pltpu.VMEM((rows, tile), jnp.bfloat16)],
+        compiler_params=settings(52),
+        name="local_ff_back",
+    )
+    return found[: len(grad_shapes)], found[len(grad_shapes) :]
+
+
+def local_heads_back_body(last, summed, first, grad_ref, grad_t_ref, a_t_ref, qkv_ref, mixed_ref, near_ref, far_ref, *refs):
+    if summed:
+        met_ref, refs = refs[0], refs[1:]
+    if not first:
+        so_far_ref, refs = refs[0], refs[1:]
+    if last:
+        grad_mid_ref, out_in_ref, code_ref, source_ref, gains_ref = refs[:5]
+        refs = refs[5:]
+    out_ref, refs = refs[0], refs[1:]
+    outs, (acc, dqkv) = refs[:-2], refs[-2:]
+    frames = grad_ref.shape[0] // CB
+    width = mixed_ref.shape[2]
+    half = D // 2
+    scale = HD ** (-0.5)
+    ones = head_sums(width)
+    queries, keys, values, dmix = ([], [], [], [])
+    for c in range(CB):
+        rows = slice(c * frames, (c + 1) * frames)
+        qkv = qkv_ref[0, rows, :].astype(jnp.float32)
+        queries.append(qkv[:, :width])
+        keys.append(qkv[:, width : 2 * width])
+        values.append(qkv[:, 2 * width :])
+        one = dot_rows(grad_ref[rows, :half], near_ref[:, 3 * width :]) + dot_rows(
+            grad_ref[rows, half:], far_ref[:, 3 * width :]
+        )
+        dmix.append(rounded_f32(one))
+    prob = frame_probs(queries, keys, ones)
+    dq, dk, dv = ([None] * CB, [None] * CB, [None] * CB)
+
+    def more(total, term):
+        return term if total is None else total + term
+
+    for c in range(CB):
+        dprob = [over_heads(dmix[c] * values[c2], ones) for c2 in range(c + 1)]
+        center = prob[c][0] * dprob[0]
+        for c2 in range(1, c + 1):
+            center = center + prob[c][c2] * dprob[c2]
+        for c2 in range(c + 1):
+            dv[c2] = more(dv[c2], rounded_f32(prob[c][c2]) * dmix[c])
+            dscore = rounded_f32(prob[c][c2] * (dprob[c2] - center))
+            dq[c] = more(dq[c], dscore * keys[c2])
+            dk[c2] = more(dk[c2], dscore * queries[c])
+    for c in range(CB):
+        rows = slice(c * frames, (c + 1) * frames)
+        dqkv[rows, :width] = (dq[c] * scale).astype(jnp.bfloat16)
+        dqkv[rows, width : 2 * width] = (dk[c] * scale).astype(jnp.bfloat16)
+        dqkv[rows, 2 * width :] = dv[c].astype(jnp.bfloat16)
+        for at, ref in enumerate((near_ref, far_ref)):
+            lanes = slice(at * half, (at + 1) * half)
+            term = dot_transposed(dqkv[rows, :], ref[:, : 3 * width])
+            acc[rows, lanes] = term if first else so_far_ref[rows, lanes] + term
+    for at in range(D // 256):
+        rows = slice(at * 256, (at + 1) * 256)
+        three = dot_rows(a_t_ref[rows, :], dqkv[...])
+        one = dot_rows(grad_t_ref[rows, :], mixed_ref[0])
+        if summed:
+            three = three + met_ref[rows, : 3 * width].astype(jnp.float32)
+            one = one + met_ref[rows, 3 * width :].astype(jnp.float32)
+        out_ref[rows, : 3 * width] = three.astype(jnp.bfloat16)
+        out_ref[rows, 3 * width :] = one.astype(jnp.bfloat16)
+    if last:
+        total_ref, small_ref, gain_ref = outs
+        owned = D // source_ref.shape[0]
+        total_gain = jnp.zeros((1, D), jnp.float32)
+        total = jnp.zeros((frames, D), jnp.float32)
+        for c in range(CB):
+            rows = slice(c * frames, (c + 1) * frames)
+            local_in = jnp.concatenate(
+                [
+                    out_in_ref[:, at * owned : (at + 1) * owned]
+                    + code_ref[c, :, lanes_of(source_ref, at, owned)].astype(jnp.float32)
+                    for at in range(source_ref.shape[0])
+                ],
+                axis=1,
+            )
+            part, gain_grad = norm_rows_back(local_in, gains_ref[2:3, :], acc[rows, :])
+            total = total + (grad_mid_ref[rows, :] + part)
+            total_gain = total_gain + gain_grad
+        total_ref[...] = total
+        small_ref[...] = total.astype(jnp.bfloat16)
+        gain_ref[...] = total_gain
+    else:
+        outs[0][...] = acc[...]
+
+
+def local_heads_back(line, rel, grad, grad_t, a_t, qkv, mixed, halves, met=None, so_far=None, tail=None):
+    rows = grad.shape[0]
+    frames = rows // CB
+    width = mixed.shape[2]
+    last, summed, first = tail is not None, met is not None, so_far is None
+    extra_args, extra = ([], [])
+    if summed:
+        extra_args.append(met)
+        extra.append(held((D, 4 * width)))
+    if not first:
+        extra_args.append(so_far)
+        extra.append(held((rows, D)))
+    if last:
+        extra_args += list(tail)
+        extra += [held((rows, D)), held((frames, D)), held((CB, frames, D)), IN_SMEM, held((4, D))]
+        outs = [
+            shaped((frames, D), jnp.float32),
+            shaped((frames, D), jnp.bfloat16),
+            shaped((1, D), jnp.float32),
+        ]
+    else:
+        outs = [shaped((rows, D), jnp.float32)]
+
+    def body(*refs):
+        local_heads_back_body(last, summed, first, *refs)
+
+    found = line.run(
+        body,
+        (grad, grad_t, a_t, qkv, mixed, *halves, *extra_args),
+        grid=(1,),
+        in_specs=[
+            held((rows, D)),
+            held((D, rows)),
+            held((D, rows)),
+            pl.BlockSpec((1, rows, 3 * width), lambda step: (rel, 0, 0)),
+            pl.BlockSpec((1, rows, width), lambda step: (rel, 0, 0)),
+        ]
+        + [held((D // 2, 4 * width))] * 2
+        + extra,
+        out_specs=[held((D, 4 * width))] + [held(one.shape) for one in outs],
+        out_shape=[shaped((D, 4 * width), jnp.bfloat16)] + outs,
+        scratch_shapes=[
+            pltpu.VMEM((rows, D), jnp.float32),
+            pltpu.VMEM((rows, 3 * width), jnp.bfloat16),
+        ],
+        compiler_params=settings(52),
+        name="local_heads_back",
+    )
+    return found[0], found[1:]
+
+
+def cast_body(master_ref, out_ref):
+    out_ref[...] = master_ref[0].astype(jnp.bfloat16)
+
+
+def cast(line, master, layer, third):
+    owned, columns = master.shape[1], master.shape[2] // 3
+    return line.run(
+        cast_body,
+        (master,),
+        grid=(1,),
+        in_specs=[pl.BlockSpec((1, owned, columns), lambda step: (layer, 0, third))],
+        out_specs=[held((owned, columns))],
+        out_shape=[shaped((owned, columns), jnp.bfloat16)],
+        compiler_params=settings(16),
+        name="cast_shard",
+    )[0]
+
+
+def stack_body(p0, p1, p2, p3, out_ref):
+    rows = p0.shape[0]
+    for at, ref in enumerate((p0, p1, p2, p3)):
+        out_ref[at * rows : (at + 1) * rows, :] = ref[...]
+
+
+def stack_rows(line, parts):
+    rows, columns = parts[0].shape
+    return line.run(
+        stack_body,
+        tuple(parts),
+        in_specs=[VMEM_WHOLE] * 4,
+        out_specs=[VMEM_WHOLE],
+        out_shape=[shaped((4 * rows, columns), jnp.bfloat16)],
+        compiler_params=settings(16),
+        name="stack_shards",
+    )[0]
+
+
+def add_body(*refs):
+    total = refs[0][...].astype(jnp.float32)
+    for ref in refs[1:-1]:
+        total = total + ref[...].astype(jnp.float32)
+    refs[-1][...] = total.astype(jnp.bfloat16)
+
+
+def add_rows(line, terms, part=0, parts=1):
+    rows = min(term.shape[0] for term in terms) if parts == 1 else terms[0].shape[0] // parts
+    columns = terms[0].shape[1]
+
+    def spec(term):
+        return pl.BlockSpec(
+            (rows, columns), (lambda step: (part, 0)) if term.shape[0] > rows else (lambda step: (0, 0))
+        )
+
+    return line.run(
+        add_body,
+        tuple(terms),
+        grid=(1,),
+        in_specs=[spec(term) for term in terms],
+        out_specs=[pl.BlockSpec((rows, columns), lambda step: (0, 0))],
+        out_shape=[shaped((rows, columns), jnp.bfloat16)],
+        compiler_params=settings(24),
+        name="add_terms",
+    )[0]
+
+
+def pieces_body(*refs):
+    terms, outs = refs[:-4], refs[-4:]
+    rows = outs[0].shape[0]
+    for at, out_ref in enumerate(outs):
+        here = slice(at * rows, (at + 1) * rows)
+        total = terms[0][here, :].astype(jnp.float32)
+        for ref in terms[1:]:
+            total = total + ref[here, :].astype(jnp.float32)
+        out_ref[...] = total.astype(jnp.bfloat16)
+
+
+def sum_pieces(line, terms):
+    half, columns = D // 2, terms[0].shape[1]
+    near = pl.BlockSpec((half, columns), lambda step: (0, 0))
+    return line.run(
+        pieces_body,
+        tuple(terms),
+        grid=(1,),
+        in_specs=[near] * len(terms),
+        out_specs=[held((half // 4, columns))] * 4,
+        out_shape=[shaped((half // 4, columns), jnp.bfloat16)] * 4,
+        compiler_params=settings(24),
+        name="sum_pieces",
+    )
+
+
+def pass_body(*refs):
+    pass
+
+
+def in_turn(line, *values):
+    return line.run(
+        pass_body,
+        tuple(values),
+        in_specs=[IN_HBM] * len(values),
+        out_specs=[IN_HBM] * len(values),
+        out_shape=[shaped(one.shape, one.dtype) for one in values],
+        aliases={at: at for at in range(len(values))},
+        name="in_turn",
+    )
+
+
+def split_dot(left, right):
+    left_high = left.astype(jnp.bfloat16)
+    left_low = (left - left_high.astype(jnp.float32)).astype(jnp.bfloat16)
+    right_high = right.astype(jnp.bfloat16)
+    right_low = (right - right_high.astype(jnp.float32)).astype(jnp.bfloat16)
+    return (
+        dot_rows(left_high, right_high) + dot_rows(left_high, right_low) + dot_rows(left_low, right_high)
+    )
+
+
+def adam_body(chained, p0, p1, p2, p3, left_ref, right_ref, master_ref, first_ref, second_ref, ema_ref, *refs):
+    grads_ref, new_master_ref, new_first_ref, new_second_ref, new_ema_ref = refs[5:] if chained else refs
+    left = left_ref[0]
+    left_t = jnp.transpose(left)
+    grads = p0[...].astype(jnp.float32)
+    for ref in (p1, p2, p3):
+        grads = grads + ref[...].astype(jnp.float32)
+    grads_ref[0] = grads
+    turned_left = split_dot(left_t, grads)
+    back = []
+    for at in range(right_ref.shape[1]):
+        tile = slice(at * 128, (at + 1) * 128)
+        right = right_ref[0, at]
+        rotated = split_dot(turned_left[:, tile], right)
+        new_first = beta_first * first_ref[0, :, tile] + (1.0 - beta_first) * rotated
+        new_second = beta_second * second_ref[0, :, tile] + (1.0 - beta_second) * rotated * rotated
+        new_first_ref[0, :, tile] = new_first
+        new_second_ref[0, :, tile] = new_second
+        turned = new_first / (jnp.sqrt(new_second) + adam_eps)
+        back.append(split_dot(turned, jnp.transpose(right)))
+    back_full = split_dot(left, jnp.concatenate(back, axis=1))
+    new_master = master_ref[0] - step_rate * back_full
+    new_master_ref[0] = new_master
+    new_ema_ref[0] = ema_decay * ema_ref[0] + (1.0 - ema_decay) * new_master
+
+
+def adam(line, layer, third, pieces, left, right, master, first, second, ema, before, tile=256):
+    owned, columns = pieces[0].shape
+    steps = columns // tile
+    first_step = third * steps
+
+    def state(step):
+        return (layer, 0, first_step + step)
+
+    state_spec = pl.BlockSpec((1, owned, tile), state)
+    chained = before is not None
+    return line.run(
+        lambda *refs: adam_body(chained, *refs),
+        (*pieces, left, right, master, first, second, ema, *(before or ()),),
+        grid=(steps,),
+        in_specs=[by_cols((owned, tile))] * 4
+        + [
+            pl.BlockSpec((1,) + left.shape[1:], lambda step: (layer, 0, 0)),
+            pl.BlockSpec(
+                (1, tile // 128) + right.shape[2:], lambda step: (layer, first_step + step, 0, 0)
+            ),
+        ]
+        + [state_spec] * 4
+        + ([IN_HBM] * 5 if chained else []),
+        out_specs=[state_spec] * 5,
+        out_shape=[shaped(master.shape, jnp.float32)] * 5,
+        aliases={10 + at: at for at in range(5)} if chained else {},
+        compiler_params=settings(32),
+        name="adam_update",
+    )
+
+
+def hop_x(values):
+    return lax.ppermute(values, "tensor", [(at, at ^ 2) for at in range(4)])
+
+
+def hop_core(values):
+    return lax.ppermute(values, "tensor", [(at, at ^ 1) for at in range(4)])
+
+
+def hop_y(values):
+    return lax.ppermute(values, "dp", [(at, at ^ 1) for at in range(8)])
+
+
+def hop_z(values, step):
+    return lax.ppermute(values, "dp", [(at, at ^ (2 * step)) for at in range(8)])
+
+
+def rows_gather(rows):
+    over_x = hop_x(rows)
+    return [rows, hop_core(rows), over_x, hop_core(over_x)]
+
+
+def depth_hops(piece):
+    return [hop_z(piece, step) for step in (1, 2, 3)]
+
+
+def total_everywhere(values):
+    for hop in (hop_core, hop_x, hop_y):
+        values = values + hop(values)
+    for step in (1, 2):
+        values = values + hop_z(values, step)
+    return values
+
+
+def shards_grid(
+    frames_in,
+    code_emb,
+    cotangent,
+    lengths,
+    owner_list,
+    master,
+    first_moment,
+    second_moment,
+    ema,
+    left_basis,
+    right_basis,
+    gains,
+    gain_first,
+    gain_second,
+):
+    share = frames_in.shape[0]
+    owned = master.shape[1]
+    groups = D // owned
+    heads_w = D // lax.axis_size("tensor")
+    ff_w = FF // lax.axis_size("tensor")
+    my_dp = lax.axis_index("dp")
+    my_group = lax.axis_index("tensor").astype(jnp.int32)
+
+    rel = jnp.array([2 * z + y for y in range(2) for z in range(4)], jnp.int32)
+    slots = jnp.arange(groups, dtype=jnp.int32)
+    source = jnp.sum(
+        jnp.where(owner_list[None, :] == (my_dp ^ rel)[:, None], slots[None, :], 0), axis=1
+    ).astype(jnp.int32)
+    info = jnp.stack([my_group, lengths[0]])
+    count = (lengths - my_group * share).astype(jnp.int32)
+
+    line = Line()
+    codes = jnp.transpose(code_emb, (1, 0, 2))
+
+    def share_shard(layer, third):
+        shard = cast(line, master, layer, third)
+        return [shard] + depth_hops(shard)
+
+    g_heads = share_shard(0, 0)
+    rows_in, gains_here, normed = prep(line, source, frames_in, gains)
+    normed_a = rows_gather(normed)
+    l_heads = share_shard(1, 0)
+    near = stack_rows(line, g_heads)
+    g_heads = (near, hop_y(near))
+    g_up = share_shard(0, 1)
+    lh_near = stack_rows(line, l_heads)
+    lh_far, lh_near_c, lh_near_x = hop_y(lh_near), hop_core(lh_near), hop_x(lh_near)
+    l_up = share_shard(1, 1)
+    qkv, mixed, lse, *parts = global_heads(line, info, normed_a, g_heads)
+    near_term, far_term = hop_core(parts[1]), hop_core(parts[3])
+    near = stack_rows(line, g_up)
+    g_up = (near, hop_y(near))
+    to_x = hop_x(add_rows(line, [parts[2], far_term]))
+    g_down = share_shard(0, 2)
+    (lh_far,) = in_turn(line, lh_far)
+    lh_far_c, lh_far_x = hop_core(lh_far), hop_x(lh_far)
+    lu_near = stack_rows(line, l_up)
+    lu_far, lu_near_c, lu_near_x = hop_y(lu_near), hop_core(lu_near), hop_x(lu_near)
+    middle, normed = merge(line, rows_in, (parts[0], near_term, to_x), gains_here, 1)
+    normed_b = rows_gather(normed)
+    l_down = share_shard(1, 2)
+    (lh_near_x,) = in_turn(line, lh_near_x)
+    lh_near_xc = hop_core(lh_near_x)
+    grad, grad_t = seed(line, source, count, jnp.transpose(cotangent, (1, 0, 2)))
+    near = stack_rows(line, g_down)
+    g_down = (near, hop_y(near))
+    (lu_far,) = in_turn(line, lu_far)
+    lu_far_c, lu_far_x = hop_core(lu_far), hop_x(lu_far)
+    ld_near = stack_rows(line, l_down)
+    ld_far, ld_near_c, ld_near_x = hop_y(ld_near), hop_core(ld_near), hop_x(ld_near)
+    active, slope, *parts = global_ff(line, normed_b, g_up, g_down)
+    near_term, far_term = hop_core(parts[1]), hop_core(parts[3])
+    (lh_far_x,) = in_turn(line, lh_far_x)
+    lh_far_xc = hop_core(lh_far_x)
+    to_x = hop_x(add_rows(line, [parts[2], far_term]))
+    (lu_near_x,) = in_turn(line, lu_near_x)
+    lu_near_xc = hop_core(lu_near_x)
+    (global_out,) = merge(line, middle, (parts[0], near_term, to_x), gains_here, 1, normed=False)
+    (ld_near_x,) = in_turn(line, ld_near_x)
+    ld_near_xc, ld_far_x = hop_core(ld_near_x), hop_y(ld_near_x)
+    (ld_far,) = in_turn(line, ld_far)
+    ld_far_c = hop_core(ld_far)
+
+    l_heads = [(lh_near, lh_far), (lh_near_c, lh_far_c), (lh_near_x, lh_far_x), (lh_near_xc, lh_far_xc)]
+    l_qkv, l_mixed, l_middle, l_normed_b, l_a_t = local_heads(
+        line, source, global_out, codes, gains_here, l_heads
+    )
+    lu_far_x, ld_far_x = in_turn(line, lu_far_x, ld_far_x)
+    lu_far_xc, ld_far_xc = hop_core(lu_far_x), hop_core(ld_far_x)
+    l_up = [(lu_near, lu_far), (lu_near_c, lu_far_c), (lu_near_x, lu_far_x), (lu_near_xc, lu_far_xc)]
+    l_down = [(ld_near, ld_far), (ld_near_c, ld_far_c), (ld_near_x, ld_far_x), (ld_near_xc, ld_far_xc)]
+    l_active, l_slope, local_out, l_b_t = local_ff(line, source, l_normed_b, l_middle, l_up, l_down)
+    local_out = jnp.transpose(local_out, (1, 0, 2))
+
+    def ff_back(rel, **more):
+        return local_ff_back(
+            line, rel, grad, grad_t, l_b_t, l_active, l_slope, l_up[rel], l_down[rel], **more
+        )
+
+    (pair,), (so_far,) = ff_back(3)
+    met_far = hop_core(pair)
+    (pair,), (so_far,) = ff_back(1, so_far=so_far)
+    met_near = hop_core(pair)
+    (d2_near, d2_far, up2), (so_far,) = ff_back(2, met=met_far, so_far=so_far)
+    d2_far, up2 = hop_y(d2_far), hop_x(up2)
+    (d0_near, d0_far, up0), (l_grad_mid, l_small, l_small_t, gain_d) = ff_back(
+        0, met=met_near, so_far=so_far, tail=(l_middle, gains_here)
+    )
+    d0_far = hop_y(d0_far)
+
+    def heads_back(rel, **more):
+        return local_heads_back(
+            line, rel, l_small, l_small_t, l_a_t, l_qkv, l_mixed, l_heads[rel], **more
+        )
+
+    far_heads, (so_far,) = heads_back(3)
+    met_far = hop_core(far_heads)
+    near_heads, (so_far,) = heads_back(1, so_far=so_far)
+    met_near = hop_core(near_heads)
+    heads2, (so_far,) = heads_back(2, met=met_far, so_far=so_far)
+    heads2 = hop_x(heads2)
+    heads0, (grad_global, small, gain_c) = heads_back(
+        0, met=met_near, so_far=so_far, tail=(l_grad_mid, global_out, codes, source, gains_here)
+    )
+
+    grad_rows = rows_gather(small)
+    up_far = hop_y(add_rows(line, [up0, up2], 1, 2))
+    d2 = hop_x(add_rows(line, [d2_near, d2_far]))
+    grad_upper, *parts = global_ff_back(line, grad_rows, slope, g_up, g_down)
+    near_term, far_term = hop_core(parts[1]), hop_core(parts[3])
+    gd_near, gd_far = global_outer(line, grad_rows, active)
+    gd_far = hop_y(gd_far)
+    to_x = hop_x(add_rows(line, [parts[2], far_term]))
+    gu_near, gu_far = global_outer(line, normed_b, grad_upper)
+    gu_far = hop_y(gu_far)
+    grad_middle, small, gain_b = merge_back(
+        line, middle, (parts[0], near_term, to_x), grad_global, gains_here, 1
+    )
+    grad_attn = rows_gather(small)
+    lu = sum_pieces(line, [up0, up2, up_far])
+    lu = [lu[0]] + [hop_z(lu[at], at) for at in (1, 2, 3)]
+    heads_far = hop_y(add_rows(line, [heads0, heads2], 1, 2))
+    grad_qkv, *parts = global_heads_back(line, info, grad_attn, g_heads, qkv, mixed, lse)
+    near_term, far_term = hop_core(parts[1]), hop_core(parts[3])
+    gh_near, gh_far = global_grads_heads(line, info, normed_a, grad_attn, grad_qkv, mixed)
+    gh_far = hop_y(gh_far)
+    to_x = hop_x(add_rows(line, [parts[2], far_term]))
+    ld = sum_pieces(line, [d0_near, d0_far, d2])
+    ld = [ld[0]] + [hop_z(ld[at], at) for at in (1, 2, 3)]
+    gd = sum_pieces(line, [gd_near, gd_far])
+    gd = [gd[0]] + [hop_z(gd[at], at) for at in (1, 2, 3)]
+    input_grad, gain_grads = finish(
+        line, source, rows_in, (parts[0], near_term, to_x), grad_middle, gains_here, (gain_b, gain_c, gain_d)
+    )
+    gain_grads = total_everywhere(gain_grads)
+    gu = sum_pieces(line, [gu_near, gu_far])
+    gu = [gu[0]] + [hop_z(gu[at], at) for at in (1, 2, 3)]
+    lh = sum_pieces(line, [heads0, heads2, heads_far])
+    lh = [lh[0]] + [hop_z(lh[at], at) for at in (1, 2, 3)]
+
+    def update(layer, third, pieces, before):
+        return adam(
+            line, layer, third, pieces, left_basis, right_basis, master, first_moment, second_moment, ema, before
+        )
+
+    found = update(1, 1, lu, None)
+    gh = sum_pieces(line, [gh_near, gh_far])
+    gh = [gh[0]] + [hop_z(gh[at], at) for at in (1, 2, 3)]
+    found = update(1, 2, ld, found)
+    found = update(0, 2, gd, found)
+    found = update(0, 1, gu, found)
+    found = update(1, 0, lh, found)
+    found = update(0, 0, gh, found)
+    weight_grads, new_master, new_first, new_second, new_ema = found
+    new_gain_first = beta_first * gain_first + (1.0 - beta_first) * gain_grads
+    new_gain_second = beta_second * gain_second + (1.0 - beta_second) * gain_grads * gain_grads
+    new_gains = gains - gain_rate * new_gain_first / (jnp.sqrt(new_gain_second) + adam_eps)
+    return (
+        local_out,
+        input_grad,
+        weight_grads,
+        gain_grads,
+        new_master,
+        new_first,
+        new_second,
+        new_ema,
+        new_gains,
+        new_gain_first,
+        new_gain_second,
+    )
+
+
 def solution(mesh):
+    fits = mesh.shape["dp"] == 8 and mesh.shape["tensor"] == 4
     return jax.shard_map(
-        shards,
+        shards_grid if fits else shards_any,
         mesh=mesh,
         in_specs=(
             P(("dp", "tensor"), None),

time: 1510 us -> 771 us (0.51)
  matrix products: 361 us -> 0 us
  local copies, waits for them, and re-layouts: 362 us -> 55 us
  Pallas kernels: 0 us -> 289 us
  waiting for transfers between devices: 596 us -> 322 us
  other arithmetic: 116 us -> 0.93 us
  starting transfers between devices: 0.67 us -> 93.1 us
  blocking collectives: 44.1 us -> 0 us
    all_gather x6 -> x0, waiting for transfers between devices: 358 us -> none  [the longest x1 172 us: shards(): lax.all_gather(master.astype(jnp.bfloat16), 'dp', axis=1, tiled=True)]
    dot_general x39 -> x0, matrix products: 342 us -> none  [the longest x8 86.6 us: dot_rows(): return jnp.dot(left, right, preferred_element_type=jnp.float32)]
    ppermute x0 -> x103, waiting for transfers between devices: none -> 322 us  [the longest x38 143 us: hop_z(): return lax.ppermute(values, 'dp', [(at, at ^ 2 * step) for at in range(8)])]
    pallas_call x0 -> x62, Pallas kernels: none -> 289 us  [run(): pl.pallas_call(inner, in_specs=[IN_HBM] * lead + list(in_specs), out_spec...]
    reduce_scatter x6 -> x0, waiting for transfers between devices: 237 us -> none  [the longest x1 104 us: shards(): lax.psum_scatter(ordered.astype(jnp.bfloat16), 'dp', scatter_dimension=1,...]
    reshape x17 -> x0, local copies, waits for them, and re-layouts: 134 us -> none  [the longest x1 49.2 us: split_layer(): grouped = layer_cols.reshape(width, groups, -1)]
    ppermute x0 -> x103, starting transfers between devices: none -> 93.1 us  [the longest x38 52 us: hop_z(): return lax.ppermute(values, 'dp', [(at, at ^ 2 * step) for at in range(8)])]
    convert_element_type x11 -> x0, other arithmetic: 53 us -> none  [the longest x1 17.9 us: one_item(): grad_scores = (probability * (grad_prob - center)).astype(jnp.bfloat16)]
  transfers between devices with their start and end apart: 12 -> 103, of which waited for: 9 -> 33; matrix products, arithmetic and copies ran while one was open for 24% -> 0% of each run, Pallas kernels for 0% -> 27%
where the time goes in v1:
time: 771 us; the launch traced here: 763 us
  waiting for transfers between devices  322 us (42%)
  Pallas kernels  289 us (37%)
  starting transfers between devices  93.1 us (12%)
  local copies, waits for them, and re-layouts  55 us (7%)
    pallas_call x62, Pallas kernels, run(): pl.pallas_call(inner, in_specs=[IN_HBM] * lead + list(in_specs), out_spec...  289 us
    ppermute x38, waiting for transfers between devices, hop_z(): return lax.ppermute(values, 'dp', [(at, at ^ 2 * step) for at in range(8)])  143 us
    ppermute x17, waiting for transfers between devices, hop_x(): return lax.ppermute(values, 'tensor', [(at, at ^ 2) for at in range(4)])  112 us
    ppermute x15, waiting for transfers between devices, hop_y(): return lax.ppermute(values, 'dp', [(at, at ^ 1) for at in range(8)])  58.9 us
    unnamed x186, local copies, waits for them, and re-layouts  55 us
    ppermute x38, starting transfers between devices, hop_z(): return lax.ppermute(values, 'dp', [(at, at ^ 2 * step) for at in range(8)])  52 us
    ppermute x17, starting transfers between devices, hop_x(): return lax.ppermute(values, 'tensor', [(at, at ^ 2) for at in range(4)])  23 us
  transfers between devices with their start and end apart: 103, of which 33 were waited for; matrix products, arithmetic and copies ran while one was open for 0% of the time, Pallas kernels for 27%

profile of v1, /device:TPU:0, one launch (start us, length us, event | category | flops | bytes accessed | tf_op | source)
XLA Modules:
  0.0 762.7 jit_solution(250427785843547483)
XLA Ops:
  2.6 5.1 collective-permute-start.2
  15.1 15.0 %collective-permute-done.1.refs_3_ = bf16[128,1024]{1,0:T(8,128)(2,1)} collective-permute-done((bf16[128,1024]{1,0:T(8,128)(2,1)S(1)}, bf16[128,1024]{1,0:T(8,128)(2,1)}, u32[]{:S(2)}, u32[]{:S(2)}) %collective-permute-start.1) | collective-permute-done | bytes 262176 | tf_op jit(solution)/shard_map/ppermute | solution.py:1681
  38.2 6.8 collective-permute-done.5.refs_4_
  46.2 10.4 %collective-permute-done.4.refs_3_ = bf16[128,1024]{1,0:T(8,128)(2,1)S(1)} collective-permute-done((bf16[128,1024]{1,0:T(8,128)(2,1)S(1)}, bf16[128,1024]{1,0:T(8,128)(2,1)S(1)}, u32[]{:S(2)}, u32[]{:S(2)}) %collective-permute-start.4) | collective-permute-done | bytes 262176 | tf_op jit(solution)/shard_map/ppermute | solution.py:1681
  60.4 13.9 %global_heads.1 = (bf16[1024,768]{1,0:T(8,128)(2,1)S(1)}, bf16[1024,256]{1,0:T(8,128)(2,1)S(1)}, f32[8,1024]{1,0:T(8,128)S(1)}, bf16[256,1024]{1,0:T(8,128)(2,1)...) custom-call(f32[8,128]{1,0:T(8,128)S(1)} %get-tuple-element.238.refs, ...), custom_call_target="tpu_custom_call" | custom-call | flops 1000 | bytes 1000 | tf_op jit(solution)/shard_map/global_heads/pallas_call | solution.py:520
  79.9 10.8 %collective-permute-done.11.refs_3_ = bf16[128,1024]{1,0:T(8,128)(2,1)S(1)} collective-permute-done((bf16[128,1024]{1,0:T(8,128)(2,1)}, bf16[128,1024]{1,0:T(8,128)(2,1)S(1)}, u32[]{:S(2)}, u32[]{:S(2)}) %collective-permute-start.11) | collective-permute-done | bytes 262176 | tf_op jit(solution)/shard_map/ppermute | solution.py:1681
  96.8 4.1 collective-permute-done.17.refs_4_
  105.6 10.3 %collective-permute-done.16.refs_3_ = bf16[128,1024]{1,0:T(8,128)(2,1)} collective-permute-done((bf16[128,1024]{1,0:T(8,128)(2,1)S(1)}, bf16[128,1024]{1,0:T(8,128)(2,1)}, u32[]{:S(2)}, u32[]{:S(2)}) %collective-permute-start.16) | collective-permute-done | bytes 262176 | tf_op jit(solution)/shard_map/ppermute | solution.py:1681
  140.0 12.6 %collective-permute-done.22.refs_3_ = bf16[128,1024]{1,0:T(8,128)(2,1)} collective-permute-done((bf16[128,1024]{1,0:T(8,128)(2,1)}, bf16[128,1024]{1,0:T(8,128)(2,1)}, u32[]{:S(2)}, u32[]{:S(2)}) %collective-permute-start.22) | collective-permute-done | bytes 262176 | tf_op jit(solution)/shard_map/ppermute | solution.py:1681
  157.4 10.9 %collective-permute-done.26.refs_3_ = bf16[128,1024]{1,0:T(8,128)(2,1)S(1)} collective-permute-done((bf16[128,1024]{1,0:T(8,128)(2,1)}, bf16[128,1024]{1,0:T(8,128)(2,1)S(1)}, u32[]{:S(2)}, u32[]{:S(2)}) %collective-permute-start.26) | collective-permute-done | bytes 262176 | tf_op jit(solution)/shard_map/ppermute | solution.py:1681
  169.0 7.5 collective-permute-done.25.refs_2_
  182.8 6.0 collective-permute-done.32.refs_8_.refs_9_
  191.0 13.2 %global_ff.1 = (bf16[1024,1024]{1,0:T(8,128)(2,1)S(1)}, bf16[1024,1024]{1,0:T(8,128)(2,1)S(1)}, bf16[256,1024]{1,0:T(8,128)(2,1)S(1)}, bf16[256,1024]{1,0:T(8,12...) custom-call(f32[8,128]{1,0:T(8,128)S(1)} %get-tuple-element.266.refs_0_, ...), custom_call_target="tpu_custom_call" | custom-call | flops 1000 | bytes 1000 | tf_op jit(solution)/shard_map/global_ff/pallas_call | solution.py:520
  215.7 10.1 %collective-permute-done.35.refs_1_ = bf16[512,1024]{1,0:T(8,128)(2,1)} collective-permute-done((bf16[512,1024]{1,0:T(8,128)(2,1)}, bf16[512,1024]{1,0:T(8,128)(2,1)}, u32[]{:S(2)}, u32[]{:S(2)}) %collective-permute-start.35) | collective-permute-done | bytes 1048608 | tf_op jit(solution)/shard_map/ppermute | solution.py:1669
  226.3 22.0 %collective-permute-done.38.refs_1_ = bf16[512,1024]{1,0:T(8,128)(2,1)} collective-permute-done((bf16[512,1024]{1,0:T(8,128)(2,1)}, bf16[512,1024]{1,0:T(8,128)(2,1)}, u32[]{:S(2)}, u32[]{:S(2)}) %collective-permute-start.38) | collective-permute-done | bytes 1048608 | tf_op jit(solution)/shard_map/ppermute | solution.py:1669
  248.8 9.7 %collective-permute-done.37.refs_4_ = bf16[256,1024]{1,0:T(8,128)(2,1)S(1)} collective-permute-done((bf16[256,1024]{1,0:T(8,128)(2,1)S(1)}, bf16[256,1024]{1,0:T(8,128)(2,1)S(1)}, u32[]{:S(2)}, u32[]{:S(2)}) %collective-permute-start.37) | collective-permute-done | bytes 524320 | tf_op jit(solution)/shard_map/ppermute | solution.py:1669
  268.2 4.9 collective-permute-done.39.refs_1_
  275.6 18.3 %local_heads.1 = (bf16[4,768,768]{2,1,0:T(8,128)(2,1)}, bf16[4,768,256]{2,1,0:T(8,128)(2,1)}, f32[768,1024]{1,0:T(8,128)}, bf16[768,1024]{1,0:T(8,128)(2,1)}, bf...) custom-call(f32[8,128]{1,0:T(8,128)S(1)} %copy-done.59, s32[8]{0:T(128)S(1)} %select_reduce_fusion.refs_1_.refs_13_, ...), custom_call_target="tpu_custom_call" | custom-call | flops 1000 | bytes 1000 | tf_op jit(solution)/shard_map/local_heads/pallas_call | solution.py:520
  304.3 35.0 %local_ff.1 = (bf16[4,768,1024]{2,1,0:T(8,128)(2,1)}, bf16[4,768,1024]{2,1,0:T(8,128)(2,1)}, bf16[3,256,1024]{2,1,0:T(8,128)(2,1)}, bf16[1024,768]{1,0:T(8,128)(2,1)}, f32[8,128]{1,0:T(8,128)}) custom-call(f32[8,128]{1,0:T(8,128)} %get-tuple-element.291.refs_0_, s32[8]{0:T(128)} %copy-done.57, bf16[768,1024]{1,0:T(8,128)(2,1)} %get-tuple-element.292.refs_2_, ...), custom_call_target="tpu_custom_call" | custom-call | flops 1000 | bytes 1000 | tf_op jit(solution)/shard_map/local_ff/pallas_call | solution.py:520
  339.9 14.0 %local_ff_back.4 = (bf16[2,1024,1024]{2,1,0:T(8,128)(2,1)}, f32[768,1024]{1,0:T(8,128)}, f32[8,128]{1,0:T(8,128)S(1)}) custom-call(f32[8,128]{1,0:T(8,128)S(1)} %copy-done.66, bf16[768,1024]{1,0:T(8,128)(2,1)} %copy-done.6, bf16[1024,768]{1,0:T(8,128)(2,1)} %copy-done.7, bf16[1024,768]{1,0:T(8,128)(2,1)} %get-tuple-element.302.refs_3_, ...), custom_call_target="tpu_custom_call" | custom-call | flops 1000 | bytes 1000 | tf_op jit(solution)/shard_map/local_ff_back/pallas_call | solution.py:520
  354.1 15.1 %local_ff_back.5 = (bf16[2,1024,1024]{2,1,0:T(8,128)(2,1)}, f32[768,1024]{1,0:T(8,128)}, f32[8,128]{1,0:T(8,128)S(1)}) custom-call(f32[8,128]{1,0:T(8,128)S(1)} %get-tuple-element.305.refs_0_, bf16[768,1024]{1,0:T(8,128)(2,1)} %copy-done.6, bf16[1024,768]{1,0:T(8,128)(2,1)} %copy-done.7, bf16[1024,768]{1,0:T(8,128)(2,1)} %get-tuple-element.302.refs_3_, ...), custom_call_target="tpu_custom_call" | custom-call | flops 1000 | bytes 1000 | tf_op jit(solution)/shard_map/local_ff_back/pallas_call | solution.py:520
  371.7 15.6 %local_ff_back.6 = (bf16[512,1024]{1,0:T(8,128)(2,1)S(1)}, bf16[512,1024]{1,0:T(8,128)(2,1)}, bf16[1024,1024]{1,0:T(8,128)(2,1)}, f32[768,1024]{1,0:T(8,128)}, f32[8,128]{1,0:T(8,128)S(1)}) custom-call(f32[8,128]{1,0:T(8,128)S(1)} %get-tuple-element.307.refs_0_, bf16[768,1024]{1,0:T(8,128)(2,1)} %copy-done.6, bf16[1024,768]{1,0:T(8,128)(2,1)} %copy-done.7, ...), custom_call_target="tpu_custom_call" | custom-call | flops 1000 | bytes 1000 | tf_op jit(solution)/shard_map/local_ff_back/pallas_call | solution.py:520
  389.3 19.7 %local_ff_back.7 = (bf16[512,1024]{1,0:T(8,128)(2,1)S(1)}, bf16[512,1024]{1,0:T(8,128)(2,1)}, bf16[1024,1024]{1,0:T(8,128)(2,1)}, f32[768,1024]{1,0:T(8,128)}, b...) custom-call(f32[8,128]{1,0:T(8,128)S(1)} %get-tuple-element.310.refs_0_, ...), custom_call_target="tpu_custom_call" | custom-call | flops 1000 | bytes 1000 | tf_op jit(solution)/shard_map/local_ff_back/pallas_call | solution.py:520
  409.9 9.8 %local_heads_back.4 = (bf16[1024,1024]{1,0:T(8,128)(2,1)}, f32[768,1024]{1,0:T(8,128)}, f32[8,128]{1,0:T(8,128)S(1)}) custom-call(f32[8,128]{1,0:T(8,128)S(1)} %get-tuple-element.313.refs_0_, bf16[768,1024]{1,0:T(8,128)(2,1)} %get-tuple-element.314.refs_1_, bf16[1024,768]{1,0:T(8,128)(2,1)} %get-tuple-element.315.refs_2_, ...), custom_call_target="tpu_custom_call" | custom-call | flops 1000 | bytes 1000 | tf_op jit(solution)/shard_map/local_heads_back/pallas_call | solution.py:520
  419.8 10.7 %local_heads_back.5 = (bf16[1024,1024]{1,0:T(8,128)(2,1)}, f32[768,1024]{1,0:T(8,128)}, f32[8,128]{1,0:T(8,128)S(1)}) custom-call(f32[8,128]{1,0:T(8,128)S(1)} %get-tuple-element.319.refs_0_, bf16[768,1024]{1,0:T(8,128)(2,1)} %get-tuple-element.314.refs_1_, bf16[1024,768]{1,0:T(8,128)(2,1)} %get-tuple-element.315.refs_2_, ...), custom_call_target="tpu_custom_call" | custom-call | flops 1000 | bytes 1000 | tf_op jit(solution)/shard_map/local_heads_back/pallas_call | solution.py:520
  433.9 11.5 %local_heads_back.6 = (bf16[1024,1024]{1,0:T(8,128)(2,1)}, f32[768,1024]{1,0:T(8,128)}, f32[8,128]{1,0:T(8,128)S(1)}) custom-call(f32[8,128]{1,0:T(8,128)S(1)} %get-tuple-element.321.refs_0_, bf16[768,1024]{1,0:T(8,128)(2,1)} %get-tuple-element.314.refs_1_, bf16[1024,768]{1,0:T(8,128)(2,1)} %get-tuple-element.315.refs_2_, ...), custom_call_target="tpu_custom_call" | custom-call | flops 1000 | bytes 1000 | tf_op jit(solution)/shard_map/local_heads_back/pallas_call | solution.py:520
  446.8 14.6 %local_heads_back.7 = (bf16[1024,1024]{1,0:T(8,128)(2,1)}, f32[256,1024]{1,0:T(8,128)S(1)}, bf16[256,1024]{1,0:T(8,128)(2,1)S(1)}, f32[1,1024]{1,0:T(1,128)S(1)}, f32[8,128]{1,0:T(8,128)S(1)}) custom-call(f32[8,128]{1,0:T(8,128)S(1)} %get-tuple-element.324.refs_0_, bf16[768,1024]{1,0:T(8,128)(2,1)} %get-tuple-element.314.refs_1_, ...), custom_call_target="tpu_custom_call" | custom-call | flops 1000 | bytes 1000 | tf_op jit(solution)/shard_map/local_heads_back/pallas_call | solution.py:520
  462.4 28.5 %collective-permute-done.61.refs_3_ = bf16[256,1024]{1,0:T(8,128)(2,1)S(1)} collective-permute-done((bf16[256,1024]{1,0:T(8,128)(2,1)S(1)}, bf16[256,1024]{1,0:T(8,128)(2,1)S(1)}, u32[]{:S(2)}, u32[]{:S(2)}) %collective-permute-start.61) | collective-permute-done | bytes 524320 | tf_op jit(solution)/shard_map/ppermute | solution.py:1669
  496.6 9.4 %global_ff_back.1 = (bf16[1024,1024]{1,0:T(8,128)(2,1)S(1)}, bf16[256,1024]{1,0:T(8,128)(2,1)S(1)}, bf16[256,1024]{1,0:T(8,128)(2,1)S(1)}, bf16[256,1024]{1,0:T(...) custom-call(f32[8,128]{1,0:T(8,128)S(1)} %get-tuple-element.334.refs_0_, ...), custom_call_target="tpu_custom_call" | custom-call | flops 1000 | bytes 1000 | tf_op jit(solution)/shard_map/global_ff_back/pallas_call | solution.py:520
  508.2 4.6 global_ff_grads.2
  513.7 5.7 global_ff_grads.3
  520.4 29.9 %collective-permute-done.65.refs_4_ = bf16[256,1024]{1,0:T(8,128)(2,1)S(1)} collective-permute-done((bf16[256,1024]{1,0:T(8,128)(2,1)S(1)}, bf16[256,1024]{1,0:T(8,128)(2,1)S(1)}, u32[]{:S(2)}, u32[]{:S(2)}) %collective-permute-start.65) | collective-permute-done | bytes 524320 | tf_op jit(solution)/shard_map/ppermute | solution.py:1669
  552.9 11.8 %collective-permute-done.69.refs_4_.refs_8_ = bf16[256,1024]{1,0:T(8,128)(2,1)S(1)} collective-permute-done((bf16[256,1024]{1,0:T(8,128)(2,1)S(1)}, bf16[256,1024]{1,0:T(8,128)(2,1)S(1)}, u32[]{:S(2)}, u32[]{:S(2)}) %collective-permute-start.69) | collective-permute-done | bytes 524320 | tf_op jit(solution)/shard_map/ppermute | solution.py:1669
  571.6 12.7 %global_heads_back.1 = (bf16[1024,768]{1,0:T(8,128)(2,1)S(1)}, bf16[256,1024]{1,0:T(8,128)(2,1)S(1)}, bf16[256,1024]{1,0:T(8,128)(2,1)}, bf16[256,1024]{1,0:T(8,...) custom-call(f32[8,128]{1,0:T(8,128)S(1)} %get-tuple-element.354.refs_0_, s32[2]{0:T(128)S(1)} %pad_add_fusion.refs_1_, ...), custom_call_target="tpu_custom_call" | custom-call | flops 1000 | bytes 1000 | tf_op jit(solution)/shard_map/global_heads_back/pallas_call | solution.py:520
  584.8 6.1 global_heads_grads.1
  593.5 20.0 %collective-permute-done.74.refs_2_ = bf16[512,1024]{1,0:T(8,128)(2,1)} collective-permute-done((bf16[512,1024]{1,0:T(8,128)(2,1)}, bf16[512,1024]{1,0:T(8,128)(2,1)}, u32[]{:S(2)}, u32[]{:S(2)}) %collective-permute-start.74) | collective-permute-done | bytes 1048608 | tf_op jit(solution)/shard_map/ppermute | solution.py:1677
  624.0 17.8 %collective-permute-done.80.refs_3_ = bf16[128,1024]{1,0:T(8,128)(2,1)S(1)} collective-permute-done((bf16[128,1024]{1,0:T(8,128)(2,1)S(1)}, bf16[128,1024]{1,0:T(8,128)(2,1)S(1)}, u32[]{:S(2)}, u32[]{:S(2)}) %collective-permute-start.80) | collective-permute-done | bytes 262176 | tf_op jit(solution)/shard_map/ppermute | solution.py:1681
  648.4 9.9 %collective-permute-done.78.refs_3_ = bf16[512,1024]{1,0:T(8,128)(2,1)S(1)} collective-permute-done((bf16[512,1024]{1,0:T(8,128)(2,1)}, bf16[512,1024]{1,0:T(8,128)(2,1)S(1)}, u32[]{:S(2)}, u32[]{:S(2)}) %collective-permute-start.78) | collective-permute-done | bytes 1048608 | tf_op jit(solution)/shard_map/ppermute | solution.py:1677
  662.7 18.0 %collective-permute-done.100 = f32[4,1024]{1,0:T(4,128)S(1)} collective-permute-done((f32[4,1024]{1,0:T(4,128)S(1)}, f32[4,1024]{1,0:T(4,128)S(1)}, u32[]{:S(2)}, u32[]{:S(2)}) %collective-permute-start.100) | collective-permute-done | bytes 16416 | tf_op jit(solution)/shard_map/ppermute | solution.py:1677
  686.0 5.7 collective-permute-done.85.refs_4_
  697.4 4.9 adam_update.6
  702.3 14.9 %collective-permute-done.102 = f32[4,1024]{1,0:T(4,128)S(1)} collective-permute-done((f32[4,1024]{1,0:T(4,128)S(1)}, f32[4,1024]{1,0:T(4,128)S(1)}, u32[]{:S(2)}, u32[]{:S(2)}) %collective-permute-start.102) | collective-permute-done | bytes 16416 | tf_op jit(solution)/shard_map/ppermute | solution.py:1681
  723.5 4.9 adam_update.7
  728.3 4.9 adam_update.8
  733.9 4.9 adam_update.9
  738.8 4.9 adam_update.10
  743.7 13.9 %collective-permute-done.96.refs_3_ = bf16[128,1024]{1,0:T(8,128)(2,1)S(1)} collective-permute-done((bf16[128,1024]{1,0:T(8,128)(2,1)S(1)}, bf16[128,1024]{1,0:T(8,128)(2,1)S(1)}, u32[]{:S(2)}, u32[]{:S(2)}) %collective-permute-start.96) | collective-permute-done | bytes 262176 | tf_op jit(solution)/shard_map/ppermute | solution.py:1681
  757.6 4.9 adam_update.11
  (414 shorter events, 184.7 us)
Async XLA Ops:
  12.8 32.2 %collective-permute-start.7 = (bf16[256,1024]{1,0:T(8,128)(2,1)}, bf16[256,1024]{1,0:T(8,128)(2,1)}, u32[]{:S(2)}, u32[]{:S(2)}) collective-permute-start(bf16[256,1024]{1,0:T(8,128)(2,1)} %get-tuple-element.239.refs_2_), channel_id=1, source_target_pairs={{0,2},{1,3},{2,0},{3,1},{4,6},{5,7},{6,4},{7,5},{8,10},{9,11},{10,... | collective-permute-start | bytes 1572872 | tf_op jit(solution)/shard_map/ppermute | solution.py:1669
  32.3 28.2 %collective-permute-start.9 = (bf16[512,1024]{1,0:T(8,128)(2,1)}, bf16[512,1024]{1,0:T(8,128)(2,1)}, u32[]{:S(2)}, u32[]{:S(2)}) collective-permute-start(bf16[512,1024]{1,0:T(8,128)(2,1)} %get-tuple-element.240.refs_6_), channel_id=1, source_target_pairs={{0,4},{4,0},{8,12},{12,8},{16,20},{20,16},{24,28},{28,24},{1,5},{5... | collective-permute-start | bytes 3145736 | tf_op jit(solution)/shard_map/ppermute | solution.py:1677
  57.6 46.7 %collective-permute-start.14 = (bf16[512,1024]{1,0:T(8,128)(2,1)}, bf16[512,1024]{1,0:T(8,128)(2,1)}, u32[]{:S(2)}, u32[]{:S(2)}) collective-permute-start(bf16[512,1024]{1,0:T(8,128)(2,1)} %get-tuple-element.248.refs_5_.refs_6_), channel_id=1, source_target_pairs={{0,4},{4,0},{8,12},{12,8},{16,20},{20,16},{24,28},{28,24},{1,5},{5... | collective-permute-start | bytes 3145736 | tf_op jit(solution)/shard_map/ppermute | solution.py:1677
  75.6 56.9 %collective-permute-start.20 = (bf16[512,1024]{1,0:T(8,128)(2,1)}, bf16[512,1024]{1,0:T(8,128)(2,1)}, u32[]{:S(2)}, u32[]{:S(2)}) collective-permute-start(bf16[512,1024]{1,0:T(8,128)(2,1)} %get-tuple-element.248.refs_5_.refs_6_), channel_id=1, source_target_pairs={{0,2},{1,3},{2,0},{3,1},{4,6},{5,7},{6,4},{7,5},{8,10},{9,11},{10,... | collective-permute-start | bytes 3145736 | tf_op jit(solution)/shard_map/ppermute | solution.py:1669
  92.3 30.4 %collective-permute-start.18 = (bf16[256,1024]{1,0:T(8,128)(2,1)}, bf16[256,1024]{1,0:T(8,128)(2,1)}, u32[]{:S(2)}, u32[]{:S(2)}) collective-permute-start(bf16[256,1024]{1,0:T(8,128)(2,1)} %get-tuple-element.254), channel_id=1, source_target_pairs={{0,1},{1,0},{2,3},{3,2},{4,5},{5,4},{6,7},{7,6},{8,9},{9,8},{10,11... | collective-permute-start | bytes 1572872 | tf_op jit(solution)/shard_map/ppermute | solution.py:1673
  95.3 29.1 %collective-permute-start.19 = (bf16[256,1024]{1,0:T(8,128)(2,1)}, bf16[256,1024]{1,0:T(8,128)(2,1)}, u32[]{:S(2)}, u32[]{:S(2)}) collective-permute-start(bf16[256,1024]{1,0:T(8,128)(2,1)} %get-tuple-element.255), channel_id=1, source_target_pairs={{0,2},{1,3},{2,0},{3,1},{4,6},{5,7},{6,4},{7,5},{8,10},{9,11},{10,... | collective-permute-start | bytes 1572872 | tf_op jit(solution)/shard_map/ppermute | solution.py:1669
  119.7 57.3 %collective-permute-start.24 = (bf16[512,1024]{1,0:T(8,128)(2,1)}, bf16[512,1024]{1,0:T(8,128)(2,1)}, u32[]{:S(2)}, u32[]{:S(2)}) collective-permute-start(bf16[512,1024]{1,0:T(8,128)(2,1)} %get-tuple-element.263.refs_4_.refs_6_), channel_id=1, source_target_pairs={{0,4},{4,0},{8,12},{12,8},{16,20},{20,16},{24,28},{28,24},{1,5},{5... | collective-permute-start | bytes 3145736 | tf_op jit(solution)/shard_map/ppermute | solution.py:1677
  122.7 29.9 %collective-permute-start.22 = (bf16[128,1024]{1,0:T(8,128)(2,1)}, bf16[128,1024]{1,0:T(8,128)(2,1)}, u32[]{:S(2)}, u32[]{:S(2)}) collective-permute-start(bf16[128,1024]{1,0:T(8,128)(2,1)} %copy-done.49), channel_id=1, source_target_pairs={{0,16},{4,20},{8,24},{12,28},{16,0},{20,4},{24,8},{28,12},{1,17},{... | collective-permute-start | bytes 786440 | tf_op jit(solution)/shard_map/ppermute | solution.py:1681
  124.4 28.2 %collective-permute-start.21 = (bf16[128,1024]{1,0:T(8,128)(2,1)}, bf16[128,1024]{1,0:T(8,128)(2,1)}, u32[]{:S(2)}, u32[]{:S(2)}) collective-permute-start(bf16[128,1024]{1,0:T(8,128)(2,1)} %copy-done.49), channel_id=1, source_target_pairs={{0,8},{4,12},{8,0},{12,4},{16,24},{20,28},{24,16},{28,20},{1,9},{5... | collective-permute-start | bytes 786440 | tf_op jit(solution)/shard_map/ppermute | solution.py:1681
  132.5 24.4 %collective-permute-start.27 = (bf16[128,1024]{1,0:T(8,128)(2,1)}, bf16[128,1024]{1,0:T(8,128)(2,1)}, u32[]{:S(2)}, u32[]{:S(2)}) collective-permute-start(bf16[128,1024]{1,0:T(8,128)(2,1)} %get-tuple-element.265.refs_1_), channel_id=1, source_target_pairs={{0,24},{4,28},{8,16},{12,20},{16,8},{20,12},{24,0},{28,4},{1,25},{... | collective-permute-start | bytes 786440 | tf_op jit(solution)/shard_map/ppermute | solution.py:1681
  139.5 42.7 %collective-permute-start.31 = (bf16[512,1024]{1,0:T(8,128)(2,1)}, bf16[512,1024]{1,0:T(8,128)(2,1)}, u32[]{:S(2)}, u32[]{:S(2)}) collective-permute-start(bf16[512,1024]{1,0:T(8,128)(2,1)} %copy-done.16), channel_id=1, source_target_pairs={{0,4},{4,0},{8,12},{12,8},{16,20},{20,16},{24,28},{28,24},{1,5},{5... | collective-permute-start | bytes 3145736 | tf_op jit(solution)/shard_map/ppermute | solution.py:1677
  156.8 31.9 %collective-permute-start.32 = (bf16[512,1024]{1,0:T(8,128)(2,1)}, bf16[512,1024]{1,0:T(8,128)(2,1)}, u32[]{:S(2)}, u32[]{:S(2)}) collective-permute-start(bf16[512,1024]{1,0:T(8,128)(2,1)} %get-tuple-element.269.refs_7_.refs_8_), channel_id=1, source_target_pairs={{0,4},{4,0},{8,12},{12,8},{16,20},{20,16},{24,28},{28,24},{1,5},{5... | collective-permute-start | bytes 3145736 | tf_op jit(solution)/shard_map/ppermute | solution.py:1677
  177.0 33.2 %collective-permute-start.33 = (bf16[512,1024]{1,0:T(8,128)(2,1)}, bf16[512,1024]{1,0:T(8,128)(2,1)}, u32[]{:S(2)}, u32[]{:S(2)}) collective-permute-start(bf16[512,1024]{1,0:T(8,128)(2,1)} %get-tuple-element.271.refs_6_.refs_7_), channel_id=1, source_target_pairs={{0,2},{1,3},{2,0},{3,1},{4,6},{5,7},{6,4},{7,5},{8,10},{9,11},{10,... | collective-permute-start | bytes 3145736 | tf_op jit(solution)/shard_map/ppermute | solution.py:1669
  182.2 43.6 %collective-permute-start.35 = (bf16[512,1024]{1,0:T(8,128)(2,1)}, bf16[512,1024]{1,0:T(8,128)(2,1)}, u32[]{:S(2)}, u32[]{:S(2)}) collective-permute-start(bf16[512,1024]{1,0:T(8,128)(2,1)} %get-tuple-element.263.refs_4_.refs_6_), channel_id=1, source_target_pairs={{0,2},{1,3},{2,0},{3,1},{4,6},{5,7},{6,4},{7,5},{8,10},{9,11},{10,... | collective-permute-start | bytes 3145736 | tf_op jit(solution)/shard_map/ppermute | solution.py:1669
  208.5 39.8 %collective-permute-start.38 = (bf16[512,1024]{1,0:T(8,128)(2,1)}, bf16[512,1024]{1,0:T(8,128)(2,1)}, u32[]{:S(2)}, u32[]{:S(2)}) collective-permute-start(bf16[512,1024]{1,0:T(8,128)(2,1)} %get-tuple-element.282.refs_12_.refs_8_), channel_id=1, source_target_pairs={{0,2},{1,3},{2,0},{3,1},{4,6},{5,7},{6,4},{7,5},{8,10},{9,11},{10,... | collective-permute-start | bytes 3145736 | tf_op jit(solution)/shard_map/ppermute | solution.py:1669
  214.2 44.3 %collective-permute-start.37 = (bf16[256,1024]{1,0:T(8,128)(2,1)S(1)}, bf16[256,1024]{1,0:T(8,128)(2,1)S(1)}, u32[]{:S(2)}, u32[]{:S(2)}) collective-permute-start(bf16[256,1024]{1,0:T(8,128)(2,1)S(1)} %get-tuple-element.280), channel_id=1, source_target_pairs={{0,2},{1,3},{2,0},{3,1},{4,6},{5,7},{6,4},{7,5},{8,10},{9,11},{10,... | collective-permute-start | bytes 1572872 | tf_op jit(solution)/shard_map/ppermute | solution.py:1669
  215.7 50.4 %collective-permute-start.40 = (bf16[512,1024]{1,0:T(8,128)(2,1)}, bf16[512,1024]{1,0:T(8,128)(2,1)}, u32[]{:S(2)}, u32[]{:S(2)}) collective-permute-start(bf16[512,1024]{1,0:T(8,128)(2,1)} %get-tuple-element.248.refs_5_.refs_6_), channel_id=1, source_target_pairs={{0,1},{1,0},{2,3},{3,2},{4,5},{5,4},{6,7},{7,6},{8,9},{9,8},{10,11... | collective-permute-start | bytes 3145736 | tf_op jit(solution)/shard_map/ppermute | solution.py:1673
  225.8 41.9 %collective-permute-start.41 = (bf16[512,1024]{1,0:T(8,128)(2,1)}, bf16[512,1024]{1,0:T(8,128)(2,1)}, u32[]{:S(2)}, u32[]{:S(2)}) collective-permute-start(bf16[512,1024]{1,0:T(8,128)(2,1)} %get-tuple-element.271.refs_6_.refs_7_), channel_id=1, source_target_pairs={{0,1},{1,0},{2,3},{3,2},{4,5},{5,4},{6,7},{7,6},{8,9},{9,8},{10,11... | collective-permute-start | bytes 3145736 | tf_op jit(solution)/shard_map/ppermute | solution.py:1673
  225.8 42.4 %collective-permute-start.42 = (bf16[512,1024]{1,0:T(8,128)(2,1)}, bf16[512,1024]{1,0:T(8,128)(2,1)}, u32[]{:S(2)}, u32[]{:S(2)}) collective-permute-start(bf16[512,1024]{1,0:T(8,128)(2,1)} %get-tuple-element.286.refs_9_.refs_6_), channel_id=1, source_target_pairs={{0,1},{1,0},{2,3},{3,2},{4,5},{5,4},{6,7},{7,6},{8,9},{9,8},{10,11... | collective-permute-start | bytes 3145736 | tf_op jit(solution)/shard_map/ppermute | solution.py:1673
  248.3 24.9 %collective-permute-start.39 = (bf16[512,1024]{1,0:T(8,128)(2,1)}, bf16[512,1024]{1,0:T(8,128)(2,1)}, u32[]{:S(2)}, u32[]{:S(2)}) collective-permute-start(bf16[512,1024]{1,0:T(8,128)(2,1)} %get-tuple-element.282.refs_12_.refs_8_), channel_id=1, source_target_pairs={{0,4},{4,0},{8,12},{12,8},{16,20},{20,16},{24,28},{28,24},{1,5},{5... | collective-permute-start | bytes 3145736 | tf_op jit(solution)/shard_map/ppermute | solution.py:1677
  266.2 28.3 %collective-permute-start.44 = (bf16[512,1024]{1,0:T(8,128)(2,1)}, bf16[512,1024]{1,0:T(8,128)(2,1)}, u32[]{:S(2)}, u32[]{:S(2)}) collective-permute-start(bf16[512,1024]{1,0:T(8,128)(2,1)} %get-tuple-element.289.refs_5_.refs_7_), channel_id=1, source_target_pairs={{0,2},{1,3},{2,0},{3,1},{4,6},{5,7},{6,4},{7,5},{8,10},{9,11},{10,... | collective-permute-start | bytes 3145736 | tf_op jit(solution)/shard_map/ppermute | solution.py:1669
  267.7 26.8 %collective-permute-start.45 = (bf16[512,1024]{1,0:T(8,128)(2,1)}, bf16[512,1024]{1,0:T(8,128)(2,1)}, u32[]{:S(2)}, u32[]{:S(2)}) collective-permute-start(bf16[512,1024]{1,0:T(8,128)(2,1)} %get-tuple-element.290.refs_16_.refs_8_), channel_id=1, source_target_pairs={{0,4},{4,0},{8,12},{12,8},{16,20},{20,16},{24,28},{28,24},{1,5},{5... | collective-permute-start | bytes 3145736 | tf_op jit(solution)/shard_map/ppermute | solution.py:1677
  268.2 26.8 %collective-permute-start.46 = (bf16[512,1024]{1,0:T(8,128)(2,1)}, bf16[512,1024]{1,0:T(8,128)(2,1)}, u32[]{:S(2)}, u32[]{:S(2)}) collective-permute-start(bf16[512,1024]{1,0:T(8,128)(2,1)} %get-tuple-element.263.refs_4_.refs_6_), channel_id=1, source_target_pairs={{0,1},{1,0},{2,3},{3,2},{4,5},{5,4},{6,7},{7,6},{8,9},{9,8},{10,11... | collective-permute-start | bytes 3145736 | tf_op jit(solution)/shard_map/ppermute | solution.py:1673
  430.9 61.6 %collective-permute-start.58 = (bf16[1024,1024]{1,0:T(8,128)(2,1)}, bf16[1024,1024]{1,0:T(8,128)(2,1)S(1)}, u32[]{:S(2)}, u32[]{:S(2)}) collective-permute-start(bf16[1024,1024]{1,0:T(8,128)(2,1)} %get-tuple-element.330), channel_id=1, source_target_pairs={{0,2},{1,3},{2,0},{3,1},{4,6},{5,7},{6,4},{7,5},{8,10},{9,11},{10,... | collective-permute-start | bytes 6291464 | tf_op jit(solution)/shard_map/ppermute | solution.py:1669
  433.5 60.3 %collective-permute-start.59 = (bf16[512,1024]{1,0:T(8,128)(2,1)}, bf16[512,1024]{1,0:T(8,128)(2,1)S(1)}, u32[]{:S(2)}, u32[]{:S(2)}) collective-permute-start(bf16[512,1024]{1,0:T(8,128)(2,1)} %get-tuple-element.333), channel_id=1, source_target_pairs={{0,4},{4,0},{8,12},{12,8},{16,20},{20,16},{24,28},{28,24},{1,5},{5... | collective-permute-start | bytes 3145736 | tf_op jit(solution)/shard_map/ppermute | solution.py:1677
  462.3 28.5 %collective-permute-start.61 = (bf16[256,1024]{1,0:T(8,128)(2,1)S(1)}, bf16[256,1024]{1,0:T(8,128)(2,1)S(1)}, u32[]{:S(2)}, u32[]{:S(2)}) collective-permute-start(bf16[256,1024]{1,0:T(8,128)(2,1)S(1)} %get-tuple-element.335.refs_1_), channel_id=1, source_target_pairs={{0,2},{1,3},{2,0},{3,1},{4,6},{5,7},{6,4},{7,5},{8,10},{9,11},{10,... | collective-permute-start | bytes 1572872 | tf_op jit(solution)/shard_map/ppermute | solution.py:1669
  462.4 32.7 %collective-permute-start.60 = (bf16[256,1024]{1,0:T(8,128)(2,1)S(1)}, bf16[256,1024]{1,0:T(8,128)(2,1)S(1)}, u32[]{:S(2)}, u32[]{:S(2)}) collective-permute-start(bf16[256,1024]{1,0:T(8,128)(2,1)S(1)} %get-tuple-element.335.refs_1_), channel_id=1, source_target_pairs={{0,1},{1,0},{2,3},{3,2},{4,5},{5,4},{6,7},{7,6},{8,9},{9,8},{10,11... | collective-permute-start | bytes 1572872 | tf_op jit(solution)/shard_map/ppermute | solution.py:1673
  490.8 76.1 %collective-permute-start.67 = (bf16[1024,1024]{1,0:T(8,128)(2,1)}, bf16[1024,1024]{1,0:T(8,128)(2,1)S(1)}, u32[]{:S(2)}, u32[]{:S(2)}) collective-permute-start(bf16[1024,1024]{1,0:T(8,128)(2,1)} %get-tuple-element.353), channel_id=1, source_target_pairs={{0,2},{1,3},{2,0},{3,1},{4,6},{5,7},{6,4},{7,5},{8,10},{9,11},{10,... | collective-permute-start | bytes 6291464 | tf_op jit(solution)/shard_map/ppermute | solution.py:1669
  512.9 37.4 %collective-permute-start.65 = (bf16[256,1024]{1,0:T(8,128)(2,1)S(1)}, bf16[256,1024]{1,0:T(8,128)(2,1)S(1)}, u32[]{:S(2)}, u32[]{:S(2)}) collective-permute-start(bf16[256,1024]{1,0:T(8,128)(2,1)S(1)} %get-tuple-element.347), channel_id=1, source_target_pairs={{0,2},{1,3},{2,0},{3,1},{4,6},{5,7},{6,4},{7,5},{8,10},{9,11},{10,... | collective-permute-start | bytes 1572872 | tf_op jit(solution)/shard_map/ppermute | solution.py:1669
  513.2 51.9 %collective-permute-start.66 = (bf16[512,1024]{1,0:T(8,128)(2,1)S(1)}, bf16[512,1024]{1,0:T(8,128)(2,1)S(1)}, u32[]{:S(2)}, u32[]{:S(2)}) collective-permute-start(bf16[512,1024]{1,0:T(8,128)(2,1)S(1)} %copy-done.77), channel_id=1, source_target_pairs={{0,4},{4,0},{8,12},{12,8},{16,20},{20,16},{24,28},{28,24},{1,5},{5... | collective-permute-start | bytes 3145736 | tf_op jit(solution)/shard_map/ppermute | solution.py:1677
  564.7 26.8 %collective-permute-start.72 = (bf16[512,1024]{1,0:T(8,128)(2,1)}, bf16[512,1024]{1,0:T(8,128)(2,1)S(1)}, u32[]{:S(2)}, u32[]{:S(2)}) collective-permute-start(bf16[512,1024]{1,0:T(8,128)(2,1)} %get-tuple-element.366), channel_id=1, source_target_pairs={{0,4},{4,0},{8,12},{12,8},{16,20},{20,16},{24,28},{28,24},{1,5},{5... | collective-permute-start | bytes 3145736 | tf_op jit(solution)/shard_map/ppermute | solution.py:1677
  565.2 26.8 %collective-permute-start.73 = (bf16[512,1024]{1,0:T(8,128)(2,1)}, bf16[512,1024]{1,0:T(8,128)(2,1)}, u32[]{:S(2)}, u32[]{:S(2)}) collective-permute-start(bf16[512,1024]{1,0:T(8,128)(2,1)} %get-tuple-element.367), channel_id=1, source_target_pairs={{0,2},{1,3},{2,0},{3,1},{4,6},{5,7},{6,4},{7,5},{8,10},{9,11},{10,... | collective-permute-start | bytes 3145736 | tf_op jit(solution)/shard_map/ppermute | solution.py:1669
  566.9 46.5 %collective-permute-start.74 = (bf16[512,1024]{1,0:T(8,128)(2,1)}, bf16[512,1024]{1,0:T(8,128)(2,1)}, u32[]{:S(2)}, u32[]{:S(2)}) collective-permute-start(bf16[512,1024]{1,0:T(8,128)(2,1)} %get-tuple-element.370), channel_id=1, source_target_pairs={{0,4},{4,0},{8,12},{12,8},{16,20},{20,16},{24,28},{28,24},{1,5},{5... | collective-permute-start | bytes 3145736 | tf_op jit(solution)/shard_map/ppermute | solution.py:1677
  584.3 32.7 %collective-permute-start.75 = (bf16[256,1024]{1,0:T(8,128)(2,1)}, bf16[256,1024]{1,0:T(8,128)(2,1)S(1)}, u32[]{:S(2)}, u32[]{:S(2)}) collective-permute-start(bf16[256,1024]{1,0:T(8,128)(2,1)} %get-tuple-element.373), channel_id=1, source_target_pairs={{0,1},{1,0},{2,3},{3,2},{4,5},{5,4},{6,7},{7,6},{8,9},{9,8},{10,11... | collective-permute-start | bytes 1572872 | tf_op jit(solution)/shard_map/ppermute | solution.py:1673
  591.1 25.9 %collective-permute-start.76 = (bf16[256,1024]{1,0:T(8,128)(2,1)S(1)}, bf16[256,1024]{1,0:T(8,128)(2,1)S(1)}, u32[]{:S(2)}, u32[]{:S(2)}) collective-permute-start(bf16[256,1024]{1,0:T(8,128)(2,1)S(1)} %get-tuple-element.374), channel_id=1, source_target_pairs={{0,2},{1,3},{2,0},{3,1},{4,6},{5,7},{6,4},{7,5},{8,10},{9,11},{10,... | collective-permute-start | bytes 1572872 | tf_op jit(solution)/shard_map/ppermute | solution.py:1669
  591.4 55.4 %collective-permute-start.77 = (bf16[512,1024]{1,0:T(8,128)(2,1)S(1)}, bf16[512,1024]{1,0:T(8,128)(2,1)S(1)}, u32[]{:S(2)}, u32[]{:S(2)}) collective-permute-start(bf16[512,1024]{1,0:T(8,128)(2,1)S(1)} %copy-done.74), channel_id=1, source_target_pairs={{0,4},{4,0},{8,12},{12,8},{16,20},{20,16},{24,28},{28,24},{1,5},{5... | collective-permute-start | bytes 3145736 | tf_op jit(solution)/shard_map/ppermute | solution.py:1677
  591.9 66.3 %collective-permute-start.78 = (bf16[512,1024]{1,0:T(8,128)(2,1)}, bf16[512,1024]{1,0:T(8,128)(2,1)S(1)}, u32[]{:S(2)}, u32[]{:S(2)}) collective-permute-start(bf16[512,1024]{1,0:T(8,128)(2,1)} %copy-done.75), channel_id=1, source_target_pairs={{0,4},{4,0},{8,12},{12,8},{16,20},{20,16},{24,28},{28,24},{1,5},{5... | collective-permute-start | bytes 3145736 | tf_op jit(solution)/shard_map/ppermute | solution.py:1677
  619.4 77.1 %collective-permute-start.82 = (bf16[512,1024]{1,0:T(8,128)(2,1)}, bf16[512,1024]{1,0:T(8,128)(2,1)S(1)}, u32[]{:S(2)}, u32[]{:S(2)}) collective-permute-start(bf16[512,1024]{1,0:T(8,128)(2,1)} %get-tuple-element.392), channel_id=1, source_target_pairs={{0,4},{4,0},{8,12},{12,8},{16,20},{20,16},{24,28},{28,24},{1,5},{5... | collective-permute-start | bytes 3145736 | tf_op jit(solution)/shard_map/ppermute | solution.py:1677
  646.8 33.9 %collective-permute-start.100 = (f32[4,1024]{1,0:T(4,128)S(1)}, f32[4,1024]{1,0:T(4,128)S(1)}, u32[]{:S(2)}, u32[]{:S(2)}) collective-permute-start(f32[4,1024]{1,0:T(4,128)S(1)} %add.28), channel_id=1, source_target_pairs={{0,4},{4,0},{8,12},{12,8},{16,20},{20,16},{24,28},{28,24},{1,5},{5... | collective-permute-start | bytes 49160 | tf_op jit(solution)/shard_map/ppermute | solution.py:1677
  658.3 24.0 %collective-permute-start.88 = (bf16[128,1024]{1,0:T(8,128)(2,1)S(1)}, bf16[128,1024]{1,0:T(8,128)(2,1)S(1)}, u32[]{:S(2)}, u32[]{:S(2)}) collective-permute-start(bf16[128,1024]{1,0:T(8,128)(2,1)S(1)} %get-tuple-element.407), channel_id=1, source_target_pairs={{0,24},{4,28},{8,16},{12,20},{16,8},{20,12},{24,0},{28,4},{1,25},{... | collective-permute-start | bytes 786440 | tf_op jit(solution)/shard_map/ppermute | solution.py:1681
  659.9 25.2 %collective-permute-start.84 = (bf16[128,1024]{1,0:T(8,128)(2,1)S(1)}, bf16[128,1024]{1,0:T(8,128)(2,1)S(1)}, u32[]{:S(2)}, u32[]{:S(2)}) collective-permute-start(bf16[128,1024]{1,0:T(8,128)(2,1)S(1)} %get-tuple-element.396), channel_id=1, source_target_pairs={{0,16},{4,20},{8,24},{12,28},{16,0},{20,4},{24,8},{28,12},{1,17},{... | collective-permute-start | bytes 786440 | tf_op jit(solution)/shard_map/ppermute | solution.py:1681
  682.6 34.5 %collective-permute-start.89 = (bf16[128,1024]{1,0:T(8,128)(2,1)S(1)}, bf16[128,1024]{1,0:T(8,128)(2,1)S(1)}, u32[]{:S(2)}, u32[]{:S(2)}) collective-permute-start(bf16[128,1024]{1,0:T(8,128)(2,1)S(1)} %get-tuple-element.415), channel_id=1, source_target_pairs={{0,8},{4,12},{8,0},{12,4},{16,24},{20,28},{24,16},{28,20},{1,9},{5... | collective-permute-start | bytes 786440 | tf_op jit(solution)/shard_map/ppermute | solution.py:1681
  685.1 33.9 %collective-permute-start.90 = (bf16[128,1024]{1,0:T(8,128)(2,1)S(1)}, bf16[128,1024]{1,0:T(8,128)(2,1)S(1)}, u32[]{:S(2)}, u32[]{:S(2)}) collective-permute-start(bf16[128,1024]{1,0:T(8,128)(2,1)S(1)} %get-tuple-element.416), channel_id=1, source_target_pairs={{0,16},{4,20},{8,24},{12,28},{16,0},{20,4},{24,8},{28,12},{1,17},{... | collective-permute-start | bytes 786440 | tf_op jit(solution)/shard_map/ppermute | solution.py:1681
  691.7 29.3 %collective-permute-start.91 = (bf16[128,1024]{1,0:T(8,128)(2,1)S(1)}, bf16[128,1024]{1,0:T(8,128)(2,1)S(1)}, u32[]{:S(2)}, u32[]{:S(2)}) collective-permute-start(bf16[128,1024]{1,0:T(8,128)(2,1)S(1)} %get-tuple-element.417), channel_id=1, source_target_pairs={{0,24},{4,28},{8,16},{12,20},{16,8},{20,12},{24,0},{28,4},{1,25},{... | collective-permute-start | bytes 786440 | tf_op jit(solution)/shard_map/ppermute | solution.py:1681
  693.3 28.6 %collective-permute-start.92 = (bf16[128,1024]{1,0:T(8,128)(2,1)S(1)}, bf16[128,1024]{1,0:T(8,128)(2,1)S(1)}, u32[]{:S(2)}, u32[]{:S(2)}) collective-permute-start(bf16[128,1024]{1,0:T(8,128)(2,1)S(1)} %get-tuple-element.425), channel_id=1, source_target_pairs={{0,8},{4,12},{8,0},{12,4},{16,24},{20,28},{24,16},{28,20},{1,9},{5... | collective-permute-start | bytes 786440 | tf_op jit(solution)/shard_map/ppermute | solution.py:1681
  719.0 24.7 %collective-permute-start.95 = (bf16[128,1024]{1,0:T(8,128)(2,1)S(1)}, bf16[128,1024]{1,0:T(8,128)(2,1)S(1)}, u32[]{:S(2)}, u32[]{:S(2)}) collective-permute-start(bf16[128,1024]{1,0:T(8,128)(2,1)S(1)} %get-tuple-element.435), channel_id=1, source_target_pairs={{0,8},{4,12},{8,0},{12,4},{16,24},{20,28},{24,16},{28,20},{1,9},{5... | collective-permute-start | bytes 786440 | tf_op jit(solution)/shard_map/ppermute | solution.py:1681
  721.0 36.6 %collective-permute-start.96 = (bf16[128,1024]{1,0:T(8,128)(2,1)S(1)}, bf16[128,1024]{1,0:T(8,128)(2,1)S(1)}, u32[]{:S(2)}, u32[]{:S(2)}) collective-permute-start(bf16[128,1024]{1,0:T(8,128)(2,1)S(1)} %get-tuple-element.436), channel_id=1, source_target_pairs={{0,16},{4,20},{8,24},{12,28},{16,0},{20,4},{24,8},{28,12},{1,17},{... | collective-permute-start | bytes 786440 | tf_op jit(solution)/shard_map/ppermute | solution.py:1681
  721.9 35.7 %collective-permute-start.97 = (bf16[128,1024]{1,0:T(8,128)(2,1)S(1)}, bf16[128,1024]{1,0:T(8,128)(2,1)S(1)}, u32[]{:S(2)}, u32[]{:S(2)}) collective-permute-start(bf16[128,1024]{1,0:T(8,128)(2,1)S(1)} %get-tuple-element.437), channel_id=1, source_target_pairs={{0,24},{4,28},{8,16},{12,20},{16,8},{20,12},{24,0},{28,4},{1,25},{... | collective-permute-start | bytes 786440 | tf_op jit(solution)/shard_map/ppermute | solution.py:1681
  (148 other events, 1696.2 us)

commit v2 on v1

--- a/solution.py
+++ b/solution.py
@@ -503,31 +503,147 @@
     return pl.CostEstimate(flops=int(flops), bytes_accessed=int(moved), transcendentals=int(exps))
 
 
-def settings(limit=48):
-    return pltpu.CompilerParams(vmem_limit_bytes=limit * MIB)
+weight_of = {
+    "global_heads": 13,
+    "global_ff": 12,
+    "local_heads": 18,
+    "local_ff": 34,
+    "local_ff_back": 14,
+    "local_heads_back": 11,
+    "global_ff_back": 9,
+    "global_ff_grads": 5,
+    "global_heads_back": 12,
+    "global_heads_grads": 5,
+    "adam_update": 5,
+}
+
+
+def group_at(rel):
+    mine = lax.axis_index("tensor")
+    return 2 * ((mine // 2 + rel // 2) % 2) + (mine % 2 + rel % 2) % 2
+
+
+def partner_of(hop):
+    dp, tensor = lax.axis_index("dp"), lax.axis_index("tensor")
+    if hop == "core":
+        return {"tensor": tensor + 1 - 2 * (tensor % 2)}
+    if hop == "x":
+        return {"tensor": (tensor + 2) % 4}
+    if hop == "y":
+        return {"dp": dp + 1 - 2 * (dp % 2)}
+    if hop == "z1":
+        return {"dp": dp + 2 - 4 * ((dp // 2) % 2)}
+    return {"dp": (dp + 4) % 8}
+
+
+def greet(hops):
+    barrier = pltpu.get_barrier_semaphore()
+    for hop in hops:
+        pl.semaphore_signal(
+            barrier, inc=1, device_id=partner_of(hop), device_id_type=pl.DeviceIdType.MESH
+        )
+    pl.semaphore_wait(barrier, len(hops))
+
+
+def to_partner(hop, source, target, send, recv):
+    return pltpu.make_async_remote_copy(
+        src_ref=source,
+        dst_ref=target,
+        send_sem=send,
+        recv_sem=recv,
+        device_id=partner_of(hop),
+        device_id_type=pl.DeviceIdType.MESH,
+    )
+
+
+def part(array, begin, rows):
+    return (array, begin, rows)
+
 
 class Line:
     def __init__(self):
         self.token = None
-
-    def run(self, body, args, in_specs, out_specs, out_shape, aliases=None, **rest):
+        self.moves = ()
+        self.arrived = []
+        self.calls = 0
+
+    def carry(self, *moves):
+        self.moves = moves
+
+    def run(self, body, args, in_specs, out_specs, out_shape, aliases=None, scratch_shapes=(), limit=32, hops=(), **rest):
+        moves, self.moves = self.moves, ()
+        sources, copies, landed = [], [], []
+        for hop, *pieces in moves:
+            offset = 0
+            for piece in pieces:
+                array, begin, rows = piece if isinstance(piece, tuple) else (piece, 0, piece.shape[0])
+                which = next((at for at, one in enumerate(sources) if one is array), len(sources))
+                if which == len(sources):
+                    sources.append(array)
+                copies.append((hop, which, begin, rows, len(landed), offset))
+                offset += rows
+            landed.append(shaped((offset,) + array.shape[1:], array.dtype))
+        reach = list(hops) + [hop for hop in dict.fromkeys(move[0] for move in moves) if hop not in hops]
         lead = 0 if self.token is None else 1
-        inputs, outputs = lead + len(args), len(out_shape)
+        inputs = lead + len(args)
+        first_out = inputs + len(sources)
+        outputs = len(out_shape)
+        first_scratch = first_out + outputs + len(landed) + 1
+        steps = rest.get("grid", (1,))[0]
 
         def inner(*refs):
-            body(*refs[lead:inputs], *refs[inputs : inputs + outputs], *refs[inputs + outputs + 1 :])
-
+            scratch = refs[first_scratch:]
+            pending = []
+            if copies:
+                *scratch, send, recv = scratch
+                for at, (hop, which, begin, rows, where, offset) in enumerate(copies):
+                    pending.append(
+                        to_partner(
+                            hop,
+                            refs[inputs + which].at[pl.ds(begin, rows)],
+                            refs[first_out + outputs + where].at[pl.ds(offset, rows)],
+                            send.at[at],
+                            recv.at[at],
+                        )
+                    )
+
+            def begin_all():
+                greet(reach)
+                for one in pending:
+                    one.start()
+
+            def end_all():
+                for one in pending:
+                    one.wait()
+
+            at_ends = (lambda step, act: pl.when(pl.program_id(0) == step)(act)) if steps > 1 else (
+                lambda step, act: act()
+            )
+            if reach:
+                at_ends(0, begin_all)
+            body(*refs[lead:inputs], *refs[first_out : first_out + outputs], *scratch)
+            if pending:
+                at_ends(steps - 1, end_all)
+
+        extra = {}
+        if reach:
+            extra = {"collective_id": self.calls, "has_side_effects": True}
+            self.calls += 1
         found = pl.pallas_call(
             inner,
-            in_specs=[IN_HBM] * lead + list(in_specs),
-            out_specs=list(out_specs) + [IN_HBM],
-            out_shape=list(out_shape) + [shaped((8, 128), jnp.float32)],
+            in_specs=[IN_HBM] * lead + list(in_specs) + [IN_HBM] * len(sources),
+            out_specs=list(out_specs) + [IN_HBM] * (len(landed) + 1),
+            out_shape=list(out_shape) + landed + [shaped((8, 128), jnp.float32)],
+            scratch_shapes=list(scratch_shapes)
+            + ([pltpu.SemaphoreType.DMA((len(copies),))] * 2 if copies else []),
             input_output_aliases={lead + at: to for at, to in (aliases or {}).items()},
-            cost_estimate=cost(1000, 1000),
+            cost_estimate=cost(weight_of.get(rest["name"], 1.0) * 0.2e9, 1000),
+            compiler_params=pltpu.CompilerParams(vmem_limit_bytes=limit * MIB, **extra),
             **rest,
-        )(*([self.token] * lead), *args)
+        )(*([self.token] * lead), *args, *sources)
         self.token = found[-1]
-        return list(found[:-1])
+        self.arrived = list(found[outputs:-1])
+        return list(found[:outputs])
 
 
 def lanes_of(source_ref, at, width):
@@ -594,7 +710,7 @@
             shaped(gains.shape, jnp.float32),
             shaped(frames.shape, jnp.bfloat16),
         ],
-        compiler_params=settings(16),
+        limit=(16),
         name="prep_rows",
     )
 
@@ -618,7 +734,7 @@
         in_specs=[VMEM_WHOLE] * 5,
         out_specs=[VMEM_WHOLE] * len(outs),
         out_shape=outs,
-        compiler_params=settings(16),
+        limit=(16),
         name="merge_rows",
     )
 
@@ -649,7 +765,7 @@
             shaped(rows.shape, jnp.bfloat16),
             shaped((1, rows.shape[1]), jnp.float32),
         ],
-        compiler_params=settings(16),
+        limit=(16),
         name="merge_rows_back",
     )
 
@@ -681,7 +797,7 @@
         in_specs=[IN_SMEM] + [VMEM_WHOLE] * 9,
         out_specs=[VMEM_WHOLE] * 2,
         out_shape=[shaped(rows.shape, jnp.float32), shaped((4, rows.shape[1]), jnp.float32)],
-        compiler_params=settings(16),
+        limit=(16),
         name="input_grad",
     )
 
@@ -692,10 +808,10 @@
     share = x0.shape[0]
     span = 4 * share
     width = mixed_ref.shape[1]
-    mine, length = info_ref[0], info_ref[1]
+    length = info_ref[1]
     scale = HD ** (-0.5)
     for rel, x_ref in enumerate((x0, x1, x2, x3)):
-        at = pl.ds(pl.multiple_of((mine ^ rel) * share, share), share)
+        at = pl.ds(pl.multiple_of(group_at(rel) * share, share), share)
         full = both(x_ref[...], near_ref[:, : 3 * width], far_ref[:, : 3 * width])
         qkv_ref[at, :] = full.astype(jnp.bfloat16)
     acc[...] = jnp.zeros_like(acc)
@@ -726,7 +842,7 @@
     lse_ref[...] = jnp.transpose(lse_wide[...])[: lse_ref.shape[0], :]
     half = near_ref.shape[0]
     for rel, p_ref in enumerate((p0, p1, p2, p3)):
-        at = pl.ds(pl.multiple_of((mine ^ rel) * share, share), share)
+        at = pl.ds(pl.multiple_of(group_at(rel) * share, share), share)
         rows = mixed_ref[at, :]
         p_ref[:, :half] = dot_transposed(rows, near_ref[:, 3 * width :]).astype(jnp.bfloat16)
         p_ref[:, half:] = dot_transposed(rows, far_ref[:, 3 * width :]).astype(jnp.bfloat16)
@@ -747,7 +863,7 @@
         ]
         + [shaped((share, D), jnp.bfloat16)] * 4,
         scratch_shapes=[pltpu.VMEM((span, width), jnp.float32), pltpu.VMEM((span, 128), jnp.float32)],
-        compiler_params=settings(40),
+        limit=(40),
         name="global_heads",
     )
 
@@ -759,10 +875,10 @@
     share = g0.shape[0]
     width = mixed_ref.shape[1]
     heads = width // HD
-    mine, length = info_ref[0], info_ref[1]
+    length = info_ref[1]
     scale = HD ** (-0.5)
     for rel, g_ref in enumerate((g0, g1, g2, g3)):
-        at = pl.ds(pl.multiple_of((mine ^ rel) * share, share), share)
+        at = pl.ds(pl.multiple_of(group_at(rel) * share, share), share)
         full = both(g_ref[...], near_ref[:, 3 * width :], far_ref[:, 3 * width :])
         dmix[at, :] = full.astype(jnp.bfloat16)
     head_of = lax.broadcasted_iota(jnp.int32, (1, width), 1) // HD
@@ -804,7 +920,7 @@
     dqkv_ref[:, 2 * width :] = dv_acc[...].astype(jnp.bfloat16)
     half = near_ref.shape[0]
     for rel, p_ref in enumerate((p0, p1, p2, p3)):
-        at = pl.ds(pl.multiple_of((mine ^ rel) * share, share), share)
+        at = pl.ds(pl.multiple_of(group_at(rel) * share, share), share)
         rows = dqkv_ref[at, :]
         p_ref[:, :half] = dot_transposed(rows, near_ref[:, : 3 * width]).astype(jnp.bfloat16)
         p_ref[:, half:] = dot_transposed(rows, far_ref[:, : 3 * width]).astype(jnp.bfloat16)
@@ -828,7 +944,7 @@
             pltpu.VMEM((8, span), jnp.float32),
             pltpu.VMEM((width, span), jnp.bfloat16),
         ],
-        compiler_params=settings(40),
+        limit=(40),
         name="global_heads_back",
     )
 
@@ -838,9 +954,8 @@
 ):
     share = a0.shape[0]
     width = mixed_ref.shape[1]
-    mine = info_ref[0]
     for rel in range(4):
-        at = pl.ds(pl.multiple_of((mine ^ rel) * share, share), share)
+        at = pl.ds(pl.multiple_of(group_at(rel) * share, share), share)
         a_t[:, at] = jnp.transpose((a0, a1, a2, a3)[rel][...])
         g_t[:, at] = jnp.transpose((g0, g1, g2, g3)[rel][...])
 
@@ -861,7 +976,7 @@
         out_specs=[VMEM_WHOLE] * 2,
         out_shape=[shaped((D // 2, 4 * width), jnp.bfloat16)] * 2,
         scratch_shapes=[pltpu.VMEM((D, span), jnp.bfloat16)] * 2,
-        compiler_params=settings(40),
+        limit=(40),
         name="global_heads_grads",
     )
 
@@ -910,7 +1025,7 @@
         out_shape=[shaped((span, hidden), jnp.bfloat16)] * 2
         + [shaped((share, D), jnp.bfloat16)] * 4,
         scratch_shapes=[pltpu.VMEM((span, D), jnp.float32)],
-        compiler_params=settings(40),
+        limit=(40),
         name="global_ff",
     )
 
@@ -950,7 +1065,7 @@
         out_specs=[by_cols((span, tile))] + [held((share, D))] * 4,
         out_shape=[shaped((span, hidden), jnp.bfloat16)] + [shaped((share, D), jnp.bfloat16)] * 4,
         scratch_shapes=[pltpu.VMEM((span, D), jnp.float32)],
-        compiler_params=settings(40),
+        limit=(40),
         name="global_ff_back",
     )
 
@@ -982,7 +1097,7 @@
         out_specs=[by_cols((D // 2, tile))] * 2,
         out_shape=[shaped((D // 2, hidden), jnp.bfloat16)] * 2,
         scratch_shapes=[pltpu.VMEM((D, span), jnp.bfloat16)],
-        compiler_params=settings(32),
+        limit=(32),
         name="global_ff_grads",
     )
 
@@ -1031,7 +1146,7 @@
 
 
 def local_heads_body(
-    source_ref, out_ref_in, code_ref, gains_ref, *refs
+    out_ref_in, code_ref, gains_ref, *refs
 ):
     count = 4
     parts = [refs[2 * at : 2 * at + 2] for at in range(count)]
@@ -1044,14 +1159,9 @@
     @pl.when(step == 0)
     def _():
         start_weights(parts, buffer, sems)
-        owned = D // source_ref.shape[0]
         for c in range(CB):
             rows = slice(c * frames, (c + 1) * frames)
-            for at in range(source_ref.shape[0]):
-                here = slice(at * owned, (at + 1) * owned)
-                local_in[rows, here] = out_ref_in[:, here] + code_ref[
-                    c, :, lanes_of(source_ref, at, owned)
-                ].astype(jnp.float32)
+            local_in[rows, :] = out_ref_in[...] + code_ref[rows, :].astype(jnp.float32)
             normed = norm_rows(local_in[rows, :], gains_ref[2:3, :]).astype(jnp.bfloat16)
             normed_a[rows, :] = normed
             a_t_ref[:, rows] = jnp.transpose(normed)
@@ -1091,7 +1201,7 @@
             )
 
 
-def local_heads(line, source, global_out, codes, gains, parts):
+def local_heads(line, global_out, codes, gains, parts):
     frames = global_out.shape[0]
     rows = CB * frames
     width = parts[0][0].shape[1] // 4
@@ -1099,9 +1209,9 @@
     flat = [ref for pair in parts for ref in pair]
     return line.run(
         local_heads_body,
-        (source, global_out, codes, gains, *flat,),
+        (global_out, codes, gains, *flat),
         grid=(4,),
-        in_specs=[IN_SMEM, held((frames, D)), held((CB, frames, D)), held((4, D))] + [IN_HBM] * 8,
+        in_specs=[held((frames, D)), held((rows, D)), held((4, D))] + [IN_HBM] * 8,
         out_specs=[
             pl.BlockSpec((1, rows, 3 * width), lambda step: (step, 0, 0)),
             pl.BlockSpec((1, rows, width), lambda step: (step, 0, 0)),
@@ -1122,7 +1232,7 @@
             pltpu.VMEM((4, 2, half, 4 * width), jnp.bfloat16),
             pltpu.SemaphoreType.DMA((4, 2)),
         ],
-        compiler_params=settings(52),
+        limit=(52),
         name="local_heads",
     )
 
@@ -1207,12 +1317,12 @@
             pltpu.SemaphoreType.DMA((4, 2)),
             pltpu.SemaphoreType.DMA((4, 2)),
         ],
-        compiler_params=settings(56),
+        limit=(56),
         name="local_ff",
     )
 
 
-def seed_body(source_ref, count_ref, cot_ref, grad_ref, grad_t_ref):
+def seed_body(source_ref, count_ref, cot_ref, code_ref, grad_ref, grad_t_ref, codes_ref):
     frames = cot_ref.shape[1]
     owned = D // source_ref.shape[0]
     keep = lax.broadcasted_iota(jnp.int32, (frames, 1), 0) < count_ref[0]
@@ -1222,19 +1332,24 @@
             here = slice(at * owned, (at + 1) * owned)
             values = cot_ref[c, :, lanes_of(source_ref, at, owned)].astype(jnp.float32)
             grad_ref[rows, here] = jnp.where(keep, values, 0.0).astype(jnp.bfloat16)
+            codes_ref[rows, here] = code_ref[c, :, lanes_of(source_ref, at, owned)]
         grad_t_ref[:, rows] = jnp.transpose(grad_ref[rows, :])
 
 
-def seed(line, source, count, cot):
+def seed(line, source, count, cot, codes):
     frames = cot.shape[1]
     rows = CB * frames
     return line.run(
         seed_body,
-        (source, count, cot,),
-        in_specs=[IN_SMEM, IN_SMEM, VMEM_WHOLE],
-        out_specs=[VMEM_WHOLE] * 2,
-        out_shape=[shaped((rows, D), jnp.bfloat16), shaped((D, rows), jnp.bfloat16)],
-        compiler_params=settings(24),
+        (source, count, cot, codes),
+        in_specs=[IN_SMEM, IN_SMEM, VMEM_WHOLE, VMEM_WHOLE],
+        out_specs=[VMEM_WHOLE] * 3,
+        out_shape=[
+            shaped((rows, D), jnp.bfloat16),
+            shaped((D, rows), jnp.bfloat16),
+            shaped((rows, D), jnp.bfloat16),
+        ],
+        limit=(24),
         name="seed_grads",
     )
 
@@ -1246,7 +1361,7 @@
     if last:
         middle_ref, gains_ref, refs = refs[0], refs[1], refs[2:]
     if summed:
-        down_near, down_far, g_up, refs = refs[0], refs[1], refs[2], refs[3:]
+        (down_near, down_far, up_near, up_far), refs = refs[:4], refs[4:]
     else:
         both_ref, refs = refs[0], refs[1:]
     outs, (acc, dup) = refs[:-2], refs[-2:]
@@ -1275,11 +1390,11 @@
         up = dot_rows(b_t_ref[rows, :], dup[...])
         if summed:
             down = (down + met_ref[0, rows, :].astype(jnp.float32)).astype(jnp.bfloat16)
-            if at * 256 < half:
-                down_near[rows, :] = down
-            else:
-                down_far[at * 256 - half : at * 256 - half + 256, :] = down
-            g_up[rows, :] = (up + met_ref[1, rows, :].astype(jnp.float32)).astype(jnp.bfloat16)
+            up = (up + met_ref[1, rows, :].astype(jnp.float32)).astype(jnp.bfloat16)
+            begin = 0 if at * 256 < half else half
+            there = slice(at * 256 - begin, at * 256 - begin + 256)
+            (down_far if begin else down_near)[there, :] = down
+            (up_far if begin else up_near)[there, :] = up
         else:
             both_ref[0, rows, :] = down.astype(jnp.bfloat16)
             both_ref[1, rows, :] = up.astype(jnp.bfloat16)
@@ -1330,8 +1445,8 @@
     else:
         outs = [shaped((rows, D), jnp.float32)]
     if summed:
-        grad_specs = [by_cols((half, tile)), by_cols((half, tile)), by_cols((D, tile))]
-        grad_shapes = [shaped((half, hidden), jnp.bfloat16)] * 2 + [shaped((D, hidden), jnp.bfloat16)]
+        grad_specs = [by_cols((half, tile))] * 4
+        grad_shapes = [shaped((half, hidden), jnp.bfloat16)] * 4
     else:
         grad_specs = [pair_block]
         grad_shapes = [shaped((2, D, hidden), jnp.bfloat16)]
@@ -1349,7 +1464,7 @@
         out_specs=grad_specs + [held(one.shape) for one in outs],
         out_shape=grad_shapes + outs,
         scratch_shapes=[pltpu.VMEM((rows, D), jnp.float32), pltpu.VMEM((rows, tile), jnp.bfloat16)],
-        compiler_params=settings(52),
+        limit=(52),
         name="local_ff_back",
     )
     return found[: len(grad_shapes)], found[len(grad_shapes) :]
@@ -1361,9 +1476,12 @@
     if not first:
         so_far_ref, refs = refs[0], refs[1:]
     if last:
-        grad_mid_ref, out_in_ref, code_ref, source_ref, gains_ref = refs[:5]
-        refs = refs[5:]
-    out_ref, refs = refs[0], refs[1:]
+        grad_mid_ref, out_in_ref, code_ref, gains_ref = refs[:4]
+        refs = refs[4:]
+    if summed:
+        (near_out, far_out), refs = refs[:2], refs[2:]
+    else:
+        out_ref, refs = refs[0], refs[1:]
     outs, (acc, dqkv) = refs[:-2], refs[-2:]
     frames = grad_ref.shape[0] // CB
     width = mixed_ref.shape[2]
@@ -1410,26 +1528,22 @@
         rows = slice(at * 256, (at + 1) * 256)
         three = dot_rows(a_t_ref[rows, :], dqkv[...])
         one = dot_rows(grad_t_ref[rows, :], mixed_ref[0])
+        there = rows
         if summed:
             three = three + met_ref[rows, : 3 * width].astype(jnp.float32)
             one = one + met_ref[rows, 3 * width :].astype(jnp.float32)
-        out_ref[rows, : 3 * width] = three.astype(jnp.bfloat16)
-        out_ref[rows, 3 * width :] = one.astype(jnp.bfloat16)
+            begin = 0 if at * 256 < half else half
+            out_ref = far_out if begin else near_out
+            there = slice(at * 256 - begin, at * 256 - begin + 256)
+        out_ref[there, : 3 * width] = three.astype(jnp.bfloat16)
+        out_ref[there, 3 * width :] = one.astype(jnp.bfloat16)
     if last:
         total_ref, small_ref, gain_ref = outs
-        owned = D // source_ref.shape[0]
         total_gain = jnp.zeros((1, D), jnp.float32)
         total = jnp.zeros((frames, D), jnp.float32)
         for c in range(CB):
             rows = slice(c * frames, (c + 1) * frames)
-            local_in = jnp.concatenate(
-                [
-                    out_in_ref[:, at * owned : (at + 1) * owned]
-                    + code_ref[c, :, lanes_of(source_ref, at, owned)].astype(jnp.float32)
-                    for at in range(source_ref.shape[0])
-                ],
-                axis=1,
-            )
+            local_in = out_in_ref[...] + code_ref[rows, :].astype(jnp.float32)
             part, gain_grad = norm_rows_back(local_in, gains_ref[2:3, :], acc[rows, :])
             total = total + (grad_mid_ref[rows, :] + part)
             total_gain = total_gain + gain_grad
@@ -1454,7 +1568,7 @@
         extra.append(held((rows, D)))
     if last:
         extra_args += list(tail)
-        extra += [held((rows, D)), held((frames, D)), held((CB, frames, D)), IN_SMEM, held((4, D))]
+        extra += [held((rows, D)), held((frames, D)), held((rows, D)), held((4, D))]
         outs = [
             shaped((frames, D), jnp.float32),
             shaped((frames, D), jnp.bfloat16),
@@ -1462,6 +1576,11 @@
         ]
     else:
         outs = [shaped((rows, D), jnp.float32)]
+
+    if summed:
+        grad_shapes = [shaped((D // 2, 4 * width), jnp.bfloat16)] * 2
+    else:
+        grad_shapes = [shaped((D, 4 * width), jnp.bfloat16)]
 
     def body(*refs):
         local_heads_back_body(last, summed, first, *refs)
@@ -1479,40 +1598,46 @@
         ]
         + [held((D // 2, 4 * width))] * 2
         + extra,
-        out_specs=[held((D, 4 * width))] + [held(one.shape) for one in outs],
-        out_shape=[shaped((D, 4 * width), jnp.bfloat16)] + outs,
+        out_specs=[held(one.shape) for one in grad_shapes + outs],
+        out_shape=grad_shapes + outs,
         scratch_shapes=[
             pltpu.VMEM((rows, D), jnp.float32),
             pltpu.VMEM((rows, 3 * width), jnp.bfloat16),
         ],
-        compiler_params=settings(52),
+        limit=(52),
         name="local_heads_back",
     )
-    return found[0], found[1:]
-
-
-def cast_body(master_ref, out_ref):
-    out_ref[...] = master_ref[0].astype(jnp.bfloat16)
-
-
-def cast(line, master, layer, third):
+    return found[: len(grad_shapes)], found[len(grad_shapes) :]
+
+
+def cast_body(*refs):
+    count = len(refs) // 2
+    for master_ref, out_ref in zip(refs[:count], refs[count:]):
+        out_ref[...] = master_ref[0].astype(jnp.bfloat16)
+
+
+def cast(line, master, which):
     owned, columns = master.shape[1], master.shape[2] // 3
+
+    def spec(layer, third):
+        return pl.BlockSpec((1, owned, columns), lambda step: (layer, 0, third))
+
     return line.run(
         cast_body,
-        (master,),
+        (master,) * len(which),
         grid=(1,),
-        in_specs=[pl.BlockSpec((1, owned, columns), lambda step: (layer, 0, third))],
-        out_specs=[held((owned, columns))],
-        out_shape=[shaped((owned, columns), jnp.bfloat16)],
-        compiler_params=settings(16),
+        in_specs=[spec(*one) for one in which],
+        out_specs=[held((owned, columns))] * len(which),
+        out_shape=[shaped((owned, columns), jnp.bfloat16)] * len(which),
+        limit=(24),
         name="cast_shard",
-    )[0]
-
-
-def stack_body(p0, p1, p2, p3, out_ref):
-    rows = p0.shape[0]
-    for at, ref in enumerate((p0, p1, p2, p3)):
-        out_ref[at * rows : (at + 1) * rows, :] = ref[...]
+    )
+
+
+def stack_body(one_ref, two_ref, out_ref):
+    rows = one_ref.shape[0]
+    out_ref[:rows, :] = one_ref[...]
+    out_ref[rows:, :] = two_ref[...]
 
 
 def stack_rows(line, parts):
@@ -1520,10 +1645,10 @@
     return line.run(
         stack_body,
         tuple(parts),
-        in_specs=[VMEM_WHOLE] * 4,
+        in_specs=[VMEM_WHOLE] * 2,
         out_specs=[VMEM_WHOLE],
-        out_shape=[shaped((4 * rows, columns), jnp.bfloat16)],
-        compiler_params=settings(16),
+        out_shape=[shaped((2 * rows, columns), jnp.bfloat16)],
+        limit=(16),
         name="stack_shards",
     )[0]
 
@@ -1551,33 +1676,33 @@
         in_specs=[spec(term) for term in terms],
         out_specs=[pl.BlockSpec((rows, columns), lambda step: (0, 0))],
         out_shape=[shaped((rows, columns), jnp.bfloat16)],
-        compiler_params=settings(24),
+        limit=(24),
         name="add_terms",
     )[0]
 
 
-def pieces_body(*refs):
-    terms, outs = refs[:-4], refs[-4:]
-    rows = outs[0].shape[0]
-    for at, out_ref in enumerate(outs):
-        here = slice(at * rows, (at + 1) * rows)
-        total = terms[0][here, :].astype(jnp.float32)
-        for ref in terms[1:]:
-            total = total + ref[here, :].astype(jnp.float32)
-        out_ref[...] = total.astype(jnp.bfloat16)
-
-
-def sum_pieces(line, terms):
-    half, columns = D // 2, terms[0].shape[1]
-    near = pl.BlockSpec((half, columns), lambda step: (0, 0))
+def sum_pieces(line, terms, split=()):
+    rows, columns = terms[0].shape[0] // 2, terms[0].shape[1]
+    whole = len(terms)
+    flat = list(terms) + [one for pair in split for one in pair]
+
+    def body(*refs):
+        for at, out_ref in enumerate(refs[-2:]):
+            here = slice(at * rows, (at + 1) * rows)
+            total = refs[0][here, :].astype(jnp.float32)
+            for ref in refs[1:whole]:
+                total = total + ref[here, :].astype(jnp.float32)
+            for ref in refs[whole + at : -2 : 2]:
+                total = total + ref[...].astype(jnp.float32)
+            out_ref[...] = total.astype(jnp.bfloat16)
+
     return line.run(
-        pieces_body,
-        tuple(terms),
-        grid=(1,),
-        in_specs=[near] * len(terms),
-        out_specs=[held((half // 4, columns))] * 4,
-        out_shape=[shaped((half // 4, columns), jnp.bfloat16)] * 4,
-        compiler_params=settings(24),
+        body,
+        tuple(flat),
+        in_specs=[VMEM_WHOLE] * len(flat),
+        out_specs=[VMEM_WHOLE] * 2,
+        out_shape=[shaped((rows, columns), jnp.bfloat16)] * 2,
+        limit=24,
         name="sum_pieces",
     )
 
@@ -1608,13 +1733,11 @@
     )
 
 
-def adam_body(chained, p0, p1, p2, p3, left_ref, right_ref, master_ref, first_ref, second_ref, ema_ref, *refs):
+def adam_body(chained, one_ref, two_ref, left_ref, right_ref, master_ref, first_ref, second_ref, ema_ref, *refs):
     grads_ref, new_master_ref, new_first_ref, new_second_ref, new_ema_ref = refs[5:] if chained else refs
     left = left_ref[0]
     left_t = jnp.transpose(left)
-    grads = p0[...].astype(jnp.float32)
-    for ref in (p1, p2, p3):
-        grads = grads + ref[...].astype(jnp.float32)
+    grads = one_ref[...].astype(jnp.float32) + two_ref[...].astype(jnp.float32)
     grads_ref[0] = grads
     turned_left = split_dot(left_t, grads)
     back = []
@@ -1648,7 +1771,7 @@
         lambda *refs: adam_body(chained, *refs),
         (*pieces, left, right, master, first, second, ema, *(before or ()),),
         grid=(steps,),
-        in_specs=[by_cols((owned, tile))] * 4
+        in_specs=[by_cols((owned, tile))] * 2
         + [
             pl.BlockSpec((1,) + left.shape[1:], lambda step: (layer, 0, 0)),
             pl.BlockSpec(
@@ -1659,8 +1782,8 @@
         + ([IN_HBM] * 5 if chained else []),
         out_specs=[state_spec] * 5,
         out_shape=[shaped(master.shape, jnp.float32)] * 5,
-        aliases={10 + at: at for at in range(5)} if chained else {},
-        compiler_params=settings(32),
+        aliases={8 + at: at for at in range(5)} if chained else {},
+        limit=(32),
         name="adam_update",
     )
 
@@ -1679,15 +1802,6 @@
 
 def hop_z(values, step):
     return lax.ppermute(values, "dp", [(at, at ^ (2 * step)) for at in range(8)])
-
-
-def rows_gather(rows):
-    over_x = hop_x(rows)
-    return [rows, hop_core(rows), over_x, hop_core(over_x)]
-
-
-def depth_hops(piece):
-    return [hop_z(piece, step) for step in (1, 2, 3)]
 
 
 def total_everywhere(values):
@@ -1722,10 +1836,11 @@
     my_dp = lax.axis_index("dp")
     my_group = lax.axis_index("tensor").astype(jnp.int32)
 
-    rel = jnp.array([2 * z + y for y in range(2) for z in range(4)], jnp.int32)
+    rel = jnp.array([2 * z + y for y in range(2) for z in (0, 2, 1, 3)], jnp.int32)
+    owner_at = my_dp ^ rel
     slots = jnp.arange(groups, dtype=jnp.int32)
     source = jnp.sum(
-        jnp.where(owner_list[None, :] == (my_dp ^ rel)[:, None], slots[None, :], 0), axis=1
+        jnp.where(owner_list[None, :] == owner_at[:, None], slots[None, :], 0), axis=1
     ).astype(jnp.int32)
     info = jnp.stack([my_group, lengths[0]])
     count = (lengths - my_group * share).astype(jnp.int32)
@@ -1733,63 +1848,66 @@
     line = Line()
     codes = jnp.transpose(code_emb, (1, 0, 2))
 
-    def share_shard(layer, third):
-        shard = cast(line, master, layer, third)
-        return [shard] + depth_hops(shard)
-
-    g_heads = share_shard(0, 0)
+    (ga,) = cast(line, master, [(0, 0)])
+    ga_z = hop_z(ga, 2)
     rows_in, gains_here, normed = prep(line, source, frames_in, gains)
-    normed_a = rows_gather(normed)
-    l_heads = share_shard(1, 0)
-    near = stack_rows(line, g_heads)
-    g_heads = (near, hop_y(near))
-    g_up = share_shard(0, 1)
-    lh_near = stack_rows(line, l_heads)
-    lh_far, lh_near_c, lh_near_x = hop_y(lh_near), hop_core(lh_near), hop_x(lh_near)
-    l_up = share_shard(1, 1)
+    normed_x = hop_x(normed)
+    la, gu, lu, gd, ld = cast(line, master, [(1, 0), (0, 1), (1, 1), (0, 2), (1, 2)])
+    ga = stack_rows(line, [ga, ga_z])
+    ga_z, la_z = hop_z(ga, 1), hop_z(la, 2)
+    (normed_x,) = in_turn(line, normed_x)
+    normed_a = [normed, hop_core(normed), normed_x, hop_core(normed_x)]
+    ga = stack_rows(line, [ga, ga_z])
+    la = stack_rows(line, [la, la_z])
+    ga_far, la_z, gu_z = hop_y(ga), hop_z(la, 1), hop_z(gu, 2)
+    la = stack_rows(line, [la, la_z])
+    gu = stack_rows(line, [gu, gu_z])
+    la_far, la_x, gu_z, lu_z = hop_y(la), hop_x(la), hop_z(gu, 1), hop_z(lu, 2)
+    g_heads = (ga, ga_far)
     qkv, mixed, lse, *parts = global_heads(line, info, normed_a, g_heads)
     near_term, far_term = hop_core(parts[1]), hop_core(parts[3])
-    near = stack_rows(line, g_up)
-    g_up = (near, hop_y(near))
+    gu = stack_rows(line, [gu, gu_z])
+    lu = stack_rows(line, [lu, lu_z])
+    gu_far, lu_z, gd_z = hop_y(gu), hop_z(lu, 1), hop_z(gd, 2)
     to_x = hop_x(add_rows(line, [parts[2], far_term]))
-    g_down = share_shard(0, 2)
-    (lh_far,) = in_turn(line, lh_far)
-    lh_far_c, lh_far_x = hop_core(lh_far), hop_x(lh_far)
-    lu_near = stack_rows(line, l_up)
-    lu_far, lu_near_c, lu_near_x = hop_y(lu_near), hop_core(lu_near), hop_x(lu_near)
+    la_far, la_x = in_turn(line, la_far, la_x)
+    lu = stack_rows(line, [lu, lu_z])
+    gd = stack_rows(line, [gd, gd_z])
+    lu_far, gd_z, ld_z = hop_y(lu), hop_z(gd, 1), hop_z(ld, 2)
     middle, normed = merge(line, rows_in, (parts[0], near_term, to_x), gains_here, 1)
-    normed_b = rows_gather(normed)
-    l_down = share_shard(1, 2)
-    (lh_near_x,) = in_turn(line, lh_near_x)
-    lh_near_xc = hop_core(lh_near_x)
-    grad, grad_t = seed(line, source, count, jnp.transpose(cotangent, (1, 0, 2)))
-    near = stack_rows(line, g_down)
-    g_down = (near, hop_y(near))
-    (lu_far,) = in_turn(line, lu_far)
-    lu_far_c, lu_far_x = hop_core(lu_far), hop_x(lu_far)
-    ld_near = stack_rows(line, l_down)
-    ld_far, ld_near_c, ld_near_x = hop_y(ld_near), hop_core(ld_near), hop_x(ld_near)
+    normed_x = hop_x(normed)
+    gd = stack_rows(line, [gd, gd_z])
+    ld = stack_rows(line, [ld, ld_z])
+    gd_far, ld_z = hop_y(gd), hop_z(ld, 1)
+    (normed_x, la_far, lu) = in_turn(line, normed_x, la_far, lu)
+    normed_b = [normed, hop_core(normed), normed_x, hop_core(normed_x)]
+    la_far_x, lu_x = hop_x(la_far), hop_x(lu)
+    grad, grad_t, codes_here = seed(line, source, count, jnp.transpose(cotangent, (1, 0, 2)), codes)
+    ld = stack_rows(line, [ld, ld_z])
+    ld_far, la_c, la_far_c = hop_y(ld), hop_core(la), hop_core(la_far)
+    g_up, g_down = (gu, gu_far), (gd, gd_far)
     active, slope, *parts = global_ff(line, normed_b, g_up, g_down)
     near_term, far_term = hop_core(parts[1]), hop_core(parts[3])
-    (lh_far_x,) = in_turn(line, lh_far_x)
-    lh_far_xc = hop_core(lh_far_x)
+    (lu_x, la_far_x, ld) = in_turn(line, lu_x, la_far_x, ld)
+    lu_far_x = hop_y(lu_x)
     to_x = hop_x(add_rows(line, [parts[2], far_term]))
-    (lu_near_x,) = in_turn(line, lu_near_x)
-    lu_near_xc = hop_core(lu_near_x)
+    ld_x = hop_x(ld)
+    la_xc, la_far_xc = hop_core(la_x), hop_core(la_far_x)
     (global_out,) = merge(line, middle, (parts[0], near_term, to_x), gains_here, 1, normed=False)
-    (ld_near_x,) = in_turn(line, ld_near_x)
-    ld_near_xc, ld_far_x = hop_core(ld_near_x), hop_y(ld_near_x)
-    (ld_far,) = in_turn(line, ld_far)
-    ld_far_c = hop_core(ld_far)
-
-    l_heads = [(lh_near, lh_far), (lh_near_c, lh_far_c), (lh_near_x, lh_far_x), (lh_near_xc, lh_far_xc)]
+    (ld_far, lu_far) = in_turn(line, ld_far, lu_far)
+
+    l_heads = [(la, la_far), (la_c, la_far_c), (la_x, la_far_x), (la_xc, la_far_xc)]
     l_qkv, l_mixed, l_middle, l_normed_b, l_a_t = local_heads(
-        line, source, global_out, codes, gains_here, l_heads
-    )
-    lu_far_x, ld_far_x = in_turn(line, lu_far_x, ld_far_x)
-    lu_far_xc, ld_far_xc = hop_core(lu_far_x), hop_core(ld_far_x)
-    l_up = [(lu_near, lu_far), (lu_near_c, lu_far_c), (lu_near_x, lu_far_x), (lu_near_xc, lu_far_xc)]
-    l_down = [(ld_near, ld_far), (ld_near_c, ld_far_c), (ld_near_x, ld_far_x), (ld_near_xc, ld_far_xc)]
+        line, global_out, codes_here, gains_here, l_heads
+    )
+    lu_c, lu_far_c, ld_c, ld_far_c = hop_core(lu), hop_core(lu_far), hop_core(ld), hop_core(ld_far)
+    (ld_x, lu_far_x) = in_turn(line, ld_x, lu_far_x)
+    ld_far_x = hop_y(ld_x)
+    lu_xc, lu_far_xc, ld_xc = hop_core(lu_x), hop_core(lu_far_x), hop_core(ld_x)
+    (ld_far_x,) = in_turn(line, ld_far_x)
+    ld_far_xc = hop_core(ld_far_x)
+    l_up = [(lu, lu_far), (lu_c, lu_far_c), (lu_x, lu_far_x), (lu_xc, lu_far_xc)]
+    l_down = [(ld, ld_far), (ld_c, ld_far_c), (ld_x, ld_far_x), (ld_xc, ld_far_xc)]
     l_active, l_slope, local_out, l_b_t = local_ff(line, source, l_normed_b, l_middle, l_up, l_down)
     local_out = jnp.transpose(local_out, (1, 0, 2))
 
@@ -1799,78 +1917,99 @@
         )
 
     (pair,), (so_far,) = ff_back(3)
-    met_far = hop_core(pair)
+    line.carry(("core", pair))
     (pair,), (so_far,) = ff_back(1, so_far=so_far)
-    met_near = hop_core(pair)
-    (d2_near, d2_far, up2), (so_far,) = ff_back(2, met=met_far, so_far=so_far)
-    d2_far, up2 = hop_y(d2_far), hop_x(up2)
-    (d0_near, d0_far, up0), (l_grad_mid, l_small, l_small_t, gain_d) = ff_back(
+    (met_far,) = line.arrived
+    line.carry(("core", pair))
+    (d2_near, d2_far, u2_near, u2_far), (so_far,) = ff_back(2, met=met_far, so_far=so_far)
+    (met_near,) = line.arrived
+    line.carry(("x", u2_far), ("y", d2_far))
+    (d0_near, d0_far, u0_near, u0_far), (l_grad_mid, l_small, l_small_t, gain_d) = ff_back(
         0, met=met_near, so_far=so_far, tail=(l_middle, gains_here)
     )
-    d0_far = hop_y(d0_far)
+    u2_far, d2_far = line.arrived
 
     def heads_back(rel, **more):
         return local_heads_back(
             line, rel, l_small, l_small_t, l_a_t, l_qkv, l_mixed, l_heads[rel], **more
         )
 
-    far_heads, (so_far,) = heads_back(3)
-    met_far = hop_core(far_heads)
-    near_heads, (so_far,) = heads_back(1, so_far=so_far)
-    met_near = hop_core(near_heads)
-    heads2, (so_far,) = heads_back(2, met=met_far, so_far=so_far)
-    heads2 = hop_x(heads2)
-    heads0, (grad_global, small, gain_c) = heads_back(
-        0, met=met_near, so_far=so_far, tail=(l_grad_mid, global_out, codes, source, gains_here)
-    )
-
-    grad_rows = rows_gather(small)
-    up_far = hop_y(add_rows(line, [up0, up2], 1, 2))
-    d2 = hop_x(add_rows(line, [d2_near, d2_far]))
+    half = D // 4
+    line.carry(("x", part(u2_near, 0, half)), ("y", part(d0_far, 0, half)))
+    (far_heads,), (so_far,) = heads_back(3)
+    u2_near_a, d0_far_a = line.arrived
+    u_far = add_rows(line, [u0_far, u2_far])
+    d2 = add_rows(line, [d2_near, d2_far])
+    line.carry(("x", part(u2_near, half, half)), ("y", part(d0_far, half, half)), ("core", far_heads))
+    (near_heads,), (so_far,) = heads_back(1, so_far=so_far)
+    u2_near_b, d0_far_b, met_far = line.arrived
+    line.carry(("x", part(d2, 0, half)), ("y", part(u_far, 0, half)), ("core", near_heads))
+    (h2_near, h2_far), (so_far,) = heads_back(2, met=met_far, so_far=so_far)
+    d2_a, u_far_a, met_near = line.arrived
+    line.carry(("x", part(d2, half, half)), ("y", part(u_far, half, half)))
+    (h0_near, h0_far), (grad_global, small, gain_c) = heads_back(
+        0, met=met_near, so_far=so_far, tail=(l_grad_mid, global_out, codes_here, gains_here)
+    )
+    d2_b, u_far_b = line.arrived
+    h2_far = hop_y(h2_far)
+    small_x = hop_x(small)
+    h0_far = hop_y(h0_far)
+
+    def update(layer, third, pieces, before):
+        return adam(
+            line, layer, third, pieces, left_basis, right_basis, master, first_moment, second_moment, ema, before
+        )
+
+    def depth_first(terms, split=()):
+        keep, send = sum_pieces(line, terms, split)
+        return keep, hop_z(send, 1)
+
+    def depth_second(keep, met):
+        keep, send = sum_pieces(line, [keep, met])
+        return keep, hop_z(send, 2)
+
+    lu = depth_first([u0_near], [[u2_near_a, u2_near_b], [u_far_a, u_far_b]])
+    (small_x,) = in_turn(line, small_x)
+    grad_rows = [small, hop_core(small), small_x, hop_core(small_x)]
+    ld = depth_first([d0_near], [[d0_far_a, d0_far_b], [d2_a, d2_b]])
+    lu = depth_second(*lu)
     grad_upper, *parts = global_ff_back(line, grad_rows, slope, g_up, g_down)
     near_term, far_term = hop_core(parts[1]), hop_core(parts[3])
     gd_near, gd_far = global_outer(line, grad_rows, active)
     gd_far = hop_y(gd_far)
     to_x = hop_x(add_rows(line, [parts[2], far_term]))
+    ld = depth_second(*ld)
     gu_near, gu_far = global_outer(line, normed_b, grad_upper)
     gu_far = hop_y(gu_far)
+    found = update(1, 1, lu, None)
     grad_middle, small, gain_b = merge_back(
         line, middle, (parts[0], near_term, to_x), grad_global, gains_here, 1
     )
-    grad_attn = rows_gather(small)
-    lu = sum_pieces(line, [up0, up2, up_far])
-    lu = [lu[0]] + [hop_z(lu[at], at) for at in (1, 2, 3)]
-    heads_far = hop_y(add_rows(line, [heads0, heads2], 1, 2))
+    small_x = hop_x(small)
+    h2 = hop_x(add_rows(line, [h2_near, h2_far]))
+    found = update(1, 2, ld, found)
+    (small_x,) = in_turn(line, small_x)
+    grad_attn = [small, hop_core(small), small_x, hop_core(small_x)]
     grad_qkv, *parts = global_heads_back(line, info, grad_attn, g_heads, qkv, mixed, lse)
     near_term, far_term = hop_core(parts[1]), hop_core(parts[3])
     gh_near, gh_far = global_grads_heads(line, info, normed_a, grad_attn, grad_qkv, mixed)
     gh_far = hop_y(gh_far)
     to_x = hop_x(add_rows(line, [parts[2], far_term]))
-    ld = sum_pieces(line, [d0_near, d0_far, d2])
-    ld = [ld[0]] + [hop_z(ld[at], at) for at in (1, 2, 3)]
-    gd = sum_pieces(line, [gd_near, gd_far])
-    gd = [gd[0]] + [hop_z(gd[at], at) for at in (1, 2, 3)]
+    gd = depth_first([gd_near, gd_far])
+    lh = depth_first([h0_near, h0_far, h2])
     input_grad, gain_grads = finish(
         line, source, rows_in, (parts[0], near_term, to_x), grad_middle, gains_here, (gain_b, gain_c, gain_d)
     )
     gain_grads = total_everywhere(gain_grads)
-    gu = sum_pieces(line, [gu_near, gu_far])
-    gu = [gu[0]] + [hop_z(gu[at], at) for at in (1, 2, 3)]
-    lh = sum_pieces(line, [heads0, heads2, heads_far])
-    lh = [lh[0]] + [hop_z(lh[at], at) for at in (1, 2, 3)]
-
-    def update(layer, third, pieces, before):
-        return adam(
-            line, layer, third, pieces, left_basis, right_basis, master, first_moment, second_moment, ema, before
-        )
-
-    found = update(1, 1, lu, None)
-    gh = sum_pieces(line, [gh_near, gh_far])
-    gh = [gh[0]] + [hop_z(gh[at], at) for at in (1, 2, 3)]
-    found = update(1, 2, ld, found)
+    gd = depth_second(*gd)
+    lh = depth_second(*lh)
+    gu = depth_first([gu_near, gu_far])
     found = update(0, 2, gd, found)
+    found = update(1, 0, lh, found)
+    gu = depth_second(*gu)
+    gh = depth_first([gh_near, gh_far])
     found = update(0, 1, gu, found)
-    found = update(1, 0, lh, found)
+    gh = depth_second(*gh)
     found = update(0, 0, gh, found)
     weight_grads, new_master, new_first, new_second, new_ema = found
     new_gain_first = beta_first * gain_first + (1.0 - beta_first) * gain_grads

time: 771 us -> 699 us (0.907)
  waiting for transfers between devices: 322 us -> 246 us
  Pallas kernels: 289 us -> 336 us
  starting transfers between devices: 93.1 us -> 73.3 us
  local copies, waits for them, and re-layouts: 55 us -> 36.4 us
    ppermute x17 -> x14, waiting for transfers between devices: 112 us -> 36.1 us  [hop_x(): return lax.ppermute(values, 'tensor', [(at, at ^ 2) for at in range(4)])]
    pallas_call x62 -> x71, Pallas kernels: 289 us -> 336 us  [run(): pl.pallas_call(inner, in_specs=[IN_HBM] * lead + list(in_specs) + [IN_HBM...]
    ppermute x15 -> x14, waiting for transfers between devices: 58.9 us -> 78.1 us  [hop_y(): return lax.ppermute(values, 'dp', [(at, at ^ 1) for at in range(8)])]
    unnamed x186 -> x206, local copies, waits for them, and re-layouts: 55 us -> 36.4 us
    ppermute x38 -> x26, waiting for transfers between devices: 143 us -> 125 us  [hop_z(): return lax.ppermute(values, 'dp', [(at, at ^ 2 * step) for at in range(8)])]
    ppermute x38 -> x26, starting transfers between devices: 52 us -> 40.2 us  [hop_z(): return lax.ppermute(values, 'dp', [(at, at ^ 2 * step) for at in range(8)])]
    ppermute x17 -> x14, starting transfers between devices: 23 us -> 12.1 us  [hop_x(): return lax.ppermute(values, 'tensor', [(at, at ^ 2) for at in range(4)])]
    ppermute x15 -> x14, starting transfers between devices: 12.6 us -> 17.6 us  [hop_y(): return lax.ppermute(values, 'dp', [(at, at ^ 1) for at in range(8)])]
  transfers between devices with their start and end apart: 103 -> 83, of which waited for: 33 -> 32; matrix products, arithmetic and copies ran while one was open for 0% -> 0% of each run, Pallas kernels for 27% -> 17%
where the time goes in v2:
time: 699 us; the launch traced here: 695 us
  Pallas kernels  336 us (48%)
  waiting for transfers between devices  246 us (35%)
  starting transfers between devices  73.3 us (10%)
  local copies, waits for them, and re-layouts  36.4 us (5%)
    pallas_call x71, Pallas kernels, run(): pl.pallas_call(inner, in_specs=[IN_HBM] * lead + list(in_specs) + [IN_HBM...  336 us
    ppermute x26, waiting for transfers between devices, hop_z(): return lax.ppermute(values, 'dp', [(at, at ^ 2 * step) for at in range(8)])  125 us
    ppermute x14, waiting for transfers between devices, hop_y(): return lax.ppermute(values, 'dp', [(at, at ^ 1) for at in range(8)])  78.1 us
    ppermute x26, starting transfers between devices, hop_z(): return lax.ppermute(values, 'dp', [(at, at ^ 2 * step) for at in range(8)])  40.2 us
    unnamed x206, local copies, waits for them, and re-layouts  36.4 us
    ppermute x14, waiting for transfers between devices, hop_x(): return lax.ppermute(values, 'tensor', [(at, at ^ 2) for at in range(4)])  36.1 us
    ppermute x14, starting transfers between devices, hop_y(): return lax.ppermute(values, 'dp', [(at, at ^ 1) for at in range(8)])  17.6 us
  transfers between devices with their start and end apart: 83, of which 32 were waited for; matrix products, arithmetic and copies ran while one was open for 0% of the time, Pallas kernels for 17%

profile of v2, /device:TPU:0, one launch (start us, length us, event | category | flops | bytes accessed | tf_op | source)
XLA Modules:
  0.0 695.1 jit_solution(11787843010848554187)
XLA Ops:
  3.3 4.0 collective-permute-start
  14.1 5.5 collective-permute-done.refs_2_
  21.4 4.0 collective-permute-done.1.refs_1_
  25.4 8.4 %collective-permute-done.2.refs_2_ = bf16[256,1024]{1,0:T(8,128)(2,1)S(1)} collective-permute-done((bf16[256,1024]{1,0:T(8,128)(2,1)S(1)}, bf16[256,1024]{1,0:T(8,128)(2,1)S(1)}, u32[]{:S(2)}, u32[]{:S(2)}) %collective-permute-start.2) | collective-permute-done | bytes 524320 | tf_op jit(solution)/shard_map/ppermute | solution.py:1804
  39.5 11.3 %collective-permute-done.3.refs_2_ = bf16[128,1024]{1,0:T(8,128)(2,1)S(1)} collective-permute-done((bf16[128,1024]{1,0:T(8,128)(2,1)S(1)}, bf16[128,1024]{1,0:T(8,128)(2,1)S(1)}, u32[]{:S(2)}, u32[]{:S(2)}) %collective-permute-start.3) | collective-permute-done | bytes 262176 | tf_op jit(solution)/shard_map/ppermute | solution.py:1804
  55.4 14.0 %collective-permute-done.4.refs_2_ = bf16[256,1024]{1,0:T(8,128)(2,1)S(1)} collective-permute-done((bf16[256,1024]{1,0:T(8,128)(2,1)S(1)}, bf16[256,1024]{1,0:T(8,128)(2,1)S(1)}, u32[]{:S(2)}, u32[]{:S(2)}) %collective-permute-start.4) | collective-permute-done | bytes 524320 | tf_op jit(solution)/shard_map/ppermute | solution.py:1804
  74.4 4.9 collective-permute-start.10
  79.3 13.3 %global_heads.1 = (bf16[1024,768]{1,0:T(8,128)(2,1)S(1)}, bf16[1024,256]{1,0:T(8,128)(2,1)S(1)}, f32[8,1024]{1,0:T(8,128)S(1)}, bf16[256,1024]{1,0:T(8,128)(2,1)...) custom-call(f32[8,128]{1,0:T(8,128)S(1)} %get-tuple-element.285.refs, ...), custom_call_target="tpu_custom_call" | custom-call | flops 2600000000 | bytes 1000 | tf_op jit(solution)/shard_map/global_heads/pallas_call | solution.py:632
  99.2 14.7 %collective-permute-done.14.refs_2_ = bf16[256,1024]{1,0:T(8,128)(2,1)S(1)} collective-permute-done((bf16[256,1024]{1,0:T(8,128)(2,1)S(1)}, bf16[256,1024]{1,0:T(8,128)(2,1)S(1)}, u32[]{:S(2)}, u32[]{:S(2)}) %collective-permute-start.14) | collective-permute-done | bytes 524320 | tf_op jit(solution)/shard_map/ppermute | solution.py:1804
  120.8 13.7 %collective-permute-done.18.refs_2_ = bf16[256,1024]{1,0:T(8,128)(2,1)S(1)} collective-permute-done((bf16[256,1024]{1,0:T(8,128)(2,1)S(1)}, bf16[256,1024]{1,0:T(8,128)(2,1)S(1)}, u32[]{:S(2)}, u32[]{:S(2)}) %collective-permute-start.18) | collective-permute-done | bytes 524320 | tf_op jit(solution)/shard_map/ppermute | solution.py:1804
  152.8 9.8 %collective-permute-done.24.refs_6_.refs_7_ = bf16[512,1024]{1,0:T(8,128)(2,1)} collective-permute-done((bf16[512,1024]{1,0:T(8,128)(2,1)}, bf16[512,1024]{1,0:T(8,128)(2,1)}, u32[]{:S(2)}, u32[]{:S(2)}) %collective-permute-start.24) | collective-permute-done | bytes 1048608 | tf_op jit(solution)/shard_map/ppermute | solution.py:1800
  164.7 20.4 %collective-permute-done.25.refs_8_.refs_9_ = bf16[512,1024]{1,0:T(8,128)(2,1)} collective-permute-done((bf16[512,1024]{1,0:T(8,128)(2,1)}, bf16[512,1024]{1,0:T(8,128)(2,1)}, u32[]{:S(2)}, u32[]{:S(2)}) %collective-permute-start.25) | collective-permute-done | bytes 1048608 | tf_op jit(solution)/shard_map/ppermute | solution.py:1800
  185.1 12.5 %global_ff.1 = (bf16[1024,1024]{1,0:T(8,128)(2,1)S(1)}, bf16[1024,1024]{1,0:T(8,128)(2,1)S(1)}, bf16[256,1024]{1,0:T(8,128)(2,1)S(1)}, bf16[256,1024]{1,0:T(8,12...) custom-call(f32[8,128]{1,0:T(8,128)S(1)} %get-tuple-element.318.refs_0_, ...), custom_call_target="tpu_custom_call" | custom-call | flops 2400000000 | bytes 1000 | tf_op jit(solution)/shard_map/global_ff/pallas_call | solution.py:632
  199.0 7.1 %collective-permute-done.31.refs_1_ = bf16[512,1024]{1,0:T(8,128)(2,1)S(1)} collective-permute-done((bf16[512,1024]{1,0:T(8,128)(2,1)S(1)}, bf16[512,1024]{1,0:T(8,128)(2,1)S(1)}, u32[]{:S(2)}, u32[]{:S(2)}) %collective-permute-start.31) | collective-permute-done | bytes 1048608 | tf_op jit(solution)/shard_map/ppermute | solution.py:1800
  209.0 12.2 %collective-permute-done.30.refs_4_ = bf16[256,1024]{1,0:T(8,128)(2,1)S(1)} collective-permute-done((bf16[256,1024]{1,0:T(8,128)(2,1)S(1)}, bf16[256,1024]{1,0:T(8,128)(2,1)S(1)}, u32[]{:S(2)}, u32[]{:S(2)}) %collective-permute-start.30) | collective-permute-done | bytes 524320 | tf_op jit(solution)/shard_map/ppermute | solution.py:1792
  227.0 17.8 %local_heads.1 = (bf16[4,768,768]{2,1,0:T(8,128)(2,1)}, bf16[4,768,256]{2,1,0:T(8,128)(2,1)}, f32[768,1024]{1,0:T(8,128)}, bf16[768,1024]{1,0:T(8,128)(2,1)}, bf...) custom-call(f32[8,128]{1,0:T(8,128)S(1)} %get-tuple-element.335.refs_0_, f32[256,1024]{1,0:T(8,128)S(1)} %copy-done.40, ...), custom_call_target="tpu_custom_call" | custom-call | flops 3600000000 | bytes 1000 | tf_op jit(solution)/shard_map/local_heads/pallas_call | solution.py:632
  246.5 19.1 %collective-permute-done.39.refs_1_ = bf16[512,1024]{1,0:T(8,128)(2,1)S(1)} collective-permute-done((bf16[512,1024]{1,0:T(8,128)(2,1)}, bf16[512,1024]{1,0:T(8,128)(2,1)S(1)}, u32[]{:S(2)}, u32[]{:S(2)}) %collective-permute-start.39) | collective-permute-done | bytes 1048608 | tf_op jit(solution)/shard_map/ppermute | solution.py:1800
  268.3 4.7 collective-permute-done.43.refs_11_.refs_7_
  274.7 35.1 %local_ff.1 = (bf16[4,768,1024]{2,1,0:T(8,128)(2,1)}, bf16[4,768,1024]{2,1,0:T(8,128)(2,1)}, bf16[3,256,1024]{2,1,0:T(8,128)(2,1)}, bf16[1024,768]{1,0:T(8,128)(2,1)}, f32[8,128]{1,0:T(8,128)}) custom-call(f32[8,128]{1,0:T(8,128)} %copy-done.87, s32[8]{0:T(128)} %copy-done.78, bf16[768,1024]{1,0:T(8,128)(2,1)} %get-tuple-element.346.refs_2_, ...), custom_call_target="tpu_custom_call" | custom-call | flops 6800000000 | bytes 1000 | tf_op jit(solution)/shard_map/local_ff/pallas_call | solution.py:632
  310.5 13.5 %local_ff_back.4 = (bf16[2,1024,1024]{2,1,0:T(8,128)(2,1)}, f32[768,1024]{1,0:T(8,128)}, f32[8,128]{1,0:T(8,128)S(1)}) custom-call(f32[8,128]{1,0:T(8,128)S(1)} %copy-done.77, bf16[768,1024]{1,0:T(8,128)(2,1)} %copy-done.7, bf16[1024,768]{1,0:T(8,128)(2,1)} %copy-done.8, bf16[1024,768]{1,0:T(8,128)(2,1)} %get-tuple-element.356.refs_3_, ...), custom_call_target="tpu_custom_call" | custom-call | flops 2800000000 | bytes 1000 | tf_op jit(solution)/shard_map/local_ff_back/pallas_call | solution.py:632
  324.0 14.8 %local_ff_back.5 = (bf16[2,1024,1024]{2,1,0:T(8,128)(2,1)}, f32[768,1024]{1,0:T(8,128)}, bf16[2,1024,1024]{2,1,0:T(8,128)(2,1)}, f32[8,128]{1,0:T(8,128)S(1)}) custom-call(f32[8,128]{1,0:T(8,128)S(1)} %get-tuple-element.359.refs_0_, bf16[768,1024]{1,0:T(8,128)(2,1)} %copy-done.7, bf16[1024,768]{1,0:T(8,128)(2,1)} %copy-done.8, ...), custom_call_target="tpu_custom_call" | custom-call | flops 2800000000 | bytes 1000 | tf_op jit(solution)/shard_map/local_ff_back/pallas_call | solution.py:632
  338.8 16.0 %local_ff_back.6 = (bf16[512,1024]{1,0:T(8,128)(2,1)S(1)}, bf16[512,1024]{1,0:T(8,128)(2,1)}, bf16[512,1024]{1,0:T(8,128)(2,1)}, bf16[512,1024]{1,0:T(8,128)(2,1...) custom-call(f32[8,128]{1,0:T(8,128)S(1)} %get-tuple-element.362.refs_0_, ...), custom_call_target="tpu_custom_call" | custom-call | flops 2800000000 | bytes 1000 | tf_op jit(solution)/shard_map/local_ff_back/pallas_call | solution.py:632
  354.8 35.8 %local_ff_back.7 = (bf16[512,1024]{1,0:T(8,128)(2,1)S(1)}, bf16[512,1024]{1,0:T(8,128)(2,1)}, bf16[512,1024]{1,0:T(8,128)(2,1)}, bf16[512,1024]{1,0:T(8,128)(2,1...) custom-call(f32[8,128]{1,0:T(8,128)S(1)} %get-tuple-element.366.refs, ...), custom_call_target="tpu_custom_call" | custom-call | flops 2800000000 | bytes 1000 | tf_op jit(solution)/shard_map/local_ff_back/pallas_call | solution.py:632
  390.6 19.3 %local_heads_back.4 = (bf16[1024,1024]{1,0:T(8,128)(2,1)}, f32[768,1024]{1,0:T(8,128)}, bf16[256,1024]{1,0:T(8,128)(2,1)S(1)}, bf16[256,1024]{1,0:T(8,128)(2,1)S(1)}, f32[8,128]{1,0:T(8,128)S(1)}) custom-call(f32[8,128]{1,0:T(8,128)S(1)} %get-tuple-element.371.refs_0_, bf16[768,1024]{1,0:T(8,128)(2,1)} %get-tuple-element.372.refs_1_, ...), custom_call_target="tpu_custom_call" | custom-call | flops 2200000000 | bytes 1000 | tf_op jit(solution)/shard_map/local_heads_back/pallas_call | solution.py:632
  412.4 20.1 %local_heads_back.5 = (bf16[1024,1024]{1,0:T(8,128)(2,1)}, f32[768,1024]{1,0:T(8,128)}, bf16[256,1024]{1,0:T(8,128)(2,1)S(1)}, bf16[256,1024]{1,0:T(8,128)(2,1)S...) custom-call(f32[8,128]{1,0:T(8,128)S(1)} %get-tuple-element.385.refs_0_, ...), custom_call_target="tpu_custom_call" | custom-call | flops 2200000000 | bytes 1000 | tf_op jit(solution)/shard_map/local_heads_back/pallas_call | solution.py:632
  432.5 21.7 %local_heads_back.6 = (bf16[512,1024]{1,0:T(8,128)(2,1)}, bf16[512,1024]{1,0:T(8,128)(2,1)}, f32[768,1024]{1,0:T(8,128)}, bf16[256,1024]{1,0:T(8,128)(2,1)S(1)},...) custom-call(f32[8,128]{1,0:T(8,128)S(1)} %get-tuple-element.388.refs_0_, ...), custom_call_target="tpu_custom_call" | custom-call | flops 2200000000 | bytes 1000 | tf_op jit(solution)/shard_map/local_heads_back/pallas_call | solution.py:632
  454.2 22.1 %local_heads_back.7 = (bf16[512,1024]{1,0:T(8,128)(2,1)}, bf16[512,1024]{1,0:T(8,128)(2,1)}, f32[256,1024]{1,0:T(8,128)}, bf16[256,1024]{1,0:T(8,128)(2,1)S(1)},...) custom-call(f32[8,128]{1,0:T(8,128)S(1)} %get-tuple-element.394.refs, ...), custom_call_target="tpu_custom_call" | custom-call | flops 2200000000 | bytes 1000 | tf_op jit(solution)/shard_map/local_heads_back/pallas_call | solution.py:632
  477.1 11.6 %collective-permute-done.48.refs_1_ = bf16[256,1024]{1,0:T(8,128)(2,1)S(1)} collective-permute-done((bf16[256,1024]{1,0:T(8,128)(2,1)S(1)}, bf16[256,1024]{1,0:T(8,128)(2,1)S(1)}, u32[]{:S(2)}, u32[]{:S(2)}) %collective-permute-start.48) | collective-permute-done | bytes 524320 | tf_op jit(solution)/shard_map/ppermute | solution.py:1792
  491.6 9.6 %global_ff_back.1 = (bf16[1024,1024]{1,0:T(8,128)(2,1)S(1)}, bf16[256,1024]{1,0:T(8,128)(2,1)S(1)}, bf16[256,1024]{1,0:T(8,128)(2,1)}, bf16[256,1024]{1,0:T(8,12...) custom-call(f32[8,128]{1,0:T(8,128)S(1)} %get-tuple-element.415.refs_0_, ...), custom_call_target="tpu_custom_call" | custom-call | flops 1800000000 | bytes 1000 | tf_op jit(solution)/shard_map/global_ff_back/pallas_call | solution.py:632
  503.3 4.6 global_ff_grads.2
  508.4 8.5 %collective-permute-done.53.refs_2_ = bf16[256,1024]{1,0:T(8,128)(2,1)S(1)} collective-permute-done((bf16[256,1024]{1,0:T(8,128)(2,1)}, bf16[256,1024]{1,0:T(8,128)(2,1)S(1)}, u32[]{:S(2)}, u32[]{:S(2)}) %collective-permute-start.53) | collective-permute-done | bytes 524320 | tf_op jit(solution)/shard_map/ppermute | solution.py:1804
  518.7 6.1 global_ff_grads.3
  527.0 4.8 adam_update.6
  536.6 11.9 %collective-permute-done.58.refs_2_ = bf16[128,1024]{1,0:T(8,128)(2,1)S(1)} collective-permute-done((bf16[128,1024]{1,0:T(8,128)(2,1)S(1)}, bf16[128,1024]{1,0:T(8,128)(2,1)S(1)}, u32[]{:S(2)}, u32[]{:S(2)}) %collective-permute-start.58) | collective-permute-done | bytes 262176 | tf_op jit(solution)/shard_map/ppermute | solution.py:1804
  548.5 5.0 adam_update.7
  556.1 12.3 %global_heads_back.1 = (bf16[1024,768]{1,0:T(8,128)(2,1)S(1)}, bf16[256,1024]{1,0:T(8,128)(2,1)S(1)}, bf16[256,1024]{1,0:T(8,128)(2,1)}, bf16[256,1024]{1,0:T(8,...) custom-call(f32[8,128]{1,0:T(8,128)S(1)} %get-tuple-element.449.refs_0_, s32[2]{0:T(128)S(1)} %pad_add_fusion.refs_1_, ...), custom_call_target="tpu_custom_call" | custom-call | flops 2400000000 | bytes 1000 | tf_op jit(solution)/shard_map/global_heads_back/pallas_call | solution.py:632
  577.4 5.5 global_heads_grads.1
  584.0 18.5 %collective-permute-done.63.refs_2_ = bf16[512,1024]{1,0:T(8,128)(2,1)} collective-permute-done((bf16[512,1024]{1,0:T(8,128)(2,1)}, bf16[512,1024]{1,0:T(8,128)(2,1)}, u32[]{:S(2)}, u32[]{:S(2)}) %collective-permute-start.63) | collective-permute-done | bytes 1048608 | tf_op jit(solution)/shard_map/ppermute | solution.py:1800
  610.1 5.4 collective-permute-done.67.refs_5_
  619.3 9.0 %collective-permute-done.69.refs_2_ = bf16[256,1024]{1,0:T(8,128)(2,1)S(1)} collective-permute-done((bf16[256,1024]{1,0:T(8,128)(2,1)S(1)}, bf16[256,1024]{1,0:T(8,128)(2,1)S(1)}, u32[]{:S(2)}, u32[]{:S(2)}) %collective-permute-start.69) | collective-permute-done | bytes 524320 | tf_op jit(solution)/shard_map/ppermute | solution.py:1804
  632.0 15.1 %collective-permute-done.71.refs_2_ = bf16[128,1024]{1,0:T(8,128)(2,1)S(1)} collective-permute-done((bf16[128,1024]{1,0:T(8,128)(2,1)S(1)}, bf16[128,1024]{1,0:T(8,128)(2,1)S(1)}, u32[]{:S(2)}, u32[]{:S(2)}) %collective-permute-start.71) | collective-permute-done | bytes 262176 | tf_op jit(solution)/shard_map/ppermute | solution.py:1804
  647.0 4.8 adam_update.8
  653.1 4.8 adam_update.9
  667.3 3.9 collective-permute-done.75.refs_2_
  671.2 4.8 adam_update.10
  676.1 3.4 collective-permute-start.77
  680.4 4.0 collective-permute-done.81
  690.2 4.8 adam_update.11
  (403 shorter events, 138.2 us)
Async XLA Ops:
  34.8 44.5 %collective-permute-start.8 = (bf16[512,1024]{1,0:T(8,128)(2,1)}, bf16[512,1024]{1,0:T(8,128)(2,1)}, u32[]{:S(2)}, u32[]{:S(2)}) collective-permute-start(bf16[512,1024]{1,0:T(8,128)(2,1)} %get-tuple-element.287.refs_6_), channel_id=1, source_target_pairs={{0,4},{4,0},{8,12},{12,8},{16,20},{20,16},{24,28},{28,24},{1,5},{5... | collective-permute-start | bytes 3145736 | tf_op jit(solution)/shard_map/ppermute | solution.py:1800
  50.8 18.6 %collective-permute-start.4 = (bf16[256,1024]{1,0:T(8,128)(2,1)S(1)}, bf16[256,1024]{1,0:T(8,128)(2,1)S(1)}, u32[]{:S(2)}, u32[]{:S(2)}) collective-permute-start(bf16[256,1024]{1,0:T(8,128)(2,1)S(1)} %get-tuple-element.282.refs_1_), channel_id=1, source_target_pairs={{0,8},{4,12},{8,0},{12,4},{16,24},{20,28},{24,16},{28,20},{1,9},{5... | collective-permute-start | bytes 1572872 | tf_op jit(solution)/shard_map/ppermute | solution.py:1804
  51.5 22.7 %collective-permute-start.6 = (bf16[256,1024]{1,0:T(8,128)(2,1)}, bf16[256,1024]{1,0:T(8,128)(2,1)}, u32[]{:S(2)}, u32[]{:S(2)}) collective-permute-start(bf16[256,1024]{1,0:T(8,128)(2,1)} %get-tuple-element.276.refs_2_), channel_id=1, source_target_pairs={{0,1},{1,0},{2,3},{3,2},{4,5},{5,4},{6,7},{7,6},{8,9},{9,8},{10,11... | collective-permute-start | bytes 1572872 | tf_op jit(solution)/shard_map/ppermute | solution.py:1796
  51.5 22.9 %collective-permute-start.7 = (bf16[256,1024]{1,0:T(8,128)(2,1)}, bf16[256,1024]{1,0:T(8,128)(2,1)}, u32[]{:S(2)}, u32[]{:S(2)}) collective-permute-start(bf16[256,1024]{1,0:T(8,128)(2,1)} %get-tuple-element.286.refs_4_), channel_id=1, source_target_pairs={{0,1},{1,0},{2,3},{3,2},{4,5},{5,4},{6,7},{7,6},{8,9},{9,8},{10,11... | collective-permute-start | bytes 1572872 | tf_op jit(solution)/shard_map/ppermute | solution.py:1796
  52.1 20.5 %collective-permute-start.5 = (bf16[128,1024]{1,0:T(8,128)(2,1)}, bf16[128,1024]{1,0:T(8,128)(2,1)}, u32[]{:S(2)}, u32[]{:S(2)}) collective-permute-start(bf16[128,1024]{1,0:T(8,128)(2,1)} %get-tuple-element.284.refs_1_), channel_id=1, source_target_pairs={{0,16},{4,20},{8,24},{12,28},{16,0},{20,4},{24,8},{28,12},{1,17},{... | collective-permute-start | bytes 786440 | tf_op jit(solution)/shard_map/ppermute | solution.py:1804
  70.4 25.9 %collective-permute-start.13 = (bf16[512,1024]{1,0:T(8,128)(2,1)}, bf16[512,1024]{1,0:T(8,128)(2,1)}, u32[]{:S(2)}, u32[]{:S(2)}) collective-permute-start(bf16[512,1024]{1,0:T(8,128)(2,1)} %get-tuple-element.296.refs_4_.refs_6_), channel_id=1, source_target_pairs={{0,2},{1,3},{2,0},{3,1},{4,6},{5,7},{6,4},{7,5},{8,10},{9,11},{10,... | collective-permute-start | bytes 3145736 | tf_op jit(solution)/shard_map/ppermute | solution.py:1792
  72.6 26.6 %collective-permute-start.12 = (bf16[512,1024]{1,0:T(8,128)(2,1)}, bf16[512,1024]{1,0:T(8,128)(2,1)S(1)}, u32[]{:S(2)}, u32[]{:S(2)}) collective-permute-start(bf16[512,1024]{1,0:T(8,128)(2,1)} %get-tuple-element.296.refs_4_.refs_6_), channel_id=1, source_target_pairs={{0,4},{4,0},{8,12},{12,8},{16,20},{20,16},{24,28},{28,24},{1,5},{5... | collective-permute-start | bytes 3145736 | tf_op jit(solution)/shard_map/ppermute | solution.py:1800
  74.2 18.5 %collective-permute-start.9 = (bf16[256,1024]{1,0:T(8,128)(2,1)S(1)}, bf16[256,1024]{1,0:T(8,128)(2,1)S(1)}, u32[]{:S(2)}, u32[]{:S(2)}) collective-permute-start(bf16[256,1024]{1,0:T(8,128)(2,1)S(1)} %get-tuple-element.289.refs_1_), channel_id=1, source_target_pairs={{0,8},{4,12},{8,0},{12,4},{16,24},{20,28},{24,16},{28,20},{1,9},{5... | collective-permute-start | bytes 1572872 | tf_op jit(solution)/shard_map/ppermute | solution.py:1804
  74.4 19.4 %collective-permute-start.10 = (bf16[128,1024]{1,0:T(8,128)(2,1)}, bf16[128,1024]{1,0:T(8,128)(2,1)S(1)}, u32[]{:S(2)}, u32[]{:S(2)}) collective-permute-start(bf16[128,1024]{1,0:T(8,128)(2,1)} %copy-done.85), channel_id=1, source_target_pairs={{0,16},{4,20},{8,24},{12,28},{16,0},{20,4},{24,8},{28,12},{1,17},{... | collective-permute-start | bytes 786440 | tf_op jit(solution)/shard_map/ppermute | solution.py:1804
  93.9 20.0 %collective-permute-start.14 = (bf16[256,1024]{1,0:T(8,128)(2,1)S(1)}, bf16[256,1024]{1,0:T(8,128)(2,1)S(1)}, u32[]{:S(2)}, u32[]{:S(2)}) collective-permute-start(bf16[256,1024]{1,0:T(8,128)(2,1)S(1)} %get-tuple-element.298.refs_1_), channel_id=1, source_target_pairs={{0,8},{4,12},{8,0},{12,4},{16,24},{20,28},{24,16},{28,20},{1,9},{5... | collective-permute-start | bytes 1572872 | tf_op jit(solution)/shard_map/ppermute | solution.py:1804
  95.6 21.0 %collective-permute-start.16 = (bf16[256,1024]{1,0:T(8,128)(2,1)S(1)}, bf16[256,1024]{1,0:T(8,128)(2,1)S(1)}, u32[]{:S(2)}, u32[]{:S(2)}) collective-permute-start(bf16[256,1024]{1,0:T(8,128)(2,1)S(1)} %get-tuple-element.304), channel_id=1, source_target_pairs={{0,1},{1,0},{2,3},{3,2},{4,5},{5,4},{6,7},{7,6},{8,9},{9,8},{10,11... | collective-permute-start | bytes 1572872 | tf_op jit(solution)/shard_map/ppermute | solution.py:1796
  95.8 20.8 %collective-permute-start.17 = (bf16[256,1024]{1,0:T(8,128)(2,1)S(1)}, bf16[256,1024]{1,0:T(8,128)(2,1)S(1)}, u32[]{:S(2)}, u32[]{:S(2)}) collective-permute-start(bf16[256,1024]{1,0:T(8,128)(2,1)S(1)} %get-tuple-element.305), channel_id=1, source_target_pairs={{0,2},{1,3},{2,0},{3,1},{4,6},{5,7},{6,4},{7,5},{8,10},{9,11},{10,... | collective-permute-start | bytes 1572872 | tf_op jit(solution)/shard_map/ppermute | solution.py:1792
  96.4 19.1 %collective-permute-start.15 = (bf16[128,1024]{1,0:T(8,128)(2,1)S(1)}, bf16[128,1024]{1,0:T(8,128)(2,1)S(1)}, u32[]{:S(2)}, u32[]{:S(2)}) collective-permute-start(bf16[128,1024]{1,0:T(8,128)(2,1)S(1)} %copy-done.84), channel_id=1, source_target_pairs={{0,16},{4,20},{8,24},{12,28},{16,0},{20,4},{24,8},{28,12},{1,17},{... | collective-permute-start | bytes 786440 | tf_op jit(solution)/shard_map/ppermute | solution.py:1804
  113.9 26.1 %collective-permute-start.32 = (bf16[512,1024]{1,0:T(8,128)(2,1)S(1)}, bf16[512,1024]{1,0:T(8,128)(2,1)S(1)}, u32[]{:S(2)}, u32[]{:S(2)}) collective-permute-start(bf16[512,1024]{1,0:T(8,128)(2,1)S(1)} %get-tuple-element.314.refs_3_), channel_id=1, source_target_pairs={{0,4},{4,0},{8,12},{12,8},{16,20},{20,16},{24,28},{28,24},{1,5},{5... | collective-permute-start | bytes 3145736 | tf_op jit(solution)/shard_map/ppermute | solution.py:1800
  115.6 18.9 %collective-permute-start.18 = (bf16[256,1024]{1,0:T(8,128)(2,1)S(1)}, bf16[256,1024]{1,0:T(8,128)(2,1)S(1)}, u32[]{:S(2)}, u32[]{:S(2)}) collective-permute-start(bf16[256,1024]{1,0:T(8,128)(2,1)S(1)} %get-tuple-element.308.refs_1_), channel_id=1, source_target_pairs={{0,8},{4,12},{8,0},{12,4},{16,24},{20,28},{24,16},{28,20},{1,9},{5... | collective-permute-start | bytes 1572872 | tf_op jit(solution)/shard_map/ppermute | solution.py:1804
  115.6 47.0 %collective-permute-start.24 = (bf16[512,1024]{1,0:T(8,128)(2,1)}, bf16[512,1024]{1,0:T(8,128)(2,1)}, u32[]{:S(2)}, u32[]{:S(2)}) collective-permute-start(bf16[512,1024]{1,0:T(8,128)(2,1)} %get-tuple-element.320.refs_5_.refs_6_), channel_id=1, source_target_pairs={{0,4},{4,0},{8,12},{12,8},{16,20},{20,16},{24,28},{28,24},{1,5},{5... | collective-permute-start | bytes 3145736 | tf_op jit(solution)/shard_map/ppermute | solution.py:1800
  117.9 19.0 %collective-permute-start.20 = (bf16[256,1024]{1,0:T(8,128)(2,1)}, bf16[256,1024]{1,0:T(8,128)(2,1)}, u32[]{:S(2)}, u32[]{:S(2)}) collective-permute-start(bf16[256,1024]{1,0:T(8,128)(2,1)} %get-tuple-element.312.refs_1_), channel_id=1, source_target_pairs={{0,2},{1,3},{2,0},{3,1},{4,6},{5,7},{6,4},{7,5},{8,10},{9,11},{10,... | collective-permute-start | bytes 1572872 | tf_op jit(solution)/shard_map/ppermute | solution.py:1792
  118.4 17.7 %collective-permute-start.19 = (bf16[128,1024]{1,0:T(8,128)(2,1)S(1)}, bf16[128,1024]{1,0:T(8,128)(2,1)S(1)}, u32[]{:S(2)}, u32[]{:S(2)}) collective-permute-start(bf16[128,1024]{1,0:T(8,128)(2,1)S(1)} %get-tuple-element.310.refs_1_), channel_id=1, source_target_pairs={{0,16},{4,20},{8,24},{12,28},{16,0},{20,4},{24,8},{28,12},{1,17},{... | collective-permute-start | bytes 786440 | tf_op jit(solution)/shard_map/ppermute | solution.py:1804
  135.6 49.5 %collective-permute-start.25 = (bf16[512,1024]{1,0:T(8,128)(2,1)}, bf16[512,1024]{1,0:T(8,128)(2,1)}, u32[]{:S(2)}, u32[]{:S(2)}) collective-permute-start(bf16[512,1024]{1,0:T(8,128)(2,1)} %get-tuple-element.321.refs_7_.refs_8_), channel_id=1, source_target_pairs={{0,4},{4,0},{8,12},{12,8},{16,20},{20,16},{24,28},{28,24},{1,5},{5... | collective-permute-start | bytes 3145736 | tf_op jit(solution)/shard_map/ppermute | solution.py:1800
  136.9 26.3 %collective-permute-start.22 = (bf16[256,1024]{1,0:T(8,128)(2,1)}, bf16[256,1024]{1,0:T(8,128)(2,1)}, u32[]{:S(2)}, u32[]{:S(2)}) collective-permute-start(bf16[256,1024]{1,0:T(8,128)(2,1)} %get-tuple-element.312.refs_1_), channel_id=1, source_target_pairs={{0,1},{1,0},{2,3},{3,2},{4,5},{5,4},{6,7},{7,6},{8,9},{9,8},{10,11... | collective-permute-start | bytes 1572872 | tf_op jit(solution)/shard_map/ppermute | solution.py:1796
  143.0 21.7 %collective-permute-start.23 = (bf16[256,1024]{1,0:T(8,128)(2,1)}, bf16[256,1024]{1,0:T(8,128)(2,1)}, u32[]{:S(2)}, u32[]{:S(2)}) collective-permute-start(bf16[256,1024]{1,0:T(8,128)(2,1)} %get-tuple-element.319.refs_3_), channel_id=1, source_target_pairs={{0,1},{1,0},{2,3},{3,2},{4,5},{5,4},{6,7},{7,6},{8,9},{9,8},{10,11... | collective-permute-start | bytes 1572872 | tf_op jit(solution)/shard_map/ppermute | solution.py:1796
  151.0 46.8 %collective-permute-start.26 = (bf16[512,1024]{1,0:T(8,128)(2,1)S(1)}, bf16[512,1024]{1,0:T(8,128)(2,1)S(1)}, u32[]{:S(2)}, u32[]{:S(2)}) collective-permute-start(bf16[512,1024]{1,0:T(8,128)(2,1)S(1)} %copy-done.13), channel_id=1, source_target_pairs={{0,2},{1,3},{2,0},{3,1},{4,6},{5,7},{6,4},{7,5},{8,10},{9,11},{10,... | collective-permute-start | bytes 3145736 | tf_op jit(solution)/shard_map/ppermute | solution.py:1792
  162.6 36.4 %collective-permute-start.27 = (bf16[512,1024]{1,0:T(8,128)(2,1)S(1)}, bf16[512,1024]{1,0:T(8,128)(2,1)S(1)}, u32[]{:S(2)}, u32[]{:S(2)}) collective-permute-start(bf16[512,1024]{1,0:T(8,128)(2,1)S(1)} %copy-done.10), channel_id=1, source_target_pairs={{0,2},{1,3},{2,0},{3,1},{4,6},{5,7},{6,4},{7,5},{8,10},{9,11},{10,... | collective-permute-start | bytes 3145736 | tf_op jit(solution)/shard_map/ppermute | solution.py:1792
  163.2 43.0 %collective-permute-start.31 = (bf16[512,1024]{1,0:T(8,128)(2,1)S(1)}, bf16[512,1024]{1,0:T(8,128)(2,1)S(1)}, u32[]{:S(2)}, u32[]{:S(2)}) collective-permute-start(bf16[512,1024]{1,0:T(8,128)(2,1)S(1)} %get-tuple-element.325.refs_3_), channel_id=1, source_target_pairs={{0,4},{4,0},{8,12},{12,8},{16,20},{20,16},{24,28},{28,24},{1,5},{5... | collective-permute-start | bytes 3145736 | tf_op jit(solution)/shard_map/ppermute | solution.py:1800
  164.7 42.7 %collective-permute-start.33 = (bf16[512,1024]{1,0:T(8,128)(2,1)}, bf16[512,1024]{1,0:T(8,128)(2,1)}, u32[]{:S(2)}, u32[]{:S(2)}) collective-permute-start(bf16[512,1024]{1,0:T(8,128)(2,1)} %get-tuple-element.296.refs_4_.refs_6_), channel_id=1, source_target_pairs={{0,1},{1,0},{2,3},{3,2},{4,5},{5,4},{6,7},{7,6},{8,9},{9,8},{10,11... | collective-permute-start | bytes 3145736 | tf_op jit(solution)/shard_map/ppermute | solution.py:1796
  207.4 37.5 %collective-permute-start.37 = (bf16[512,1024]{1,0:T(8,128)(2,1)S(1)}, bf16[512,1024]{1,0:T(8,128)(2,1)}, u32[]{:S(2)}, u32[]{:S(2)}) collective-permute-start(bf16[512,1024]{1,0:T(8,128)(2,1)S(1)} %get-tuple-element.341.refs_12_.refs_8_), channel_id=1, source_target_pairs={{0,2},{1,3},{2,0},{3,1},{4,6},{5,7},{6,4},{7,5},{8,10},{9,11},{10,... | collective-permute-start | bytes 3145736 | tf_op jit(solution)/shard_map/ppermute | solution.py:1792
  221.2 23.7 %collective-permute-start.38 = (bf16[512,1024]{1,0:T(8,128)(2,1)S(1)}, bf16[512,1024]{1,0:T(8,128)(2,1)}, u32[]{:S(2)}, u32[]{:S(2)}) collective-permute-start(bf16[512,1024]{1,0:T(8,128)(2,1)S(1)} %get-tuple-element.342.refs_8_.refs_6_), channel_id=1, source_target_pairs={{0,4},{4,0},{8,12},{12,8},{16,20},{20,16},{24,28},{28,24},{1,5},{5... | collective-permute-start | bytes 3145736 | tf_op jit(solution)/shard_map/ppermute | solution.py:1800
  244.9 20.7 %collective-permute-start.39 = (bf16[512,1024]{1,0:T(8,128)(2,1)}, bf16[512,1024]{1,0:T(8,128)(2,1)S(1)}, u32[]{:S(2)}, u32[]{:S(2)}) collective-permute-start(bf16[512,1024]{1,0:T(8,128)(2,1)} %get-tuple-element.344.refs_16_.refs_8_), channel_id=1, source_target_pairs={{0,4},{4,0},{8,12},{12,8},{16,20},{20,16},{24,28},{28,24},{1,5},{5... | collective-permute-start | bytes 3145736 | tf_op jit(solution)/shard_map/ppermute | solution.py:1800
  245.5 20.7 %collective-permute-start.40 = (bf16[512,1024]{1,0:T(8,128)(2,1)S(1)}, bf16[512,1024]{1,0:T(8,128)(2,1)S(1)}, u32[]{:S(2)}, u32[]{:S(2)}) collective-permute-start(bf16[512,1024]{1,0:T(8,128)(2,1)S(1)} %copy-done.13), channel_id=1, source_target_pairs={{0,1},{1,0},{2,3},{3,2},{4,5},{5,4},{6,7},{7,6},{8,9},{9,8},{10,11... | collective-permute-start | bytes 3145736 | tf_op jit(solution)/shard_map/ppermute | solution.py:1796
  245.5 21.2 %collective-permute-start.44 = (bf16[512,1024]{1,0:T(8,128)(2,1)S(1)}, bf16[512,1024]{1,0:T(8,128)(2,1)S(1)}, u32[]{:S(2)}, u32[]{:S(2)}) collective-permute-start(bf16[512,1024]{1,0:T(8,128)(2,1)S(1)} %get-tuple-element.341.refs_12_.refs_8_), channel_id=1, source_target_pairs={{0,1},{1,0},{2,3},{3,2},{4,5},{5,4},{6,7},{7,6},{8,9},{9,8},{10,11... | collective-permute-start | bytes 3145736 | tf_op jit(solution)/shard_map/ppermute | solution.py:1796
  246.0 20.8 %collective-permute-start.42 = (bf16[512,1024]{1,0:T(8,128)(2,1)S(1)}, bf16[512,1024]{1,0:T(8,128)(2,1)S(1)}, u32[]{:S(2)}, u32[]{:S(2)}) collective-permute-start(bf16[512,1024]{1,0:T(8,128)(2,1)S(1)} %get-tuple-element.342.refs_8_.refs_6_), channel_id=1, source_target_pairs={{0,1},{1,0},{2,3},{3,2},{4,5},{5,4},{6,7},{7,6},{8,9},{9,8},{10,11... | collective-permute-start | bytes 3145736 | tf_op jit(solution)/shard_map/ppermute | solution.py:1796
  246.1 21.8 %collective-permute-start.41 = (bf16[512,1024]{1,0:T(8,128)(2,1)S(1)}, bf16[512,1024]{1,0:T(8,128)(2,1)S(1)}, u32[]{:S(2)}, u32[]{:S(2)}) collective-permute-start(bf16[512,1024]{1,0:T(8,128)(2,1)S(1)} %get-tuple-element.348.refs_5_.refs_7_), channel_id=1, source_target_pairs={{0,1},{1,0},{2,3},{3,2},{4,5},{5,4},{6,7},{7,6},{8,9},{9,8},{10,11... | collective-permute-start | bytes 3145736 | tf_op jit(solution)/shard_map/ppermute | solution.py:1796
  501.5 33.9 %collective-permute-start.57 = (bf16[512,1024]{1,0:T(8,128)(2,1)}, bf16[512,1024]{1,0:T(8,128)(2,1)S(1)}, u32[]{:S(2)}, u32[]{:S(2)}) collective-permute-start(bf16[512,1024]{1,0:T(8,128)(2,1)} %get-tuple-element.438), channel_id=1, source_target_pairs={{0,4},{4,0},{8,12},{12,8},{16,20},{20,16},{24,28},{28,24},{1,5},{5... | collective-permute-start | bytes 3145736 | tf_op jit(solution)/shard_map/ppermute | solution.py:1800
  503.2 28.6 %collective-permute-start.55 = (bf16[256,1024]{1,0:T(8,128)(2,1)}, bf16[256,1024]{1,0:T(8,128)(2,1)S(1)}, u32[]{:S(2)}, u32[]{:S(2)}) collective-permute-start(bf16[256,1024]{1,0:T(8,128)(2,1)} %get-tuple-element.433), channel_id=1, source_target_pairs={{0,1},{1,0},{2,3},{3,2},{4,5},{5,4},{6,7},{7,6},{8,9},{9,8},{10,11... | collective-permute-start | bytes 1572872 | tf_op jit(solution)/shard_map/ppermute | solution.py:1796
  508.1 23.8 %collective-permute-start.56 = (bf16[256,1024]{1,0:T(8,128)(2,1)S(1)}, bf16[256,1024]{1,0:T(8,128)(2,1)S(1)}, u32[]{:S(2)}, u32[]{:S(2)}) collective-permute-start(bf16[256,1024]{1,0:T(8,128)(2,1)S(1)} %get-tuple-element.434), channel_id=1, source_target_pairs={{0,2},{1,3},{2,0},{3,1},{4,6},{5,7},{6,4},{7,5},{8,10},{9,11},{10,... | collective-permute-start | bytes 1572872 | tf_op jit(solution)/shard_map/ppermute | solution.py:1792
  533.6 19.9 %collective-permute-start.59 = (bf16[256,1024]{1,0:T(8,128)(2,1)S(1)}, bf16[256,1024]{1,0:T(8,128)(2,1)S(1)}, u32[]{:S(2)}, u32[]{:S(2)}) collective-permute-start(bf16[256,1024]{1,0:T(8,128)(2,1)S(1)} %get-tuple-element.448.refs_2_.refs_6_), channel_id=1, source_target_pairs={{0,2},{1,3},{2,0},{3,1},{4,6},{5,7},{6,4},{7,5},{8,10},{9,11},{10,... | collective-permute-start | bytes 1572872 | tf_op jit(solution)/shard_map/ppermute | solution.py:1792
  535.4 20.7 %collective-permute-start.60 = (bf16[256,1024]{1,0:T(8,128)(2,1)S(1)}, bf16[256,1024]{1,0:T(8,128)(2,1)S(1)}, u32[]{:S(2)}, u32[]{:S(2)}) collective-permute-start(bf16[256,1024]{1,0:T(8,128)(2,1)S(1)} %get-tuple-element.448.refs_2_.refs_6_), channel_id=1, source_target_pairs={{0,1},{1,0},{2,3},{3,2},{4,5},{5,4},{6,7},{7,6},{8,9},{9,8},{10,11... | collective-permute-start | bytes 1572872 | tf_op jit(solution)/shard_map/ppermute | solution.py:1796
  553.7 50.6 %collective-permute-start.64 = (bf16[512,1024]{1,0:T(8,128)(2,1)}, bf16[512,1024]{1,0:T(8,128)(2,1)}, u32[]{:S(2)}, u32[]{:S(2)}) collective-permute-start(bf16[512,1024]{1,0:T(8,128)(2,1)} %get-tuple-element.464), channel_id=1, source_target_pairs={{0,4},{4,0},{8,12},{12,8},{16,20},{20,16},{24,28},{28,24},{1,5},{5... | collective-permute-start | bytes 3145736 | tf_op jit(solution)/shard_map/ppermute | solution.py:1800
  554.0 48.5 %collective-permute-start.63 = (bf16[512,1024]{1,0:T(8,128)(2,1)}, bf16[512,1024]{1,0:T(8,128)(2,1)}, u32[]{:S(2)}, u32[]{:S(2)}) collective-permute-start(bf16[512,1024]{1,0:T(8,128)(2,1)} %get-tuple-element.461), channel_id=1, source_target_pairs={{0,4},{4,0},{8,12},{12,8},{16,20},{20,16},{24,28},{28,24},{1,5},{5... | collective-permute-start | bytes 3145736 | tf_op jit(solution)/shard_map/ppermute | solution.py:1800
  555.7 48.6 %collective-permute-start.65 = (bf16[512,1024]{1,0:T(8,128)(2,1)}, bf16[512,1024]{1,0:T(8,128)(2,1)}, u32[]{:S(2)}, u32[]{:S(2)}) collective-permute-start(bf16[512,1024]{1,0:T(8,128)(2,1)} %get-tuple-element.465), channel_id=1, source_target_pairs={{0,2},{1,3},{2,0},{3,1},{4,6},{5,7},{6,4},{7,5},{8,10},{9,11},{10,... | collective-permute-start | bytes 3145736 | tf_op jit(solution)/shard_map/ppermute | solution.py:1792
  570.1 58.3 %collective-permute-start.70 = (bf16[512,1024]{1,0:T(8,128)(2,1)}, bf16[512,1024]{1,0:T(8,128)(2,1)S(1)}, u32[]{:S(2)}, u32[]{:S(2)}) collective-permute-start(bf16[512,1024]{1,0:T(8,128)(2,1)} %get-tuple-element.483), channel_id=1, source_target_pairs={{0,4},{4,0},{8,12},{12,8},{16,20},{20,16},{24,28},{28,24},{1,5},{5... | collective-permute-start | bytes 3145736 | tf_op jit(solution)/shard_map/ppermute | solution.py:1800
  572.0 36.3 %collective-permute-start.66 = (bf16[256,1024]{1,0:T(8,128)(2,1)}, bf16[256,1024]{1,0:T(8,128)(2,1)}, u32[]{:S(2)}, u32[]{:S(2)}) collective-permute-start(bf16[256,1024]{1,0:T(8,128)(2,1)} %get-tuple-element.468), channel_id=1, source_target_pairs={{0,1},{1,0},{2,3},{3,2},{4,5},{5,4},{6,7},{7,6},{8,9},{9,8},{10,11... | collective-permute-start | bytes 1572872 | tf_op jit(solution)/shard_map/ppermute | solution.py:1796
  606.3 22.0 %collective-permute-start.69 = (bf16[256,1024]{1,0:T(8,128)(2,1)S(1)}, bf16[256,1024]{1,0:T(8,128)(2,1)S(1)}, u32[]{:S(2)}, u32[]{:S(2)}) collective-permute-start(bf16[256,1024]{1,0:T(8,128)(2,1)S(1)} %get-tuple-element.480), channel_id=1, source_target_pairs={{0,8},{4,12},{8,0},{12,4},{16,24},{20,28},{24,16},{28,20},{1,9},{5... | collective-permute-start | bytes 1572872 | tf_op jit(solution)/shard_map/ppermute | solution.py:1804
  608.4 49.6 %collective-permute-start.74 = (bf16[512,1024]{1,0:T(8,128)(2,1)S(1)}, bf16[512,1024]{1,0:T(8,128)(2,1)S(1)}, u32[]{:S(2)}, u32[]{:S(2)}) collective-permute-start(bf16[512,1024]{1,0:T(8,128)(2,1)S(1)} %copy-done.81), channel_id=1, source_target_pairs={{0,4},{4,0},{8,12},{12,8},{16,20},{20,16},{24,28},{28,24},{1,5},{5... | collective-permute-start | bytes 3145736 | tf_op jit(solution)/shard_map/ppermute | solution.py:1800
  628.7 29.2 %collective-permute-start.73 = (bf16[256,1024]{1,0:T(8,128)(2,1)S(1)}, bf16[256,1024]{1,0:T(8,128)(2,1)S(1)}, u32[]{:S(2)}, u32[]{:S(2)}) collective-permute-start(bf16[256,1024]{1,0:T(8,128)(2,1)S(1)} %get-tuple-element.502), channel_id=1, source_target_pairs={{0,8},{4,12},{8,0},{12,4},{16,24},{20,28},{24,16},{28,20},{1,9},{5... | collective-permute-start | bytes 1572872 | tf_op jit(solution)/shard_map/ppermute | solution.py:1804
  629.0 18.0 %collective-permute-start.71 = (bf16[128,1024]{1,0:T(8,128)(2,1)S(1)}, bf16[128,1024]{1,0:T(8,128)(2,1)S(1)}, u32[]{:S(2)}, u32[]{:S(2)}) collective-permute-start(bf16[128,1024]{1,0:T(8,128)(2,1)S(1)} %get-tuple-element.486), channel_id=1, source_target_pairs={{0,16},{4,20},{8,24},{12,28},{16,0},{20,4},{24,8},{28,12},{1,17},{... | collective-permute-start | bytes 786440 | tf_op jit(solution)/shard_map/ppermute | solution.py:1804
  630.2 22.9 %collective-permute-start.72 = (bf16[128,1024]{1,0:T(8,128)(2,1)S(1)}, bf16[128,1024]{1,0:T(8,128)(2,1)S(1)}, u32[]{:S(2)}, u32[]{:S(2)}) collective-permute-start(bf16[128,1024]{1,0:T(8,128)(2,1)S(1)} %get-tuple-element.494), channel_id=1, source_target_pairs={{0,16},{4,20},{8,24},{12,28},{16,0},{20,4},{24,8},{28,12},{1,17},{... | collective-permute-start | bytes 786440 | tf_op jit(solution)/shard_map/ppermute | solution.py:1804
  658.2 17.8 %collective-permute-start.76 = (bf16[256,1024]{1,0:T(8,128)(2,1)S(1)}, bf16[256,1024]{1,0:T(8,128)(2,1)S(1)}, u32[]{:S(2)}, u32[]{:S(2)}) collective-permute-start(bf16[256,1024]{1,0:T(8,128)(2,1)S(1)} %get-tuple-element.516), channel_id=1, source_target_pairs={{0,8},{4,12},{8,0},{12,4},{16,24},{20,28},{24,16},{28,20},{1,9},{5... | collective-permute-start | bytes 1572872 | tf_op jit(solution)/shard_map/ppermute | solution.py:1804
  (138 other events, 1691.7 us)

commit v3 on v2

--- a/solution.py
+++ b/solution.py
@@ -508,8 +508,7 @@
     "global_ff": 12,
     "local_heads": 18,
     "local_ff": 34,
-    "local_ff_back": 14,
-    "local_heads_back": 11,
+    "local_back": 90,
     "global_ff_back": 9,
     "global_ff_grads": 5,
     "global_heads_back": 12,
@@ -583,7 +582,7 @@
                 copies.append((hop, which, begin, rows, len(landed), offset))
                 offset += rows
             landed.append(shaped((offset,) + array.shape[1:], array.dtype))
-        reach = list(hops) + [hop for hop in dict.fromkeys(move[0] for move in moves) if hop not in hops]
+        reach = list(hops) or list(dict.fromkeys(move[0] for move in moves))
         lead = 0 if self.token is None else 1
         inputs = lead + len(args)
         first_out = inputs + len(sources)
@@ -619,7 +618,7 @@
             at_ends = (lambda step, act: pl.when(pl.program_id(0) == step)(act)) if steps > 1 else (
                 lambda step, act: act()
             )
-            if reach:
+            if pending:
                 at_ends(0, begin_all)
             body(*refs[lead:inputs], *refs[first_out : first_out + outputs], *scratch)
             if pending:
@@ -1354,260 +1353,256 @@
     )
 
 
-def local_ff_back_body(last, summed, first, grad_ref, grad_t_ref, b_t_ref, active_ref, slope_ref, up0, up1, down0, down1, *refs):
-    if summed:
-        met_ref, refs = refs[0], refs[1:]
-    so_far_ref, refs = (None, refs) if first else (refs[0], refs[1:])
-    if last:
-        middle_ref, gains_ref, refs = refs[0], refs[1], refs[2:]
-    if summed:
-        (down_near, down_far, up_near, up_far), refs = refs[:4], refs[4:]
-    else:
-        both_ref, refs = refs[0], refs[1:]
-    outs, (acc, dup) = refs[:-2], refs[-2:]
-    step = pl.program_id(0)
-    frames = grad_ref.shape[0] // CB
+def local_back_body(
+    grad_h, grad_t_h, b_t_h, a_t_h, active_h, slope_h, qkv_h, mixed_h, middle_h, gout_h, codes_h, gains_ref, *refs
+):
+    heads_h, ups_h, downs_h, refs = refs[:8], refs[8:16], refs[16:24], refs[24:]
+    total_ref, small_out_ref, gain_c_ref, gain_d_ref, *results_h = refs[:12]
+    (
+        grad_v, grad_t, other_t, weights, act, slp, dup, acc, mid, gout_v, codes_v,
+        pair_out, pair_far, pair_near, head_out, head_far, head_near, x_in, y_far, y_near,
+        sems, send, recv,
+    ) = refs[12:]
+    frames = gout_v.shape[0]
+    rows_all = grad_v.shape[0]
     half = D // 2
-
-    @pl.when(step == 0)
-    def _():
-        if so_far_ref is not None:
-            acc[...] = so_far_ref[...]
+    width = mixed_h.shape[2]
+    scale = HD ** (-0.5)
+    greet(("core", "x", "y"))
+
+    def fetch(at, source, target):
+        copy = pltpu.make_async_copy(source, target, sems.at[at])
+        copy.start()
+        return copy
+
+    def give(at, hop, source, target):
+        copy = to_partner(hop, source, target, send.at[at], recv.at[at])
+        copy.start()
+        return copy
+
+    def fetch_ff(rel):
+        found = [fetch(at, downs_h[2 * rel + at], weights.at[2 + at]) for at in range(2)]
+        found.append(fetch(2, slope_h.at[rel], slp))
+        return found + [fetch(3 + at, ups_h[2 * rel + at], weights.at[at]) for at in range(2)]
+
+    order = (3, 1, 2, 0)
+    waits = [fetch(5, grad_h, grad_v)] + fetch_ff(order[0])
+    late = [fetch(6, grad_t_h, grad_t), fetch(7, active_h.at[order[0]], act), fetch(8, b_t_h, other_t)]
+    later = [fetch(9, middle_h, mid), fetch(10, gout_h, gout_v), fetch(11, codes_h, codes_v)]
+    acc[...] = jnp.zeros_like(acc)
+    sent = []
+    for step, rel in enumerate(order):
+        for one in waits:
+            one.wait()
+        for tile in range(2):
+            lanes = slice(tile * half, (tile + 1) * half)
+            grad = dot_rows(grad_v[:, :half], weights[2, :, lanes]) + dot_rows(
+                grad_v[:, half:], weights[3, :, lanes]
+            )
+            dup[:, lanes] = (grad * slp[:, lanes].astype(jnp.float32)).astype(jnp.bfloat16)
+        for at in range(2):
+            lanes = slice(at * half, (at + 1) * half)
+            acc[:, lanes] += dot_transposed(dup[...], weights[at])
+        if step < 3:
+            waits = fetch_ff(order[step + 1])
+        for one in late:
+            one.wait()
+        if step == 1:
+            sent[0].wait_send()
+        if step >= 2:
+            sent[step - 2].wait_recv()
+        met = (None, None, pair_far, pair_near)[step]
+        for at in range(2):
+            rows = slice(at * half, (at + 1) * half)
+            for tile in range(2):
+                lanes = slice(tile * half, (tile + 1) * half)
+                down = dot_rows(grad_t[rows, :], act[:, lanes])
+                up = dot_rows(other_t[rows, :], dup[:, lanes])
+                if met is None:
+                    pair_out[0, rows, lanes] = down.astype(jnp.bfloat16)
+                    pair_out[1, rows, lanes] = up.astype(jnp.bfloat16)
+                else:
+                    met[0, rows, lanes] = (down + met[0, rows, lanes].astype(jnp.float32)).astype(jnp.bfloat16)
+                    met[1, rows, lanes] = (up + met[1, rows, lanes].astype(jnp.float32)).astype(jnp.bfloat16)
+        if step < 3:
+            late = [fetch(7, active_h.at[order[step + 1]], act)]
+        if step == 0:
+            sent.append(give(0, "core", pair_out, pair_far))
+        elif step == 1:
+            sent.append(give(1, "core", pair_out, pair_near))
+        elif step == 2:
+            x_far = give(2, "x", pair_far.at[1, pl.ds(half, half)], x_in.at[pl.ds(half, half)])
+            y_two = give(3, "y", pair_far.at[0, pl.ds(half, half)], y_far)
+            x_near = give(4, "x", pair_far.at[1, pl.ds(0, half)], x_in.at[pl.ds(0, half)])
         else:
-            acc[...] = jnp.zeros_like(acc)
-
+            y_zero = give(5, "y", pair_near.at[0, pl.ds(half, half)], y_near)
+
+    def fetch_heads(rel):
+        found = [fetch(at, heads_h[2 * rel + at], weights.at[at]) for at in range(2)]
+        found.append(fetch(2, qkv_h.at[rel], act.at[:, pl.ds(0, 3 * width)]))
+        return found + [fetch(3, mixed_h.at[rel], slp.at[:, pl.ds(0, width)])]
+
+    waits = fetch_heads(order[0]) + [fetch(8, a_t_h, other_t)]
+    sent[1].wait_send()
+    for one in later:
+        one.wait()
+    total_gain = jnp.zeros((1, D), jnp.float32)
     for c in range(CB):
         rows = slice(c * frames, (c + 1) * frames)
-        grad = dot_rows(grad_ref[rows, :half], down0[...]) + dot_rows(grad_ref[rows, half:], down1[...])
-        one = (grad * slope_ref[0, rows, :].astype(jnp.float32)).astype(jnp.bfloat16)
-        dup[rows, :] = one
-        for at, up in enumerate((up0, up1)):
+        part_back, gain_grad = norm_rows_back(mid[rows, :], gains_ref[3:4, :], acc[rows, :])
+        total = grad_v[rows, :].astype(jnp.float32) + part_back
+        mid[rows, :] = total
+        small = total.astype(jnp.bfloat16)
+        grad_v[rows, :] = small
+        grad_t[:, rows] = jnp.transpose(small)
+        total_gain = total_gain + gain_grad
+    gain_d_ref[...] = total_gain
+
+    ones = head_sums(width)
+    heads_sent = []
+
+    def more(total, term):
+        return term if total is None else total + term
+
+    for step, rel in enumerate(order):
+        for one in waits:
+            one.wait()
+        queries, keys, values, dmix = ([], [], [], [])
+        back = rounded_f32(
+            dot_rows(grad_v[:, :half], weights[0, :, 3 * width :])
+            + dot_rows(grad_v[:, half:], weights[1, :, 3 * width :])
+        )
+        for c in range(CB):
+            rows = slice(c * frames, (c + 1) * frames)
+            qkv = act[rows, : 3 * width].astype(jnp.float32)
+            queries.append(qkv[:, :width])
+            keys.append(qkv[:, width : 2 * width])
+            values.append(qkv[:, 2 * width :])
+            dmix.append(back[rows, :])
+        prob = frame_probs(queries, keys, ones)
+        dq, dk, dv = ([None] * CB, [None] * CB, [None] * CB)
+        for c in range(CB):
+            dprob = [over_heads(dmix[c] * values[c2], ones) for c2 in range(c + 1)]
+            center = prob[c][0] * dprob[0]
+            for c2 in range(1, c + 1):
+                center = center + prob[c][c2] * dprob[c2]
+            for c2 in range(c + 1):
+                dv[c2] = more(dv[c2], rounded_f32(prob[c][c2]) * dmix[c])
+                dscore = rounded_f32(prob[c][c2] * (dprob[c2] - center))
+                dq[c] = more(dq[c], dscore * keys[c2])
+                dk[c2] = more(dk[c2], dscore * queries[c])
+        for c in range(CB):
+            rows = slice(c * frames, (c + 1) * frames)
+            dup[rows, :width] = (dq[c] * scale).astype(jnp.bfloat16)
+            dup[rows, width : 2 * width] = (dk[c] * scale).astype(jnp.bfloat16)
+            dup[rows, 2 * width : 3 * width] = dv[c].astype(jnp.bfloat16)
+        for at in range(2):
             lanes = slice(at * half, (at + 1) * half)
-            acc[rows, lanes] += dot_transposed(one, up[...])
-    for at in range(D // 256):
-        rows = slice(at * 256, (at + 1) * 256)
-        down = dot_rows(grad_t_ref[rows, :], active_ref[0])
-        up = dot_rows(b_t_ref[rows, :], dup[...])
-        if summed:
-            down = (down + met_ref[0, rows, :].astype(jnp.float32)).astype(jnp.bfloat16)
-            up = (up + met_ref[1, rows, :].astype(jnp.float32)).astype(jnp.bfloat16)
-            begin = 0 if at * 256 < half else half
-            there = slice(at * 256 - begin, at * 256 - begin + 256)
-            (down_far if begin else down_near)[there, :] = down
-            (up_far if begin else up_near)[there, :] = up
-        else:
-            both_ref[0, rows, :] = down.astype(jnp.bfloat16)
-            both_ref[1, rows, :] = up.astype(jnp.bfloat16)
-
-    @pl.when(step == pl.num_programs(0) - 1)
-    def _():
-        if last:
-            grad_mid_ref, small_ref, small_t_ref, gain_ref = outs
-            total_gain = jnp.zeros((1, D), jnp.float32)
-            for c in range(CB):
-                rows = slice(c * frames, (c + 1) * frames)
-                part, gain_grad = norm_rows_back(middle_ref[rows, :], gains_ref[3:4, :], acc[rows, :])
-                total = grad_ref[rows, :].astype(jnp.float32) + part
-                grad_mid_ref[rows, :] = total
-                small = total.astype(jnp.bfloat16)
-                small_ref[rows, :] = small
-                small_t_ref[:, rows] = jnp.transpose(small)
-                total_gain = total_gain + gain_grad
-            gain_ref[...] = total_gain
-        else:
-            outs[0][...] = acc[...]
-
-
-def local_ff_back(line, rel, grad, grad_t, b_t, active, slope, up, down, met=None, so_far=None, tail=None, tile=512):
-    rows = grad.shape[0]
-    hidden = active.shape[2]
+            term = dot_transposed(dup[:, : 3 * width], weights[at, :, : 3 * width])
+            acc[:, lanes] = term if step == 0 else acc[:, lanes] + term
+        if step == 1:
+            heads_sent[0].wait_send()
+        if step >= 2:
+            heads_sent[step - 2].wait_recv()
+        met = (None, None, head_far, head_near)[step]
+        for at in range(2):
+            rows = slice(at * half, (at + 1) * half)
+            three = dot_rows(other_t[rows, :], dup[:, : 3 * width])
+            one = dot_rows(grad_t[rows, :], slp[:, :width])
+            if met is None:
+                head_out[rows, : 3 * width] = three.astype(jnp.bfloat16)
+                head_out[rows, 3 * width :] = one.astype(jnp.bfloat16)
+            else:
+                three = three + met[rows, : 3 * width].astype(jnp.float32)
+                one = one + met[rows, 3 * width :].astype(jnp.float32)
+                met[rows, : 3 * width] = three.astype(jnp.bfloat16)
+                met[rows, 3 * width :] = one.astype(jnp.bfloat16)
+        if step < 3:
+            waits = fetch_heads(order[step + 1])
+        if step == 0:
+            heads_sent.append(give(6, "core", head_out, head_far))
+        elif step == 1:
+            heads_sent.append(give(7, "core", head_out, head_near))
+    total_gain = jnp.zeros((1, D), jnp.float32)
+    total = jnp.zeros((frames, D), jnp.float32)
+    for c in range(CB):
+        rows = slice(c * frames, (c + 1) * frames)
+        local_in = gout_v[...] + codes_v[rows, :].astype(jnp.float32)
+        part_back, gain_grad = norm_rows_back(local_in, gains_ref[2:3, :], acc[rows, :])
+        total = total + (mid[rows, :] + part_back)
+        total_gain = total_gain + gain_grad
+    total_ref[...] = total
+    small_out_ref[...] = total.astype(jnp.bfloat16)
+    gain_c_ref[...] = total_gain
+
+    heads_sent[1].wait_send()
+    x_far.wait()
+    x_near.wait()
+    y_two.wait()
+    y_zero.wait()
+
+    def summed(one, two):
+        return (one.astype(jnp.float32) + two.astype(jnp.float32)).astype(jnp.bfloat16)
+
+    pair_near[1] = summed(pair_near[1], x_in[...])
+    pair_far[0, :half, :] = summed(pair_far[0, :half, :], y_far[...])
+    pair_near[0, :half, :] = summed(pair_near[0, :half, :], y_near[...])
+    near, far = pl.ds(0, half), pl.ds(half, half)
+    leaving = (
+        pair_near.at[1, near], pair_near.at[1, far], pair_far.at[0, near], pair_near.at[0, near],
+        head_far.at[near], head_far.at[far], head_near.at[near], head_near.at[far],
+    )
+    for one in [fetch(at, source, target) for at, (source, target) in enumerate(zip(leaving, results_h))]:
+        one.wait()
+
+
+def local_back(line, grad, grad_t, b_t, a_t, active, slope, qkv, mixed, middle, global_out, codes, gains, heads, ups, downs):
+    rows, frames = grad.shape[0], global_out.shape[0]
     half = D // 2
-    last, summed = tail is not None, met is not None
-    hidden_block = pl.BlockSpec((1, rows, tile), lambda step: (rel, 0, step))
-    pair_block = pl.BlockSpec((2, D, tile), lambda step: (0, 0, step))
-    extra_args, extra = ([], [])
-    if summed:
-        extra_args.append(met)
-        extra.append(pair_block)
-    if so_far is not None:
-        extra_args.append(so_far)
-        extra.append(held((rows, D)))
-    first = so_far is None
-    if last:
-        extra_args += list(tail)
-        extra += [held((rows, D)), held((4, D))]
-        outs = [
-            shaped((rows, D), jnp.float32),
-            shaped((rows, D), jnp.bfloat16),
-            shaped((D, rows), jnp.bfloat16),
+    flat = [one for parts in (heads, ups, downs) for pair in parts for one in pair]
+    columns = ups[0][0].shape[1]
+    small = jnp.bfloat16
+    return line.run(
+        local_back_body,
+        (grad, grad_t, b_t, a_t, active, slope, qkv, mixed, middle, global_out, codes, gains, *flat),
+        in_specs=[IN_HBM] * 11 + [VMEM_WHOLE] + [IN_HBM] * 24,
+        out_specs=[VMEM_WHOLE] * 4 + [IN_HBM] * 8,
+        out_shape=[
+            shaped((frames, D), jnp.float32),
+            shaped((frames, D), small),
+            shaped((1, D), jnp.float32),
             shaped((1, D), jnp.float32),
         ]
-    else:
-        outs = [shaped((rows, D), jnp.float32)]
-    if summed:
-        grad_specs = [by_cols((half, tile))] * 4
-        grad_shapes = [shaped((half, hidden), jnp.bfloat16)] * 4
-    else:
-        grad_specs = [pair_block]
-        grad_shapes = [shaped((2, D, hidden), jnp.bfloat16)]
-
-    def body(*refs):
-        local_ff_back_body(last, summed, first, *refs)
-
-    found = line.run(
-        body,
-        (grad, grad_t, b_t, active, slope, *up, *down, *extra_args),
-        grid=(hidden // tile,),
-        in_specs=[held((rows, D)), held((D, rows)), held((D, rows)), hidden_block, hidden_block]
-        + [by_cols((half, tile))] * 4
-        + extra,
-        out_specs=grad_specs + [held(one.shape) for one in outs],
-        out_shape=grad_shapes + outs,
-        scratch_shapes=[pltpu.VMEM((rows, D), jnp.float32), pltpu.VMEM((rows, tile), jnp.bfloat16)],
-        limit=(52),
-        name="local_ff_back",
-    )
-    return found[: len(grad_shapes)], found[len(grad_shapes) :]
-
-
-def local_heads_back_body(last, summed, first, grad_ref, grad_t_ref, a_t_ref, qkv_ref, mixed_ref, near_ref, far_ref, *refs):
-    if summed:
-        met_ref, refs = refs[0], refs[1:]
-    if not first:
-        so_far_ref, refs = refs[0], refs[1:]
-    if last:
-        grad_mid_ref, out_in_ref, code_ref, gains_ref = refs[:4]
-        refs = refs[4:]
-    if summed:
-        (near_out, far_out), refs = refs[:2], refs[2:]
-    else:
-        out_ref, refs = refs[0], refs[1:]
-    outs, (acc, dqkv) = refs[:-2], refs[-2:]
-    frames = grad_ref.shape[0] // CB
-    width = mixed_ref.shape[2]
-    half = D // 2
-    scale = HD ** (-0.5)
-    ones = head_sums(width)
-    queries, keys, values, dmix = ([], [], [], [])
-    for c in range(CB):
-        rows = slice(c * frames, (c + 1) * frames)
-        qkv = qkv_ref[0, rows, :].astype(jnp.float32)
-        queries.append(qkv[:, :width])
-        keys.append(qkv[:, width : 2 * width])
-        values.append(qkv[:, 2 * width :])
-        one = dot_rows(grad_ref[rows, :half], near_ref[:, 3 * width :]) + dot_rows(
-            grad_ref[rows, half:], far_ref[:, 3 * width :]
-        )
-        dmix.append(rounded_f32(one))
-    prob = frame_probs(queries, keys, ones)
-    dq, dk, dv = ([None] * CB, [None] * CB, [None] * CB)
-
-    def more(total, term):
-        return term if total is None else total + term
-
-    for c in range(CB):
-        dprob = [over_heads(dmix[c] * values[c2], ones) for c2 in range(c + 1)]
-        center = prob[c][0] * dprob[0]
-        for c2 in range(1, c + 1):
-            center = center + prob[c][c2] * dprob[c2]
-        for c2 in range(c + 1):
-            dv[c2] = more(dv[c2], rounded_f32(prob[c][c2]) * dmix[c])
-            dscore = rounded_f32(prob[c][c2] * (dprob[c2] - center))
-            dq[c] = more(dq[c], dscore * keys[c2])
-            dk[c2] = more(dk[c2], dscore * queries[c])
-    for c in range(CB):
-        rows = slice(c * frames, (c + 1) * frames)
-        dqkv[rows, :width] = (dq[c] * scale).astype(jnp.bfloat16)
-        dqkv[rows, width : 2 * width] = (dk[c] * scale).astype(jnp.bfloat16)
-        dqkv[rows, 2 * width :] = dv[c].astype(jnp.bfloat16)
-        for at, ref in enumerate((near_ref, far_ref)):
-            lanes = slice(at * half, (at + 1) * half)
-            term = dot_transposed(dqkv[rows, :], ref[:, : 3 * width])
-            acc[rows, lanes] = term if first else so_far_ref[rows, lanes] + term
-    for at in range(D // 256):
-        rows = slice(at * 256, (at + 1) * 256)
-        three = dot_rows(a_t_ref[rows, :], dqkv[...])
-        one = dot_rows(grad_t_ref[rows, :], mixed_ref[0])
-        there = rows
-        if summed:
-            three = three + met_ref[rows, : 3 * width].astype(jnp.float32)
-            one = one + met_ref[rows, 3 * width :].astype(jnp.float32)
-            begin = 0 if at * 256 < half else half
-            out_ref = far_out if begin else near_out
-            there = slice(at * 256 - begin, at * 256 - begin + 256)
-        out_ref[there, : 3 * width] = three.astype(jnp.bfloat16)
-        out_ref[there, 3 * width :] = one.astype(jnp.bfloat16)
-    if last:
-        total_ref, small_ref, gain_ref = outs
-        total_gain = jnp.zeros((1, D), jnp.float32)
-        total = jnp.zeros((frames, D), jnp.float32)
-        for c in range(CB):
-            rows = slice(c * frames, (c + 1) * frames)
-            local_in = out_in_ref[...] + code_ref[rows, :].astype(jnp.float32)
-            part, gain_grad = norm_rows_back(local_in, gains_ref[2:3, :], acc[rows, :])
-            total = total + (grad_mid_ref[rows, :] + part)
-            total_gain = total_gain + gain_grad
-        total_ref[...] = total
-        small_ref[...] = total.astype(jnp.bfloat16)
-        gain_ref[...] = total_gain
-    else:
-        outs[0][...] = acc[...]
-
-
-def local_heads_back(line, rel, grad, grad_t, a_t, qkv, mixed, halves, met=None, so_far=None, tail=None):
-    rows = grad.shape[0]
-    frames = rows // CB
-    width = mixed.shape[2]
-    last, summed, first = tail is not None, met is not None, so_far is None
-    extra_args, extra = ([], [])
-    if summed:
-        extra_args.append(met)
-        extra.append(held((D, 4 * width)))
-    if not first:
-        extra_args.append(so_far)
-        extra.append(held((rows, D)))
-    if last:
-        extra_args += list(tail)
-        extra += [held((rows, D)), held((frames, D)), held((rows, D)), held((4, D))]
-        outs = [
-            shaped((frames, D), jnp.float32),
-            shaped((frames, D), jnp.bfloat16),
-            shaped((1, D), jnp.float32),
-        ]
-    else:
-        outs = [shaped((rows, D), jnp.float32)]
-
-    if summed:
-        grad_shapes = [shaped((D // 2, 4 * width), jnp.bfloat16)] * 2
-    else:
-        grad_shapes = [shaped((D, 4 * width), jnp.bfloat16)]
-
-    def body(*refs):
-        local_heads_back_body(last, summed, first, *refs)
-
-    found = line.run(
-        body,
-        (grad, grad_t, a_t, qkv, mixed, *halves, *extra_args),
-        grid=(1,),
-        in_specs=[
-            held((rows, D)),
-            held((D, rows)),
-            held((D, rows)),
-            pl.BlockSpec((1, rows, 3 * width), lambda step: (rel, 0, 0)),
-            pl.BlockSpec((1, rows, width), lambda step: (rel, 0, 0)),
-        ]
-        + [held((D // 2, 4 * width))] * 2
-        + extra,
-        out_specs=[held(one.shape) for one in grad_shapes + outs],
-        out_shape=grad_shapes + outs,
+        + [shaped((half, columns), small)] * 8,
         scratch_shapes=[
+            pltpu.VMEM((rows, D), small),
+            pltpu.VMEM((D, rows), small),
+            pltpu.VMEM((D, rows), small),
+            pltpu.VMEM((4, half, columns), small),
+            pltpu.VMEM((rows, columns), small),
+            pltpu.VMEM((rows, columns), small),
+            pltpu.VMEM((rows, columns), small),
             pltpu.VMEM((rows, D), jnp.float32),
-            pltpu.VMEM((rows, 3 * width), jnp.bfloat16),
+            pltpu.VMEM((rows, D), jnp.float32),
+            pltpu.VMEM((frames, D), jnp.float32),
+            pltpu.VMEM((rows, D), small),
+            pltpu.VMEM((2, D, columns), small),
+            pltpu.VMEM((2, D, columns), small),
+            pltpu.VMEM((2, D, columns), small),
+            pltpu.VMEM((D, columns), small),
+            pltpu.VMEM((D, columns), small),
+            pltpu.VMEM((D, columns), small),
+            pltpu.VMEM((D, columns), small),
+            pltpu.VMEM((half, columns), small),
+            pltpu.VMEM((half, columns), small),
+            pltpu.SemaphoreType.DMA((12,)),
+            pltpu.SemaphoreType.DMA((8,)),
+            pltpu.SemaphoreType.DMA((8,)),
         ],
-        limit=(52),
-        name="local_heads_back",
-    )
-    return found[: len(grad_shapes)], found[len(grad_shapes) :]
+        hops=("core", "x", "y"),
+        limit=58,
+        name="local_back",
+    )
 
 
 def cast_body(*refs):
@@ -1911,49 +1906,16 @@
     l_active, l_slope, local_out, l_b_t = local_ff(line, source, l_normed_b, l_middle, l_up, l_down)
     local_out = jnp.transpose(local_out, (1, 0, 2))
 
-    def ff_back(rel, **more):
-        return local_ff_back(
-            line, rel, grad, grad_t, l_b_t, l_active, l_slope, l_up[rel], l_down[rel], **more
-        )
-
-    (pair,), (so_far,) = ff_back(3)
-    line.carry(("core", pair))
-    (pair,), (so_far,) = ff_back(1, so_far=so_far)
-    (met_far,) = line.arrived
-    line.carry(("core", pair))
-    (d2_near, d2_far, u2_near, u2_far), (so_far,) = ff_back(2, met=met_far, so_far=so_far)
-    (met_near,) = line.arrived
-    line.carry(("x", u2_far), ("y", d2_far))
-    (d0_near, d0_far, u0_near, u0_far), (l_grad_mid, l_small, l_small_t, gain_d) = ff_back(
-        0, met=met_near, so_far=so_far, tail=(l_middle, gains_here)
-    )
-    u2_far, d2_far = line.arrived
-
-    def heads_back(rel, **more):
-        return local_heads_back(
-            line, rel, l_small, l_small_t, l_a_t, l_qkv, l_mixed, l_heads[rel], **more
-        )
-
-    half = D // 4
-    line.carry(("x", part(u2_near, 0, half)), ("y", part(d0_far, 0, half)))
-    (far_heads,), (so_far,) = heads_back(3)
-    u2_near_a, d0_far_a = line.arrived
-    u_far = add_rows(line, [u0_far, u2_far])
-    d2 = add_rows(line, [d2_near, d2_far])
-    line.carry(("x", part(u2_near, half, half)), ("y", part(d0_far, half, half)), ("core", far_heads))
-    (near_heads,), (so_far,) = heads_back(1, so_far=so_far)
-    u2_near_b, d0_far_b, met_far = line.arrived
-    line.carry(("x", part(d2, 0, half)), ("y", part(u_far, 0, half)), ("core", near_heads))
-    (h2_near, h2_far), (so_far,) = heads_back(2, met=met_far, so_far=so_far)
-    d2_a, u_far_a, met_near = line.arrived
-    line.carry(("x", part(d2, half, half)), ("y", part(u_far, half, half)))
-    (h0_near, h0_far), (grad_global, small, gain_c) = heads_back(
-        0, met=met_near, so_far=so_far, tail=(l_grad_mid, global_out, codes_here, gains_here)
-    )
-    d2_b, u_far_b = line.arrived
+    (
+        grad_global, small, gain_c, gain_d, u_near, u_far, d2, d0, h2_near, h2_far, h0_near, h0_far,
+    ) = local_back(
+        line, grad, grad_t, l_b_t, l_a_t, l_active, l_slope, l_qkv, l_mixed, l_middle, global_out, codes_here,
+        gains_here, l_heads, l_up, l_down,
+    )
+    small_x = hop_x(small)
+    u_far = hop_y(u_far)
+    d2 = hop_x(d2)
     h2_far = hop_y(h2_far)
-    small_x = hop_x(small)
-    h0_far = hop_y(h0_far)
 
     def update(layer, third, pieces, before):
         return adam(
@@ -1968,26 +1930,26 @@
         keep, send = sum_pieces(line, [keep, met])
         return keep, hop_z(send, 2)
 
-    lu = depth_first([u0_near], [[u2_near_a, u2_near_b], [u_far_a, u_far_b]])
     (small_x,) = in_turn(line, small_x)
     grad_rows = [small, hop_core(small), small_x, hop_core(small_x)]
-    ld = depth_first([d0_near], [[d0_far_a, d0_far_b], [d2_a, d2_b]])
-    lu = depth_second(*lu)
+    h0_far = hop_y(h0_far)
     grad_upper, *parts = global_ff_back(line, grad_rows, slope, g_up, g_down)
     near_term, far_term = hop_core(parts[1]), hop_core(parts[3])
     gd_near, gd_far = global_outer(line, grad_rows, active)
     gd_far = hop_y(gd_far)
     to_x = hop_x(add_rows(line, [parts[2], far_term]))
-    ld = depth_second(*ld)
+    ld = depth_first([d0, d2])
+    lu = depth_first([u_near, u_far])
     gu_near, gu_far = global_outer(line, normed_b, grad_upper)
     gu_far = hop_y(gu_far)
-    found = update(1, 1, lu, None)
+    ld = depth_second(*ld)
     grad_middle, small, gain_b = merge_back(
         line, middle, (parts[0], near_term, to_x), grad_global, gains_here, 1
     )
     small_x = hop_x(small)
     h2 = hop_x(add_rows(line, [h2_near, h2_far]))
-    found = update(1, 2, ld, found)
+    lu = depth_second(*lu)
+    found = update(1, 2, ld, None)
     (small_x,) = in_turn(line, small_x)
     grad_attn = [small, hop_core(small), small_x, hop_core(small_x)]
     grad_qkv, *parts = global_heads_back(line, info, grad_attn, g_heads, qkv, mixed, lse)
@@ -1995,6 +1957,7 @@
     gh_near, gh_far = global_grads_heads(line, info, normed_a, grad_attn, grad_qkv, mixed)
     gh_far = hop_y(gh_far)
     to_x = hop_x(add_rows(line, [parts[2], far_term]))
+    found = update(1, 1, lu, found)
     gd = depth_first([gd_near, gd_far])
     lh = depth_first([h0_near, h0_far, h2])
     input_grad, gain_grads = finish(

time: 699 us -> 621 us (0.89)
  Pallas kernels: 336 us -> 253 us
    pallas_call x71 -> x62, Pallas kernels: 336 us -> 253 us  [run(): pl.pallas_call(inner, in_specs=[IN_HBM] * lead + list(in_specs) + [IN_HBM...]
    ppermute x14 -> x15, waiting for transfers between devices: 78.1 us -> 63.6 us  [hop_y(): return lax.ppermute(values, 'dp', [(at, at ^ 1) for at in range(8)])]
    ppermute x26, waiting for transfers between devices: 125 us -> 136 us  [hop_z(): return lax.ppermute(values, 'dp', [(at, at ^ 2 * step) for at in range(8)])]
    ppermute x14 -> x15, waiting for transfers between devices: 36.1 us -> 43.2 us  [hop_x(): return lax.ppermute(values, 'tensor', [(at, at ^ 2) for at in range(4)])]
    unnamed x206 -> x194, local copies, waits for them, and re-layouts: 36.4 us -> 32.7 us
    ppermute x14 -> x15, starting transfers between devices: 12.1 us -> 15.4 us  [hop_x(): return lax.ppermute(values, 'tensor', [(at, at ^ 2) for at in range(4)])]
    ppermute x14 -> x15, starting transfers between devices: 17.6 us -> 16.6 us  [hop_y(): return lax.ppermute(values, 'dp', [(at, at ^ 1) for at in range(8)])]
  transfers between devices with their start and end apart: 83 -> 85, of which waited for: 32 -> 32; matrix products, arithmetic and copies ran while one was open for 0% -> 0% of each run, Pallas kernels for 17% -> 21%
where the time goes in v3:
time: 621 us; the launch traced here: 617 us
  Pallas kernels  253 us (41%)
  waiting for transfers between devices  250 us (40%)
  starting transfers between devices  77.4 us (12%)
  local copies, waits for them, and re-layouts  32.7 us (5%)
    pallas_call x62, Pallas kernels, run(): pl.pallas_call(inner, in_specs=[IN_HBM] * lead + list(in_specs) + [IN_HBM...  253 us
    ppermute x26, waiting for transfers between devices, hop_z(): return lax.ppermute(values, 'dp', [(at, at ^ 2 * step) for at in range(8)])  136 us
    ppermute x15, waiting for transfers between devices, hop_y(): return lax.ppermute(values, 'dp', [(at, at ^ 1) for at in range(8)])  63.6 us
    ppermute x15, waiting for transfers between devices, hop_x(): return lax.ppermute(values, 'tensor', [(at, at ^ 2) for at in range(4)])  43.2 us
    ppermute x26, starting transfers between devices, hop_z(): return lax.ppermute(values, 'dp', [(at, at ^ 2 * step) for at in range(8)])  41.4 us
    unnamed x194, local copies, waits for them, and re-layouts  32.7 us
    ppermute x15, starting transfers between devices, hop_y(): return lax.ppermute(values, 'dp', [(at, at ^ 1) for at in range(8)])  16.6 us
    ppermute x15, starting transfers between devices, hop_x(): return lax.ppermute(values, 'tensor', [(at, at ^ 2) for at in range(4)])  15.4 us
  transfers between devices with their start and end apart: 85, of which 32 were waited for; matrix products, arithmetic and copies ran while one was open for 0% of the time, Pallas kernels for 21%

profile of v3, /device:TPU:0, one launch (start us, length us, event | category | flops | bytes accessed | tf_op | source)
XLA Modules:
  0.0 616.6 jit_solution(2932811875380360729)
XLA Ops:
  3.3 4.0 collective-permute-start
  14.1 5.5 collective-permute-done.refs_2_
  21.4 4.0 collective-permute-done.1.refs_1_
  25.4 8.4 %collective-permute-done.2.refs_2_ = bf16[256,1024]{1,0:T(8,128)(2,1)S(1)} collective-permute-done((bf16[256,1024]{1,0:T(8,128)(2,1)S(1)}, bf16[256,1024]{1,0:T(8,128)(2,1)S(1)}, u32[]{:S(2)}, u32[]{:S(2)}) %collective-permute-start.2) | collective-permute-done | bytes 524320 | tf_op jit(solution)/shard_map/ppermute | solution.py:1799
  36.1 3.3 collective-permute-start.3
  39.5 11.3 %collective-permute-done.3.refs_2_ = bf16[128,1024]{1,0:T(8,128)(2,1)S(1)} collective-permute-done((bf16[128,1024]{1,0:T(8,128)(2,1)S(1)}, bf16[128,1024]{1,0:T(8,128)(2,1)S(1)}, u32[]{:S(2)}, u32[]{:S(2)}) %collective-permute-start.3) | collective-permute-done | bytes 262176 | tf_op jit(solution)/shard_map/ppermute | solution.py:1799
  52.1 3.4 collective-permute-start.5
  55.4 14.0 %collective-permute-done.4.refs_2_ = bf16[256,1024]{1,0:T(8,128)(2,1)S(1)} collective-permute-done((bf16[256,1024]{1,0:T(8,128)(2,1)S(1)}, bf16[256,1024]{1,0:T(8,128)(2,1)S(1)}, u32[]{:S(2)}, u32[]{:S(2)}) %collective-permute-start.4) | collective-permute-done | bytes 524320 | tf_op jit(solution)/shard_map/ppermute | solution.py:1799
  74.5 4.9 collective-permute-start.10
  79.4 13.2 %global_heads.1 = (bf16[1024,768]{1,0:T(8,128)(2,1)S(1)}, bf16[1024,256]{1,0:T(8,128)(2,1)S(1)}, f32[8,1024]{1,0:T(8,128)S(1)}, bf16[256,1024]{1,0:T(8,128)(2,1)...) custom-call(f32[8,128]{1,0:T(8,128)S(1)} %get-tuple-element.243.refs, ...), custom_call_target="tpu_custom_call" | custom-call | flops 2600000000 | bytes 1000 | tf_op jit(solution)/shard_map/global_heads/pallas_call | solution.py:631
  99.3 14.6 %collective-permute-done.14.refs_2_ = bf16[256,1024]{1,0:T(8,128)(2,1)S(1)} collective-permute-done((bf16[256,1024]{1,0:T(8,128)(2,1)S(1)}, bf16[256,1024]{1,0:T(8,128)(2,1)S(1)}, u32[]{:S(2)}, u32[]{:S(2)}) %collective-permute-start.14) | collective-permute-done | bytes 524320 | tf_op jit(solution)/shard_map/ppermute | solution.py:1799
  121.1 13.5 %collective-permute-done.18.refs_2_ = bf16[256,1024]{1,0:T(8,128)(2,1)S(1)} collective-permute-done((bf16[256,1024]{1,0:T(8,128)(2,1)S(1)}, bf16[256,1024]{1,0:T(8,128)(2,1)S(1)}, u32[]{:S(2)}, u32[]{:S(2)}) %collective-permute-start.18) | collective-permute-done | bytes 524320 | tf_op jit(solution)/shard_map/ppermute | solution.py:1799
  136.9 3.1 collective-permute-done.32.refs_2_
  153.9 8.8 %collective-permute-done.24.refs_6_.refs_7_ = bf16[512,1024]{1,0:T(8,128)(2,1)} collective-permute-done((bf16[512,1024]{1,0:T(8,128)(2,1)}, bf16[512,1024]{1,0:T(8,128)(2,1)}, u32[]{:S(2)}, u32[]{:S(2)}) %collective-permute-start.24) | collective-permute-done | bytes 1048608 | tf_op jit(solution)/shard_map/ppermute | solution.py:1795
  164.7 20.4 %collective-permute-done.25.refs_8_.refs_9_ = bf16[512,1024]{1,0:T(8,128)(2,1)} collective-permute-done((bf16[512,1024]{1,0:T(8,128)(2,1)}, bf16[512,1024]{1,0:T(8,128)(2,1)}, u32[]{:S(2)}, u32[]{:S(2)}) %collective-permute-start.25) | collective-permute-done | bytes 1048608 | tf_op jit(solution)/shard_map/ppermute | solution.py:1795
  185.1 12.5 %global_ff.1 = (bf16[1024,1024]{1,0:T(8,128)(2,1)S(1)}, bf16[1024,1024]{1,0:T(8,128)(2,1)S(1)}, bf16[256,1024]{1,0:T(8,128)(2,1)S(1)}, bf16[256,1024]{1,0:T(8,12...) custom-call(f32[8,128]{1,0:T(8,128)S(1)} %get-tuple-element.276.refs_0_, ...), custom_call_target="tpu_custom_call" | custom-call | flops 2400000000 | bytes 1000 | tf_op jit(solution)/shard_map/global_ff/pallas_call | solution.py:631
  199.2 7.0 %collective-permute-done.31.refs_1_ = bf16[512,1024]{1,0:T(8,128)(2,1)S(1)} collective-permute-done((bf16[512,1024]{1,0:T(8,128)(2,1)}, bf16[512,1024]{1,0:T(8,128)(2,1)S(1)}, u32[]{:S(2)}, u32[]{:S(2)}) %collective-permute-start.31) | collective-permute-done | bytes 1048608 | tf_op jit(solution)/shard_map/ppermute | solution.py:1795
  209.0 12.2 %collective-permute-done.30.refs_4_ = bf16[256,1024]{1,0:T(8,128)(2,1)S(1)} collective-permute-done((bf16[256,1024]{1,0:T(8,128)(2,1)S(1)}, bf16[256,1024]{1,0:T(8,128)(2,1)S(1)}, u32[]{:S(2)}, u32[]{:S(2)}) %collective-permute-start.30) | collective-permute-done | bytes 524320 | tf_op jit(solution)/shard_map/ppermute | solution.py:1787
  226.3 17.9 %local_heads.1 = (bf16[4,768,768]{2,1,0:T(8,128)(2,1)}, bf16[4,768,256]{2,1,0:T(8,128)(2,1)}, f32[768,1024]{1,0:T(8,128)}, bf16[768,1024]{1,0:T(8,128)(2,1)}, bf...) custom-call(f32[8,128]{1,0:T(8,128)S(1)} %get-tuple-element.293.refs_0_, f32[256,1024]{1,0:T(8,128)S(1)} %copy-done.71, ...), custom_call_target="tpu_custom_call" | custom-call | flops 3600000000 | bytes 1000 | tf_op jit(solution)/shard_map/local_heads/pallas_call | solution.py:631
  245.9 19.1 %collective-permute-done.39.refs_1_ = bf16[512,1024]{1,0:T(8,128)(2,1)S(1)} collective-permute-done((bf16[512,1024]{1,0:T(8,128)(2,1)}, bf16[512,1024]{1,0:T(8,128)(2,1)S(1)}, u32[]{:S(2)}, u32[]{:S(2)}) %collective-permute-start.39) | collective-permute-done | bytes 1048608 | tf_op jit(solution)/shard_map/ppermute | solution.py:1795
  268.1 4.3 collective-permute-done.43.refs_11_.refs_28_
  274.0 35.1 %local_ff.1 = (bf16[4,768,1024]{2,1,0:T(8,128)(2,1)}, bf16[4,768,1024]{2,1,0:T(8,128)(2,1)}, bf16[3,256,1024]{2,1,0:T(8,128)(2,1)}, bf16[1024,768]{1,0:T(8,128)(2,1)}, f32[8,128]{1,0:T(8,128)}) custom-call(f32[8,128]{1,0:T(8,128)} %copy-done.77, s32[8]{0:T(128)} %copy-done.63, bf16[768,1024]{1,0:T(8,128)(2,1)} %get-tuple-element.304.refs_2_, ...), custom_call_target="tpu_custom_call" | custom-call | flops 6800000000 | bytes 1000 | tf_op jit(solution)/shard_map/local_ff/pallas_call | solution.py:631
  309.1 81.2 %local_back.1 = (f32[256,1024]{1,0:T(8,128)}, bf16[256,1024]{1,0:T(8,128)(2,1)}, f32[1,1024]{1,0:T(1,128)}, f32[1,1024]{1,0:T(1,128)}, bf16[512,1024]{1,0:T(8,12...) custom-call(f32[8,128]{1,0:T(8,128)} %get-tuple-element.311.refs_0_,, ...), custom_call_target="tpu_custom_call" | custom-call | flops 17999998976 | bytes 1000 | tf_op jit(solution)/shard_map/local_back/pallas_call | solution.py:631
  391.7 12.0 %collective-permute-done.48.refs_1_ = bf16[256,1024]{1,0:T(8,128)(2,1)S(1)} collective-permute-done((bf16[256,1024]{1,0:T(8,128)(2,1)}, bf16[256,1024]{1,0:T(8,128)(2,1)S(1)}, u32[]{:S(2)}, u32[]{:S(2)}) %collective-permute-start.48) | collective-permute-done | bytes 524320 | tf_op jit(solution)/shard_map/ppermute | solution.py:1787
  409.1 9.5 %global_ff_back.1 = (bf16[1024,1024]{1,0:T(8,128)(2,1)S(1)}, bf16[256,1024]{1,0:T(8,128)(2,1)S(1)}, bf16[256,1024]{1,0:T(8,128)(2,1)}, bf16[256,1024]{1,0:T(8,12...) custom-call(f32[8,128]{1,0:T(8,128)S(1)} %get-tuple-element.322.refs_0_, ...), custom_call_target="tpu_custom_call" | custom-call | flops 1800000000 | bytes 1000 | tf_op jit(solution)/shard_map/global_ff_back/pallas_call | solution.py:631
  420.8 4.6 global_ff_grads.2
  425.5 4.7 collective-permute-done.52.refs_2_
  434.3 6.3 %global_ff_grads.3 = (bf16[512,1024]{1,0:T(8,128)(2,1)S(1)}, bf16[512,1024]{1,0:T(8,128)(2,1)}, f32[8,128]{1,0:T(8,128)S(1)}) custom-call(f32[8,128]{1,0:T(8,128)S(1)} %get-tuple-element.336.refs_0_, bf16[256,1024]{1,0:T(8,128)(2,1)} %get-tuple-element.270.refs_1_, bf16[256,1024]{1,0:T(8,128)(2,1)} %collective-permute-done.22.refs_2_, ...), custom_call_target="tpu_custom_call" | custom-call | flops 1000000000 | bytes 1000 | tf_op jit(solution)/shard_map/global_ff_grads/pallas_call | solution.py:631
  440.5 4.8 collective-permute-done.54.refs_2_
  448.7 5.1 collective-permute-done.57.refs_2_
  456.9 5.3 collective-permute-done.59.refs_2_
  462.3 5.0 adam_update.6
  470.2 12.2 %global_heads_back.1 = (bf16[1024,768]{1,0:T(8,128)(2,1)S(1)}, bf16[256,1024]{1,0:T(8,128)(2,1)S(1)}, bf16[256,1024]{1,0:T(8,128)(2,1)}, bf16[256,1024]{1,0:T(8,...) custom-call(f32[8,128]{1,0:T(8,128)S(1)} %get-tuple-element.357.refs_0_, s32[2]{0:T(128)S(1)} %pad_add_fusion.refs_1_, ...), custom_call_target="tpu_custom_call" | custom-call | flops 2400000000 | bytes 1000 | tf_op jit(solution)/shard_map/global_heads_back/pallas_call | solution.py:631
  484.0 13.6 %collective-permute-done.64.refs_2_ = bf16[128,1024]{1,0:T(8,128)(2,1)S(1)} collective-permute-done((bf16[128,1024]{1,0:T(8,128)(2,1)S(1)}, bf16[128,1024]{1,0:T(8,128)(2,1)S(1)}, u32[]{:S(2)}, u32[]{:S(2)}) %collective-permute-start.64) | collective-permute-done | bytes 262176 | tf_op jit(solution)/shard_map/ppermute | solution.py:1799
  504.2 5.1 global_heads_grads.1
  512.2 4.8 adam_update.7
  524.7 6.7 %collective-permute-done.69.refs_5_ = bf16[256,1024]{1,0:T(8,128)(2,1)S(1)} collective-permute-done((bf16[256,1024]{1,0:T(8,128)(2,1)S(1)}, bf16[256,1024]{1,0:T(8,128)(2,1)S(1)}, u32[]{:S(2)}, u32[]{:S(2)}) %collective-permute-start.69) | collective-permute-done | bytes 524320 | tf_op jit(solution)/shard_map/ppermute | solution.py:1787
  531.5 2.9 input_grad.1
  534.5 10.3 %collective-permute-done.71.refs_2_ = bf16[256,1024]{1,0:T(8,128)(2,1)S(1)} collective-permute-done((bf16[256,1024]{1,0:T(8,128)(2,1)S(1)}, bf16[256,1024]{1,0:T(8,128)(2,1)S(1)}, u32[]{:S(2)}, u32[]{:S(2)}) %collective-permute-start.71) | collective-permute-done | bytes 524320 | tf_op jit(solution)/shard_map/ppermute | solution.py:1799
  548.5 15.1 %collective-permute-done.73.refs_2_ = bf16[128,1024]{1,0:T(8,128)(2,1)S(1)} collective-permute-done((bf16[128,1024]{1,0:T(8,128)(2,1)S(1)}, bf16[128,1024]{1,0:T(8,128)(2,1)S(1)}, u32[]{:S(2)}, u32[]{:S(2)}) %collective-permute-start.73) | collective-permute-done | bytes 262176 | tf_op jit(solution)/shard_map/ppermute | solution.py:1799
  563.5 4.8 adam_update.8
  571.0 4.8 adam_update.9
  585.2 7.1 %collective-permute-done.77.refs_2_ = bf16[128,1024]{1,0:T(8,128)(2,1)S(1)} collective-permute-done((bf16[128,1024]{1,0:T(8,128)(2,1)S(1)}, bf16[128,1024]{1,0:T(8,128)(2,1)S(1)}, u32[]{:S(2)}, u32[]{:S(2)}) %collective-permute-start.77) | collective-permute-done | bytes 262176 | tf_op jit(solution)/shard_map/ppermute | solution.py:1799
  592.4 4.8 adam_update.10
  597.3 3.4 collective-permute-start.79
  600.8 4.2 collective-permute-done.83
  607.4 3.4 collective-permute-done.84
  611.6 4.8 adam_update.11
  (386 shorter events, 126.7 us)
Async XLA Ops:
  34.8 44.6 %collective-permute-start.8 = (bf16[512,1024]{1,0:T(8,128)(2,1)}, bf16[512,1024]{1,0:T(8,128)(2,1)}, u32[]{:S(2)}, u32[]{:S(2)}) collective-permute-start(bf16[512,1024]{1,0:T(8,128)(2,1)} %get-tuple-element.245.refs_6_), channel_id=1, source_target_pairs={{0,4},{4,0},{8,12},{12,8},{16,20},{20,16},{24,28},{28,24},{1,5},{5... | collective-permute-start | bytes 3145736 | tf_op jit(solution)/shard_map/ppermute | solution.py:1795
  50.8 18.6 %collective-permute-start.4 = (bf16[256,1024]{1,0:T(8,128)(2,1)S(1)}, bf16[256,1024]{1,0:T(8,128)(2,1)S(1)}, u32[]{:S(2)}, u32[]{:S(2)}) collective-permute-start(bf16[256,1024]{1,0:T(8,128)(2,1)S(1)} %get-tuple-element.240.refs_1_), channel_id=1, source_target_pairs={{0,8},{4,12},{8,0},{12,4},{16,24},{20,28},{24,16},{28,20},{1,9},{5... | collective-permute-start | bytes 1572872 | tf_op jit(solution)/shard_map/ppermute | solution.py:1799
  51.5 22.8 %collective-permute-start.6 = (bf16[256,1024]{1,0:T(8,128)(2,1)}, bf16[256,1024]{1,0:T(8,128)(2,1)}, u32[]{:S(2)}, u32[]{:S(2)}) collective-permute-start(bf16[256,1024]{1,0:T(8,128)(2,1)} %get-tuple-element.234.refs_2_), channel_id=1, source_target_pairs={{0,1},{1,0},{2,3},{3,2},{4,5},{5,4},{6,7},{7,6},{8,9},{9,8},{10,11... | collective-permute-start | bytes 1572872 | tf_op jit(solution)/shard_map/ppermute | solution.py:1791
  51.5 22.9 %collective-permute-start.7 = (bf16[256,1024]{1,0:T(8,128)(2,1)}, bf16[256,1024]{1,0:T(8,128)(2,1)}, u32[]{:S(2)}, u32[]{:S(2)}) collective-permute-start(bf16[256,1024]{1,0:T(8,128)(2,1)} %get-tuple-element.244.refs_4_), channel_id=1, source_target_pairs={{0,1},{1,0},{2,3},{3,2},{4,5},{5,4},{6,7},{7,6},{8,9},{9,8},{10,11... | collective-permute-start | bytes 1572872 | tf_op jit(solution)/shard_map/ppermute | solution.py:1791
  52.1 20.6 %collective-permute-start.5 = (bf16[128,1024]{1,0:T(8,128)(2,1)}, bf16[128,1024]{1,0:T(8,128)(2,1)}, u32[]{:S(2)}, u32[]{:S(2)}) collective-permute-start(bf16[128,1024]{1,0:T(8,128)(2,1)} %get-tuple-element.242.refs_1_), channel_id=1, source_target_pairs={{0,16},{4,20},{8,24},{12,28},{16,0},{20,4},{24,8},{28,12},{1,17},{... | collective-permute-start | bytes 786440 | tf_op jit(solution)/shard_map/ppermute | solution.py:1799
  70.5 25.9 %collective-permute-start.13 = (bf16[512,1024]{1,0:T(8,128)(2,1)}, bf16[512,1024]{1,0:T(8,128)(2,1)}, u32[]{:S(2)}, u32[]{:S(2)}) collective-permute-start(bf16[512,1024]{1,0:T(8,128)(2,1)} %get-tuple-element.254.refs_4_.refs_13_), channel_id=1, source_target_pairs={{0,2},{1,3},{2,0},{3,1},{4,6},{5,7},{6,4},{7,5},{8,10},{9,11},{10,... | collective-permute-start | bytes 3145736 | tf_op jit(solution)/shard_map/ppermute | solution.py:1787
  72.7 26.6 %collective-permute-start.12 = (bf16[512,1024]{1,0:T(8,128)(2,1)}, bf16[512,1024]{1,0:T(8,128)(2,1)S(1)}, u32[]{:S(2)}, u32[]{:S(2)}) collective-permute-start(bf16[512,1024]{1,0:T(8,128)(2,1)} %get-tuple-element.254.refs_4_.refs_13_), channel_id=1, source_target_pairs={{0,4},{4,0},{8,12},{12,8},{16,20},{20,16},{24,28},{28,24},{1,5},{5... | collective-permute-start | bytes 3145736 | tf_op jit(solution)/shard_map/ppermute | solution.py:1795
  74.3 18.5 %collective-permute-start.9 = (bf16[256,1024]{1,0:T(8,128)(2,1)S(1)}, bf16[256,1024]{1,0:T(8,128)(2,1)S(1)}, u32[]{:S(2)}, u32[]{:S(2)}) collective-permute-start(bf16[256,1024]{1,0:T(8,128)(2,1)S(1)} %get-tuple-element.247.refs_1_), channel_id=1, source_target_pairs={{0,8},{4,12},{8,0},{12,4},{16,24},{20,28},{24,16},{28,20},{1,9},{5... | collective-permute-start | bytes 1572872 | tf_op jit(solution)/shard_map/ppermute | solution.py:1799
  74.5 19.4 %collective-permute-start.10 = (bf16[128,1024]{1,0:T(8,128)(2,1)S(1)}, bf16[128,1024]{1,0:T(8,128)(2,1)S(1)}, u32[]{:S(2)}, u32[]{:S(2)}) collective-permute-start(bf16[128,1024]{1,0:T(8,128)(2,1)S(1)} %get-tuple-element.249.refs_1_), channel_id=1, source_target_pairs={{0,16},{4,20},{8,24},{12,28},{16,0},{20,4},{24,8},{28,12},{1,17},{... | collective-permute-start | bytes 786440 | tf_op jit(solution)/shard_map/ppermute | solution.py:1799
  93.9 20.0 %collective-permute-start.14 = (bf16[256,1024]{1,0:T(8,128)(2,1)S(1)}, bf16[256,1024]{1,0:T(8,128)(2,1)S(1)}, u32[]{:S(2)}, u32[]{:S(2)}) collective-permute-start(bf16[256,1024]{1,0:T(8,128)(2,1)S(1)} %get-tuple-element.256.refs_1_), channel_id=1, source_target_pairs={{0,8},{4,12},{8,0},{12,4},{16,24},{20,28},{24,16},{28,20},{1,9},{5... | collective-permute-start | bytes 1572872 | tf_op jit(solution)/shard_map/ppermute | solution.py:1799
  95.7 21.2 %collective-permute-start.16 = (bf16[256,1024]{1,0:T(8,128)(2,1)S(1)}, bf16[256,1024]{1,0:T(8,128)(2,1)S(1)}, u32[]{:S(2)}, u32[]{:S(2)}) collective-permute-start(bf16[256,1024]{1,0:T(8,128)(2,1)S(1)} %get-tuple-element.262), channel_id=1, source_target_pairs={{0,1},{1,0},{2,3},{3,2},{4,5},{5,4},{6,7},{7,6},{8,9},{9,8},{10,11... | collective-permute-start | bytes 1572872 | tf_op jit(solution)/shard_map/ppermute | solution.py:1791
  95.8 21.1 %collective-permute-start.17 = (bf16[256,1024]{1,0:T(8,128)(2,1)S(1)}, bf16[256,1024]{1,0:T(8,128)(2,1)S(1)}, u32[]{:S(2)}, u32[]{:S(2)}) collective-permute-start(bf16[256,1024]{1,0:T(8,128)(2,1)S(1)} %get-tuple-element.263), channel_id=1, source_target_pairs={{0,2},{1,3},{2,0},{3,1},{4,6},{5,7},{6,4},{7,5},{8,10},{9,11},{10,... | collective-permute-start | bytes 1572872 | tf_op jit(solution)/shard_map/ppermute | solution.py:1787
  96.4 19.1 %collective-permute-start.15 = (bf16[128,1024]{1,0:T(8,128)(2,1)S(1)}, bf16[128,1024]{1,0:T(8,128)(2,1)S(1)}, u32[]{:S(2)}, u32[]{:S(2)}) collective-permute-start(bf16[128,1024]{1,0:T(8,128)(2,1)S(1)} %copy-done.76), channel_id=1, source_target_pairs={{0,16},{4,20},{8,24},{12,28},{16,0},{20,4},{24,8},{28,12},{1,17},{... | collective-permute-start | bytes 786440 | tf_op jit(solution)/shard_map/ppermute | solution.py:1799
  114.0 26.1 %collective-permute-start.32 = (bf16[512,1024]{1,0:T(8,128)(2,1)S(1)}, bf16[512,1024]{1,0:T(8,128)(2,1)S(1)}, u32[]{:S(2)}, u32[]{:S(2)}) collective-permute-start(bf16[512,1024]{1,0:T(8,128)(2,1)S(1)} %get-tuple-element.272.refs_3_), channel_id=1, source_target_pairs={{0,4},{4,0},{8,12},{12,8},{16,20},{20,16},{24,28},{28,24},{1,5},{5... | collective-permute-start | bytes 3145736 | tf_op jit(solution)/shard_map/ppermute | solution.py:1795
  115.6 18.9 %collective-permute-start.18 = (bf16[256,1024]{1,0:T(8,128)(2,1)S(1)}, bf16[256,1024]{1,0:T(8,128)(2,1)S(1)}, u32[]{:S(2)}, u32[]{:S(2)}) collective-permute-start(bf16[256,1024]{1,0:T(8,128)(2,1)S(1)} %get-tuple-element.266.refs_1_), channel_id=1, source_target_pairs={{0,8},{4,12},{8,0},{12,4},{16,24},{20,28},{24,16},{28,20},{1,9},{5... | collective-permute-start | bytes 1572872 | tf_op jit(solution)/shard_map/ppermute | solution.py:1799
  115.7 47.0 %collective-permute-start.24 = (bf16[512,1024]{1,0:T(8,128)(2,1)}, bf16[512,1024]{1,0:T(8,128)(2,1)}, u32[]{:S(2)}, u32[]{:S(2)}) collective-permute-start(bf16[512,1024]{1,0:T(8,128)(2,1)} %get-tuple-element.278.refs_5_.refs_6_), channel_id=1, source_target_pairs={{0,4},{4,0},{8,12},{12,8},{16,20},{20,16},{24,28},{28,24},{1,5},{5... | collective-permute-start | bytes 3145736 | tf_op jit(solution)/shard_map/ppermute | solution.py:1795
  118.1 18.8 %collective-permute-start.20 = (bf16[256,1024]{1,0:T(8,128)(2,1)}, bf16[256,1024]{1,0:T(8,128)(2,1)}, u32[]{:S(2)}, u32[]{:S(2)}) collective-permute-start(bf16[256,1024]{1,0:T(8,128)(2,1)} %get-tuple-element.270.refs_1_), channel_id=1, source_target_pairs={{0,2},{1,3},{2,0},{3,1},{4,6},{5,7},{6,4},{7,5},{8,10},{9,11},{10,... | collective-permute-start | bytes 1572872 | tf_op jit(solution)/shard_map/ppermute | solution.py:1787
  135.6 49.5 %collective-permute-start.25 = (bf16[512,1024]{1,0:T(8,128)(2,1)}, bf16[512,1024]{1,0:T(8,128)(2,1)}, u32[]{:S(2)}, u32[]{:S(2)}) collective-permute-start(bf16[512,1024]{1,0:T(8,128)(2,1)} %get-tuple-element.279.refs_7_.refs_8_), channel_id=1, source_target_pairs={{0,4},{4,0},{8,12},{12,8},{16,20},{20,16},{24,28},{28,24},{1,5},{5... | collective-permute-start | bytes 3145736 | tf_op jit(solution)/shard_map/ppermute | solution.py:1795
  136.9 26.3 %collective-permute-start.22 = (bf16[256,1024]{1,0:T(8,128)(2,1)}, bf16[256,1024]{1,0:T(8,128)(2,1)}, u32[]{:S(2)}, u32[]{:S(2)}) collective-permute-start(bf16[256,1024]{1,0:T(8,128)(2,1)} %get-tuple-element.270.refs_1_), channel_id=1, source_target_pairs={{0,1},{1,0},{2,3},{3,2},{4,5},{5,4},{6,7},{7,6},{8,9},{9,8},{10,11... | collective-permute-start | bytes 1572872 | tf_op jit(solution)/shard_map/ppermute | solution.py:1791
  143.1 21.7 %collective-permute-start.23 = (bf16[256,1024]{1,0:T(8,128)(2,1)}, bf16[256,1024]{1,0:T(8,128)(2,1)}, u32[]{:S(2)}, u32[]{:S(2)}) collective-permute-start(bf16[256,1024]{1,0:T(8,128)(2,1)} %get-tuple-element.277.refs_3_), channel_id=1, source_target_pairs={{0,1},{1,0},{2,3},{3,2},{4,5},{5,4},{6,7},{7,6},{8,9},{9,8},{10,11... | collective-permute-start | bytes 1572872 | tf_op jit(solution)/shard_map/ppermute | solution.py:1791
  151.1 46.7 %collective-permute-start.26 = (bf16[512,1024]{1,0:T(8,128)(2,1)S(1)}, bf16[512,1024]{1,0:T(8,128)(2,1)S(1)}, u32[]{:S(2)}, u32[]{:S(2)}) collective-permute-start(bf16[512,1024]{1,0:T(8,128)(2,1)S(1)} %copy-done.23), channel_id=1, source_target_pairs={{0,2},{1,3},{2,0},{3,1},{4,6},{5,7},{6,4},{7,5},{8,10},{9,11},{10,... | collective-permute-start | bytes 3145736 | tf_op jit(solution)/shard_map/ppermute | solution.py:1787
  162.7 36.5 %collective-permute-start.27 = (bf16[512,1024]{1,0:T(8,128)(2,1)S(1)}, bf16[512,1024]{1,0:T(8,128)(2,1)S(1)}, u32[]{:S(2)}, u32[]{:S(2)}) collective-permute-start(bf16[512,1024]{1,0:T(8,128)(2,1)S(1)} %copy-done.9), channel_id=1, source_target_pairs={{0,2},{1,3},{2,0},{3,1},{4,6},{5,7},{6,4},{7,5},{8,10},{9,11},{10,... | collective-permute-start | bytes 3145736 | tf_op jit(solution)/shard_map/ppermute | solution.py:1787
  163.2 43.0 %collective-permute-start.31 = (bf16[512,1024]{1,0:T(8,128)(2,1)}, bf16[512,1024]{1,0:T(8,128)(2,1)S(1)}, u32[]{:S(2)}, u32[]{:S(2)}) collective-permute-start(bf16[512,1024]{1,0:T(8,128)(2,1)} %get-tuple-element.283.refs_3_), channel_id=1, source_target_pairs={{0,4},{4,0},{8,12},{12,8},{16,20},{20,16},{24,28},{28,24},{1,5},{5... | collective-permute-start | bytes 3145736 | tf_op jit(solution)/shard_map/ppermute | solution.py:1795
  164.7 42.7 %collective-permute-start.33 = (bf16[512,1024]{1,0:T(8,128)(2,1)}, bf16[512,1024]{1,0:T(8,128)(2,1)S(1)}, u32[]{:S(2)}, u32[]{:S(2)}) collective-permute-start(bf16[512,1024]{1,0:T(8,128)(2,1)} %get-tuple-element.254.refs_4_.refs_13_), channel_id=1, source_target_pairs={{0,1},{1,0},{2,3},{3,2},{4,5},{5,4},{6,7},{7,6},{8,9},{9,8},{10,11... | collective-permute-start | bytes 3145736 | tf_op jit(solution)/shard_map/ppermute | solution.py:1791
  207.5 36.7 %collective-permute-start.37 = (bf16[512,1024]{1,0:T(8,128)(2,1)}, bf16[512,1024]{1,0:T(8,128)(2,1)}, u32[]{:S(2)}, u32[]{:S(2)}) collective-permute-start(bf16[512,1024]{1,0:T(8,128)(2,1)} %get-tuple-element.299.refs_12_.refs_29_), channel_id=1, source_target_pairs={{0,2},{1,3},{2,0},{3,1},{4,6},{5,7},{6,4},{7,5},{8,10},{9,11},{10,... | collective-permute-start | bytes 3145736 | tf_op jit(solution)/shard_map/ppermute | solution.py:1787
  221.3 23.0 %collective-permute-start.38 = (bf16[512,1024]{1,0:T(8,128)(2,1)S(1)}, bf16[512,1024]{1,0:T(8,128)(2,1)}, u32[]{:S(2)}, u32[]{:S(2)}) collective-permute-start(bf16[512,1024]{1,0:T(8,128)(2,1)S(1)} %get-tuple-element.300.refs_8_.refs_25_), channel_id=1, source_target_pairs={{0,4},{4,0},{8,12},{12,8},{16,20},{20,16},{24,28},{28,24},{1,5},{5... | collective-permute-start | bytes 3145736 | tf_op jit(solution)/shard_map/ppermute | solution.py:1795
  244.3 20.7 %collective-permute-start.39 = (bf16[512,1024]{1,0:T(8,128)(2,1)}, bf16[512,1024]{1,0:T(8,128)(2,1)S(1)}, u32[]{:S(2)}, u32[]{:S(2)}) collective-permute-start(bf16[512,1024]{1,0:T(8,128)(2,1)} %get-tuple-element.302.refs_16_.refs_33_), channel_id=1, source_target_pairs={{0,4},{4,0},{8,12},{12,8},{16,20},{20,16},{24,28},{28,24},{1,5},{5... | collective-permute-start | bytes 3145736 | tf_op jit(solution)/shard_map/ppermute | solution.py:1795
  244.8 20.2 %collective-permute-start.40 = (bf16[512,1024]{1,0:T(8,128)(2,1)S(1)}, bf16[512,1024]{1,0:T(8,128)(2,1)S(1)}, u32[]{:S(2)}, u32[]{:S(2)}) collective-permute-start(bf16[512,1024]{1,0:T(8,128)(2,1)S(1)} %copy-done.23), channel_id=1, source_target_pairs={{0,1},{1,0},{2,3},{3,2},{4,5},{5,4},{6,7},{7,6},{8,9},{9,8},{10,11... | collective-permute-start | bytes 3145736 | tf_op jit(solution)/shard_map/ppermute | solution.py:1791
  244.8 20.8 %collective-permute-start.44 = (bf16[512,1024]{1,0:T(8,128)(2,1)}, bf16[512,1024]{1,0:T(8,128)(2,1)S(1)}, u32[]{:S(2)}, u32[]{:S(2)}) collective-permute-start(bf16[512,1024]{1,0:T(8,128)(2,1)} %get-tuple-element.299.refs_12_.refs_29_), channel_id=1, source_target_pairs={{0,1},{1,0},{2,3},{3,2},{4,5},{5,4},{6,7},{7,6},{8,9},{9,8},{10,11... | collective-permute-start | bytes 3145736 | tf_op jit(solution)/shard_map/ppermute | solution.py:1791
  245.3 20.3 %collective-permute-start.42 = (bf16[512,1024]{1,0:T(8,128)(2,1)S(1)}, bf16[512,1024]{1,0:T(8,128)(2,1)S(1)}, u32[]{:S(2)}, u32[]{:S(2)}) collective-permute-start(bf16[512,1024]{1,0:T(8,128)(2,1)S(1)} %get-tuple-element.300.refs_8_.refs_25_), channel_id=1, source_target_pairs={{0,1},{1,0},{2,3},{3,2},{4,5},{5,4},{6,7},{7,6},{8,9},{9,8},{10,11... | collective-permute-start | bytes 3145736 | tf_op jit(solution)/shard_map/ppermute | solution.py:1791
  245.3 20.8 %collective-permute-start.41 = (bf16[512,1024]{1,0:T(8,128)(2,1)S(1)}, bf16[512,1024]{1,0:T(8,128)(2,1)S(1)}, u32[]{:S(2)}, u32[]{:S(2)}) collective-permute-start(bf16[512,1024]{1,0:T(8,128)(2,1)S(1)} %get-tuple-element.306.refs_5_.refs_22_), channel_id=1, source_target_pairs={{0,1},{1,0},{2,3},{3,2},{4,5},{5,4},{6,7},{7,6},{8,9},{9,8},{10,11... | collective-permute-start | bytes 3145736 | tf_op jit(solution)/shard_map/ppermute | solution.py:1791
  404.4 25.8 %collective-permute-start.52 = (bf16[512,1024]{1,0:T(8,128)(2,1)}, bf16[512,1024]{1,0:T(8,128)(2,1)S(1)}, u32[]{:S(2)}, u32[]{:S(2)}) collective-permute-start(bf16[512,1024]{1,0:T(8,128)(2,1)} %get-tuple-element.332), channel_id=1, source_target_pairs={{0,2},{1,3},{2,0},{3,1},{4,6},{5,7},{6,4},{7,5},{8,10},{9,11},{10,... | collective-permute-start | bytes 3145736 | tf_op jit(solution)/shard_map/ppermute | solution.py:1787
  405.8 26.3 %collective-permute-start.53 = (bf16[512,1024]{1,0:T(8,128)(2,1)}, bf16[512,1024]{1,0:T(8,128)(2,1)S(1)}, u32[]{:S(2)}, u32[]{:S(2)}) collective-permute-start(bf16[512,1024]{1,0:T(8,128)(2,1)} %get-tuple-element.335), channel_id=1, source_target_pairs={{0,4},{4,0},{8,12},{12,8},{16,20},{20,16},{24,28},{28,24},{1,5},{5... | collective-permute-start | bytes 3145736 | tf_op jit(solution)/shard_map/ppermute | solution.py:1795
  419.4 34.4 %collective-permute-start.57 = (bf16[512,1024]{1,0:T(8,128)(2,1)}, bf16[512,1024]{1,0:T(8,128)(2,1)S(1)}, u32[]{:S(2)}, u32[]{:S(2)}) collective-permute-start(bf16[512,1024]{1,0:T(8,128)(2,1)} %get-tuple-element.348), channel_id=1, source_target_pairs={{0,4},{4,0},{8,12},{12,8},{16,20},{20,16},{24,28},{28,24},{1,5},{5... | collective-permute-start | bytes 3145736 | tf_op jit(solution)/shard_map/ppermute | solution.py:1795
  432.3 24.5 %collective-permute-start.58 = (bf16[256,1024]{1,0:T(8,128)(2,1)S(1)}, bf16[256,1024]{1,0:T(8,128)(2,1)S(1)}, u32[]{:S(2)}, u32[]{:S(2)}) collective-permute-start(bf16[256,1024]{1,0:T(8,128)(2,1)S(1)} %get-tuple-element.351), channel_id=1, source_target_pairs={{0,8},{4,12},{8,0},{12,4},{16,24},{20,28},{24,16},{28,20},{1,9},{5... | collective-permute-start | bytes 1572872 | tf_op jit(solution)/shard_map/ppermute | solution.py:1799
  447.3 20.1 %collective-permute-start.60 = (bf16[256,1024]{1,0:T(8,128)(2,1)S(1)}, bf16[256,1024]{1,0:T(8,128)(2,1)S(1)}, u32[]{:S(2)}, u32[]{:S(2)}) collective-permute-start(bf16[256,1024]{1,0:T(8,128)(2,1)S(1)} %get-tuple-element.356.refs_2_.refs_6_), channel_id=1, source_target_pairs={{0,2},{1,3},{2,0},{3,1},{4,6},{5,7},{6,4},{7,5},{8,10},{9,11},{10,... | collective-permute-start | bytes 1572872 | tf_op jit(solution)/shard_map/ppermute | solution.py:1787
  448.7 21.5 %collective-permute-start.61 = (bf16[256,1024]{1,0:T(8,128)(2,1)S(1)}, bf16[256,1024]{1,0:T(8,128)(2,1)S(1)}, u32[]{:S(2)}, u32[]{:S(2)}) collective-permute-start(bf16[256,1024]{1,0:T(8,128)(2,1)S(1)} %get-tuple-element.356.refs_2_.refs_6_), channel_id=1, source_target_pairs={{0,1},{1,0},{2,3},{3,2},{4,5},{5,4},{6,7},{7,6},{8,9},{9,8},{10,11... | collective-permute-start | bytes 1572872 | tf_op jit(solution)/shard_map/ppermute | solution.py:1791
  467.4 51.9 %collective-permute-start.66 = (bf16[512,1024]{1,0:T(8,128)(2,1)}, bf16[512,1024]{1,0:T(8,128)(2,1)}, u32[]{:S(2)}, u32[]{:S(2)}) collective-permute-start(bf16[512,1024]{1,0:T(8,128)(2,1)} %get-tuple-element.380), channel_id=1, source_target_pairs={{0,4},{4,0},{8,12},{12,8},{16,20},{20,16},{24,28},{28,24},{1,5},{5... | collective-permute-start | bytes 3145736 | tf_op jit(solution)/shard_map/ppermute | solution.py:1795
  468.1 48.9 %collective-permute-start.65 = (bf16[512,1024]{1,0:T(8,128)(2,1)}, bf16[512,1024]{1,0:T(8,128)(2,1)}, u32[]{:S(2)}, u32[]{:S(2)}) collective-permute-start(bf16[512,1024]{1,0:T(8,128)(2,1)} %get-tuple-element.377), channel_id=1, source_target_pairs={{0,4},{4,0},{8,12},{12,8},{16,20},{20,16},{24,28},{28,24},{1,5},{5... | collective-permute-start | bytes 3145736 | tf_op jit(solution)/shard_map/ppermute | solution.py:1795
  469.5 49.9 %collective-permute-start.67 = (bf16[512,1024]{1,0:T(8,128)(2,1)}, bf16[512,1024]{1,0:T(8,128)(2,1)}, u32[]{:S(2)}, u32[]{:S(2)}) collective-permute-start(bf16[512,1024]{1,0:T(8,128)(2,1)} %get-tuple-element.381), channel_id=1, source_target_pairs={{0,2},{1,3},{2,0},{3,1},{4,6},{5,7},{6,4},{7,5},{8,10},{9,11},{10,... | collective-permute-start | bytes 3145736 | tf_op jit(solution)/shard_map/ppermute | solution.py:1787
  497.6 47.4 %collective-permute-start.72 = (bf16[512,1024]{1,0:T(8,128)(2,1)}, bf16[512,1024]{1,0:T(8,128)(2,1)S(1)}, u32[]{:S(2)}, u32[]{:S(2)}) collective-permute-start(bf16[512,1024]{1,0:T(8,128)(2,1)} %get-tuple-element.399), channel_id=1, source_target_pairs={{0,4},{4,0},{8,12},{12,8},{16,20},{20,16},{24,28},{28,24},{1,5},{5... | collective-permute-start | bytes 3145736 | tf_op jit(solution)/shard_map/ppermute | solution.py:1795
  499.0 24.5 %collective-permute-start.68 = (bf16[256,1024]{1,0:T(8,128)(2,1)}, bf16[256,1024]{1,0:T(8,128)(2,1)}, u32[]{:S(2)}, u32[]{:S(2)}) collective-permute-start(bf16[256,1024]{1,0:T(8,128)(2,1)} %get-tuple-element.384), channel_id=1, source_target_pairs={{0,1},{1,0},{2,3},{3,2},{4,5},{5,4},{6,7},{7,6},{8,9},{9,8},{10,11... | collective-permute-start | bytes 1572872 | tf_op jit(solution)/shard_map/ppermute | solution.py:1791
  521.4 23.4 %collective-permute-start.71 = (bf16[256,1024]{1,0:T(8,128)(2,1)S(1)}, bf16[256,1024]{1,0:T(8,128)(2,1)S(1)}, u32[]{:S(2)}, u32[]{:S(2)}) collective-permute-start(bf16[256,1024]{1,0:T(8,128)(2,1)S(1)} %get-tuple-element.396), channel_id=1, source_target_pairs={{0,8},{4,12},{8,0},{12,4},{16,24},{20,28},{24,16},{28,20},{1,9},{5... | collective-permute-start | bytes 1572872 | tf_op jit(solution)/shard_map/ppermute | solution.py:1799
  523.5 52.4 %collective-permute-start.76 = (bf16[512,1024]{1,0:T(8,128)(2,1)S(1)}, bf16[512,1024]{1,0:T(8,128)(2,1)S(1)}, u32[]{:S(2)}, u32[]{:S(2)}) collective-permute-start(bf16[512,1024]{1,0:T(8,128)(2,1)S(1)} %copy-done.69), channel_id=1, source_target_pairs={{0,4},{4,0},{8,12},{12,8},{16,20},{20,16},{24,28},{28,24},{1,5},{5... | collective-permute-start | bytes 3145736 | tf_op jit(solution)/shard_map/ppermute | solution.py:1795
  545.2 30.6 %collective-permute-start.75 = (bf16[256,1024]{1,0:T(8,128)(2,1)S(1)}, bf16[256,1024]{1,0:T(8,128)(2,1)S(1)}, u32[]{:S(2)}, u32[]{:S(2)}) collective-permute-start(bf16[256,1024]{1,0:T(8,128)(2,1)S(1)} %get-tuple-element.418), channel_id=1, source_target_pairs={{0,8},{4,12},{8,0},{12,4},{16,24},{20,28},{24,16},{28,20},{1,9},{5... | collective-permute-start | bytes 1572872 | tf_op jit(solution)/shard_map/ppermute | solution.py:1799
  545.5 18.0 %collective-permute-start.73 = (bf16[128,1024]{1,0:T(8,128)(2,1)S(1)}, bf16[128,1024]{1,0:T(8,128)(2,1)S(1)}, u32[]{:S(2)}, u32[]{:S(2)}) collective-permute-start(bf16[128,1024]{1,0:T(8,128)(2,1)S(1)} %get-tuple-element.402), channel_id=1, source_target_pairs={{0,16},{4,20},{8,24},{12,28},{16,0},{20,4},{24,8},{28,12},{1,17},{... | collective-permute-start | bytes 786440 | tf_op jit(solution)/shard_map/ppermute | solution.py:1799
  548.2 22.9 %collective-permute-start.74 = (bf16[128,1024]{1,0:T(8,128)(2,1)S(1)}, bf16[128,1024]{1,0:T(8,128)(2,1)S(1)}, u32[]{:S(2)}, u32[]{:S(2)}) collective-permute-start(bf16[128,1024]{1,0:T(8,128)(2,1)S(1)} %get-tuple-element.410), channel_id=1, source_target_pairs={{0,16},{4,20},{8,24},{12,28},{16,0},{20,4},{24,8},{28,12},{1,17},{... | collective-permute-start | bytes 786440 | tf_op jit(solution)/shard_map/ppermute | solution.py:1799
  576.2 21.0 %collective-permute-start.78 = (bf16[256,1024]{1,0:T(8,128)(2,1)S(1)}, bf16[256,1024]{1,0:T(8,128)(2,1)S(1)}, u32[]{:S(2)}, u32[]{:S(2)}) collective-permute-start(bf16[256,1024]{1,0:T(8,128)(2,1)S(1)} %get-tuple-element.432), channel_id=1, source_target_pairs={{0,8},{4,12},{8,0},{12,4},{16,24},{20,28},{24,16},{28,20},{1,9},{5... | collective-permute-start | bytes 1572872 | tf_op jit(solution)/shard_map/ppermute | solution.py:1799
  (134 other events, 1769.8 us)

commit v4 on v3

--- a/solution.py
+++ b/solution.py
@@ -504,15 +504,11 @@
 
 
 weight_of = {
-    "global_heads": 13,
-    "global_ff": 12,
+    "forward_global": 170,
     "local_heads": 18,
     "local_ff": 34,
-    "local_back": 90,
-    "global_ff_back": 9,
-    "global_ff_grads": 5,
-    "global_heads_back": 12,
-    "global_heads_grads": 5,
+    "local_back": 81,
+    "backward_global": 90,
     "adam_update": 5,
 }
 
@@ -687,7 +683,18 @@
     return dot_rows(rows[:, :depth], near) + dot_rows(rows[:, depth:], far)
 
 
-def prep_body(source_ref, frames_ref, gains_ref, rows_ref, gains_out_ref, normed_ref):
+def held(shape):
+    return pl.BlockSpec(shape, lambda step: (0,) * len(shape), pipeline_mode=pl.Buffered(1))
+
+
+def by_cols(shape):
+    return pl.BlockSpec(shape, lambda step: (0, step))
+
+
+def prep_body(source_ref, frames_ref, gains_ref, *refs):
+    masters, (rows_ref, gains_out_ref, normed_ref), shards = refs[:6], refs[6:9], refs[9:]
+    for master_ref, shard_ref in zip(masters, shards):
+        shard_ref[...] = master_ref[0].astype(jnp.bfloat16)
     owned = frames_ref.shape[1] // source_ref.shape[0]
     for at in range(source_ref.shape[0]):
         here = slice(at * owned, (at + 1) * owned)
@@ -698,86 +705,34 @@
     )
 
 
-def prep(line, source, frames, gains):
-    return line.run(
+def prep(line, source, frames, gains, master):
+    owned, columns = master.shape[1], master.shape[2] // 3
+
+    def spec(layer, third):
+        return pl.BlockSpec((1, owned, columns), lambda step: (layer, 0, third))
+
+    shapes = [
+        shaped(frames.shape, jnp.bfloat16),
+        shaped(gains.shape, jnp.float32),
+        shaped(frames.shape, jnp.bfloat16),
+    ] + [shaped((owned, columns), jnp.bfloat16)] * 6
+    found = line.run(
         prep_body,
-        (source, frames, gains,),
-        in_specs=[IN_SMEM, VMEM_WHOLE, VMEM_WHOLE],
-        out_specs=[VMEM_WHOLE] * 3,
-        out_shape=[
-            shaped(frames.shape, jnp.bfloat16),
-            shaped(gains.shape, jnp.float32),
-            shaped(frames.shape, jnp.bfloat16),
-        ],
-        limit=(16),
+        (source, frames, gains) + (master,) * 6,
+        grid=(1,),
+        in_specs=[IN_SMEM, held(frames.shape), held(gains.shape)]
+        + [spec(layer, third) for layer in range(2) for third in range(3)],
+        out_specs=[held(one.shape) for one in shapes],
+        out_shape=shapes,
+        limit=24,
         name="prep_rows",
     )
-
-
-def merge_body(which, base_ref, one_ref, two_ref, three_ref, gains_ref, middle_ref, normed_ref=None):
-    total = base_ref[...].astype(jnp.float32)
-    for ref in (one_ref, two_ref, three_ref):
-        total = total + ref[...].astype(jnp.float32)
-    middle_ref[...] = total
-    if normed_ref is not None:
-        normed_ref[...] = norm_rows(total, gains_ref[which : which + 1, :]).astype(jnp.bfloat16)
-
-
-def merge(line, base, terms, gains, which, normed=True):
-    outs = [shaped(base.shape, jnp.float32)]
-    if normed:
-        outs.append(shaped(base.shape, jnp.bfloat16))
-    return line.run(
-        lambda *refs: merge_body(which, *refs),
-        (base, *terms, gains,),
-        in_specs=[VMEM_WHOLE] * 5,
-        out_specs=[VMEM_WHOLE] * len(outs),
-        out_shape=outs,
-        limit=(16),
-        name="merge_rows",
-    )
-
-
-def merge_back_body(
-    which, rows_ref, one_ref, two_ref, three_ref, grad_ref, gains_ref, total_ref, small_ref, gain_ref
-):
-    grad = one_ref[...].astype(jnp.float32)
-    for ref in (two_ref, three_ref):
-        grad = grad + ref[...].astype(jnp.float32)
-    part, gain_grad = norm_rows_back(
-        rows_ref[...].astype(jnp.float32), gains_ref[which : which + 1, :], grad
-    )
-    total = grad_ref[...] + part
-    total_ref[...] = total
-    small_ref[...] = total.astype(jnp.bfloat16)
-    gain_ref[...] = gain_grad
-
-
-def merge_back(line, rows, terms, grad, gains, which):
-    return line.run(
-        lambda *refs: merge_back_body(which, *refs),
-        (rows, *terms, grad, gains,),
-        in_specs=[VMEM_WHOLE] * 6,
-        out_specs=[VMEM_WHOLE] * 3,
-        out_shape=[
-            shaped(rows.shape, jnp.float32),
-            shaped(rows.shape, jnp.bfloat16),
-            shaped((1, rows.shape[1]), jnp.float32),
-        ],
-        limit=(16),
-        name="merge_rows_back",
-    )
-
-
-def finish_body(
-    source_ref, rows_ref, one_ref, two_ref, three_ref, grad_ref, gains_ref, gb_ref, gc_ref, gd_ref,
-    out_ref, gain_ref,
-):
-    grad = one_ref[...].astype(jnp.float32)
-    for ref in (two_ref, three_ref):
-        grad = grad + ref[...].astype(jnp.float32)
-    part, gain_grad = norm_rows_back(rows_ref[...].astype(jnp.float32), gains_ref[0:1, :], grad)
-    total = grad_ref[...] + part
+    return found[:3], found[3:]
+
+
+def finish_body(source_ref, rows_ref, sum_ref, grad_ref, gains_ref, gb_ref, gc_ref, gd_ref, out_ref, gain_ref):
+    back, gain_grad = norm_rows_back(rows_ref[...].astype(jnp.float32), gains_ref[0:1, :], sum_ref[...])
+    total = grad_ref[...] + back
     owned = out_ref.shape[1] // source_ref.shape[0]
     for at in range(source_ref.shape[0]):
         here = slice(at * owned, (at + 1) * owned)
@@ -789,42 +744,121 @@
         gain_ref[3:4, there] = gd_ref[:, here]
 
 
-def finish(line, source, rows, terms, grad, gains, others):
+def finish(line, source, rows, total, grad, gains, others):
     return line.run(
         finish_body,
-        (source, rows, *terms, grad, gains, *others,),
-        in_specs=[IN_SMEM] + [VMEM_WHOLE] * 9,
+        (source, rows, total, grad, gains, *others),
+        in_specs=[IN_SMEM] + [VMEM_WHOLE] * 7,
         out_specs=[VMEM_WHOLE] * 2,
         out_shape=[shaped(rows.shape, jnp.float32), shaped((4, rows.shape[1]), jnp.float32)],
-        limit=(16),
+        limit=16,
         name="input_grad",
     )
 
 
-def global_heads_body(
-    info_ref, x0, x1, x2, x3, near_ref, far_ref, qkv_ref, mixed_ref, lse_ref, p0, p1, p2, p3, acc, lse_wide
+def forward_body(
+    info_ref, rows_ref, normed_ref, gains_ref, ga_s, gu_s, gd_s, la_s, lu_s, ld_s,
+    ga, gu, gd, la, lu, ld, qkv_ref, mixed_ref, lse_ref, middle_ref, out_ref, na_h, nb_h, active_h, slope_h,
+    na, nb, a_v, u_v, d_v, acc, lse_wide, act, slp, parts, met_core, met_x, sends_x, sems, send, recv,
 ):
-    share = x0.shape[0]
+    share = rows_ref.shape[0]
+    owned = ga_s.shape[0]
+    half = D // 2
+    width = mixed_ref.shape[1]
     span = 4 * share
-    width = mixed_ref.shape[1]
     length = info_ref[1]
     scale = HD ** (-0.5)
-    for rel, x_ref in enumerate((x0, x1, x2, x3)):
+    flying, filed, from_parts, numbers = [], [], [], []
+
+    def fly(hop, source, target):
+        at = len(numbers)
+        copy = to_partner(hop, source, target, send.at[at], recv.at[at])
+        copy.start()
+        numbers.append(at)
+        flying.append(copy)
+        return copy
+
+    def file(source, target):
+        copy = pltpu.make_async_copy(source, target, sems.at[len(filed)])
+        copy.start()
+        filed.append(copy)
+        return copy
+
+    def first(shard, whole):
+        return fly("z2", shard, whole.at[pl.ds(owned, owned)])
+
+    def second(whole, begin=0):
+        return fly("z1", whole.at[pl.ds(begin, 2 * owned)], whole.at[pl.ds(begin + 2 * owned, 2 * owned)])
+
+    def across(whole):
+        return fly("y", whole.at[pl.ds(0, half)], whole.at[pl.ds(half, half)])
+
+    def over(hop, stack, begin, to, rows=half, start=0):
+        here = pl.ds(start, rows)
+        return fly(hop, stack.at[begin, here], stack.at[to, here])
+
+    greet(("core", "x", "y", "z1", "z2"))
+    ga_2 = first(ga_s, ga)
+    normed_x = fly("x", normed_ref, na.at[pl.ds(2 * share, share)])
+    normed_core = fly("core", normed_ref, na.at[pl.ds(share, share)])
+    ld_x = fly("x", ld_s, ld.at[2, pl.ds(0, owned)])
+    ld_y = fly("y", ld_s, ld.at[0, pl.ds(half, owned)])
+    la_2 = first(la_s, la.at[0])
+    own = [
+        file(shard, whole.at[pl.ds(0, owned)])
+        for shard, whole in ((ga_s, ga), (la_s, la.at[0]), (gu_s, gu), (gd_s, gd), (lu_s, lu.at[0]), (ld_s, ld.at[0]))
+    ]
+    na[pl.ds(0, share), :] = normed_ref[...]
+    for one in own:
+        one.wait()
+    ga_2.wait_recv()
+    ga_1 = second(ga)
+    gu_2 = first(gu_s, gu)
+    normed_x.wait_recv()
+    normed_xc = fly("core", na.at[pl.ds(2 * share, share)], na.at[pl.ds(3 * share, share)])
+    ld_x.wait_recv()
+    ld_xy = fly("y", ld.at[2, pl.ds(0, owned)], ld.at[2, pl.ds(half, owned)])
+    la_2.wait_recv()
+    la_1 = second(la.at[0])
+    gd_2 = first(gd_s, gd)
+    ga_1.wait_recv()
+    ga_y = across(ga)
+    a_near = file(ga.at[pl.ds(0, half)], a_v.at[pl.ds(0, half)])
+    gu_2.wait_recv()
+    gu_1 = second(gu)
+    lu_2 = first(lu_s, lu.at[0])
+    la_1.wait_recv()
+    la_x = over("x", la, 0, 2)
+    la_y = across(la.at[0])
+    la_c = over("core", la, 0, 1)
+    gd_2.wait_recv()
+    gd_1 = second(gd)
+    gu_1.wait_recv()
+    gu_y = across(gu)
+    u_near = file(gu.at[pl.ds(0, half)], u_v.at[pl.ds(0, half)])
+    normed_core.wait_recv()
+    normed_xc.wait_recv()
+    ga_y.wait_recv()
+    a_far = file(ga.at[pl.ds(half, half)], a_v.at[pl.ds(half, half)])
+    na_out = file(na, na_h)
+    a_near.wait()
+    a_far.wait()
+
+    for rel in range(4):
         at = pl.ds(pl.multiple_of(group_at(rel) * share, share), share)
-        full = both(x_ref[...], near_ref[:, : 3 * width], far_ref[:, : 3 * width])
+        full = both(na[rel * share : (rel + 1) * share, :], a_v[:half, : 3 * width], a_v[half:, : 3 * width])
         qkv_ref[at, :] = full.astype(jnp.bfloat16)
-    acc[...] = jnp.zeros_like(acc)
+    acc[:, :width] = jnp.zeros((span, width), jnp.float32)
     lse_wide[...] = jnp.zeros_like(lse_wide)
     head_of = lax.broadcasted_iota(jnp.int32, (1, width), 1) // HD
     lane = lax.broadcasted_iota(jnp.int32, (1, 128), 1)
 
-    @pl.loop(0, width // HD)
     def per_head(head):
-        own = head_of == head
+        own_lanes = head_of == head
         for block in range(4):
             rows = slice(block * share, (block + 1) * share)
             reach = (block + 1) * share
-            query = jnp.where(own, qkv_ref[rows, :width] * scale, 0.0).astype(jnp.bfloat16)
+            query = jnp.where(own_lanes, qkv_ref[rows, :width] * scale, 0.0).astype(jnp.bfloat16)
             scores = dot_transposed(query, qkv_ref[:reach, width : 2 * width])
             row_at = block * share + lax.broadcasted_iota(jnp.int32, scores.shape, 0)
             col_at = lax.broadcasted_iota(jnp.int32, scores.shape, 1)
@@ -833,271 +867,498 @@
             expanded = jnp.exp(scores - top)
             total = jnp.sum(expanded, axis=-1, keepdims=True)
             prob = (expanded * (1.0 / total)).astype(jnp.bfloat16)
-            value = jnp.where(own, qkv_ref[:reach, 2 * width :], 0.0).astype(jnp.bfloat16)
-            acc[rows, :] += dot_rows(prob, value)
+            value = jnp.where(own_lanes, qkv_ref[:reach, 2 * width :], 0.0).astype(jnp.bfloat16)
+            acc[rows, :width] += dot_rows(prob, value)
             lse_wide[rows, :] = jnp.where(lane == head, top + jnp.log(total), lse_wide[rows, :])
 
-    mixed_ref[...] = acc[...].astype(jnp.bfloat16)
+    heads = width // HD
+    pl.loop(0, heads // 2)(per_head)
+    gd_1.wait_recv()
+    gd_y = across(gd)
+    d_near = file(gd.at[pl.ds(0, half)], d_v.at[pl.ds(0, half)])
+    lu_2.wait_recv()
+    lu_1 = second(lu.at[0])
+    ld_y.wait_recv()
+    ld_xy.wait_recv()
+    ld_blocks = [(index, begin) for index in (0, 2) for begin in (0, half)]
+
+    def ld_first(index, begin):
+        return fly("z2", ld.at[index, pl.ds(begin, owned)], ld.at[index, pl.ds(begin + owned, owned)])
+
+    ld_2 = [ld_first(*ld_blocks[0]), ld_first(*ld_blocks[1])]
+    pl.loop(heads // 2, heads)(per_head)
+    mixed_ref[...] = acc[:, :width].astype(jnp.bfloat16)
     lse_ref[...] = jnp.transpose(lse_wide[...])[: lse_ref.shape[0], :]
-    half = near_ref.shape[0]
-    for rel, p_ref in enumerate((p0, p1, p2, p3)):
+
+    def out_part(rel):
         at = pl.ds(pl.multiple_of(group_at(rel) * share, share), share)
         rows = mixed_ref[at, :]
-        p_ref[:, :half] = dot_transposed(rows, near_ref[:, 3 * width :]).astype(jnp.bfloat16)
-        p_ref[:, half:] = dot_transposed(rows, far_ref[:, 3 * width :]).astype(jnp.bfloat16)
-
-
-def global_heads(line, info, rows, halves):
-    share, width = rows[0].shape[0], halves[0].shape[1] // 4
+        parts[rel, :, :half] = dot_transposed(rows, a_v[:half, 3 * width :]).astype(jnp.bfloat16)
+        parts[rel, :, half:] = dot_transposed(rows, a_v[half:, 3 * width :]).astype(jnp.bfloat16)
+
+    strip = share // 2
+    strips = [pl.ds(at * strip, strip) for at in range(2)]
+
+    def scatter(which, fill):
+        fill(3)
+        from_far = [fly("core", parts.at[3, rows], met_core.at[2 * which, rows]) for rows in strips]
+        fill(2)
+        fill(1)
+        from_near = fly("core", parts.at[1], met_core.at[2 * which + 1])
+        from_parts.extend(from_far + [from_near])
+        fill(0)
+        from_x = []
+        for rows, one in zip(strips, from_far):
+            one.wait_recv()
+            total = parts[2, rows, :].astype(jnp.float32) + met_core[2 * which, rows, :].astype(jnp.float32)
+            sends_x[which, rows, :] = total.astype(jnp.bfloat16)
+            from_x.append(fly("x", sends_x.at[which, rows], met_x.at[which, rows]))
+        from_near.wait_recv()
+        return from_x
+
+    def gathered(which, rows, base):
+        return (
+            base
+            + parts[0, rows, :].astype(jnp.float32)
+            + met_core[2 * which + 1, rows, :].astype(jnp.float32)
+            + met_x[which, rows, :].astype(jnp.float32)
+        )
+
+    from_x = scatter(0, out_part)
+    over_x = []
+    for rows, one in zip(strips, from_x):
+        one.wait_recv()
+        total = gathered(0, rows, rows_ref[rows, :].astype(jnp.float32))
+        middle_ref[rows, :] = total
+        nb[rows, :] = norm_rows(total, gains_ref[1:2, :]).astype(jnp.bfloat16)
+        over_x.append(fly("x", nb.at[rows], nb.at[pl.ds(2 * share + rows.start, strip)]))
+    normed_core = fly("core", nb.at[pl.ds(0, share)], nb.at[pl.ds(share, share)])
+    la_y.wait_recv()
+    la_fx = over("x", la, 0, 2, start=half)
+    la_fc = over("core", la, 0, 1, start=half)
+    la_x.wait_recv()
+    la_xc = over("core", la, 2, 3)
+    lu_1.wait_recv()
+    lu_x = over("x", lu, 0, 2)
+    lu_y = across(lu.at[0])
+    lu_c = over("core", lu, 0, 1)
+    ld_1 = []
+    for at in range(2):
+        ld_2[at].wait_recv()
+        index, begin = ld_blocks[at]
+        ld_1.append(second(ld.at[index], begin))
+        ld_2.append(ld_first(*ld_blocks[2 + at]))
+    for one in over_x:
+        one.wait_recv()
+    normed_xc = fly("core", nb.at[pl.ds(2 * share, share)], nb.at[pl.ds(3 * share, share)])
+    gu_y.wait_recv()
+    u_far = file(gu.at[pl.ds(half, half)], u_v.at[pl.ds(half, half)])
+    acc[...] = jnp.zeros_like(acc)
+    normed_core.wait_recv()
+    normed_xc.wait_recv()
+    nb_out = file(nb, nb_h)
+    gd_y.wait_recv()
+    d_far = file(gd.at[pl.ds(half, half)], d_v.at[pl.ds(half, half)])
+    for one in (u_near, u_far, d_near, d_far):
+        one.wait()
+    tile = 256
+    hidden_out = []
+    for at in range(u_v.shape[1] // tile):
+        lanes = slice(at * tile, (at + 1) * tile)
+        active, slope = gelu_both(both(nb[...], u_v[:half, lanes], u_v[half:, lanes]))
+        act[:, lanes] = active
+        slp[:, lanes] = slope
+        for side in range(2):
+            cols_at = slice(side * half, (side + 1) * half)
+            acc[:, cols_at] += dot_transposed(active, d_v[side * half : (side + 1) * half, lanes])
+        if at == 1:
+            for which in (2, 3):
+                ld_2[which].wait_recv()
+                index, begin = ld_blocks[which]
+                ld_1.append(second(ld.at[index], begin))
+    hidden_out = [file(act, active_h), file(slp, slope_h)]
+
+    def down_part(rel):
+        parts[rel] = acc[rel * share : (rel + 1) * share, :].astype(jnp.bfloat16)
+
+    for one in from_parts:
+        one.wait_send()
+        flying[:] = [other for other in flying if other is not one]
+    from_x = scatter(1, down_part)
+    la_fx.wait_recv()
+    la_fxc = over("core", la, 2, 3, start=half)
+    lu_x.wait_recv()
+    lu_xy = across(lu.at[2])
+    lu_xc = over("core", lu, 2, 3)
+    for rows, one in zip(strips, from_x):
+        one.wait_recv()
+        out_ref[rows, :] = gathered(1, rows, middle_ref[rows, :])
+    lu_y.wait_recv()
+    lu_fc = over("core", lu, 0, 1, start=half)
+    for one in ld_1[:2]:
+        one.wait_recv()
+    ld_c = over("core", ld, 0, 1, rows=D)
+    for one in ld_1[2:]:
+        one.wait_recv()
+    ld_xc = over("core", ld, 2, 3, rows=D)
+    lu_xy.wait_recv()
+    lu_fxc = over("core", lu, 2, 3, start=half)
+    for one in (la_c, la_fc, la_xc, la_fxc, lu_c, lu_fc, lu_xc, lu_fxc, ld_c, ld_xc):
+        one.wait_recv()
+    for one in [na_out, nb_out] + hidden_out:
+        one.wait()
+    for one in flying:
+        one.wait_send()
+
+
+def forward_global(line, info, rows, normed, gains, shards):
+    share, owned = rows.shape[0], shards[0].shape[0]
+    span, columns = 4 * share, shards[0].shape[1]
+    width = columns // 4
+    small = jnp.bfloat16
+    weights = [shaped((D, columns), small)] * 3 + [shaped((4, D, columns), small)] * 3
+    return line.run(
+        forward_body,
+        (info, rows, normed, gains, *shards),
+        in_specs=[IN_SMEM] + [VMEM_WHOLE] * 3 + [IN_HBM] * 6,
+        out_specs=[IN_HBM] * 6 + [VMEM_WHOLE] * 5 + [IN_HBM] * 4,
+        out_shape=weights
+        + [
+            shaped((span, 3 * width), small),
+            shaped((span, width), small),
+            shaped((8, span), jnp.float32),
+            shaped((share, D), jnp.float32),
+            shaped((share, D), jnp.float32),
+            shaped((span, D), small),
+            shaped((span, D), small),
+            shaped((span, columns), small),
+            shaped((span, columns), small),
+        ],
+        scratch_shapes=[
+            pltpu.VMEM((span, D), small),
+            pltpu.VMEM((span, D), small),
+            pltpu.VMEM((D, columns), small),
+            pltpu.VMEM((D, columns), small),
+            pltpu.VMEM((D, columns), small),
+            pltpu.VMEM((span, D), jnp.float32),
+            pltpu.VMEM((span, 128), jnp.float32),
+            pltpu.VMEM((span, columns), small),
+            pltpu.VMEM((span, columns), small),
+            pltpu.VMEM((4, share, D), small),
+            pltpu.VMEM((4, share, D), small),
+            pltpu.VMEM((2, share, D), small),
+            pltpu.VMEM((2, share, D), small),
+            pltpu.SemaphoreType.DMA((20,)),
+            pltpu.SemaphoreType.DMA((64,)),
+            pltpu.SemaphoreType.DMA((64,)),
+        ],
+        hops=("core", "x", "y", "z1", "z2"),
+        limit=56,
+        name="forward_global",
+    )
+
+
+def backward_body(
+    info_ref, small_ref, grad_ref, middle_ref, gains_ref, lse_ref, up_h, down_h, heads_h, active_h, slope_h,
+    nb_h, na_h, qkv_h, mixed_h, u_near_h, u_far_h, d2_h, d0_h, h2_far_h, h0_far_h,
+    mid_ref, sum_ref, gain_ref, gd_near_h, gd_met_h, gu_near_h, gu_far_h, gh_near_h, gh_far_h, lu_keep_h,
+    lu_met_h, ld_keep_h, ld_met_h, h2_met_h, h0_met_h,
+    rows_one, rows_two, up_v, down_v, heads_v, act, slp, dup, left_t, right_v, grads_v, qkv_v, mixed_v, dqkv,
+    dmix, dq_t, dk_acc, dv_acc, center, k_t, parts, met_core, met_x, sends_x, u_v, u_met, d_v, d_met, z_met,
+    sems, send, recv,
+):
+    share = small_ref.shape[0]
+    half = D // 2
+    quarter = half // 2
+    owned = quarter // 2
+    width = mixed_v.shape[1]
+    heads = width // HD
     span = 4 * share
-    return line.run(
-        global_heads_body,
-        (info, *rows, *halves,),
-        in_specs=[IN_SMEM] + [VMEM_WHOLE] * 6,
-        out_specs=[VMEM_WHOLE] * 7,
-        out_shape=[
-            shaped((span, 3 * width), jnp.bfloat16),
-            shaped((span, width), jnp.bfloat16),
-            shaped((8, span), jnp.float32),
-        ]
-        + [shaped((share, D), jnp.bfloat16)] * 4,
-        scratch_shapes=[pltpu.VMEM((span, width), jnp.float32), pltpu.VMEM((span, 128), jnp.float32)],
-        limit=(40),
-        name="global_heads",
-    )
-
-
-def global_heads_back_body(
-    info_ref, g0, g1, g2, g3, near_ref, far_ref, qkv_ref, mixed_ref, lse_ref, dqkv_ref, p0, p1, p2, p3,
-    dmix, dq_t, dk_acc, dv_acc, center, k_t,
-):
-    share = g0.shape[0]
-    width = mixed_ref.shape[1]
-    heads = width // HD
     length = info_ref[1]
     scale = HD ** (-0.5)
-    for rel, g_ref in enumerate((g0, g1, g2, g3)):
-        at = pl.ds(pl.multiple_of(group_at(rel) * share, share), share)
-        full = both(g_ref[...], near_ref[:, 3 * width :], far_ref[:, 3 * width :])
-        dmix[at, :] = full.astype(jnp.bfloat16)
+    numbers, flying, filed = [], [], []
+
+    def fly(hop, source, target):
+        at = len(numbers)
+        copy = to_partner(hop, source, target, send.at[at], recv.at[at])
+        copy.start()
+        numbers.append(at)
+        flying.append(copy)
+        return copy
+
+    def over(copy):
+        copy.wait_send()
+        flying[:] = [other for other in flying if other is not copy]
+
+    def file(source, target):
+        copy = pltpu.make_async_copy(source, target, sems.at[len(filed)])
+        copy.start()
+        filed.append(copy)
+        return copy
+
+    def block(rel):
+        return slice(rel * share, (rel + 1) * share)
+
+    def place(rel):
+        return pl.ds(pl.multiple_of(group_at(rel) * share, share), share)
+
+    def summed(*terms):
+        total = terms[0].astype(jnp.float32)
+        for term in terms[1:]:
+            total = total + term.astype(jnp.float32)
+        return total
+
+    greet(("core", "x", "y", "z1", "z2"))
+    small_x = fly("x", small_ref, rows_one.at[pl.ds(2 * share, share)])
+    small_core = fly("core", small_ref, rows_one.at[pl.ds(share, share)])
+    u_y = fly("y", u_far_h, u_met)
+    d_first = fly("x", d2_h.at[pl.ds(0, quarter)], d_met.at[pl.ds(0, quarter)])
+    h2_y = fly("y", h2_far_h, h2_met_h)
+    h0_y = fly("y", h0_far_h, h0_met_h)
+    first = [file(down_h, down_v), file(slope_h, slp), file(up_h, up_v)]
+    active_in = file(active_h, act)
+    nb_in = file(nb_h, right_v)
+    u_in = file(u_near_h, u_v)
+    attention_in = [file(heads_h, heads_v), file(qkv_h, qkv_v), file(mixed_h, mixed_v)]
+    d_in = file(d0_h, d_v)
+    rows_one[pl.ds(0, share), :] = small_ref[...]
+    for one in first:
+        one.wait()
+
+    def ff_back(rel):
+        rows = block(rel)
+        for tile in range(2):
+            lanes = slice(tile * half, (tile + 1) * half)
+            grad = both(rows_one[rows, :], down_v[:half, lanes], down_v[half:, lanes])
+            dup[rows, lanes] = (grad * slp[rows, lanes].astype(jnp.float32)).astype(jnp.bfloat16)
+        for side in range(2):
+            lanes = slice(side * half, (side + 1) * half)
+            parts[rel, :, lanes] = dot_transposed(dup[rows, :], up_v[lanes, :]).astype(jnp.bfloat16)
+
+    ff_back(0)
+    small_core.wait_recv()
+    ff_back(1)
+    small_x.wait_recv()
+    small_xc = fly("core", rows_one.at[pl.ds(2 * share, share)], rows_one.at[pl.ds(3 * share, share)])
+    ff_back(2)
+    small_xc.wait_recv()
+    ff_back(3)
+    strip = share // 2
+    strips = [pl.ds(at * strip, strip) for at in range(2)]
+
+    def scatter_start(which):
+        from_far = [fly("core", parts.at[3, rows], met_core.at[2 * which, rows]) for rows in strips]
+        return from_far, fly("core", parts.at[1], met_core.at[2 * which + 1])
+
+    def scatter_on(which, from_far):
+        from_x = []
+        for rows, one in zip(strips, from_far):
+            one.wait_recv()
+            sends_x[which, rows, :] = summed(parts[2, rows, :], met_core[2 * which, rows, :]).astype(jnp.bfloat16)
+            from_x.append(fly("x", sends_x.at[which, rows], met_x.at[which, rows]))
+        return from_x
+
+    def gathered(which, rows):
+        return summed(parts[0, rows, :], met_core[2 * which + 1, rows, :], met_x[which, rows, :])
+
+    from_far, from_near = scatter_start(0)
+    for rel in range(4):
+        left_t[:, block(rel)] = jnp.transpose(rows_one[block(rel), :])
+    from_x = scatter_on(0, from_far)
+    active_in.wait()
+    for side in range(2):
+        rows = slice(side * half, (side + 1) * half)
+        for tile in range(2):
+            lanes = slice(tile * half, (tile + 1) * half)
+            grads_v[0, rows, lanes] = dot_rows(left_t[rows, :], act[:, lanes]).astype(jnp.bfloat16)
+    gd_y = fly("y", grads_v.at[0, pl.ds(half, half)], gd_met_h)
+    results = [file(grads_v.at[0, pl.ds(0, half)], gd_near_h)]
+    from_near.wait_recv()
+    gain_total = jnp.zeros((1, D), jnp.float32)
+    over_x = []
+    for rows, one in zip(strips, from_x):
+        one.wait_recv()
+        back, gain_grad = norm_rows_back(middle_ref[rows, :], gains_ref[1:2, :], gathered(0, rows))
+        total = grad_ref[rows, :] + back
+        mid_ref[rows, :] = total
+        rows_two[rows, :] = total.astype(jnp.bfloat16)
+        gain_total = gain_total + gain_grad
+        over_x.append(fly("x", rows_two.at[rows], rows_two.at[pl.ds(2 * share + rows.start, strip)]))
+    gain_ref[...] = gain_total
+    small_core = fly("core", rows_two.at[pl.ds(0, share)], rows_two.at[pl.ds(share, share)])
+    d_second = fly("x", d2_h.at[pl.ds(quarter, quarter)], d_met.at[pl.ds(quarter, quarter)])
+    u_y.wait_recv()
+    u_in.wait()
+    u_v[...] = summed(u_v[...], u_met[...]).astype(jnp.bfloat16)
+    u_1 = fly("z1", u_v.at[pl.ds(quarter, quarter)], z_met.at[0])
+    nb_in.wait()
+    left_t[...] = jnp.transpose(right_v[...])
+    na_in = file(na_h, right_v)
+    for side in range(2):
+        rows = slice(side * half, (side + 1) * half)
+        for tile in range(2):
+            lanes = slice(tile * half, (tile + 1) * half)
+            grads_v[1, rows, lanes] = dot_rows(left_t[rows, :], dup[:, lanes]).astype(jnp.bfloat16)
+    results += [
+        file(grads_v.at[1, pl.ds(0, half)], gu_near_h),
+        file(grads_v.at[1, pl.ds(half, half)], gu_far_h),
+    ]
+    for one in attention_in:
+        one.wait()
+
+    def mix_back(rel):
+        full = both(rows_two[block(rel), :], heads_v[:half, 3 * width :], heads_v[half:, 3 * width :])
+        dmix[place(rel), :] = full.astype(jnp.bfloat16)
+
     head_of = lax.broadcasted_iota(jnp.int32, (1, width), 1) // HD
     pick = (
         lax.broadcasted_iota(jnp.int32, (8, width), 1) // HD
         == lax.broadcasted_iota(jnp.int32, (8, width), 0)
     ).astype(jnp.bfloat16)
-    product = dmix[...].astype(jnp.float32) * mixed_ref[...].astype(jnp.float32)
+    k_t[...] = jnp.transpose(qkv_v[:, width : 2 * width])
+    dq_t[...] = jnp.zeros_like(dq_t)
+    dk_acc[...] = jnp.zeros_like(dk_acc)
+    dv_acc[...] = jnp.zeros_like(dv_acc)
+    mix_back(0)
+    small_core.wait_recv()
+    mix_back(1)
+    for one in over_x:
+        one.wait_recv()
+    small_xc = fly("core", rows_two.at[pl.ds(2 * share, share)], rows_two.at[pl.ds(3 * share, share)])
+    mix_back(2)
+    u_1.wait_recv()
+    u_v[:quarter, :] = summed(u_v[:quarter, :], z_met[0]).astype(jnp.bfloat16)
+    u_2 = fly("z2", u_v.at[pl.ds(owned, owned)], lu_met_h)
+    results.append(file(u_v.at[pl.ds(0, owned)], lu_keep_h))
+    small_xc.wait_recv()
+    mix_back(3)
+    product = dmix[...].astype(jnp.float32) * mixed_v[...].astype(jnp.float32)
     high = product.astype(jnp.bfloat16)
     low = (product - high.astype(jnp.float32)).astype(jnp.bfloat16)
     center[...] = dot_transposed(pick, high) + dot_transposed(pick, low)
-    k_t[...] = jnp.transpose(qkv_ref[:, width : 2 * width])
-    dq_t[...] = jnp.zeros_like(dq_t)
-    dk_acc[...] = jnp.zeros_like(dk_acc)
-    dv_acc[...] = jnp.zeros_like(dv_acc)
     for head in range(heads):
-        own = head_of == head
-        for block in range(4):
-            rows = slice(block * share, (block + 1) * share)
-            reach = (block + 1) * share
-            query = jnp.where(own, qkv_ref[rows, :width] * scale, 0.0).astype(jnp.bfloat16)
-            grad = jnp.where(own, dmix[rows, :], 0.0).astype(jnp.bfloat16)
-            scores = dot_transposed(qkv_ref[:reach, width : 2 * width], query)
+        own_lanes = head_of == head
+        for at in range(4):
+            rows = block(at)
+            reach = (at + 1) * share
+            query = jnp.where(own_lanes, qkv_v[rows, :width] * scale, 0.0).astype(jnp.bfloat16)
+            grad = jnp.where(own_lanes, dmix[rows, :], 0.0).astype(jnp.bfloat16)
+            scores = dot_transposed(qkv_v[:reach, width : 2 * width], query)
             key_at = lax.broadcasted_iota(jnp.int32, scores.shape, 0)
-            row_at = block * share + lax.broadcasted_iota(jnp.int32, scores.shape, 1)
+            row_at = at * share + lax.broadcasted_iota(jnp.int32, scores.shape, 1)
             prob = jnp.where(
                 (key_at <= row_at) & (key_at < length),
                 jnp.exp(scores - lse_ref[head : head + 1, rows]),
                 0.0,
             )
-            dprob = dot_transposed(qkv_ref[:reach, 2 * width :], grad)
+            dprob = dot_transposed(qkv_v[:reach, 2 * width :], grad)
             dscore = (prob * (dprob - center[head : head + 1, rows])).astype(jnp.bfloat16)
             dv_acc[:reach, :] += dot_rows(prob.astype(jnp.bfloat16), grad)
             dk_acc[:reach, :] += dot_rows(dscore, query)
             lanes = slice(head * HD, (head + 1) * HD)
             dq_t[lanes, rows] += dot_rows(k_t[lanes, :reach], dscore)
-    dqkv_ref[:, :width] = (jnp.transpose(dq_t[...]) * scale).astype(jnp.bfloat16)
-    dqkv_ref[:, width : 2 * width] = dk_acc[...].astype(jnp.bfloat16)
-    dqkv_ref[:, 2 * width :] = dv_acc[...].astype(jnp.bfloat16)
-    half = near_ref.shape[0]
-    for rel, p_ref in enumerate((p0, p1, p2, p3)):
-        at = pl.ds(pl.multiple_of(group_at(rel) * share, share), share)
-        rows = dqkv_ref[at, :]
-        p_ref[:, :half] = dot_transposed(rows, near_ref[:, : 3 * width]).astype(jnp.bfloat16)
-        p_ref[:, half:] = dot_transposed(rows, far_ref[:, : 3 * width]).astype(jnp.bfloat16)
-
-
-def global_heads_back(line, info, grads, halves, qkv, mixed, lse):
-    share, width = grads[0].shape[0], mixed.shape[1]
-    span = 4 * share
+    dqkv[:, :width] = (jnp.transpose(dq_t[...]) * scale).astype(jnp.bfloat16)
+    dqkv[:, width : 2 * width] = dk_acc[...].astype(jnp.bfloat16)
+    dqkv[:, 2 * width :] = dv_acc[...].astype(jnp.bfloat16)
+    d_in.wait()
+    d_first.wait_recv()
+    d_second.wait_recv()
+    d_v[...] = summed(d_v[...], d_met[...]).astype(jnp.bfloat16)
+    d_1 = fly("z1", d_v.at[pl.ds(quarter, quarter)], z_met.at[1])
+    for one in from_far + [from_near]:
+        over(one)
+
+    def back_part(rel):
+        rows = dqkv[place(rel), :]
+        for side in range(2):
+            lanes = slice(side * half, (side + 1) * half)
+            parts[rel, :, lanes] = dot_transposed(rows, heads_v[lanes, : 3 * width]).astype(jnp.bfloat16)
+
+    back_part(3)
+    back_part(1)
+    from_far, from_near = scatter_start(1)
+    back_part(2)
+    from_x = scatter_on(1, from_far)
+    back_part(0)
+    na_in.wait()
+    for rel in range(4):
+        left_t[:, place(rel)] = jnp.transpose(right_v[block(rel), :])
+    over(gd_y)
+    results[0].wait()
+    for side in range(2):
+        rows = slice(side * half, (side + 1) * half)
+        grads_v[0, rows, : 3 * width] = dot_rows(left_t[rows, :], dqkv[...]).astype(jnp.bfloat16)
+    for rel in range(4):
+        left_t[:, place(rel)] = jnp.transpose(rows_two[block(rel), :])
+    for side in range(2):
+        rows = slice(side * half, (side + 1) * half)
+        grads_v[0, rows, 3 * width :] = dot_rows(left_t[rows, :], mixed_v[...]).astype(jnp.bfloat16)
+    results += [
+        file(grads_v.at[0, pl.ds(0, half)], gh_near_h),
+        file(grads_v.at[0, pl.ds(half, half)], gh_far_h),
+    ]
+    d_1.wait_recv()
+    d_v[:quarter, :] = summed(d_v[:quarter, :], z_met[1]).astype(jnp.bfloat16)
+    d_2 = fly("z2", d_v.at[pl.ds(owned, owned)], ld_met_h)
+    results.append(file(d_v.at[pl.ds(0, owned)], ld_keep_h))
+    from_near.wait_recv()
+    for rows, one in zip(strips, from_x):
+        one.wait_recv()
+        sum_ref[rows, :] = gathered(1, rows)
+    for one in (h2_y, h0_y, gd_y, u_2, d_2):
+        one.wait_recv()
+    for one in results[1:]:
+        one.wait()
+    for one in flying:
+        one.wait_send()
+
+
+def backward_global(line, info, small, grad, middle, gains, lse, weights, active, slope, nb, na, qkv, mixed, sums):
+    share, columns = small.shape[0], active.shape[1]
+    span, width = 4 * share, mixed.shape[1]
+    half, owned = D // 2, D // 8
+    low = jnp.bfloat16
+    up, down, heads = weights
     return line.run(
-        global_heads_back_body,
-        (info, *grads, *halves, qkv, mixed, lse,),
-        in_specs=[IN_SMEM] + [VMEM_WHOLE] * 9,
-        out_specs=[VMEM_WHOLE] * 5,
-        out_shape=[shaped((span, 3 * width), jnp.bfloat16)]
-        + [shaped((share, D), jnp.bfloat16)] * 4,
-        scratch_shapes=[
-            pltpu.VMEM((span, width), jnp.bfloat16),
+        backward_body,
+        (info, small, grad, middle, gains, lse, up, down, heads, active, slope, nb, na, qkv, mixed, *sums),
+        in_specs=[IN_SMEM] + [VMEM_WHOLE] * 5 + [IN_HBM] * 15,
+        out_specs=[VMEM_WHOLE] * 3 + [IN_HBM] * 12,
+        out_shape=[
+            shaped((share, D), jnp.float32),
+            shaped((share, D), jnp.float32),
+            shaped((1, D), jnp.float32),
+        ]
+        + [shaped((half, columns), low)] * 6
+        + [shaped((owned, columns), low)] * 4
+        + [shaped((half, columns), low)] * 2,
+        scratch_shapes=[pltpu.VMEM((span, D), low)] * 2
+        + [pltpu.VMEM((D, columns), low)] * 3
+        + [pltpu.VMEM((span, columns), low)] * 3
+        + [pltpu.VMEM((D, span), low), pltpu.VMEM((span, D), low), pltpu.VMEM((2, D, columns), low)]
+        + [pltpu.VMEM((span, 3 * width), low), pltpu.VMEM((span, width), low), pltpu.VMEM((span, 3 * width), low)]
+        + [
+            pltpu.VMEM((span, width), low),
             pltpu.VMEM((width, span), jnp.float32),
             pltpu.VMEM((span, width), jnp.float32),
             pltpu.VMEM((span, width), jnp.float32),
             pltpu.VMEM((8, span), jnp.float32),
-            pltpu.VMEM((width, span), jnp.bfloat16),
+            pltpu.VMEM((width, span), low),
+            pltpu.VMEM((4, share, D), low),
+            pltpu.VMEM((4, share, D), low),
+            pltpu.VMEM((2, share, D), low),
+            pltpu.VMEM((2, share, D), low),
+        ]
+        + [pltpu.VMEM((half, columns), low)] * 4
+        + [
+            pltpu.VMEM((2, half // 2, columns), low),
+            pltpu.SemaphoreType.DMA((24,)),
+            pltpu.SemaphoreType.DMA((40,)),
+            pltpu.SemaphoreType.DMA((40,)),
         ],
-        limit=(40),
-        name="global_heads_back",
-    )
-
-
-def global_grads_heads_body(
-    info_ref, a0, a1, a2, a3, g0, g1, g2, g3, dqkv_ref, mixed_ref, near_ref, far_ref, a_t, g_t
-):
-    share = a0.shape[0]
-    width = mixed_ref.shape[1]
-    for rel in range(4):
-        at = pl.ds(pl.multiple_of(group_at(rel) * share, share), share)
-        a_t[:, at] = jnp.transpose((a0, a1, a2, a3)[rel][...])
-        g_t[:, at] = jnp.transpose((g0, g1, g2, g3)[rel][...])
-
-    for at in range(D // 256):
-        rows = slice(at * 256, (at + 1) * 256)
-        out_ref, begin = (near_ref, 0) if at * 256 < D // 2 else (far_ref, D // 2)
-        there = slice(at * 256 - begin, at * 256 - begin + 256)
-        out_ref[there, : 3 * width] = dot_rows(a_t[rows, :], dqkv_ref[...]).astype(jnp.bfloat16)
-        out_ref[there, 3 * width :] = dot_rows(g_t[rows, :], mixed_ref[...]).astype(jnp.bfloat16)
-
-
-def global_grads_heads(line, info, normed, grads, dqkv, mixed):
-    span, width = mixed.shape
-    return line.run(
-        global_grads_heads_body,
-        (info, *normed, *grads, dqkv, mixed,),
-        in_specs=[IN_SMEM] + [VMEM_WHOLE] * 10,
-        out_specs=[VMEM_WHOLE] * 2,
-        out_shape=[shaped((D // 2, 4 * width), jnp.bfloat16)] * 2,
-        scratch_shapes=[pltpu.VMEM((D, span), jnp.bfloat16)] * 2,
-        limit=(40),
-        name="global_heads_grads",
-    )
-
-
-def global_ff_body(x0, x1, x2, x3, up0, up1, down0, down1, active_ref, slope_ref, p0, p1, p2, p3, acc):
-    step = pl.program_id(0)
-    share = x0.shape[0]
-    half = up0.shape[0]
-
-    @pl.when(step == 0)
-    def _():
-        acc[...] = jnp.zeros_like(acc)
-
-    for rel, x_ref in enumerate((x0, x1, x2, x3)):
-        rows = slice(rel * share, (rel + 1) * share)
-        active, slope = gelu_both(both(x_ref[...], up0[...], up1[...]))
-        active_ref[rows, :] = active
-        slope_ref[rows, :] = slope
-        for at, down in enumerate((down0, down1)):
-            lanes = slice(at * half, (at + 1) * half)
-            acc[rows, lanes] += dot_transposed(active, down[...])
-
-    @pl.when(step == pl.num_programs(0) - 1)
-    def _():
-        for rel, p_ref in enumerate((p0, p1, p2, p3)):
-            p_ref[...] = acc[rel * share : (rel + 1) * share, :].astype(jnp.bfloat16)
-
-
-def held(shape):
-    return pl.BlockSpec(shape, lambda step: (0,) * len(shape), pipeline_mode=pl.Buffered(1))
-
-
-def by_cols(shape):
-    return pl.BlockSpec(shape, lambda step: (0, step))
-
-
-def global_ff(line, rows, up, down, tile=256):
-    share = rows[0].shape[0]
-    span, hidden, half = 4 * share, up[0].shape[1], up[0].shape[0]
-    return line.run(
-        global_ff_body,
-        (*rows, *up, *down,),
-        grid=(hidden // tile,),
-        in_specs=[held((share, D))] * 4 + [by_cols((half, tile))] * 4,
-        out_specs=[by_cols((span, tile))] * 2 + [held((share, D))] * 4,
-        out_shape=[shaped((span, hidden), jnp.bfloat16)] * 2
-        + [shaped((share, D), jnp.bfloat16)] * 4,
-        scratch_shapes=[pltpu.VMEM((span, D), jnp.float32)],
-        limit=(40),
-        name="global_ff",
-    )
-
-
-def global_ff_back_body(g0, g1, g2, g3, slope_ref, up0, up1, down0, down1, dup_ref, p0, p1, p2, p3, acc):
-    step = pl.program_id(0)
-    share = g0.shape[0]
-    half = up0.shape[0]
-
-    @pl.when(step == 0)
-    def _():
-        acc[...] = jnp.zeros_like(acc)
-
-    for rel, g_ref in enumerate((g0, g1, g2, g3)):
-        rows = slice(rel * share, (rel + 1) * share)
-        grad = both(g_ref[...], down0[...], down1[...])
-        dup = (grad * slope_ref[rows, :].astype(jnp.float32)).astype(jnp.bfloat16)
-        dup_ref[rows, :] = dup
-        for at, up in enumerate((up0, up1)):
-            lanes = slice(at * half, (at + 1) * half)
-            acc[rows, lanes] += dot_transposed(dup, up[...])
-
-    @pl.when(step == pl.num_programs(0) - 1)
-    def _():
-        for rel, p_ref in enumerate((p0, p1, p2, p3)):
-            p_ref[...] = acc[rel * share : (rel + 1) * share, :].astype(jnp.bfloat16)
-
-
-def global_ff_back(line, grads, slope, up, down, tile=256):
-    share = grads[0].shape[0]
-    span, hidden, half = 4 * share, up[0].shape[1], up[0].shape[0]
-    return line.run(
-        global_ff_back_body,
-        (*grads, slope, *up, *down,),
-        grid=(hidden // tile,),
-        in_specs=[held((share, D))] * 4 + [by_cols((span, tile))] + [by_cols((half, tile))] * 4,
-        out_specs=[by_cols((span, tile))] + [held((share, D))] * 4,
-        out_shape=[shaped((span, hidden), jnp.bfloat16)] + [shaped((share, D), jnp.bfloat16)] * 4,
-        scratch_shapes=[pltpu.VMEM((span, D), jnp.float32)],
-        limit=(40),
-        name="global_ff_back",
-    )
-
-
-def outer_body(r0, r1, r2, r3, right_ref, near_ref, far_ref, left_t):
-    share = r0.shape[0]
-
-    @pl.when(pl.program_id(0) == 0)
-    def _():
-        for rel, ref in enumerate((r0, r1, r2, r3)):
-            left_t[:, rel * share : (rel + 1) * share] = jnp.transpose(ref[...])
-
-    for at in range(D // 256):
-        rows = slice(at * 256, (at + 1) * 256)
-        out_ref, begin = (near_ref, 0) if at * 256 < D // 2 else (far_ref, D // 2)
-        out_ref[at * 256 - begin : at * 256 - begin + 256, :] = dot_rows(
-            left_t[rows, :], right_ref[...]
-        ).astype(jnp.bfloat16)
-
-
-def global_outer(line, rows, right, tile=256):
-    share = rows[0].shape[0]
-    span, hidden = right.shape
-    return line.run(
-        outer_body,
-        (*rows, right,),
-        grid=(hidden // tile,),
-        in_specs=[held((share, D))] * 4 + [by_cols((span, tile))],
-        out_specs=[by_cols((D // 2, tile))] * 2,
-        out_shape=[shaped((D // 2, hidden), jnp.bfloat16)] * 2,
-        scratch_shapes=[pltpu.VMEM((D, span), jnp.bfloat16)],
-        limit=(32),
-        name="global_ff_grads",
+        hops=("core", "x", "y", "z1", "z2"),
+        limit=56,
+        name="backward_global",
     )
 
 
@@ -1133,6 +1394,11 @@
     return values.astype(jnp.bfloat16).astype(jnp.float32)
 
 
+def halves_of(stack):
+    half = stack.shape[1] // 2
+    return [(stack.at[at, pl.ds(0, half)], stack.at[at, pl.ds(half, half)]) for at in range(stack.shape[0])]
+
+
 def start_weights(parts, buffer, sems):
     for at, pair in enumerate(parts):
         for half, ref in enumerate(pair):
@@ -1148,8 +1414,8 @@
     out_ref_in, code_ref, gains_ref, *refs
 ):
     count = 4
-    parts = [refs[2 * at : 2 * at + 2] for at in range(count)]
-    qkv_ref, mixed_ref, middle_ref, normed_b_ref, a_t_ref, normed_a, local_in, buffer, sems = refs[2 * count :]
+    parts = halves_of(refs[0])
+    qkv_ref, mixed_ref, middle_ref, normed_b_ref, a_t_ref, normed_a, local_in, buffer, sems = refs[1:]
     step = pl.program_id(0)
     frames = out_ref_in.shape[0]
     width = mixed_ref.shape[2]
@@ -1203,14 +1469,13 @@
 def local_heads(line, global_out, codes, gains, parts):
     frames = global_out.shape[0]
     rows = CB * frames
-    width = parts[0][0].shape[1] // 4
+    width = parts.shape[2] // 4
     half = D // 2
-    flat = [ref for pair in parts for ref in pair]
     return line.run(
         local_heads_body,
-        (global_out, codes, gains, *flat),
+        (global_out, codes, gains, parts),
         grid=(4,),
-        in_specs=[held((frames, D)), held((rows, D)), held((4, D))] + [IN_HBM] * 8,
+        in_specs=[held((frames, D)), held((rows, D)), held((4, D)), IN_HBM],
         out_specs=[
             pl.BlockSpec((1, rows, 3 * width), lambda step: (step, 0, 0)),
             pl.BlockSpec((1, rows, width), lambda step: (step, 0, 0)),
@@ -1238,9 +1503,8 @@
 
 def local_ff_body(source_ref, normed_ref, middle_ref, *refs):
     count = 4
-    ups = [refs[2 * at : 2 * at + 2] for at in range(count)]
-    downs = [refs[2 * count + 2 * at : 2 * count + 2 * at + 2] for at in range(count)]
-    active_ref, slope_ref, out_ref, b_t_ref, acc, up_buf, down_buf, up_sems, down_sems = refs[4 * count :]
+    ups, downs = halves_of(refs[0]), halves_of(refs[1])
+    active_ref, slope_ref, out_ref, b_t_ref, acc, up_buf, down_buf, up_sems, down_sems = refs[2:]
     step = pl.program_id(0)
     rows_all = normed_ref.shape[0]
     frames = rows_all // CB
@@ -1292,16 +1556,15 @@
 
 def local_ff(line, source, normed, middle, ups, downs, tile=512):
     rows = normed.shape[0]
-    hidden = ups[0][0].shape[1]
+    hidden = ups.shape[2]
     half = D // 2
     per = hidden // tile
-    flat = [ref for pair in ups for ref in pair] + [ref for pair in downs for ref in pair]
     hidden_block = pl.BlockSpec((1, rows, tile), lambda step: (step // per, 0, step % per))
     return line.run(
         local_ff_body,
-        (source, normed, middle, *flat,),
+        (source, normed, middle, ups, downs),
         grid=(4 * per,),
-        in_specs=[IN_SMEM, held((rows, D)), held((rows, D))] + [IN_HBM] * 16,
+        in_specs=[IN_SMEM, held((rows, D)), held((rows, D)), IN_HBM, IN_HBM],
         out_specs=[hidden_block, hidden_block, held((CB, rows // CB, D)), held((D, rows))],
         out_shape=[
             shaped((4, rows, hidden), jnp.bfloat16),
@@ -1356,7 +1619,8 @@
 def local_back_body(
     grad_h, grad_t_h, b_t_h, a_t_h, active_h, slope_h, qkv_h, mixed_h, middle_h, gout_h, codes_h, gains_ref, *refs
 ):
-    heads_h, ups_h, downs_h, refs = refs[:8], refs[8:16], refs[16:24], refs[24:]
+    heads_h, ups_h, downs_h = ([half for pair in halves_of(one) for half in pair] for one in refs[:3])
+    refs = refs[3:]
     total_ref, small_out_ref, gain_c_ref, gain_d_ref, *results_h = refs[:12]
     (
         grad_v, grad_t, other_t, weights, act, slp, dup, acc, mid, gout_v, codes_v,
@@ -1559,13 +1823,12 @@
 def local_back(line, grad, grad_t, b_t, a_t, active, slope, qkv, mixed, middle, global_out, codes, gains, heads, ups, downs):
     rows, frames = grad.shape[0], global_out.shape[0]
     half = D // 2
-    flat = [one for parts in (heads, ups, downs) for pair in parts for one in pair]
-    columns = ups[0][0].shape[1]
+    columns = ups.shape[2]
     small = jnp.bfloat16
     return line.run(
         local_back_body,
-        (grad, grad_t, b_t, a_t, active, slope, qkv, mixed, middle, global_out, codes, gains, *flat),
-        in_specs=[IN_HBM] * 11 + [VMEM_WHOLE] + [IN_HBM] * 24,
+        (grad, grad_t, b_t, a_t, active, slope, qkv, mixed, middle, global_out, codes, gains, heads, ups, downs),
+        in_specs=[IN_HBM] * 11 + [VMEM_WHOLE] + [IN_HBM] * 3,
         out_specs=[VMEM_WHOLE] * 4 + [IN_HBM] * 8,
         out_shape=[
             shaped((frames, D), jnp.float32),
@@ -1605,49 +1868,6 @@
     )
 
 
-def cast_body(*refs):
-    count = len(refs) // 2
-    for master_ref, out_ref in zip(refs[:count], refs[count:]):
-        out_ref[...] = master_ref[0].astype(jnp.bfloat16)
-
-
-def cast(line, master, which):
-    owned, columns = master.shape[1], master.shape[2] // 3
-
-    def spec(layer, third):
-        return pl.BlockSpec((1, owned, columns), lambda step: (layer, 0, third))
-
-    return line.run(
-        cast_body,
-        (master,) * len(which),
-        grid=(1,),
-        in_specs=[spec(*one) for one in which],
-        out_specs=[held((owned, columns))] * len(which),
-        out_shape=[shaped((owned, columns), jnp.bfloat16)] * len(which),
-        limit=(24),
-        name="cast_shard",
-    )
-
-
-def stack_body(one_ref, two_ref, out_ref):
-    rows = one_ref.shape[0]
-    out_ref[:rows, :] = one_ref[...]
-    out_ref[rows:, :] = two_ref[...]
-
-
-def stack_rows(line, parts):
-    rows, columns = parts[0].shape
-    return line.run(
-        stack_body,
-        tuple(parts),
-        in_specs=[VMEM_WHOLE] * 2,
-        out_specs=[VMEM_WHOLE],
-        out_shape=[shaped((2 * rows, columns), jnp.bfloat16)],
-        limit=(16),
-        name="stack_shards",
-    )[0]
-
-
 def add_body(*refs):
     total = refs[0][...].astype(jnp.float32)
     for ref in refs[1:-1]:
@@ -1843,66 +2063,16 @@
     line = Line()
     codes = jnp.transpose(code_emb, (1, 0, 2))
 
-    (ga,) = cast(line, master, [(0, 0)])
-    ga_z = hop_z(ga, 2)
-    rows_in, gains_here, normed = prep(line, source, frames_in, gains)
-    normed_x = hop_x(normed)
-    la, gu, lu, gd, ld = cast(line, master, [(1, 0), (0, 1), (1, 1), (0, 2), (1, 2)])
-    ga = stack_rows(line, [ga, ga_z])
-    ga_z, la_z = hop_z(ga, 1), hop_z(la, 2)
-    (normed_x,) = in_turn(line, normed_x)
-    normed_a = [normed, hop_core(normed), normed_x, hop_core(normed_x)]
-    ga = stack_rows(line, [ga, ga_z])
-    la = stack_rows(line, [la, la_z])
-    ga_far, la_z, gu_z = hop_y(ga), hop_z(la, 1), hop_z(gu, 2)
-    la = stack_rows(line, [la, la_z])
-    gu = stack_rows(line, [gu, gu_z])
-    la_far, la_x, gu_z, lu_z = hop_y(la), hop_x(la), hop_z(gu, 1), hop_z(lu, 2)
-    g_heads = (ga, ga_far)
-    qkv, mixed, lse, *parts = global_heads(line, info, normed_a, g_heads)
-    near_term, far_term = hop_core(parts[1]), hop_core(parts[3])
-    gu = stack_rows(line, [gu, gu_z])
-    lu = stack_rows(line, [lu, lu_z])
-    gu_far, lu_z, gd_z = hop_y(gu), hop_z(lu, 1), hop_z(gd, 2)
-    to_x = hop_x(add_rows(line, [parts[2], far_term]))
-    la_far, la_x = in_turn(line, la_far, la_x)
-    lu = stack_rows(line, [lu, lu_z])
-    gd = stack_rows(line, [gd, gd_z])
-    lu_far, gd_z, ld_z = hop_y(lu), hop_z(gd, 1), hop_z(ld, 2)
-    middle, normed = merge(line, rows_in, (parts[0], near_term, to_x), gains_here, 1)
-    normed_x = hop_x(normed)
-    gd = stack_rows(line, [gd, gd_z])
-    ld = stack_rows(line, [ld, ld_z])
-    gd_far, ld_z = hop_y(gd), hop_z(ld, 1)
-    (normed_x, la_far, lu) = in_turn(line, normed_x, la_far, lu)
-    normed_b = [normed, hop_core(normed), normed_x, hop_core(normed_x)]
-    la_far_x, lu_x = hop_x(la_far), hop_x(lu)
+    (rows_in, gains_here, normed), shards = prep(line, source, frames_in, gains, master)
     grad, grad_t, codes_here = seed(line, source, count, jnp.transpose(cotangent, (1, 0, 2)), codes)
-    ld = stack_rows(line, [ld, ld_z])
-    ld_far, la_c, la_far_c = hop_y(ld), hop_core(la), hop_core(la_far)
-    g_up, g_down = (gu, gu_far), (gd, gd_far)
-    active, slope, *parts = global_ff(line, normed_b, g_up, g_down)
-    near_term, far_term = hop_core(parts[1]), hop_core(parts[3])
-    (lu_x, la_far_x, ld) = in_turn(line, lu_x, la_far_x, ld)
-    lu_far_x = hop_y(lu_x)
-    to_x = hop_x(add_rows(line, [parts[2], far_term]))
-    ld_x = hop_x(ld)
-    la_xc, la_far_xc = hop_core(la_x), hop_core(la_far_x)
-    (global_out,) = merge(line, middle, (parts[0], near_term, to_x), gains_here, 1, normed=False)
-    (ld_far, lu_far) = in_turn(line, ld_far, lu_far)
-
-    l_heads = [(la, la_far), (la_c, la_far_c), (la_x, la_far_x), (la_xc, la_far_xc)]
+    (
+        g_heads, g_up, g_down, l_heads, l_up, l_down, qkv, mixed, lse, middle, global_out, normed_a, normed_b,
+        active, slope,
+    ) = forward_global(line, info, rows_in, normed, gains_here, shards)
+
     l_qkv, l_mixed, l_middle, l_normed_b, l_a_t = local_heads(
         line, global_out, codes_here, gains_here, l_heads
     )
-    lu_c, lu_far_c, ld_c, ld_far_c = hop_core(lu), hop_core(lu_far), hop_core(ld), hop_core(ld_far)
-    (ld_x, lu_far_x) = in_turn(line, ld_x, lu_far_x)
-    ld_far_x = hop_y(ld_x)
-    lu_xc, lu_far_xc, ld_xc = hop_core(lu_x), hop_core(lu_far_x), hop_core(ld_x)
-    (ld_far_x,) = in_turn(line, ld_far_x)
-    ld_far_xc = hop_core(ld_far_x)
-    l_up = [(lu, lu_far), (lu_c, lu_far_c), (lu_x, lu_far_x), (lu_xc, lu_far_xc)]
-    l_down = [(ld, ld_far), (ld_c, ld_far_c), (ld_x, ld_far_x), (ld_xc, ld_far_xc)]
     l_active, l_slope, local_out, l_b_t = local_ff(line, source, l_normed_b, l_middle, l_up, l_down)
     local_out = jnp.transpose(local_out, (1, 0, 2))
 
@@ -1912,11 +2082,6 @@
         line, grad, grad_t, l_b_t, l_a_t, l_active, l_slope, l_qkv, l_mixed, l_middle, global_out, codes_here,
         gains_here, l_heads, l_up, l_down,
     )
-    small_x = hop_x(small)
-    u_far = hop_y(u_far)
-    d2 = hop_x(d2)
-    h2_far = hop_y(h2_far)
-
     def update(layer, third, pieces, before):
         return adam(
             line, layer, third, pieces, left_basis, right_basis, master, first_moment, second_moment, ema, before
@@ -1930,47 +2095,31 @@
         keep, send = sum_pieces(line, [keep, met])
         return keep, hop_z(send, 2)
 
-    (small_x,) = in_turn(line, small_x)
-    grad_rows = [small, hop_core(small), small_x, hop_core(small_x)]
-    h0_far = hop_y(h0_far)
-    grad_upper, *parts = global_ff_back(line, grad_rows, slope, g_up, g_down)
-    near_term, far_term = hop_core(parts[1]), hop_core(parts[3])
-    gd_near, gd_far = global_outer(line, grad_rows, active)
-    gd_far = hop_y(gd_far)
-    to_x = hop_x(add_rows(line, [parts[2], far_term]))
-    ld = depth_first([d0, d2])
-    lu = depth_first([u_near, u_far])
-    gu_near, gu_far = global_outer(line, normed_b, grad_upper)
-    gu_far = hop_y(gu_far)
-    ld = depth_second(*ld)
-    grad_middle, small, gain_b = merge_back(
-        line, middle, (parts[0], near_term, to_x), grad_global, gains_here, 1
-    )
-    small_x = hop_x(small)
-    h2 = hop_x(add_rows(line, [h2_near, h2_far]))
-    lu = depth_second(*lu)
-    found = update(1, 2, ld, None)
-    (small_x,) = in_turn(line, small_x)
-    grad_attn = [small, hop_core(small), small_x, hop_core(small_x)]
-    grad_qkv, *parts = global_heads_back(line, info, grad_attn, g_heads, qkv, mixed, lse)
-    near_term, far_term = hop_core(parts[1]), hop_core(parts[3])
-    gh_near, gh_far = global_grads_heads(line, info, normed_a, grad_attn, grad_qkv, mixed)
-    gh_far = hop_y(gh_far)
-    to_x = hop_x(add_rows(line, [parts[2], far_term]))
-    found = update(1, 1, lu, found)
-    gd = depth_first([gd_near, gd_far])
-    lh = depth_first([h0_near, h0_far, h2])
+    (
+        grad_middle, grad_sum, gain_b, gd_near, gd_met, gu_near, gu_far, gh_near, gh_far, lu_keep, lu_met, ld_keep,
+        ld_met, h2_met, h0_met,
+    ) = backward_global(
+        line, info, small, grad_global, middle, gains_here, lse, (g_up, g_down, g_heads), active, slope, normed_b,
+        normed_a, qkv, mixed, (u_near, u_far, d2, d0, h2_far, h0_far),
+    )
+    gu_met = hop_y(gu_far)
+    gh_met = hop_y(gh_far)
+    h2 = hop_x(add_rows(line, [h2_near, h2_met]))
+    gd = depth_first([gd_near, gd_met])
     input_grad, gain_grads = finish(
-        line, source, rows_in, (parts[0], near_term, to_x), grad_middle, gains_here, (gain_b, gain_c, gain_d)
+        line, source, rows_in, grad_sum, grad_middle, gains_here, (gain_b, gain_c, gain_d)
     )
     gain_grads = total_everywhere(gain_grads)
+    found = update(1, 1, (lu_keep, lu_met), None)
     gd = depth_second(*gd)
+    found = update(1, 2, (ld_keep, ld_met), found)
+    lh = depth_first([h0_near, h0_met, h2])
+    gu = depth_first([gu_near, gu_met])
+    found = update(0, 2, gd, found)
     lh = depth_second(*lh)
-    gu = depth_first([gu_near, gu_far])
-    found = update(0, 2, gd, found)
+    gu = depth_second(*gu)
+    gh = depth_first([gh_near, gh_met])
     found = update(1, 0, lh, found)
-    gu = depth_second(*gu)
-    gh = depth_first([gh_near, gh_far])
     found = update(0, 1, gu, found)
     gh = depth_second(*gh)
     found = update(0, 0, gh, found)

time: 621 us -> 608 us (0.979)
  Pallas kernels: 253 us -> 507 us
  waiting for transfers between devices: 250 us -> 39.9 us
  starting transfers between devices: 77.4 us -> 26.1 us
  local copies, waits for them, and re-layouts: 32.7 us -> 23.7 us
    pallas_call x62 -> x23, Pallas kernels: 253 us -> 507 us  [run(): pl.pallas_call(inner, in_specs=[IN_HBM] * lead + list(in_specs) + [IN_HBM...]
    ppermute x26 -> x10, waiting for transfers between devices: 136 us -> 35.6 us  [hop_z(): return lax.ppermute(values, 'dp', [(at, at ^ 2 * step) for at in range(8)])]
    ppermute x15 -> x3, waiting for transfers between devices: 63.6 us -> 0.01 us  [hop_y(): return lax.ppermute(values, 'dp', [(at, at ^ 1) for at in range(8)])]
    ppermute x15 -> x2, waiting for transfers between devices: 43.2 us -> 3.12 us  [hop_x(): return lax.ppermute(values, 'tensor', [(at, at ^ 2) for at in range(4)])]
    ppermute x26 -> x10, starting transfers between devices: 41.4 us -> 21 us  [hop_z(): return lax.ppermute(values, 'dp', [(at, at ^ 2 * step) for at in range(8)])]
    ppermute x15 -> x3, starting transfers between devices: 16.6 us -> 2.7 us  [hop_y(): return lax.ppermute(values, 'dp', [(at, at ^ 1) for at in range(8)])]
    ppermute x15 -> x2, starting transfers between devices: 15.4 us -> 2.44 us  [hop_x(): return lax.ppermute(values, 'tensor', [(at, at ^ 2) for at in range(4)])]
    unnamed x194 -> x106, local copies, waits for them, and re-layouts: 32.7 us -> 23.7 us
  transfers between devices with their start and end apart: 85 -> 16, of which waited for: 32 -> 6; matrix products, arithmetic and copies ran while one was open for 0% -> 0% of each run, Pallas kernels for 21% -> 5%
where the time goes in v4:
time: 608 us; the launch traced here: 601 us
  Pallas kernels  507 us (83%)
  waiting for transfers between devices  39.9 us (7%)
  starting transfers between devices  26.1 us (4%)
  local copies, waits for them, and re-layouts  23.7 us (4%)
    pallas_call x23, Pallas kernels, run(): pl.pallas_call(inner, in_specs=[IN_HBM] * lead + list(in_specs) + [IN_HBM...  507 us
    ppermute x10, waiting for transfers between devices, hop_z(): return lax.ppermute(values, 'dp', [(at, at ^ 2 * step) for at in range(8)])  35.6 us
    unnamed x106, local copies, waits for them, and re-layouts  23.7 us
    ppermute x10, starting transfers between devices, hop_z(): return lax.ppermute(values, 'dp', [(at, at ^ 2 * step) for at in range(8)])  21 us
  transfers between devices with their start and end apart: 16, of which 6 were waited for; matrix products, arithmetic and copies ran while one was open for 0% of the time, Pallas kernels for 5%

profile of v4, /device:TPU:0, one launch (start us, length us, event | category | flops | bytes accessed | tf_op | source)
XLA Modules:
  0.0 601.3 jit_solution(4256350711379964430)
XLA Ops:
  2.5 0.8 select_reduce_fusion.refs_0_.refs_1_
  3.4 1.9 copy-done
  5.3 1.0 copy-done.19
  7.0 1.0 prep_rows.1
  8.0 0.8 copy-done.20
  9.4 0.8 copy-done.40
  10.3 1.6 seed_grads.1
  11.9 1.1 copy-done.37
  13.0 1.1 copy-done.38
  14.1 1.1 copy-done.39
  15.9 228.0 %forward_global.1 = (bf16[1024,1024]{1,0:T(8,128)(2,1)}, bf16[1024,1024]{1,0:T(8,128)(2,1)}, bf16[1024,1024]{1,0:T(8,128)(2,1)}, bf16[4,1024,1024]{2,1,0:T(8,128...) custom-call(f32[8,128]{1,0:T(8,128)} %copy-done.47, ...), custom_call_target="tpu_custom_call" | custom-call | flops 33999998976 | bytes 1000 | tf_op jit(solution)/shard_map/forward_global/pallas_call | solution.py:627
  243.9 1.2 copy-done.48
  245.8 17.8 %local_heads.1 = (bf16[4,768,768]{2,1,0:T(8,128)(2,1)}, bf16[4,768,256]{2,1,0:T(8,128)(2,1)}, f32[768,1024]{1,0:T(8,128)}, bf16[768,1024]{1,0:T(8,128)(2,1)}, bf...) custom-call(f32[8,128]{1,0:T(8,128)S(1)} %copy-done.49, f32[256,1024]{1,0:T(8,128)S(1)} %copy-done.48, ...), custom_call_target="tpu_custom_call" | custom-call | flops 3600000000 | bytes 1000 | tf_op jit(solution)/shard_map/local_heads/pallas_call | solution.py:627
  264.2 34.4 %local_ff.1 = (bf16[4,768,1024]{2,1,0:T(8,128)(2,1)}, bf16[4,768,1024]{2,1,0:T(8,128)(2,1)}, bf16[3,256,1024]{2,1,0:T(8,128)(2,1)}, bf16[1024,768]{1,0:T(8,128)(2,1)}, f32[8,128]{1,0:T(8,128)}) custom-call(f32[8,128]{1,0:T(8,128)} %copy-done.50, s32[8]{0:T(128)} %copy-done.31, bf16[768,1024]{1,0:T(8,128)(2,1)} %get-tuple-element.161.refs_2_, ...), custom_call_target="tpu_custom_call" | custom-call | flops 6800000000 | bytes 1000 | tf_op jit(solution)/shard_map/local_ff/pallas_call | solution.py:627
  298.6 81.3 %local_back.1 = (f32[256,1024]{1,0:T(8,128)}, bf16[256,1024]{1,0:T(8,128)(2,1)}, f32[1,1024]{1,0:T(1,128)}, f32[1,1024]{1,0:T(1,128)}, bf16[512,1024]{1,0:T(8,12...) custom-call(f32[8,128]{1,0:T(8,128)} %get-tuple-element.166.refs_0_,, ...), custom_call_target="tpu_custom_call" | custom-call | flops 16199999488 | bytes 1000 | tf_op jit(solution)/shard_map/local_back/pallas_call | solution.py:627
  380.0 109.8 %backward_global.1 = (f32[256,1024]{1,0:T(8,128)}, f32[256,1024]{1,0:T(8,128)}, f32[1,1024]{1,0:T(1,128)}, bf16[512,1024]{1,0:T(8,128)(2,1)}, bf16[512,1024]{1,0...) custom-call(f32[8,128]{1,0:T(8,128)} %get-tuple-element.175.refs_0_,, ...), custom_call_target="tpu_custom_call" | custom-call | flops 17999998976 | bytes 1000 | tf_op jit(solution)/shard_map/backward_global/pallas_call | solution.py:627
  489.8 1.2 copy-done.18
  492.0 1.8 collective-permute-start.1
  494.1 1.2 copy-done.16
  495.3 1.2 copy-done.17
  496.9 1.8 collective-permute-start.6
  498.7 1.2 copy-done.13
  499.9 1.2 copy-done.14
  501.8 2.2 input_grad.1
  504.1 1.9 copy-done.5
  506.0 0.9 copy-done.24
  506.9 0.9 copy-done.25
  507.9 4.8 adam_update.6
  512.9 4.8 adam_update.7
  518.1 2.0 collective-permute-start.4
  520.3 0.8 collective-permute-start.5
  521.2 2.0 collective-permute-start.3
  523.2 24.1 %collective-permute-done.3.refs_2_ = bf16[128,1024]{1,0:T(8,128)(2,1)S(1)} collective-permute-done((bf16[128,1024]{1,0:T(8,128)(2,1)S(1)}, bf16[128,1024]{1,0:T(8,128)(2,1)S(1)}, u32[]{:S(2)}, u32[]{:S(2)}) %collective-permute-start.3) | collective-permute-done | bytes 262176 | tf_op jit(solution)/shard_map/ppermute | solution.py:2019
  547.3 4.8 adam_update.8
  552.6 2.2 collective-permute-start.9
  554.8 1.3 collective-permute-start.7
  556.1 1.6 collective-permute-start.8
  557.7 1.2 collective-permute-done.11
  559.6 3.1 collective-permute-done.12
  563.3 8.0 %collective-permute-done.7.refs_2_ = bf16[128,1024]{1,0:T(8,128)(2,1)S(1)} collective-permute-done((bf16[128,1024]{1,0:T(8,128)(2,1)S(1)}, bf16[128,1024]{1,0:T(8,128)(2,1)S(1)}, u32[]{:S(2)}, u32[]{:S(2)}) %collective-permute-start.7) | collective-permute-done | bytes 262176 | tf_op jit(solution)/shard_map/ppermute | solution.py:2019
  571.3 4.8 adam_update.9
  576.1 4.8 adam_update.10
  581.1 3.5 collective-permute-start.10
  584.6 4.4 collective-permute-start.14
  589.0 1.7 collective-permute-done.14
  590.7 3.0 collective-permute-start.15
  593.7 1.7 collective-permute-done.15
  596.1 4.8 adam_update.11
  (121 shorter events, 10.0 us)
Async XLA Ops:
  3.4 1.9 copy-start
  7.0 3.2 copy-start.31
  7.0 3.2 copy-start.7
  7.0 3.2 copy-start.8
  10.2 5.1 copy-start.41
  10.2 5.1 copy-start.42
  10.2 5.1 copy-start.43
  10.2 5.1 copy-start.44
  10.2 5.1 copy-start.45
  10.2 5.1 copy-start.46
  15.9 228.0 %copy-start.29 = (f32[4,1024]{1,0:T(4,128)S(1)}, f32[4,1024]{1,0:T(4,128)}, u32[]{:S(2)}) copy-start(f32[4,1024]{1,0:T(4,128)} %copy-done.28) | copy-start | bytes 49156
  379.9 109.9 %copy-start.15 = (bf16[512,1024]{1,0:T(8,128)(2,1)S(1)}, bf16[512,1024]{1,0:T(8,128)(2,1)}, u32[]{:S(2)}) copy-start(bf16[512,1024]{1,0:T(8,128)(2,1)} %get-tuple-element.196.refs_1_) | copy-start | bytes 3145732
  379.9 118.8 %copy-start.21 = (bf16[256,1024]{1,0:T(8,128)(2,1)S(1)}, bf16[256,1024]{1,0:T(8,128)(2,1)}, u32[]{:S(2)}) copy-start(bf16[256,1024]{1,0:T(8,128)(2,1)} %copy-done.20) | copy-start | bytes 1572868
  379.9 118.7 %copy-start.30 = (f32[4,1024]{1,0:T(4,128)S(1)}, f32[4,1024]{1,0:T(4,128)}, u32[]{:S(2)}) copy-start(f32[4,1024]{1,0:T(4,128)} %copy-done.28) | copy-start | bytes 49156
  379.9 118.7 %copy-start.34 = (f32[1,1024]{1,0:T(1,128)S(1)}, f32[1,1024]{1,0:T(1,128)}, u32[]{:S(2)}) copy-start(f32[1,1024]{1,0:T(1,128)} %get-tuple-element.206.refs_8_) | copy-start | bytes 12292
  380.0 124.1 %copy-start.3 = (f32[2,128,3072]{2,1,0:T(8,128)S(1)}, f32[2,128,3072]{2,1,0:T(8,128)}, u32[]{:S(2)}) copy-start(f32[2,128,3072]{2,1,0:T(8,128)} %refs_6_.13) | copy-start | bytes 9437188
  380.0 124.1 %copy-start.4 = (f32[2,128,3072]{2,1,0:T(8,128)S(1)}, f32[2,128,3072]{2,1,0:T(8,128)}, u32[]{:S(2)}) copy-start(f32[2,128,3072]{2,1,0:T(8,128)} %refs_7_.13) | copy-start | bytes 9437188
  489.8 8.9 %copy-start.32 = (s32[8]{0:T(128)S(1)}, s32[8]{0:T(128)}, u32[]{:S(2)}) copy-start(s32[8]{0:T(128)} %copy-done.31) | copy-start | bytes 100
  489.8 8.9 %copy-start.33 = (f32[1,1024]{1,0:T(1,128)S(1)}, f32[1,1024]{1,0:T(1,128)}, u32[]{:S(2)}) copy-start(f32[1,1024]{1,0:T(1,128)} %get-tuple-element.205.refs_7_) | copy-start | bytes 12292
  491.7 12.3 %copy-start.1 = (f32[2,128,3072]{2,1,0:T(8,128)S(1)}, f32[2,128,3072]{2,1,0:T(8,128)}, u32[]{:S(2)}) copy-start(f32[2,128,3072]{2,1,0:T(8,128)} %refs_5_.13) | copy-start | bytes 9437188
  491.7 12.3 %copy-start.2 = (f32[2,24,128,128]{3,2,1,0:T(8,128)S(1)}, f32[2,24,128,128]{3,2,1,0:T(8,128)}, u32[]{:S(2)}) copy-start(f32[2,24,128,128]{3,2,1,0:T(8,128)} %refs_4_.13) | copy-start | bytes 9437188
  491.7 12.3 %copy-start.6 = (f32[2,128,128]{2,1,0:T(8,128)S(1)}, f32[2,128,128]{2,1,0:T(8,128)}, u32[]{:S(2)}) copy-start(f32[2,128,128]{2,1,0:T(8,128)} %refs_3_.13) | copy-start | bytes 393220
  492.0 25.7 %collective-permute-start.1 = (bf16[512,1024]{1,0:T(8,128)(2,1)S(1)}, bf16[512,1024]{1,0:T(8,128)(2,1)S(1)}, u32[]{:S(2)}, u32[]{:S(2)}) collective-permute-start(bf16[512,1024]{1,0:T(8,128)(2,1)S(1)} %get-tuple-element.225), channel_id=1, source_target_pairs={{0,2},{1,3},{2,0},{3,1},{4,6},{5,7},{6,4},{7,5},{8,10},{9,11},{10,... | collective-permute-start | bytes 3145736 | tf_op jit(solution)/shard_map/ppermute | solution.py:2007
  493.8 26.3 %collective-permute-start.2 = (bf16[512,1024]{1,0:T(8,128)(2,1)}, bf16[512,1024]{1,0:T(8,128)(2,1)S(1)}, u32[]{:S(2)}, u32[]{:S(2)}) collective-permute-start(bf16[512,1024]{1,0:T(8,128)(2,1)} %get-tuple-element.228), channel_id=1, source_target_pairs={{0,4},{4,0},{8,12},{12,8},{16,20},{20,16},{24,28},{28,24},{1,5},{5... | collective-permute-start | bytes 3145736 | tf_op jit(solution)/shard_map/ppermute | solution.py:2015
  496.8 15.9 %collective-permute-start = (bf16[256,1024]{1,0:T(8,128)(2,1)S(1)}, bf16[256,1024]{1,0:T(8,128)(2,1)S(1)}, u32[]{:S(2)}, u32[]{:S(2)}) collective-permute-start(bf16[256,1024]{1,0:T(8,128)(2,1)S(1)} %get-tuple-element.213), channel_id=1, source_target_pairs={{0,8},{4,12},{8,0},{12,4},{16,24},{20,28},{24,16},{28,20},{1,9},{5... | collective-permute-start | bytes 1572872 | tf_op jit(solution)/shard_map/ppermute | solution.py:2019
  496.9 55.5 %collective-permute-start.6 = (bf16[512,1024]{1,0:T(8,128)(2,1)}, bf16[512,1024]{1,0:T(8,128)(2,1)S(1)}, u32[]{:S(2)}, u32[]{:S(2)}) collective-permute-start(bf16[512,1024]{1,0:T(8,128)(2,1)} %get-tuple-element.245), channel_id=1, source_target_pairs={{0,4},{4,0},{8,12},{12,8},{16,20},{20,16},{24,28},{28,24},{1,5},{5... | collective-permute-start | bytes 3145736 | tf_op jit(solution)/shard_map/ppermute | solution.py:2015
  504.1 1.9 copy-start.5
  507.9 4.9 copy-start.22
  507.9 5.0 copy-start.23
  512.8 4.8 copy-start.10
  512.8 4.8 copy-start.12
  517.7 2.4 copy-start.11
  518.1 34.0 %collective-permute-start.4 = (bf16[256,1024]{1,0:T(8,128)(2,1)S(1)}, bf16[256,1024]{1,0:T(8,128)(2,1)S(1)}, u32[]{:S(2)}, u32[]{:S(2)}) collective-permute-start(bf16[256,1024]{1,0:T(8,128)(2,1)S(1)} %get-tuple-element.239), channel_id=1, source_target_pairs={{0,8},{4,12},{8,0},{12,4},{16,24},{20,28},{24,16},{28,20},{1,9},{5... | collective-permute-start | bytes 1572872 | tf_op jit(solution)/shard_map/ppermute | solution.py:2019
  520.3 31.9 %collective-permute-start.5 = (bf16[256,1024]{1,0:T(8,128)(2,1)S(1)}, bf16[256,1024]{1,0:T(8,128)(2,1)S(1)}, u32[]{:S(2)}, u32[]{:S(2)}) collective-permute-start(bf16[256,1024]{1,0:T(8,128)(2,1)S(1)} %get-tuple-element.242), channel_id=1, source_target_pairs={{0,8},{4,12},{8,0},{12,4},{16,24},{20,28},{24,16},{28,20},{1,9},{5... | collective-permute-start | bytes 1572872 | tf_op jit(solution)/shard_map/ppermute | solution.py:2019
  521.2 26.1 %collective-permute-start.3 = (bf16[128,1024]{1,0:T(8,128)(2,1)S(1)}, bf16[128,1024]{1,0:T(8,128)(2,1)S(1)}, u32[]{:S(2)}, u32[]{:S(2)}) collective-permute-start(bf16[128,1024]{1,0:T(8,128)(2,1)S(1)} %get-tuple-element.231), channel_id=1, source_target_pairs={{0,16},{4,20},{8,24},{12,28},{16,0},{20,4},{24,8},{28,12},{1,17},{... | collective-permute-start | bytes 786440 | tf_op jit(solution)/shard_map/ppermute | solution.py:2019
  547.3 5.1 copy-start.9
  552.6 28.3 %collective-permute-start.9 = (bf16[256,1024]{1,0:T(8,128)(2,1)S(1)}, bf16[256,1024]{1,0:T(8,128)(2,1)S(1)}, u32[]{:S(2)}, u32[]{:S(2)}) collective-permute-start(bf16[256,1024]{1,0:T(8,128)(2,1)S(1)} %get-tuple-element.264), channel_id=1, source_target_pairs={{0,8},{4,12},{8,0},{12,4},{16,24},{20,28},{24,16},{28,20},{1,9},{5... | collective-permute-start | bytes 1572872 | tf_op jit(solution)/shard_map/ppermute | solution.py:2019
  554.8 16.5 %collective-permute-start.7 = (bf16[128,1024]{1,0:T(8,128)(2,1)S(1)}, bf16[128,1024]{1,0:T(8,128)(2,1)S(1)}, u32[]{:S(2)}, u32[]{:S(2)}) collective-permute-start(bf16[128,1024]{1,0:T(8,128)(2,1)S(1)} %get-tuple-element.248), channel_id=1, source_target_pairs={{0,16},{4,20},{8,24},{12,28},{16,0},{20,4},{24,8},{28,12},{1,17},{... | collective-permute-start | bytes 786440 | tf_op jit(solution)/shard_map/ppermute | solution.py:2019
  556.1 20.0 %collective-permute-start.8 = (bf16[128,1024]{1,0:T(8,128)(2,1)S(1)}, bf16[128,1024]{1,0:T(8,128)(2,1)S(1)}, u32[]{:S(2)}, u32[]{:S(2)}) collective-permute-start(bf16[128,1024]{1,0:T(8,128)(2,1)S(1)} %get-tuple-element.256), channel_id=1, source_target_pairs={{0,16},{4,20},{8,24},{12,28},{16,0},{20,4},{24,8},{28,12},{1,17},{... | collective-permute-start | bytes 786440 | tf_op jit(solution)/shard_map/ppermute | solution.py:2019
  557.7 1.2 collective-permute-start.11
  558.9 3.7 collective-permute-start.12
  562.7 21.9 %collective-permute-start.13 = (f32[4,1024]{1,0:T(4,128)S(1)}, f32[4,1024]{1,0:T(4,128)S(1)}, u32[]{:S(2)}, u32[]{:S(2)}) collective-permute-start(f32[4,1024]{1,0:T(4,128)S(1)} %add.28), channel_id=1, source_target_pairs={{0,4},{4,0},{8,12},{12,8},{16,20},{20,16},{24,28},{28,24},{1,5},{5... | collective-permute-start | bytes 49160 | tf_op jit(solution)/shard_map/ppermute | solution.py:2015
  576.1 19.3 %copy-start.27 = (f32[4,1024]{1,0:T(4,128)S(1)}, f32[4,1024]{1,0:T(4,128)}, u32[]{:S(2)}) copy-start(f32[4,1024]{1,0:T(4,128)} %refs_2_.1) | copy-start | bytes 49156
  576.1 19.3 %copy-start.51 = (f32[4,1024]{1,0:T(4,128)S(1)}, f32[4,1024]{1,0:T(4,128)}, u32[]{:S(2)}) copy-start(f32[4,1024]{1,0:T(4,128)} %param.27) | copy-start | bytes 49156
  576.1 19.3 %copy-start.52 = (f32[4,1024]{1,0:T(4,128)S(1)}, f32[4,1024]{1,0:T(4,128)}, u32[]{:S(2)}) copy-start(f32[4,1024]{1,0:T(4,128)} %param.28) | copy-start | bytes 49156
  581.1 15.0 %collective-permute-start.10 = (bf16[128,1024]{1,0:T(8,128)(2,1)S(1)}, bf16[128,1024]{1,0:T(8,128)(2,1)S(1)}, u32[]{:S(2)}, u32[]{:S(2)}) collective-permute-start(bf16[128,1024]{1,0:T(8,128)(2,1)S(1)} %get-tuple-element.267), channel_id=1, source_target_pairs={{0,16},{4,20},{8,24},{12,28},{16,0},{20,4},{24,8},{28,12},{1,17},{... | collective-permute-start | bytes 786440 | tf_op jit(solution)/shard_map/ppermute | solution.py:2019
  584.6 6.1 %collective-permute-start.14 = (f32[4,1024]{1,0:T(4,128)S(1)}, f32[4,1024]{1,0:T(4,128)S(1)}, u32[]{:S(2)}, u32[]{:S(2)}) collective-permute-start(f32[4,1024]{1,0:T(4,128)S(1)} %add.29), channel_id=1, source_target_pairs={{0,8},{4,12},{8,0},{12,4},{16,24},{20,28},{24,16},{28,20},{1,9},{5... | collective-permute-start | bytes 49160 | tf_op jit(solution)/shard_map/ppermute | solution.py:2019
  590.7 4.7 collective-permute-start.15
  (21 other events, 19.9 us)

commit v5 on v4

--- a/solution.py
+++ b/solution.py
@@ -7,6 +7,7 @@
 from jax.experimental.pallas import tpu as pltpu
 from jax.sharding import PartitionSpec as P
 
+DP, TENSOR = "dp", "tensor"
 D = 1024
 HD = 64
 FF = 4096
@@ -354,27 +355,27 @@
     gain_first,
     gain_second,
 ):
-    tensor_count = lax.axis_size("tensor")
-    group_count = lax.axis_size("dp")
+    tensor_count = lax.axis_size(TENSOR)
+    group_count = lax.axis_size(DP)
     head_cols = D // tensor_count
     ff_cols = FF // tensor_count
     share = frames_in.shape[0]
     owned_rows = master.shape[1]
-    gathered = lax.all_gather(master.astype(jnp.bfloat16), "dp", axis=1, tiled=True)
+    gathered = lax.all_gather(master.astype(jnp.bfloat16), DP, axis=1, tiled=True)
     layers = jnp.take(gathered.reshape(2, group_count, owned_rows, -1), owner_list, axis=1).reshape(
         2, group_count * owned_rows, -1
     )
 
     def gather_rows(values):
-        return lax.all_gather(values, "tensor", axis=0, tiled=True)
+        return lax.all_gather(values, TENSOR, axis=0, tiled=True)
 
     def gather_grads(values):
-        return lax.all_gather(values, "tensor", axis=0, tiled=True)
+        return lax.all_gather(values, TENSOR, axis=0, tiled=True)
 
     def sum_rows(operand, weight):
         return lax.psum_scatter(
             row_term(operand, weight).astype(jnp.bfloat16),
-            "tensor",
+            TENSOR,
             scatter_dimension=0,
             tiled=True,
         ).astype(jnp.float32)
@@ -382,7 +383,7 @@
     def sum_back(operand, weight):
         return lax.psum_scatter(
             row_term(operand, weight).astype(jnp.bfloat16),
-            "tensor",
+            TENSOR,
             scatter_dimension=0,
             tiled=True,
         ).astype(jnp.float32)
@@ -406,13 +407,13 @@
         attend_global,
     )
     local_in = (global_out[:, None, :] + code_emb.astype(jnp.float32)).reshape(share * CB, -1)
-    local_layer = lax.all_gather(layers[1], "tensor", axis=1, tiled=True)
+    local_layer = lax.all_gather(layers[1], TENSOR, axis=1, tiled=True)
     local_matrices = split_layer(local_layer, tensor_count, head_cols, ff_cols)
     local_result, local_kept = block_forward(
         local_in, local_matrices, gains[2], gains[3], rows_path, local_attend
     )
     local_out = local_result.reshape(share, CB, -1).astype(jnp.bfloat16)
-    frame_at = lax.axis_index("tensor") * share + jnp.arange(share, dtype=jnp.int32)
+    frame_at = lax.axis_index(TENSOR) * share + jnp.arange(share, dtype=jnp.int32)
     item_at = frame_at // LMAX
     item_slots = jnp.arange(lengths.shape[0], dtype=jnp.int32)
     item_length = jnp.sum(
@@ -435,7 +436,7 @@
     )
     local_grads = join_layer(local_weight_grads, tensor_count)
     local_grads = lax.psum_scatter(
-        local_grads.astype(jnp.bfloat16), "tensor", scatter_dimension=1, tiled=True
+        local_grads.astype(jnp.bfloat16), TENSOR, scatter_dimension=1, tiled=True
     ).astype(jnp.float32)
     layer_grads = jnp.stack([join_layer(global_weight_grads, 1), local_grads])
     slots = jnp.arange(group_count, dtype=jnp.int32)
@@ -444,10 +445,10 @@
         layer_grads.reshape(2, group_count, owned_rows, -1), inverse, axis=1
     ).reshape(2, group_count * owned_rows, -1)
     weight_grads = lax.psum_scatter(
-        ordered.astype(jnp.bfloat16), "dp", scatter_dimension=1, tiled=True
+        ordered.astype(jnp.bfloat16), DP, scatter_dimension=1, tiled=True
     ).astype(jnp.float32)
     gain_grads = lax.psum(
-        jnp.stack([gain_a_grad, gain_b_grad, gain_c_grad, gain_d_grad]), ("dp", "tensor")
+        jnp.stack([gain_a_grad, gain_b_grad, gain_c_grad, gain_d_grad]), (DP, TENSOR)
     )
     tile_count = right_basis.shape[1]
     turned_left = jnp.einsum("lab,lac->lbc", left_basis, weight_grads, precision=highest)
@@ -509,26 +510,30 @@
     "local_ff": 34,
     "local_back": 81,
     "backward_global": 90,
+    "last_transfers": 60,
     "adam_update": 5,
 }
 
 
 def group_at(rel):
-    mine = lax.axis_index("tensor")
+    mine = lax.axis_index(TENSOR)
     return 2 * ((mine // 2 + rel // 2) % 2) + (mine % 2 + rel % 2) % 2
 
 
+CORE, X, Y, Z1, Z2 = range(5)
+
+
 def partner_of(hop):
-    dp, tensor = lax.axis_index("dp"), lax.axis_index("tensor")
-    if hop == "core":
-        return {"tensor": tensor + 1 - 2 * (tensor % 2)}
-    if hop == "x":
-        return {"tensor": (tensor + 2) % 4}
-    if hop == "y":
-        return {"dp": dp + 1 - 2 * (dp % 2)}
-    if hop == "z1":
-        return {"dp": dp + 2 - 4 * ((dp // 2) % 2)}
-    return {"dp": (dp + 4) % 8}
+    dp, tensor = lax.axis_index(DP), lax.axis_index(TENSOR)
+    if hop == CORE:
+        return {TENSOR: tensor + 1 - 2 * (tensor % 2)}
+    if hop == X:
+        return {TENSOR: (tensor + 2) % 4}
+    if hop == Y:
+        return {DP: dp + 1 - 2 * (dp % 2)}
+    if hop == Z1:
+        return {DP: dp + 2 - 4 * ((dp // 2) % 2)}
+    return {DP: (dp + 4) % 8}
 
 
 def greet(hops):
@@ -724,7 +729,7 @@
         + [spec(layer, third) for layer in range(2) for third in range(3)],
         out_specs=[held(one.shape) for one in shapes],
         out_shape=shapes,
-        limit=24,
+        limit=60,
         name="prep_rows",
     )
     return found[:3], found[3:]
@@ -751,9 +756,17 @@
         in_specs=[IN_SMEM] + [VMEM_WHOLE] * 7,
         out_specs=[VMEM_WHOLE] * 2,
         out_shape=[shaped(rows.shape, jnp.float32), shaped((4, rows.shape[1]), jnp.float32)],
-        limit=16,
+        limit=60,
         name="input_grad",
     )
+
+
+forward_order = (
+    0, 12, 37, 4, 36, 50, 49, 66, 38, 8, 2, 1, 51, 43, 13, 15, 14, 24, 5, 3, 6, 16, 39, 9, 10, 67, 68, 18, 17,
+    20, 85, 86, 45, 87, 44, 88, 69, 72, 52, 53, 73, 54, 74, 75, 55, 41, 22, 76, 56, 25, 7, 27, 26, 77, 62, 78,
+    64, 63, 21, 40, 11, 19, 28, 70, 46, 65, 23, 71, 42, 89, 30, 32, 29, 90, 91, 92, 79, 57, 58, 80, 59, 81,
+    60, 82, 61, 31, 34, 33, 83, 48, 84, 35, 47,
+)
 
 
 def forward_body(
@@ -768,7 +781,7 @@
     span = 4 * share
     length = info_ref[1]
     scale = HD ** (-0.5)
-    flying, filed, from_parts, numbers = [], [], [], []
+    flying, filed, numbers = [], [], []
 
     def fly(hop, source, target):
         at = len(numbers)
@@ -784,76 +797,126 @@
         filed.append(copy)
         return copy
 
-    def first(shard, whole):
-        return fly("z2", shard, whole.at[pl.ds(owned, owned)])
-
-    def second(whole, begin=0):
-        return fly("z1", whole.at[pl.ds(begin, 2 * owned)], whole.at[pl.ds(begin + 2 * owned, 2 * owned)])
-
-    def across(whole):
-        return fly("y", whole.at[pl.ds(0, half)], whole.at[pl.ds(half, half)])
-
-    def over(hop, stack, begin, to, rows=half, start=0):
+    quarter = half // 2
+    arrived = set()
+    named = {}
+
+    def need(*names):
+        for name in names:
+            if name not in arrived:
+                arrived.add(name)
+                named[name].wait_recv()
+
+    def same(hop, whole, begin, rows, shift):
+        return lambda: fly(hop, whole.at[pl.ds(begin, rows)], whole.at[pl.ds(begin + shift, rows)])
+
+    def level(hop, stack, begin, to, start, rows):
         here = pl.ds(start, rows)
-        return fly(hop, stack.at[begin, here], stack.at[to, here])
-
-    greet(("core", "x", "y", "z1", "z2"))
-    ga_2 = first(ga_s, ga)
-    normed_x = fly("x", normed_ref, na.at[pl.ds(2 * share, share)])
-    normed_core = fly("core", normed_ref, na.at[pl.ds(share, share)])
-    ld_x = fly("x", ld_s, ld.at[2, pl.ds(0, owned)])
-    ld_y = fly("y", ld_s, ld.at[0, pl.ds(half, owned)])
-    la_2 = first(la_s, la.at[0])
-    own = [
-        file(shard, whole.at[pl.ds(0, owned)])
-        for shard, whole in ((ga_s, ga), (la_s, la.at[0]), (gu_s, gu), (gd_s, gd), (lu_s, lu.at[0]), (ld_s, ld.at[0]))
-    ]
-    na[pl.ds(0, share), :] = normed_ref[...]
-    for one in own:
-        one.wait()
-    ga_2.wait_recv()
-    ga_1 = second(ga)
-    gu_2 = first(gu_s, gu)
-    normed_x.wait_recv()
-    normed_xc = fly("core", na.at[pl.ds(2 * share, share)], na.at[pl.ds(3 * share, share)])
-    ld_x.wait_recv()
-    ld_xy = fly("y", ld.at[2, pl.ds(0, owned)], ld.at[2, pl.ds(half, owned)])
-    la_2.wait_recv()
-    la_1 = second(la.at[0])
-    gd_2 = first(gd_s, gd)
-    ga_1.wait_recv()
-    ga_y = across(ga)
-    a_near = file(ga.at[pl.ds(0, half)], a_v.at[pl.ds(0, half)])
-    gu_2.wait_recv()
-    gu_1 = second(gu)
-    lu_2 = first(lu_s, lu.at[0])
-    la_1.wait_recv()
-    la_x = over("x", la, 0, 2)
-    la_y = across(la.at[0])
-    la_c = over("core", la, 0, 1)
-    gd_2.wait_recv()
-    gd_1 = second(gd)
-    gu_1.wait_recv()
-    gu_y = across(gu)
-    u_near = file(gu.at[pl.ds(0, half)], u_v.at[pl.ds(0, half)])
-    normed_core.wait_recv()
-    normed_xc.wait_recv()
-    ga_y.wait_recv()
-    a_far = file(ga.at[pl.ds(half, half)], a_v.at[pl.ds(half, half)])
-    na_out = file(na, na_h)
-    a_near.wait()
-    a_far.wait()
-
-    for rel in range(4):
-        at = pl.ds(pl.multiple_of(group_at(rel) * share, share), share)
-        full = both(na[rel * share : (rel + 1) * share, :], a_v[:half, : 3 * width], a_v[half:, : 3 * width])
-        qkv_ref[at, :] = full.astype(jnp.bfloat16)
-    acc[:, :width] = jnp.zeros((span, width), jnp.float32)
-    lse_wide[...] = jnp.zeros_like(lse_wide)
+        return lambda: fly(hop, stack.at[begin, here], stack.at[to, here])
+
+    moves = {}
+    for letter, shard, whole in (("A", ga_s, ga), ("U", gu_s, gu), ("D", gd_s, gd)):
+        moves["g2" + letter] = (
+            (lambda shard, whole: lambda: fly(Z2, shard, whole.at[pl.ds(owned, owned)]))(shard, whole),
+            (),
+        )
+        moves["g1" + letter] = (same(Z1, whole, 0, quarter, quarter), ("g2" + letter, "own"))
+        moves["gy0" + letter] = (same(Y, whole, 0, quarter, half), ("g2" + letter, "own"))
+        moves["gy1" + letter] = (same(Y, whole, quarter, quarter, half), ("g1" + letter,))
+    for letter, shard, stack in (("A", la_s, la), ("U", lu_s, lu)):
+        near = stack.at[0]
+        moves["l2" + letter] = (
+            (lambda shard, near: lambda: fly(Z2, shard, near.at[pl.ds(owned, owned)]))(shard, near),
+            (),
+        )
+        moves["l1" + letter] = (same(Z1, near, 0, quarter, quarter), ("l2" + letter, "own"))
+        for at in range(2):
+            source = ("l2" + letter, "own") if at == 0 else ("l1" + letter,)
+            moves[f"ly{at}{letter}"] = (same(Y, near, at * quarter, quarter, half), source)
+            moves[f"lx{at}{letter}"] = (level(X, stack, 0, 2, at * quarter, quarter), source)
+            if letter == "A":
+                moves[f"lf{at}{letter}"] = (
+                    level(X, stack, 0, 2, half + at * quarter, quarter),
+                    (f"ly{at}{letter}",),
+                )
+            else:
+                moves[f"lf{at}{letter}"] = (
+                    same(Y, stack.at[2], at * quarter, quarter, half),
+                    (f"lx{at}{letter}",),
+                )
+        moves["cn" + letter] = (level(CORE, stack, 0, 1, 0, half), ("l2" + letter, "l1" + letter, "own"))
+        moves["cf" + letter] = (level(CORE, stack, 0, 1, half, half), ("ly0" + letter, "ly1" + letter))
+        moves["cx" + letter] = (level(CORE, stack, 2, 3, 0, half), ("lx0" + letter, "lx1" + letter))
+        moves["cxf" + letter] = (level(CORE, stack, 2, 3, half, half), ("lf0" + letter, "lf1" + letter))
+    moves["dx"] = (lambda: fly(X, ld_s, ld.at[2, pl.ds(0, owned)]), ())
+    moves["dy"] = (lambda: fly(Y, ld_s, ld.at[0, pl.ds(half, owned)]), ())
+    moves["dxy"] = (same(Y, ld.at[2], 0, owned, half), ("dx",))
+    for at, source in enumerate((("own",), ("dy",), ("dx",), ("dxy",))):
+        stack, begin = ld.at[2 * (at // 2)], half * (at % 2)
+        moves[f"d2{at}"] = (same(Z2, stack, begin, owned, owned), source)
+        moves[f"d1{at}"] = (same(Z1, stack, begin, quarter, quarter), (f"d2{at}",) + source)
+    moves["cdn"] = (level(CORE, ld, 0, 1, 0, D), ("d10", "d11", "d20", "d21", "dy", "own"))
+    moves["cdx"] = (level(CORE, ld, 2, 3, 0, D), ("d12", "d13", "d22", "d23", "dx", "dxy"))
+    moves["nx"] = (lambda: fly(X, normed_ref, na.at[pl.ds(2 * share, share)]), ())
+    moves["nc"] = (lambda: fly(CORE, normed_ref, na.at[pl.ds(share, share)]), ())
+    moves["nxc"] = (same(CORE, na, 2 * share, share, share), ("nx",))
+    strip = share // 2
+    strips = [pl.ds(at * strip, strip) for at in range(2)]
+
+    def sums_moves(far, near, over, which):
+        for at, name in enumerate(far):
+            moves[name] = (
+                (lambda rows: lambda: fly(CORE, parts.at[3, rows], met_core.at[2 * which, rows]))(strips[at]),
+                (),
+            )
+        moves[near] = (lambda: fly(CORE, parts.at[1], met_core.at[2 * which + 1]), ())
+        for at, name in enumerate(over):
+            moves[name] = (
+                (lambda rows: lambda: fly(X, sends_x.at[which, rows], met_x.at[which, rows]))(strips[at]),
+                (),
+            )
+
+    sums_moves(("c3a", "c3b"), "c1", ("sx0", "sx1"), 0)
+    sums_moves(("e3a", "e3b"), "e1", ("tx0", "tx1"), 1)
+    for at in range(2):
+        moves[f"ox{at}"] = (same(X, nb, at * strip, strip, 2 * share), ())
+    moves["oc"] = (same(CORE, nb, 0, share, share), ())
+    moves["oxc"] = (same(CORE, nb, 2 * share, share, share), ("ox0", "ox1"))
+
+    def do_own():
+        copies = [
+            file(shard, whole.at[pl.ds(0, owned)])
+            for shard, whole in (
+                (ga_s, ga), (la_s, la.at[0]), (gu_s, gu), (gd_s, gd), (lu_s, lu.at[0]), (ld_s, ld.at[0]),
+            )
+        ]
+        na[pl.ds(0, share), :] = normed_ref[...]
+        for one in copies:
+            one.wait()
+
+    def load(letter, whole, target):
+        need("g2" + letter, "g1" + letter, "gy0" + letter, "gy1" + letter)
+        return file(whole, target)
+
+    def do_load_a():
+        load("A", ga, a_v).wait()
+
+    def do_qkv():
+        need("nx", "nc", "nxc")
+        outgoing.append(file(na, na_h))
+        for rel in range(4):
+            at = pl.ds(pl.multiple_of(group_at(rel) * share, share), share)
+            full = both(
+                na[rel * share : (rel + 1) * share, :], a_v[:half, : 3 * width], a_v[half:, : 3 * width]
+            )
+            qkv_ref[at, :] = full.astype(jnp.bfloat16)
+        acc[:, :width] = jnp.zeros((span, width), jnp.float32)
+        lse_wide[...] = jnp.zeros_like(lse_wide)
+
     head_of = lax.broadcasted_iota(jnp.int32, (1, width), 1) // HD
     lane = lax.broadcasted_iota(jnp.int32, (1, 128), 1)
 
-    def per_head(head):
+    def do_head(head):
         own_lanes = head_of == head
         for block in range(4):
             rows = slice(block * share, (block + 1) * share)
@@ -871,24 +934,9 @@
             acc[rows, :width] += dot_rows(prob, value)
             lse_wide[rows, :] = jnp.where(lane == head, top + jnp.log(total), lse_wide[rows, :])
 
-    heads = width // HD
-    pl.loop(0, heads // 2)(per_head)
-    gd_1.wait_recv()
-    gd_y = across(gd)
-    d_near = file(gd.at[pl.ds(0, half)], d_v.at[pl.ds(0, half)])
-    lu_2.wait_recv()
-    lu_1 = second(lu.at[0])
-    ld_y.wait_recv()
-    ld_xy.wait_recv()
-    ld_blocks = [(index, begin) for index in (0, 2) for begin in (0, half)]
-
-    def ld_first(index, begin):
-        return fly("z2", ld.at[index, pl.ds(begin, owned)], ld.at[index, pl.ds(begin + owned, owned)])
-
-    ld_2 = [ld_first(*ld_blocks[0]), ld_first(*ld_blocks[1])]
-    pl.loop(heads // 2, heads)(per_head)
-    mixed_ref[...] = acc[:, :width].astype(jnp.bfloat16)
-    lse_ref[...] = jnp.transpose(lse_wide[...])[: lse_ref.shape[0], :]
+    def do_mix():
+        mixed_ref[...] = acc[:, :width].astype(jnp.bfloat16)
+        lse_ref[...] = jnp.transpose(lse_wide[...])[: lse_ref.shape[0], :]
 
     def out_part(rel):
         at = pl.ds(pl.multiple_of(group_at(rel) * share, share), share)
@@ -896,25 +944,24 @@
         parts[rel, :, :half] = dot_transposed(rows, a_v[:half, 3 * width :]).astype(jnp.bfloat16)
         parts[rel, :, half:] = dot_transposed(rows, a_v[half:, 3 * width :]).astype(jnp.bfloat16)
 
-    strip = share // 2
-    strips = [pl.ds(at * strip, strip) for at in range(2)]
-
-    def scatter(which, fill):
-        fill(3)
-        from_far = [fly("core", parts.at[3, rows], met_core.at[2 * which, rows]) for rows in strips]
-        fill(2)
-        fill(1)
-        from_near = fly("core", parts.at[1], met_core.at[2 * which + 1])
-        from_parts.extend(from_far + [from_near])
-        fill(0)
-        from_x = []
-        for rows, one in zip(strips, from_far):
-            one.wait_recv()
+    def down_part(rel):
+        parts[rel] = acc[rel * share : (rel + 1) * share, :].astype(jnp.bfloat16)
+
+    def several(act_on, *values):
+        def do():
+            for value in values:
+                act_on(value)
+
+        return do
+
+    def do_add(which, at, name):
+        def do():
+            need(name)
+            rows = strips[at]
             total = parts[2, rows, :].astype(jnp.float32) + met_core[2 * which, rows, :].astype(jnp.float32)
             sends_x[which, rows, :] = total.astype(jnp.bfloat16)
-            from_x.append(fly("x", sends_x.at[which, rows], met_x.at[which, rows]))
-        from_near.wait_recv()
-        return from_x
+
+        return do
 
     def gathered(which, rows, base):
         return (
@@ -924,88 +971,76 @@
             + met_x[which, rows, :].astype(jnp.float32)
         )
 
-    from_x = scatter(0, out_part)
-    over_x = []
-    for rows, one in zip(strips, from_x):
-        one.wait_recv()
-        total = gathered(0, rows, rows_ref[rows, :].astype(jnp.float32))
-        middle_ref[rows, :] = total
-        nb[rows, :] = norm_rows(total, gains_ref[1:2, :]).astype(jnp.bfloat16)
-        over_x.append(fly("x", nb.at[rows], nb.at[pl.ds(2 * share + rows.start, strip)]))
-    normed_core = fly("core", nb.at[pl.ds(0, share)], nb.at[pl.ds(share, share)])
-    la_y.wait_recv()
-    la_fx = over("x", la, 0, 2, start=half)
-    la_fc = over("core", la, 0, 1, start=half)
-    la_x.wait_recv()
-    la_xc = over("core", la, 2, 3)
-    lu_1.wait_recv()
-    lu_x = over("x", lu, 0, 2)
-    lu_y = across(lu.at[0])
-    lu_c = over("core", lu, 0, 1)
-    ld_1 = []
-    for at in range(2):
-        ld_2[at].wait_recv()
-        index, begin = ld_blocks[at]
-        ld_1.append(second(ld.at[index], begin))
-        ld_2.append(ld_first(*ld_blocks[2 + at]))
-    for one in over_x:
-        one.wait_recv()
-    normed_xc = fly("core", nb.at[pl.ds(2 * share, share)], nb.at[pl.ds(3 * share, share)])
-    gu_y.wait_recv()
-    u_far = file(gu.at[pl.ds(half, half)], u_v.at[pl.ds(half, half)])
-    acc[...] = jnp.zeros_like(acc)
-    normed_core.wait_recv()
-    normed_xc.wait_recv()
-    nb_out = file(nb, nb_h)
-    gd_y.wait_recv()
-    d_far = file(gd.at[pl.ds(half, half)], d_v.at[pl.ds(half, half)])
-    for one in (u_near, u_far, d_near, d_far):
-        one.wait()
-    tile = 256
-    hidden_out = []
-    for at in range(u_v.shape[1] // tile):
-        lanes = slice(at * tile, (at + 1) * tile)
+    def do_middle(at):
+        def do():
+            need("c1", f"sx{at}")
+            rows = strips[at]
+            total = gathered(0, rows, rows_ref[rows, :].astype(jnp.float32))
+            middle_ref[rows, :] = total
+            nb[rows, :] = norm_rows(total, gains_ref[1:2, :]).astype(jnp.bfloat16)
+
+        return do
+
+    def do_load_u():
+        load("U", gu, u_v).wait()
+        acc[...] = jnp.zeros_like(acc)
+
+    def do_load_d():
+        copy = load("D", gd, d_v)
+        need("oc", "oxc", "ox0", "ox1")
+        outgoing.append(file(nb, nb_h))
+        copy.wait()
+
+    def do_ff(at):
+        lanes = slice(at * 256, (at + 1) * 256)
         active, slope = gelu_both(both(nb[...], u_v[:half, lanes], u_v[half:, lanes]))
         act[:, lanes] = active
         slp[:, lanes] = slope
         for side in range(2):
             cols_at = slice(side * half, (side + 1) * half)
             acc[:, cols_at] += dot_transposed(active, d_v[side * half : (side + 1) * half, lanes])
-        if at == 1:
-            for which in (2, 3):
-                ld_2[which].wait_recv()
-                index, begin = ld_blocks[which]
-                ld_1.append(second(ld.at[index], begin))
-    hidden_out = [file(act, active_h), file(slp, slope_h)]
-
-    def down_part(rel):
-        parts[rel] = acc[rel * share : (rel + 1) * share, :].astype(jnp.bfloat16)
-
-    for one in from_parts:
-        one.wait_send()
-        flying[:] = [other for other in flying if other is not one]
-    from_x = scatter(1, down_part)
-    la_fx.wait_recv()
-    la_fxc = over("core", la, 2, 3, start=half)
-    lu_x.wait_recv()
-    lu_xy = across(lu.at[2])
-    lu_xc = over("core", lu, 2, 3)
-    for rows, one in zip(strips, from_x):
-        one.wait_recv()
-        out_ref[rows, :] = gathered(1, rows, middle_ref[rows, :])
-    lu_y.wait_recv()
-    lu_fc = over("core", lu, 0, 1, start=half)
-    for one in ld_1[:2]:
-        one.wait_recv()
-    ld_c = over("core", ld, 0, 1, rows=D)
-    for one in ld_1[2:]:
-        one.wait_recv()
-    ld_xc = over("core", ld, 2, 3, rows=D)
-    lu_xy.wait_recv()
-    lu_fxc = over("core", lu, 2, 3, start=half)
-    for one in (la_c, la_fc, la_xc, la_fxc, lu_c, lu_fc, lu_xc, lu_fxc, ld_c, ld_xc):
-        one.wait_recv()
-    for one in [na_out, nb_out] + hidden_out:
+
+    def do_q3():
+        outgoing.extend([file(act, active_h), file(slp, slope_h)])
+        for name in ("c3a", "c3b", "c1"):
+            named[name].wait_send()
+            flying[:] = [other for other in flying if other is not named[name]]
+        down_part(3)
+
+    def do_result(at):
+        def do():
+            need("e1", f"tx{at}")
+            rows = strips[at]
+            out_ref[rows, :] = gathered(1, rows, middle_ref[rows, :])
+
+        return do
+
+    outgoing = []
+    steps = {
+        "own": do_own, "load_a": do_load_a, "qkv": do_qkv, "mix": do_mix, "load_u": do_load_u, "load_d": do_load_d,
+        "p3": several(out_part, 3), "p2": several(out_part, 2, 1), "p0": several(out_part, 0),
+        "s0": do_add(0, 0, "c3a"), "s1": do_add(0, 1, "c3b"), "m0": do_middle(0), "m1": do_middle(1),
+        "q3": do_q3, "q1": several(down_part, 2, 1, 0), "t0": do_add(1, 0, "e3a"), "t1": do_add(1, 1, "e3b"),
+        "r0": do_result(0), "r1": do_result(1),
+    }
+    for at in range(width // HD):
+        steps[f"h{at}"] = several(do_head, at)
+    for at in range(u_v.shape[1] // 256):
+        steps[f"f{at}"] = several(do_ff, at)
+
+    greet((CORE, X, Y, Z1, Z2))
+    names = list(moves) + list(steps)
+    for place in forward_order:
+        name = names[place]
+        if name in steps:
+            steps[name]()
+            arrived.add(name)
+        else:
+            start, before = moves[name]
+            need(*before)
+            named[name] = start()
+    need(*named)
+    for one in outgoing:
         one.wait()
     for one in flying:
         one.wait_send()
@@ -1048,11 +1083,11 @@
             pltpu.VMEM((4, share, D), small),
             pltpu.VMEM((2, share, D), small),
             pltpu.VMEM((2, share, D), small),
-            pltpu.SemaphoreType.DMA((20,)),
-            pltpu.SemaphoreType.DMA((64,)),
-            pltpu.SemaphoreType.DMA((64,)),
+            pltpu.SemaphoreType.DMA((24,)),
+            pltpu.SemaphoreType.DMA((96,)),
+            pltpu.SemaphoreType.DMA((96,)),
         ],
-        hops=("core", "x", "y", "z1", "z2"),
+        hops=(CORE, X, Y, Z1, Z2),
         limit=56,
         name="forward_global",
     )
@@ -1060,11 +1095,12 @@
 
 def backward_body(
     info_ref, small_ref, grad_ref, middle_ref, gains_ref, lse_ref, up_h, down_h, heads_h, active_h, slope_h,
-    nb_h, na_h, qkv_h, mixed_h, u_near_h, u_far_h, d2_h, d0_h, h2_far_h, h0_far_h,
-    mid_ref, sum_ref, gain_ref, gd_near_h, gd_met_h, gu_near_h, gu_far_h, gh_near_h, gh_far_h, lu_keep_h,
-    lu_met_h, ld_keep_h, ld_met_h, h2_met_h, h0_met_h,
+    nb_h, na_h, qkv_h, mixed_h, u_near_h, u_far_h, h2_far_h,
+    h0_far_h, h2_near_h,
+    mid_ref, sum_ref, gain_ref, gu_near_h, gu_met_h, gh_near_h, gh_far_h, lu_keep_h, lu_met_h, gd_keep_h,
+    gd_met_h, h2_met_h, h_first_h, h2_first_h,
     rows_one, rows_two, up_v, down_v, heads_v, act, slp, dup, left_t, right_v, grads_v, qkv_v, mixed_v, dqkv,
-    dmix, dq_t, dk_acc, dv_acc, center, k_t, parts, met_core, met_x, sends_x, u_v, u_met, d_v, d_met, z_met,
+    dmix, dq_t, dk_acc, dv_acc, center, k_t, parts, met_core, met_x, sends_x, u_v, u_met, d_v, d_met, z_met, h_v,
     sems, send, recv,
 ):
     share = small_ref.shape[0]
@@ -1108,19 +1144,17 @@
             total = total + term.astype(jnp.float32)
         return total
 
-    greet(("core", "x", "y", "z1", "z2"))
-    small_x = fly("x", small_ref, rows_one.at[pl.ds(2 * share, share)])
-    small_core = fly("core", small_ref, rows_one.at[pl.ds(share, share)])
-    u_y = fly("y", u_far_h, u_met)
-    d_first = fly("x", d2_h.at[pl.ds(0, quarter)], d_met.at[pl.ds(0, quarter)])
-    h2_y = fly("y", h2_far_h, h2_met_h)
-    h0_y = fly("y", h0_far_h, h0_met_h)
+    greet((CORE, X, Y, Z1, Z2))
+    small_x = fly(X, small_ref, rows_one.at[pl.ds(2 * share, share)])
+    small_core = fly(CORE, small_ref, rows_one.at[pl.ds(share, share)])
+    u_y = fly(Y, u_far_h, u_met)
+    h_first = fly(X, h2_far_h.at[pl.ds(0, quarter)], h_v.at[0])
     first = [file(down_h, down_v), file(slope_h, slp), file(up_h, up_v)]
     active_in = file(active_h, act)
     nb_in = file(nb_h, right_v)
     u_in = file(u_near_h, u_v)
+    h_in = file(h0_far_h.at[pl.ds(0, quarter)], h_v.at[1])
     attention_in = [file(heads_h, heads_v), file(qkv_h, qkv_v), file(mixed_h, mixed_v)]
-    d_in = file(d0_h, d_v)
     rows_one[pl.ds(0, share), :] = small_ref[...]
     for one in first:
         one.wait()
@@ -1139,7 +1173,7 @@
     small_core.wait_recv()
     ff_back(1)
     small_x.wait_recv()
-    small_xc = fly("core", rows_one.at[pl.ds(2 * share, share)], rows_one.at[pl.ds(3 * share, share)])
+    small_xc = fly(CORE, rows_one.at[pl.ds(2 * share, share)], rows_one.at[pl.ds(3 * share, share)])
     ff_back(2)
     small_xc.wait_recv()
     ff_back(3)
@@ -1147,15 +1181,15 @@
     strips = [pl.ds(at * strip, strip) for at in range(2)]
 
     def scatter_start(which):
-        from_far = [fly("core", parts.at[3, rows], met_core.at[2 * which, rows]) for rows in strips]
-        return from_far, fly("core", parts.at[1], met_core.at[2 * which + 1])
+        from_far = [fly(CORE, parts.at[3, rows], met_core.at[2 * which, rows]) for rows in strips]
+        return from_far, fly(CORE, parts.at[1], met_core.at[2 * which + 1])
 
     def scatter_on(which, from_far):
         from_x = []
         for rows, one in zip(strips, from_far):
             one.wait_recv()
             sends_x[which, rows, :] = summed(parts[2, rows, :], met_core[2 * which, rows, :]).astype(jnp.bfloat16)
-            from_x.append(fly("x", sends_x.at[which, rows], met_x.at[which, rows]))
+            from_x.append(fly(X, sends_x.at[which, rows], met_x.at[which, rows]))
         return from_x
 
     def gathered(which, rows):
@@ -1165,14 +1199,18 @@
     for rel in range(4):
         left_t[:, block(rel)] = jnp.transpose(rows_one[block(rel), :])
     from_x = scatter_on(0, from_far)
+    h_in.wait()
+    h_first.wait_recv()
+    h_v[1] = summed(h_v[0], h_v[1]).astype(jnp.bfloat16)
+    h_y = fly(Y, h_v.at[1], h_first_h)
     active_in.wait()
     for side in range(2):
         rows = slice(side * half, (side + 1) * half)
         for tile in range(2):
             lanes = slice(tile * half, (tile + 1) * half)
             grads_v[0, rows, lanes] = dot_rows(left_t[rows, :], act[:, lanes]).astype(jnp.bfloat16)
-    gd_y = fly("y", grads_v.at[0, pl.ds(half, half)], gd_met_h)
-    results = [file(grads_v.at[0, pl.ds(0, half)], gd_near_h)]
+    gd_y = fly(Y, grads_v.at[0, pl.ds(half, half)], d_met)
+    results = []
     from_near.wait_recv()
     gain_total = jnp.zeros((1, D), jnp.float32)
     over_x = []
@@ -1183,14 +1221,15 @@
         mid_ref[rows, :] = total
         rows_two[rows, :] = total.astype(jnp.bfloat16)
         gain_total = gain_total + gain_grad
-        over_x.append(fly("x", rows_two.at[rows], rows_two.at[pl.ds(2 * share + rows.start, strip)]))
+        over_x.append(fly(X, rows_two.at[rows], rows_two.at[pl.ds(2 * share + rows.start, strip)]))
     gain_ref[...] = gain_total
-    small_core = fly("core", rows_two.at[pl.ds(0, share)], rows_two.at[pl.ds(share, share)])
-    d_second = fly("x", d2_h.at[pl.ds(quarter, quarter)], d_met.at[pl.ds(quarter, quarter)])
+    small_core = fly(CORE, rows_two.at[pl.ds(0, share)], rows_two.at[pl.ds(share, share)])
+    h_second = fly(X, h2_far_h.at[pl.ds(quarter, quarter)], h2_met_h)
+    h_third = fly(X, h2_near_h.at[pl.ds(0, quarter)], h2_first_h)
     u_y.wait_recv()
     u_in.wait()
     u_v[...] = summed(u_v[...], u_met[...]).astype(jnp.bfloat16)
-    u_1 = fly("z1", u_v.at[pl.ds(quarter, quarter)], z_met.at[0])
+    u_1 = fly(Z1, u_v.at[pl.ds(quarter, quarter)], z_met.at[0])
     nb_in.wait()
     left_t[...] = jnp.transpose(right_v[...])
     na_in = file(na_h, right_v)
@@ -1199,10 +1238,8 @@
         for tile in range(2):
             lanes = slice(tile * half, (tile + 1) * half)
             grads_v[1, rows, lanes] = dot_rows(left_t[rows, :], dup[:, lanes]).astype(jnp.bfloat16)
-    results += [
-        file(grads_v.at[1, pl.ds(0, half)], gu_near_h),
-        file(grads_v.at[1, pl.ds(half, half)], gu_far_h),
-    ]
+    gu_y = fly(Y, grads_v.at[1, pl.ds(half, half)], gu_met_h)
+    results.append(file(grads_v.at[1, pl.ds(0, half)], gu_near_h))
     for one in attention_in:
         one.wait()
 
@@ -1224,11 +1261,11 @@
     mix_back(1)
     for one in over_x:
         one.wait_recv()
-    small_xc = fly("core", rows_two.at[pl.ds(2 * share, share)], rows_two.at[pl.ds(3 * share, share)])
+    small_xc = fly(CORE, rows_two.at[pl.ds(2 * share, share)], rows_two.at[pl.ds(3 * share, share)])
     mix_back(2)
     u_1.wait_recv()
     u_v[:quarter, :] = summed(u_v[:quarter, :], z_met[0]).astype(jnp.bfloat16)
-    u_2 = fly("z2", u_v.at[pl.ds(owned, owned)], lu_met_h)
+    u_2 = fly(Z2, u_v.at[pl.ds(owned, owned)], lu_met_h)
     results.append(file(u_v.at[pl.ds(0, owned)], lu_keep_h))
     small_xc.wait_recv()
     mix_back(3)
@@ -1260,11 +1297,9 @@
     dqkv[:, :width] = (jnp.transpose(dq_t[...]) * scale).astype(jnp.bfloat16)
     dqkv[:, width : 2 * width] = dk_acc[...].astype(jnp.bfloat16)
     dqkv[:, 2 * width :] = dv_acc[...].astype(jnp.bfloat16)
-    d_in.wait()
-    d_first.wait_recv()
-    d_second.wait_recv()
-    d_v[...] = summed(d_v[...], d_met[...]).astype(jnp.bfloat16)
-    d_1 = fly("z1", d_v.at[pl.ds(quarter, quarter)], z_met.at[1])
+    gd_y.wait_recv()
+    d_v[...] = summed(grads_v[0, :half, :], d_met[...]).astype(jnp.bfloat16)
+    d_1 = fly(Z1, d_v.at[pl.ds(quarter, quarter)], z_met.at[1])
     for one in from_far + [from_near]:
         over(one)
 
@@ -1284,7 +1319,6 @@
     for rel in range(4):
         left_t[:, place(rel)] = jnp.transpose(right_v[block(rel), :])
     over(gd_y)
-    results[0].wait()
     for side in range(2):
         rows = slice(side * half, (side + 1) * half)
         grads_v[0, rows, : 3 * width] = dot_rows(left_t[rows, :], dqkv[...]).astype(jnp.bfloat16)
@@ -1299,15 +1333,15 @@
     ]
     d_1.wait_recv()
     d_v[:quarter, :] = summed(d_v[:quarter, :], z_met[1]).astype(jnp.bfloat16)
-    d_2 = fly("z2", d_v.at[pl.ds(owned, owned)], ld_met_h)
-    results.append(file(d_v.at[pl.ds(0, owned)], ld_keep_h))
+    d_2 = fly(Z2, d_v.at[pl.ds(owned, owned)], gd_met_h)
+    results.append(file(d_v.at[pl.ds(0, owned)], gd_keep_h))
     from_near.wait_recv()
     for rows, one in zip(strips, from_x):
         one.wait_recv()
         sum_ref[rows, :] = gathered(1, rows)
-    for one in (h2_y, h0_y, gd_y, u_2, d_2):
+    for one in (h_y, h_second, h_third, gu_y, u_2, d_2):
         one.wait_recv()
-    for one in results[1:]:
+    for one in results:
         one.wait()
     for one in flying:
         one.wait_send()
@@ -1322,16 +1356,16 @@
     return line.run(
         backward_body,
         (info, small, grad, middle, gains, lse, up, down, heads, active, slope, nb, na, qkv, mixed, *sums),
-        in_specs=[IN_SMEM] + [VMEM_WHOLE] * 5 + [IN_HBM] * 15,
-        out_specs=[VMEM_WHOLE] * 3 + [IN_HBM] * 12,
+        in_specs=[IN_SMEM] + [VMEM_WHOLE] * 5 + [IN_HBM] * 14,
+        out_specs=[VMEM_WHOLE] * 3 + [IN_HBM] * 11,
         out_shape=[
             shaped((share, D), jnp.float32),
             shaped((share, D), jnp.float32),
             shaped((1, D), jnp.float32),
         ]
-        + [shaped((half, columns), low)] * 6
+        + [shaped((half, columns), low)] * 4
         + [shaped((owned, columns), low)] * 4
-        + [shaped((half, columns), low)] * 2,
+        + [shaped((half // 2, columns), low)] * 3,
         scratch_shapes=[pltpu.VMEM((span, D), low)] * 2
         + [pltpu.VMEM((D, columns), low)] * 3
         + [pltpu.VMEM((span, columns), low)] * 3
@@ -1352,11 +1386,12 @@
         + [pltpu.VMEM((half, columns), low)] * 4
         + [
             pltpu.VMEM((2, half // 2, columns), low),
+            pltpu.VMEM((2, half // 2, columns), low),
             pltpu.SemaphoreType.DMA((24,)),
             pltpu.SemaphoreType.DMA((40,)),
             pltpu.SemaphoreType.DMA((40,)),
         ],
-        hops=("core", "x", "y", "z1", "z2"),
+        hops=(CORE, X, Y, Z1, Z2),
         limit=56,
         name="backward_global",
     )
@@ -1496,7 +1531,7 @@
             pltpu.VMEM((4, 2, half, 4 * width), jnp.bfloat16),
             pltpu.SemaphoreType.DMA((4, 2)),
         ],
-        limit=(52),
+        limit=52,
         name="local_heads",
     )
 
@@ -1579,7 +1614,7 @@
             pltpu.SemaphoreType.DMA((4, 2)),
             pltpu.SemaphoreType.DMA((4, 2)),
         ],
-        limit=(56),
+        limit=56,
         name="local_ff",
     )
 
@@ -1611,7 +1646,7 @@
             shaped((D, rows), jnp.bfloat16),
             shaped((rows, D), jnp.bfloat16),
         ],
-        limit=(24),
+        limit=60,
         name="seed_grads",
     )
 
@@ -1632,7 +1667,7 @@
     half = D // 2
     width = mixed_h.shape[2]
     scale = HD ** (-0.5)
-    greet(("core", "x", "y"))
+    greet((CORE, X, Y))
 
     def fetch(at, source, target):
         copy = pltpu.make_async_copy(source, target, sems.at[at])
@@ -1649,7 +1684,7 @@
         found.append(fetch(2, slope_h.at[rel], slp))
         return found + [fetch(3 + at, ups_h[2 * rel + at], weights.at[at]) for at in range(2)]
 
-    order = (3, 1, 2, 0)
+    order = (3, 2, 1, 0)
     waits = [fetch(5, grad_h, grad_v)] + fetch_ff(order[0])
     late = [fetch(6, grad_t_h, grad_t), fetch(7, active_h.at[order[0]], act), fetch(8, b_t_h, other_t)]
     later = [fetch(9, middle_h, mid), fetch(10, gout_h, gout_v), fetch(11, codes_h, codes_v)]
@@ -1671,11 +1706,11 @@
             waits = fetch_ff(order[step + 1])
         for one in late:
             one.wait()
-        if step == 1:
+        if step == 2:
             sent[0].wait_send()
-        if step >= 2:
-            sent[step - 2].wait_recv()
-        met = (None, None, pair_far, pair_near)[step]
+        if step % 2 == 1:
+            sent[step // 2].wait_recv()
+        met = (None, pair_far, None, pair_near)[step]
         for at in range(2):
             rows = slice(at * half, (at + 1) * half)
             for tile in range(2):
@@ -1691,15 +1726,15 @@
         if step < 3:
             late = [fetch(7, active_h.at[order[step + 1]], act)]
         if step == 0:
-            sent.append(give(0, "core", pair_out, pair_far))
+            sent.append(give(0, CORE, pair_out, pair_far))
+        elif step == 2:
+            sent.append(give(1, CORE, pair_out, pair_near))
         elif step == 1:
-            sent.append(give(1, "core", pair_out, pair_near))
-        elif step == 2:
-            x_far = give(2, "x", pair_far.at[1, pl.ds(half, half)], x_in.at[pl.ds(half, half)])
-            y_two = give(3, "y", pair_far.at[0, pl.ds(half, half)], y_far)
-            x_near = give(4, "x", pair_far.at[1, pl.ds(0, half)], x_in.at[pl.ds(0, half)])
+            x_far = give(2, X, pair_far.at[1, pl.ds(half, half)], x_in.at[pl.ds(half, half)])
+            y_two = give(3, Y, pair_far.at[0, pl.ds(half, half)], y_far)
+            x_near = give(4, X, pair_far.at[1, pl.ds(0, half)], x_in.at[pl.ds(0, half)])
         else:
-            y_zero = give(5, "y", pair_near.at[0, pl.ds(half, half)], y_near)
+            y_zero = give(5, Y, pair_near.at[0, pl.ds(half, half)], y_near)
 
     def fetch_heads(rel):
         found = [fetch(at, heads_h[2 * rel + at], weights.at[at]) for at in range(2)]
@@ -1764,11 +1799,11 @@
             lanes = slice(at * half, (at + 1) * half)
             term = dot_transposed(dup[:, : 3 * width], weights[at, :, : 3 * width])
             acc[:, lanes] = term if step == 0 else acc[:, lanes] + term
-        if step == 1:
+        if step == 2:
             heads_sent[0].wait_send()
-        if step >= 2:
-            heads_sent[step - 2].wait_recv()
-        met = (None, None, head_far, head_near)[step]
+        if step % 2 == 1:
+            heads_sent[step // 2].wait_recv()
+        met = (None, head_far, None, head_near)[step]
         for at in range(2):
             rows = slice(at * half, (at + 1) * half)
             three = dot_rows(other_t[rows, :], dup[:, : 3 * width])
@@ -1784,9 +1819,9 @@
         if step < 3:
             waits = fetch_heads(order[step + 1])
         if step == 0:
-            heads_sent.append(give(6, "core", head_out, head_far))
-        elif step == 1:
-            heads_sent.append(give(7, "core", head_out, head_near))
+            heads_sent.append(give(6, CORE, head_out, head_far))
+        elif step == 2:
+            heads_sent.append(give(7, CORE, head_out, head_near))
     total_gain = jnp.zeros((1, D), jnp.float32)
     total = jnp.zeros((frames, D), jnp.float32)
     for c in range(CB):
@@ -1862,9 +1897,143 @@
             pltpu.SemaphoreType.DMA((8,)),
             pltpu.SemaphoreType.DMA((8,)),
         ],
-        hops=("core", "x", "y"),
+        hops=(CORE, X, Y),
         limit=58,
         name="local_back",
+    )
+
+
+def last_body(
+    gains_ref, gu_near_h, gu_met_h, gh_near_h, gh_far_h, d0_h, d2_h, h0_near_h, h2_near_h, h0_far_h, h2_far_h,
+    h_first_h, h2_first_h,
+    gain_out_ref, gu_keep_h, gu_last_h, gh_keep_h, gh_last_h, d_keep_h, d_last_h, h_keep_h, h_send_h,
+    gain_v, gain_met, held_v, met_v, extra_v, z_met, sems, send, recv,
+):
+    half = D // 2
+    quarter = half // 2
+    owned = quarter // 2
+    flying, filed = [], []
+
+    def fly(hop, source, target):
+        at = len(flying)
+        copy = to_partner(hop, source, target, send.at[at], recv.at[at])
+        copy.start()
+        flying.append(copy)
+        return copy
+
+    def file(source, target):
+        copy = pltpu.make_async_copy(source, target, sems.at[len(filed)])
+        copy.start()
+        filed.append(copy)
+        return copy
+
+    def summed(*terms):
+        total = terms[0].astype(jnp.float32)
+        for term in terms[1:]:
+            total = total + term.astype(jnp.float32)
+        return total.astype(jnp.bfloat16)
+
+    greet((CORE, X, Y, Z1, Z2))
+    upper, lower = pl.ds(0, quarter), pl.ds(quarter, quarter)
+    gain_core = fly(CORE, gains_ref, gain_met.at[0])
+    gh_low, gh_up = [fly(Y, gh_far_h.at[rows], met_v.at[1, rows]) for rows in (lower, upper)]
+    d_low, d_up = [fly(X, d2_h.at[rows], met_v.at[2, rows]) for rows in (lower, upper)]
+    gu_in = [file(gu_near_h, held_v.at[0]), file(gu_met_h, met_v.at[0])]
+    far_in = [file(h0_far_h.at[lower], extra_v.at[0, lower]), file(h2_far_h, extra_v.at[1, lower])]
+    rest_in = [file(gh_near_h, held_v.at[1]), file(d0_h, held_v.at[2]), file(h0_near_h, held_v.at[3])]
+    rest_in += [file(h2_first_h, met_v.at[3, upper]), file(h_first_h, extra_v.at[2, upper])]
+    for one in gu_in:
+        one.wait()
+    held_v[0] = summed(held_v[0], met_v[0])
+    gu_1 = fly(Z1, held_v.at[0, lower], z_met.at[0])
+    gain_core.wait_recv()
+    gain_v[0] = gains_ref[...] + gain_met[0]
+    gain_x = fly(X, gain_v.at[0], gain_met.at[1])
+    h_x = fly(X, h2_near_h.at[lower], met_v.at[3, lower])
+    for one in far_in:
+        one.wait()
+    extra_v[0, quarter:, :] = summed(extra_v[0, quarter:, :], extra_v[1, quarter:, :])
+    h_y = fly(Y, extra_v.at[0, lower], extra_v.at[2, lower])
+    for one in rest_in:
+        one.wait()
+    done = []
+
+    def add(at, first):
+        rows = slice(0, quarter) if first else slice(quarter, half)
+        held_v[at, rows, :] = summed(held_v[at, rows, :], met_v[at, rows, :])
+
+    def second(at, first, last_h, keep_h):
+        first.wait_recv()
+        held_v[at, :quarter, :] = summed(held_v[at, :quarter, :], z_met[at])
+        done.append(file(held_v.at[at, pl.ds(0, owned)], keep_h))
+        return fly(Z2, held_v.at[at, pl.ds(owned, owned)], last_h)
+
+    gh_low.wait_recv()
+    add(1, False)
+    gh_1 = fly(Z1, held_v.at[1, lower], z_met.at[1])
+    d_low.wait_recv()
+    add(2, False)
+    gu_2 = second(0, gu_1, gu_last_h, gu_keep_h)
+    gh_up.wait_recv()
+    add(1, True)
+    gh_2 = second(1, gh_1, gh_last_h, gh_keep_h)
+    d_1 = fly(Z1, held_v.at[2, lower], z_met.at[2])
+    d_up.wait_recv()
+    add(2, True)
+    gain_x.wait_recv()
+    gain_v[1] = gain_v[0] + gain_met[1]
+    gain_y = fly(Y, gain_v.at[1], gain_met.at[2])
+    h_x.wait_recv()
+    h_y.wait_recv()
+    held_v[3] = summed(held_v[3], met_v[3], extra_v[2])
+    done.append(file(held_v.at[3, upper], h_keep_h))
+    done.append(file(held_v.at[3, lower], h_send_h))
+    gain_y.wait_recv()
+    gain_v[2] = gain_v[1] + gain_met[2]
+    gain_1 = fly(Z1, gain_v.at[2], gain_met.at[3])
+    d_1.wait_recv()
+    held_v[2, :quarter, :] = summed(held_v[2, :quarter, :], z_met[2])
+    done.append(file(held_v.at[2, pl.ds(0, owned)], d_keep_h))
+    done.append(file(held_v.at[2, pl.ds(owned, owned)], d_last_h))
+    gain_1.wait_recv()
+    gain_v[3] = gain_v[2] + gain_met[3]
+    gain_2 = fly(Z2, gain_v.at[3], gain_met.at[4])
+    gain_2.wait_recv()
+    gain_out_ref[...] = gain_v[3] + gain_met[4]
+    for one in (gu_2, gh_2):
+        one.wait_recv()
+    for one in done:
+        one.wait()
+    for one in flying:
+        one.wait_send()
+
+
+def last_transfers(line, gains, parts):
+    half, columns = parts[0].shape
+    owned = half // 4
+    low = jnp.bfloat16
+    return line.run(
+        last_body,
+        (gains, *parts),
+        in_specs=[VMEM_WHOLE] + [IN_HBM] * 12,
+        out_specs=[VMEM_WHOLE] + [IN_HBM] * 8,
+        out_shape=[shaped(gains.shape, jnp.float32)]
+        + [shaped((owned, columns), low)] * 6
+        + [shaped((2 * owned, columns), low)] * 2,
+        scratch_shapes=[
+            pltpu.VMEM((4,) + gains.shape, jnp.float32),
+            pltpu.VMEM((5,) + gains.shape, jnp.float32),
+            pltpu.VMEM((4, half, columns), low),
+            pltpu.VMEM((4, half, columns), low),
+            pltpu.VMEM((3, half, columns), low),
+            pltpu.VMEM((3, half // 2, columns), low),
+            pltpu.SemaphoreType.DMA((16,)),
+            pltpu.SemaphoreType.DMA((16,)),
+            pltpu.SemaphoreType.DMA((16,)),
+        ],
+        hops=(CORE, X, Y, Z1, Z2),
+        limit=60,
+        name="last_transfers",
     )
 
 
@@ -1891,7 +2060,7 @@
         in_specs=[spec(term) for term in terms],
         out_specs=[pl.BlockSpec((rows, columns), lambda step: (0, 0))],
         out_shape=[shaped((rows, columns), jnp.bfloat16)],
-        limit=(24),
+        limit=24,
         name="add_terms",
     )[0]
 
@@ -1972,7 +2141,7 @@
     new_ema_ref[0] = ema_decay * ema_ref[0] + (1.0 - ema_decay) * new_master
 
 
-def adam(line, layer, third, pieces, left, right, master, first, second, ema, before, tile=256):
+def adam(line, layer, third, pieces, left, right, master, first, second, ema, before, tile=512):
     owned, columns = pieces[0].shape
     steps = columns // tile
     first_step = third * steps
@@ -1998,33 +2167,25 @@
         out_specs=[state_spec] * 5,
         out_shape=[shaped(master.shape, jnp.float32)] * 5,
         aliases={8 + at: at for at in range(5)} if chained else {},
-        limit=(32),
+        limit=32,
         name="adam_update",
     )
 
 
 def hop_x(values):
-    return lax.ppermute(values, "tensor", [(at, at ^ 2) for at in range(4)])
+    return lax.ppermute(values, TENSOR, [(at, at ^ 2) for at in range(4)])
 
 
 def hop_core(values):
-    return lax.ppermute(values, "tensor", [(at, at ^ 1) for at in range(4)])
+    return lax.ppermute(values, TENSOR, [(at, at ^ 1) for at in range(4)])
 
 
 def hop_y(values):
-    return lax.ppermute(values, "dp", [(at, at ^ 1) for at in range(8)])
+    return lax.ppermute(values, DP, [(at, at ^ 1) for at in range(8)])
 
 
 def hop_z(values, step):
-    return lax.ppermute(values, "dp", [(at, at ^ (2 * step)) for at in range(8)])
-
-
-def total_everywhere(values):
-    for hop in (hop_core, hop_x, hop_y):
-        values = values + hop(values)
-    for step in (1, 2):
-        values = values + hop_z(values, step)
-    return values
+    return lax.ppermute(values, DP, [(at, at ^ (2 * step)) for at in range(8)])
 
 
 def shards_grid(
@@ -2046,10 +2207,10 @@
     share = frames_in.shape[0]
     owned = master.shape[1]
     groups = D // owned
-    heads_w = D // lax.axis_size("tensor")
-    ff_w = FF // lax.axis_size("tensor")
-    my_dp = lax.axis_index("dp")
-    my_group = lax.axis_index("tensor").astype(jnp.int32)
+    heads_w = D // lax.axis_size(TENSOR)
+    ff_w = FF // lax.axis_size(TENSOR)
+    my_dp = lax.axis_index(DP)
+    my_group = lax.axis_index(TENSOR).astype(jnp.int32)
 
     rel = jnp.array([2 * z + y for y in range(2) for z in (0, 2, 1, 3)], jnp.int32)
     owner_at = my_dp ^ rel
@@ -2087,42 +2248,36 @@
             line, layer, third, pieces, left_basis, right_basis, master, first_moment, second_moment, ema, before
         )
 
-    def depth_first(terms, split=()):
-        keep, send = sum_pieces(line, terms, split)
-        return keep, hop_z(send, 1)
-
     def depth_second(keep, met):
         keep, send = sum_pieces(line, [keep, met])
         return keep, hop_z(send, 2)
 
     (
-        grad_middle, grad_sum, gain_b, gd_near, gd_met, gu_near, gu_far, gh_near, gh_far, lu_keep, lu_met, ld_keep,
-        ld_met, h2_met, h0_met,
+        grad_middle, grad_sum, gain_b, gu_near, gu_met, gh_near, gh_far, lu_keep, lu_met, gd_keep, gd_met, h2_met,
+        h_first, h2_first,
     ) = backward_global(
         line, info, small, grad_global, middle, gains_here, lse, (g_up, g_down, g_heads), active, slope, normed_b,
-        normed_a, qkv, mixed, (u_near, u_far, d2, d0, h2_far, h0_far),
-    )
-    gu_met = hop_y(gu_far)
-    gh_met = hop_y(gh_far)
-    h2 = hop_x(add_rows(line, [h2_near, h2_met]))
-    gd = depth_first([gd_near, gd_met])
+        normed_a, qkv, mixed, (u_near, u_far, h2_far, h0_far, h2_near),
+    )
     input_grad, gain_grads = finish(
         line, source, rows_in, grad_sum, grad_middle, gains_here, (gain_b, gain_c, gain_d)
     )
-    gain_grads = total_everywhere(gain_grads)
+    (
+        gain_grads, gu_keep, gu_met, gh_keep, gh_met, ld_keep, ld_send, lh_keep, lh_send,
+    ) = last_transfers(
+        line,
+        gain_grads,
+        (gu_near, gu_met, gh_near, gh_far, d0, d2, h0_near, h2_near, h0_far, h2_met, h_first, h2_first),
+    )
+    lh_met = hop_z(lh_send, 1)
+    ld_met = hop_z(ld_send, 2)
     found = update(1, 1, (lu_keep, lu_met), None)
-    gd = depth_second(*gd)
+    found = update(0, 2, (gd_keep, gd_met), found)
+    found = update(0, 1, (gu_keep, gu_met), found)
+    lh = depth_second(lh_keep, lh_met)
+    found = update(0, 0, (gh_keep, gh_met), found)
     found = update(1, 2, (ld_keep, ld_met), found)
-    lh = depth_first([h0_near, h0_met, h2])
-    gu = depth_first([gu_near, gu_met])
-    found = update(0, 2, gd, found)
-    lh = depth_second(*lh)
-    gu = depth_second(*gu)
-    gh = depth_first([gh_near, gh_met])
     found = update(1, 0, lh, found)
-    found = update(0, 1, gu, found)
-    gh = depth_second(*gh)
-    found = update(0, 0, gh, found)
     weight_grads, new_master, new_first, new_second, new_ema = found
     new_gain_first = beta_first * gain_first + (1.0 - beta_first) * gain_grads
     new_gain_second = beta_second * gain_second + (1.0 - beta_second) * gain_grads * gain_grads
@@ -2143,35 +2298,35 @@
 
 
 def solution(mesh):
-    fits = mesh.shape["dp"] == 8 and mesh.shape["tensor"] == 4
+    fits = mesh.shape[DP] == 8 and mesh.shape[TENSOR] == 4
     return jax.shard_map(
         shards_grid if fits else shards_any,
         mesh=mesh,
         in_specs=(
-            P(("dp", "tensor"), None),
-            P(("dp", "tensor"), None, None),
-            P(("dp", "tensor"), None, None),
-            P("dp"),
+            P((DP, TENSOR), None),
+            P((DP, TENSOR), None, None),
+            P((DP, TENSOR), None, None),
+            P(DP),
             P(),
-            P(None, "dp", "tensor"),
-            P(None, "dp", "tensor"),
-            P(None, "dp", "tensor"),
-            P(None, "dp", "tensor"),
-            P(None, "dp", "tensor"),
-            P(None, "dp", None, "tensor"),
+            P(None, DP, TENSOR),
+            P(None, DP, TENSOR),
+            P(None, DP, TENSOR),
+            P(None, DP, TENSOR),
+            P(None, DP, TENSOR),
+            P(None, DP, None, TENSOR),
             P(),
             P(),
             P(),
         ),
         out_specs=(
-            P(("dp", "tensor"), None, None),
-            P(("dp", "tensor"), None),
-            P(None, "dp", "tensor"),
+            P((DP, TENSOR), None, None),
+            P((DP, TENSOR), None),
+            P(None, DP, TENSOR),
             P(),
-            P(None, "dp", "tensor"),
-            P(None, "dp", "tensor"),
-            P(None, "dp", "tensor"),
-            P(None, "dp", "tensor"),
+            P(None, DP, TENSOR),
+            P(None, DP, TENSOR),
+            P(None, DP, TENSOR),
+            P(None, DP, TENSOR),
             P(),
             P(),
             P(),

time: 608 us -> 540 us (0.89)
  waiting for transfers between devices: 39.9 us -> 2.1 us
  starting transfers between devices: 26.1 us -> 3.13 us
  local copies, waits for them, and re-layouts: 23.7 us -> 11.4 us
    ppermute x16 -> x3, waiting for transfers between devices: 39.9 us -> 2.1 us  [hop_z(): return lax.ppermute(values, DP, [(at, at ^ 2 * step) for at in range(8)])]
    ppermute x16 -> x3, starting transfers between devices: 26.1 us -> 3.13 us  [hop_z(): return lax.ppermute(values, DP, [(at, at ^ 2 * step) for at in range(8)])]
    unnamed x106 -> x51, local copies, waits for them, and re-layouts: 23.7 us -> 11.4 us
    pallas_call x23 -> x16, Pallas kernels: 507 us -> 509 us  [run(): pl.pallas_call(inner, in_specs=[IN_HBM] * lead + list(in_specs) + [IN_HBM...]
  transfers between devices with their start and end apart: 16 -> 3, of which waited for: 6 -> 1; matrix products, arithmetic and copies ran while one was open for 0% -> 0% of each run, Pallas kernels for 5% -> 3%
where the time goes in v5:
time: 540 us; the launch traced here: 530 us
  Pallas kernels  509 us (94%)
  local copies, waits for them, and re-layouts  11.4 us (2%)
    pallas_call x16, Pallas kernels, run(): pl.pallas_call(inner, in_specs=[IN_HBM] * lead + list(in_specs) + [IN_HBM...  509 us
    unnamed x51, local copies, waits for them, and re-layouts  11.4 us
  transfers between devices with their start and end apart: 3, of which 1 were waited for; matrix products, arithmetic and copies ran while one was open for 0% of the time, Pallas kernels for 3%

profile of v5, /device:TPU:0, one launch (start us, length us, event | category | flops | bytes accessed | tf_op | source)
XLA Modules:
  0.0 530.5 jit_solution(4005205896906873984)
XLA Ops:
  1.3 0.7 pad_add_fusion.refs_1_
  1.9 0.7 broadcast_xor_fusion
  2.6 1.3 select_reduce_fusion.refs_0_.refs_1_
  4.0 3.7 prep_rows.1
  7.6 4.6 seed_grads.1
  12.3 206.4 %forward_global.1 = (bf16[1024,1024]{1,0:T(8,128)(2,1)}, bf16[1024,1024]{1,0:T(8,128)(2,1)}, bf16[1024,1024]{1,0:T(8,128)(2,1)}, bf16[4,1024,1024]{2,1,0:T(8,128...) custom-call(f32[8,128]{1,0:T(8,128)} %get-tuple-element.132.refs_0_,, ...), custom_call_target="tpu_custom_call" | custom-call | flops 33999998976 | bytes 1000 | tf_op jit(solution)/shard_map/forward_global/pallas_call | solution.py:632
  218.7 0.0 copy-done.16
  218.7 0.0 copy-start.18
  218.7 1.2 copy-done.18
  219.9 0.7 copy-done.19
  220.6 17.9 %local_heads.1 = (bf16[4,768,768]{2,1,0:T(8,128)(2,1)}, bf16[4,768,256]{2,1,0:T(8,128)(2,1)}, f32[768,1024]{1,0:T(8,128)}, bf16[768,1024]{1,0:T(8,128)(2,1)}, bf...) custom-call(f32[8,128]{1,0:T(8,128)S(1)} %copy-done.19, f32[256,1024]{1,0:T(8,128)S(1)} %copy-done.18, ...), custom_call_target="tpu_custom_call" | custom-call | flops 3600000000 | bytes 1000 | tf_op jit(solution)/shard_map/local_heads/pallas_call | solution.py:632
  238.4 0.0 copy-start.20
  238.4 0.6 copy-done.20
  239.0 34.4 %local_ff.1 = (bf16[4,768,1024]{2,1,0:T(8,128)(2,1)}, bf16[4,768,1024]{2,1,0:T(8,128)(2,1)}, bf16[3,256,1024]{2,1,0:T(8,128)(2,1)}, bf16[1024,768]{1,0:T(8,128)(2,1)}, f32[8,128]{1,0:T(8,128)}) custom-call(f32[8,128]{1,0:T(8,128)} %copy-done.20, s32[8]{0:T(128)} %select_reduce_fusion.refs_0_.refs_1_, bf16[768,1024]{1,0:T(8,128)(2,1)} %get-tuple-element.147.refs_2_, ...), custom_call_target="tpu_custom_call" | custom-call | flops 6800000000 | bytes 1000 | tf_op jit(solution)/shard_map/local_ff/pallas_call | solution.py:632
  273.4 74.5 %local_back.1 = (f32[256,1024]{1,0:T(8,128)}, bf16[256,1024]{1,0:T(8,128)(2,1)}, f32[1,1024]{1,0:T(1,128)}, f32[1,1024]{1,0:T(1,128)}, bf16[512,1024]{1,0:T(8,12...) custom-call(f32[8,128]{1,0:T(8,128)} %get-tuple-element.152.refs_0_,, ...), custom_call_target="tpu_custom_call" | custom-call | flops 16199999488 | bytes 1000 | tf_op jit(solution)/shard_map/local_back/pallas_call | solution.py:632
  347.9 88.1 %backward_global.1 = (f32[256,1024]{1,0:T(8,128)}, f32[256,1024]{1,0:T(8,128)}, f32[1,1024]{1,0:T(1,128)}, bf16[512,1024]{1,0:T(8,128)(2,1)}, bf16[512,1024]{1,0...) custom-call(f32[8,128]{1,0:T(8,128)} %get-tuple-element.161.refs_0_,, ...), custom_call_target="tpu_custom_call" | custom-call | flops 17999998976 | bytes 1000 | tf_op jit(solution)/shard_map/backward_global/pallas_call | solution.py:632
  436.0 3.3 input_grad.1
  439.3 0.0 copy-start.12
  439.3 0.0 copy-start.13
  439.4 56.2 %last_transfers.1 = (f32[4,1024]{1,0:T(4,128)}, bf16[128,1024]{1,0:T(8,128)(2,1)}, bf16[128,1024]{1,0:T(8,128)(2,1)}, bf16[128,1024]{1,0:T(8,128)(2,1)}, bf16[12...) custom-call(f32[8,128]{1,0:T(8,128)} %get-tuple-element.187.refs_0_,, ...), custom_call_target="tpu_custom_call" | custom-call | flops 12000000000 | bytes 1000 | tf_op jit(solution)/shard_map/last_transfers/pallas_call | solution.py:632
  495.6 0.1 collective-permute-start
  495.6 2.6 collective-permute-start.1
  498.3 0.0 copy-done
  498.3 0.0 copy-start.1
  498.3 1.9 copy-done.1
  500.2 1.9 copy-done.2
  502.1 1.9 copy-done.3
  504.0 1.9 copy-done.4
  505.9 0.7 copy-done.17
  506.5 3.2 adam_update.6
  509.8 0.0 copy-start.15
  509.8 3.3 adam_update.7
  513.1 0.0 copy-start.21
  513.1 0.0 copy-start.23
  513.1 0.0 copy-start.24
  513.1 3.3 adam_update.8
  516.4 0.0 collective-permute-done.refs_2_
  516.4 0.0 copy-done.6
  516.4 0.1 sum_pieces.1
  516.5 0.4 collective-permute-start.2
  516.9 0.0 copy-done.22
  517.0 0.6 divide_subtract_fusion
  517.6 3.2 adam_update.9
  520.8 0.0 collective-permute-done.1.refs_2_
  520.8 3.3 adam_update.10
  524.1 2.1 collective-permute-done.2.refs_2_
  526.2 3.2 adam_update.11
  529.4 0.6 copy.78
  (29 shorter events, 0.1 us)
Async XLA Ops:
  12.3 206.4 %copy-start.16 = (f32[4,1024]{1,0:T(4,128)S(1)}, f32[4,1024]{1,0:T(4,128)}, u32[]{:S(2)}) copy-start(f32[4,1024]{1,0:T(4,128)} %get-tuple-element.135.refs_4_.refs_3_.refs_12_.refs_5_) | copy-start | bytes 49156
  218.7 1.2 copy-start.18
  219.9 0.7 copy-start.19
  238.4 0.6 copy-start.20
  439.3 59.0 %copy-start = (f32[2,128,3072]{2,1,0:T(8,128)S(1)}, f32[2,128,3072]{2,1,0:T(8,128)}, u32[]{:S(2)}) copy-start(f32[2,128,3072]{2,1,0:T(8,128)} %refs_5_.13) | copy-start | bytes 9437188
  439.3 59.0 %copy-start.5 = (f32[2,128,128]{2,1,0:T(8,128)S(1)}, f32[2,128,128]{2,1,0:T(8,128)}, u32[]{:S(2)}) copy-start(f32[2,128,128]{2,1,0:T(8,128)} %refs_3_.13) | copy-start | bytes 393220
  439.3 59.0 %copy-start.12 = (bf16[128,1024]{1,0:T(8,128)(2,1)S(1)}, bf16[128,1024]{1,0:T(8,128)(2,1)}, u32[]{:S(2)}) copy-start(bf16[128,1024]{1,0:T(8,128)(2,1)} %get-tuple-element.200.refs_1_) | copy-start | bytes 786436
  439.3 58.9 %copy-start.13 = (bf16[128,1024]{1,0:T(8,128)(2,1)S(1)}, bf16[128,1024]{1,0:T(8,128)(2,1)}, u32[]{:S(2)}) copy-start(bf16[128,1024]{1,0:T(8,128)(2,1)} %get-tuple-element.201.refs_2_) | copy-start | bytes 786436
  495.6 20.8 %collective-permute-start = (bf16[256,1024]{1,0:T(8,128)(2,1)}, bf16[256,1024]{1,0:T(8,128)(2,1)S(1)}, u32[]{:S(2)}, u32[]{:S(2)}) collective-permute-start(bf16[256,1024]{1,0:T(8,128)(2,1)} %get-tuple-element.220), channel_id=1, source_target_pairs={{0,8},{4,12},{8,0},{12,4},{16,24},{20,28},{24,16},{28,20},{1,9},{5... | collective-permute-start | bytes 1572872 | tf_op jit(solution)/shard_map/ppermute | solution.py:2188
  495.6 25.2 %collective-permute-start.1 = (bf16[128,1024]{1,0:T(8,128)(2,1)}, bf16[128,1024]{1,0:T(8,128)(2,1)S(1)}, u32[]{:S(2)}, u32[]{:S(2)}) collective-permute-start(bf16[128,1024]{1,0:T(8,128)(2,1)} %get-tuple-element.231), channel_id=1, source_target_pairs={{0,16},{4,20},{8,24},{12,28},{16,0},{20,4},{24,8},{28,12},{1,17},{... | collective-permute-start | bytes 786440 | tf_op jit(solution)/shard_map/ppermute | solution.py:2188
  498.3 1.9 copy-start.1
  500.2 1.9 copy-start.2
  502.1 1.9 copy-start.3
  504.0 1.9 copy-start.4
  505.9 0.7 copy-start.17
  506.5 3.2 copy-start.10
  506.5 3.2 copy-start.11
  509.8 3.3 copy-start.14
  509.8 3.3 copy-start.15
  513.1 3.3 copy-start.6
  513.1 3.9 copy-start.21
  513.1 3.9 copy-start.22
  513.1 3.9 copy-start.23
  513.1 3.8 copy-start.24
  513.1 4.5 copy-start.8
  513.1 4.5 copy-start.9
  516.5 9.7 %collective-permute-start.2 = (bf16[128,1024]{1,0:T(8,128)(2,1)S(1)}, bf16[128,1024]{1,0:T(8,128)(2,1)S(1)}, u32[]{:S(2)}, u32[]{:S(2)}) collective-permute-start(bf16[128,1024]{1,0:T(8,128)(2,1)S(1)} %get-tuple-element.239), channel_id=1, source_target_pairs={{0,16},{4,20},{8,24},{12,28},{16,0},{20,4},{24,8},{28,12},{1,17},{... | collective-permute-start | bytes 786440 | tf_op jit(solution)/shard_map/ppermute | solution.py:2188
  517.6 3.2 copy-start.7

commit v6 on v5

--- a/solution.py
+++ b/solution.py
@@ -1547,7 +1547,6 @@
     tile = active_ref.shape[2]
     per = up_buf.shape[3] // tile
     group = step // per
-    cols_at = pl.ds(pl.multiple_of((step % per) * tile, tile), tile)
 
     @pl.when(step == 0)
     def _():
@@ -1562,17 +1561,29 @@
         wait_weights(ups, up_buf, up_sems, group)
         wait_weights(downs, down_buf, down_sems, group)
 
-    for c in range(CB):
-        rows = slice(c * frames, (c + 1) * frames)
-        upper = dot_rows(normed_ref[rows, :half], up_buf[group, 0, :, cols_at]) + dot_rows(
-            normed_ref[rows, half:], up_buf[group, 1, :, cols_at]
+    piece = 512
+    pieces = [
+        (slice(begin, begin + rows_all), pl.ds(pl.multiple_of((step % per) * tile + at * piece, piece), piece), at)
+        for at in range(tile // piece)
+        for begin in (0,)
+    ]
+
+    def raised(rows, lanes):
+        return dot_rows(normed_ref[rows, :half], up_buf[group, 0, :, lanes]) + dot_rows(
+            normed_ref[rows, half:], up_buf[group, 1, :, lanes]
         )
+
+    upper = raised(*pieces[0][:2])
+    for at, (rows, lanes, place) in enumerate(pieces):
+        coming = raised(*pieces[at + 1][:2]) if at + 1 < len(pieces) else None
         active, slope = gelu_both(upper)
-        active_ref[0, rows, :] = active
-        slope_ref[0, rows, :] = slope
-        for at in range(2):
-            lanes = slice(at * half, (at + 1) * half)
-            acc[rows, lanes] += dot_transposed(active, down_buf[group, at, :, cols_at])
+        here = slice(place * piece, (place + 1) * piece)
+        active_ref[0, rows, here] = active
+        slope_ref[0, rows, here] = slope
+        for side in range(2):
+            sides = slice(side * half, (side + 1) * half)
+            acc[rows, sides] += dot_transposed(active, down_buf[group, side, :, lanes])
+        upper = coming
 
     @pl.when(step == pl.num_programs(0) - 1)
     def _():
@@ -1589,7 +1600,7 @@
         pltpu.make_async_copy(parts[at][half], buffer.at[at, half], sems.at[at, half]).start()
 
 
-def local_ff(line, source, normed, middle, ups, downs, tile=512):
+def local_ff(line, source, normed, middle, ups, downs, tile=1024):
     rows = normed.shape[0]
     hidden = ups.shape[2]
     half = D // 2
@@ -1936,24 +1947,31 @@
     greet((CORE, X, Y, Z1, Z2))
     upper, lower = pl.ds(0, quarter), pl.ds(quarter, quarter)
     gain_core = fly(CORE, gains_ref, gain_met.at[0])
-    gh_low, gh_up = [fly(Y, gh_far_h.at[rows], met_v.at[1, rows]) for rows in (lower, upper)]
-    d_low, d_up = [fly(X, d2_h.at[rows], met_v.at[2, rows]) for rows in (lower, upper)]
+    gh_low = fly(Y, gh_far_h.at[lower], met_v.at[1, lower])
+    d_low = fly(X, d2_h.at[lower], met_v.at[2, lower])
     gu_in = [file(gu_near_h, held_v.at[0]), file(gu_met_h, met_v.at[0])]
     far_in = [file(h0_far_h.at[lower], extra_v.at[0, lower]), file(h2_far_h, extra_v.at[1, lower])]
     rest_in = [file(gh_near_h, held_v.at[1]), file(d0_h, held_v.at[2]), file(h0_near_h, held_v.at[3])]
     rest_in += [file(h2_first_h, met_v.at[3, upper]), file(h_first_h, extra_v.at[2, upper])]
+    gain_core.wait_recv()
+    gain_v[0] = gains_ref[...] + gain_met[0]
+    gain_1 = fly(Z1, gain_v.at[0], gain_met.at[1])
     for one in gu_in:
         one.wait()
     held_v[0] = summed(held_v[0], met_v[0])
     gu_1 = fly(Z1, held_v.at[0, lower], z_met.at[0])
-    gain_core.wait_recv()
-    gain_v[0] = gains_ref[...] + gain_met[0]
-    gain_x = fly(X, gain_v.at[0], gain_met.at[1])
+    gain_1.wait_recv()
+    gain_v[1] = gain_v[0] + gain_met[1]
+    gain_2 = fly(Z2, gain_v.at[1], gain_met.at[2])
+    gh_up = fly(Y, gh_far_h.at[upper], met_v.at[1, upper])
+    gain_2.wait_recv()
+    gain_v[2] = gain_v[1] + gain_met[2]
+    gain_x = fly(X, gain_v.at[2], gain_met.at[3])
+    d_up = fly(X, d2_h.at[upper], met_v.at[2, upper])
     h_x = fly(X, h2_near_h.at[lower], met_v.at[3, lower])
     for one in far_in:
         one.wait()
     extra_v[0, quarter:, :] = summed(extra_v[0, quarter:, :], extra_v[1, quarter:, :])
-    h_y = fly(Y, extra_v.at[0, lower], extra_v.at[2, lower])
     for one in rest_in:
         one.wait()
     done = []
@@ -1973,6 +1991,10 @@
     gh_1 = fly(Z1, held_v.at[1, lower], z_met.at[1])
     d_low.wait_recv()
     add(2, False)
+    gain_x.wait_recv()
+    gain_v[3] = gain_v[2] + gain_met[3]
+    gain_y = fly(Y, gain_v.at[3], gain_met.at[4])
+    h_y = fly(Y, extra_v.at[0, lower], extra_v.at[2, lower])
     gu_2 = second(0, gu_1, gu_last_h, gu_keep_h)
     gh_up.wait_recv()
     add(1, True)
@@ -1980,26 +2002,17 @@
     d_1 = fly(Z1, held_v.at[2, lower], z_met.at[2])
     d_up.wait_recv()
     add(2, True)
-    gain_x.wait_recv()
-    gain_v[1] = gain_v[0] + gain_met[1]
-    gain_y = fly(Y, gain_v.at[1], gain_met.at[2])
+    gain_y.wait_recv()
+    gain_out_ref[...] = gain_v[3] + gain_met[4]
     h_x.wait_recv()
     h_y.wait_recv()
     held_v[3] = summed(held_v[3], met_v[3], extra_v[2])
     done.append(file(held_v.at[3, upper], h_keep_h))
     done.append(file(held_v.at[3, lower], h_send_h))
-    gain_y.wait_recv()
-    gain_v[2] = gain_v[1] + gain_met[2]
-    gain_1 = fly(Z1, gain_v.at[2], gain_met.at[3])
     d_1.wait_recv()
     held_v[2, :quarter, :] = summed(held_v[2, :quarter, :], z_met[2])
     done.append(file(held_v.at[2, pl.ds(0, owned)], d_keep_h))
     done.append(file(held_v.at[2, pl.ds(owned, owned)], d_last_h))
-    gain_1.wait_recv()
-    gain_v[3] = gain_v[2] + gain_met[3]
-    gain_2 = fly(Z2, gain_v.at[3], gain_met.at[4])
-    gain_2.wait_recv()
-    gain_out_ref[...] = gain_v[3] + gain_met[4]
     for one in (gu_2, gh_2):
         one.wait_recv()
     for one in done:

time: 540 us -> 535 us (level)
  Pallas kernels: 509 us -> 502 us
    pallas_call x16, Pallas kernels: 509 us -> 502 us  [run(): pl.pallas_call(inner, in_specs=[IN_HBM] * lead + list(in_specs) + [IN_HBM...]
where the time goes in v6:
time: 535 us; the launch traced here: 526 us
  Pallas kernels  502 us (94%)
  local copies, waits for them, and re-layouts  11.4 us (2%)
  starting transfers between devices  6.48 us (1%)
    pallas_call x16, Pallas kernels, run(): pl.pallas_call(inner, in_specs=[IN_HBM] * lead + list(in_specs) + [IN_HBM...  502 us
    unnamed x51, local copies, waits for them, and re-layouts  11.4 us
  transfers between devices with their start and end apart: 3, of which 1 were waited for; matrix products, arithmetic and copies ran while one was open for 0% of the time, Pallas kernels for 3%

profile of v6, /device:TPU:0, one launch (start us, length us, event | category | flops | bytes accessed | tf_op | source)
XLA Modules:
  0.0 525.6 jit_solution(5399571829812388421)
XLA Ops:
  1.3 0.7 pad_add_fusion.refs_1_
  1.9 0.7 broadcast_xor_fusion
  2.6 1.3 select_reduce_fusion.refs_0_.refs_1_
  4.0 3.7 prep_rows.1
  7.6 4.7 seed_grads.1
  12.3 206.4 %forward_global.1 = (bf16[1024,1024]{1,0:T(8,128)(2,1)}, bf16[1024,1024]{1,0:T(8,128)(2,1)}, bf16[1024,1024]{1,0:T(8,128)(2,1)}, bf16[4,1024,1024]{2,1,0:T(8,128...) custom-call(f32[8,128]{1,0:T(8,128)} %get-tuple-element.132.refs_0_,, ...), custom_call_target="tpu_custom_call" | custom-call | flops 33999998976 | bytes 1000 | tf_op jit(solution)/shard_map/forward_global/pallas_call | solution.py:632
  218.7 0.0 copy-done.16
  218.7 1.2 copy-done.18
  219.9 0.7 copy-done.19
  220.6 17.8 %local_heads.1 = (bf16[4,768,768]{2,1,0:T(8,128)(2,1)}, bf16[4,768,256]{2,1,0:T(8,128)(2,1)}, f32[768,1024]{1,0:T(8,128)}, bf16[768,1024]{1,0:T(8,128)(2,1)}, bf...) custom-call(f32[8,128]{1,0:T(8,128)S(1)} %copy-done.19, f32[256,1024]{1,0:T(8,128)S(1)} %copy-done.18, ...), custom_call_target="tpu_custom_call" | custom-call | flops 3600000000 | bytes 1000 | tf_op jit(solution)/shard_map/local_heads/pallas_call | solution.py:632
  238.4 0.0 copy-start.20
  238.4 0.6 copy-done.20
  239.0 28.8 %local_ff.1 = (bf16[4,768,1024]{2,1,0:T(8,128)(2,1)}, bf16[4,768,1024]{2,1,0:T(8,128)(2,1)}, bf16[3,256,1024]{2,1,0:T(8,128)(2,1)}, bf16[1024,768]{1,0:T(8,128)(2,1)}, f32[8,128]{1,0:T(8,128)}) custom-call(f32[8,128]{1,0:T(8,128)} %copy-done.20, s32[8]{0:T(128)} %select_reduce_fusion.refs_0_.refs_1_, bf16[768,1024]{1,0:T(8,128)(2,1)} %get-tuple-element.147.refs_2_, ...), custom_call_target="tpu_custom_call" | custom-call | flops 6800000000 | bytes 1000 | tf_op jit(solution)/shard_map/local_ff/pallas_call | solution.py:632
  267.8 74.5 %local_back.1 = (f32[256,1024]{1,0:T(8,128)}, bf16[256,1024]{1,0:T(8,128)(2,1)}, f32[1,1024]{1,0:T(1,128)}, f32[1,1024]{1,0:T(1,128)}, bf16[512,1024]{1,0:T(8,12...) custom-call(f32[8,128]{1,0:T(8,128)} %get-tuple-element.152.refs_0_,, ...), custom_call_target="tpu_custom_call" | custom-call | flops 16199999488 | bytes 1000 | tf_op jit(solution)/shard_map/local_back/pallas_call | solution.py:632
  342.3 88.1 %backward_global.1 = (f32[256,1024]{1,0:T(8,128)}, f32[256,1024]{1,0:T(8,128)}, f32[1,1024]{1,0:T(1,128)}, bf16[512,1024]{1,0:T(8,128)(2,1)}, bf16[512,1024]{1,0...) custom-call(f32[8,128]{1,0:T(8,128)} %get-tuple-element.161.refs_0_,, ...), custom_call_target="tpu_custom_call" | custom-call | flops 17999998976 | bytes 1000 | tf_op jit(solution)/shard_map/backward_global/pallas_call | solution.py:632
  430.4 3.3 input_grad.1
  433.8 0.0 copy-start.12
  433.8 0.0 copy-start.13
  433.8 55.5 %last_transfers.1 = (f32[4,1024]{1,0:T(4,128)}, bf16[128,1024]{1,0:T(8,128)(2,1)}, bf16[128,1024]{1,0:T(8,128)(2,1)}, bf16[128,1024]{1,0:T(8,128)(2,1)}, bf16[12...) custom-call(f32[8,128]{1,0:T(8,128)} %get-tuple-element.187.refs_0_,, ...), custom_call_target="tpu_custom_call" | custom-call | flops 12000000000 | bytes 1000 | tf_op jit(solution)/shard_map/last_transfers/pallas_call | solution.py:632
  489.3 3.5 collective-permute-start
  492.8 0.1 collective-permute-start.1
  493.0 0.0 copy-done.13
  493.0 0.0 copy-start.1
  493.0 1.9 copy-done.1
  494.9 1.9 copy-done.2
  496.7 1.9 copy-done.3
  498.6 1.9 copy-done.4
  500.5 0.7 copy-done.17
  501.2 3.2 adam_update.6
  504.4 0.0 copy-done.11
  504.5 3.3 adam_update.7
  507.7 0.0 copy-start.21
  507.8 0.0 copy-start.23
  507.8 0.0 copy-start.24
  507.8 3.3 adam_update.8
  511.1 0.0 collective-permute-done.refs_2_
  511.1 0.1 sum_pieces.1
  511.2 2.9 collective-permute-start.2
  514.1 0.0 copy-done.24
  514.1 0.6 divide_subtract_fusion
  514.7 0.0 copy-done.8
  514.7 3.2 adam_update.9
  518.0 0.0 collective-permute-done.1.refs_2_
  518.0 0.0 copy-done.7
  518.0 3.3 adam_update.10
  521.2 0.1 collective-permute-done.2.refs_2_
  521.4 3.2 adam_update.11
  524.6 0.6 copy.78
  (29 shorter events, 0.1 us)
Async XLA Ops:
  12.3 206.4 %copy-start.16 = (f32[4,1024]{1,0:T(4,128)S(1)}, f32[4,1024]{1,0:T(4,128)}, u32[]{:S(2)}) copy-start(f32[4,1024]{1,0:T(4,128)} %get-tuple-element.135.refs_4_.refs_3_.refs_12_.refs_5_) | copy-start | bytes 49156
  218.7 1.2 copy-start.18
  219.9 0.7 copy-start.19
  238.4 0.6 copy-start.20
  433.8 59.2 %copy-start = (f32[2,128,3072]{2,1,0:T(8,128)S(1)}, f32[2,128,3072]{2,1,0:T(8,128)}, u32[]{:S(2)}) copy-start(f32[2,128,3072]{2,1,0:T(8,128)} %refs_5_.13) | copy-start | bytes 9437188
  433.8 59.2 %copy-start.5 = (f32[2,128,128]{2,1,0:T(8,128)S(1)}, f32[2,128,128]{2,1,0:T(8,128)}, u32[]{:S(2)}) copy-start(f32[2,128,128]{2,1,0:T(8,128)} %refs_3_.13) | copy-start | bytes 393220
  433.8 59.2 %copy-start.12 = (bf16[128,1024]{1,0:T(8,128)(2,1)S(1)}, bf16[128,1024]{1,0:T(8,128)(2,1)}, u32[]{:S(2)}) copy-start(bf16[128,1024]{1,0:T(8,128)(2,1)} %get-tuple-element.200.refs_1_) | copy-start | bytes 786436
  433.8 59.2 %copy-start.13 = (bf16[128,1024]{1,0:T(8,128)(2,1)S(1)}, bf16[128,1024]{1,0:T(8,128)(2,1)}, u32[]{:S(2)}) copy-start(bf16[128,1024]{1,0:T(8,128)(2,1)} %get-tuple-element.201.refs_2_) | copy-start | bytes 786436
  489.3 21.7 %collective-permute-start = (bf16[256,1024]{1,0:T(8,128)(2,1)}, bf16[256,1024]{1,0:T(8,128)(2,1)S(1)}, u32[]{:S(2)}, u32[]{:S(2)}) collective-permute-start(bf16[256,1024]{1,0:T(8,128)(2,1)} %get-tuple-element.220), channel_id=1, source_target_pairs={{0,8},{4,12},{8,0},{12,4},{16,24},{20,28},{24,16},{28,20},{1,9},{5... | collective-permute-start | bytes 1572872 | tf_op jit(solution)/shard_map/ppermute | solution.py:2201
  492.8 25.1 %collective-permute-start.1 = (bf16[128,1024]{1,0:T(8,128)(2,1)}, bf16[128,1024]{1,0:T(8,128)(2,1)S(1)}, u32[]{:S(2)}, u32[]{:S(2)}) collective-permute-start(bf16[128,1024]{1,0:T(8,128)(2,1)} %get-tuple-element.231), channel_id=1, source_target_pairs={{0,16},{4,20},{8,24},{12,28},{16,0},{20,4},{24,8},{28,12},{1,17},{... | collective-permute-start | bytes 786440 | tf_op jit(solution)/shard_map/ppermute | solution.py:2201
  493.0 1.9 copy-start.1
  494.9 1.9 copy-start.2
  496.7 1.9 copy-start.3
  498.6 1.9 copy-start.4
  500.5 0.7 copy-start.17
  501.2 3.2 copy-start.10
  501.2 3.2 copy-start.11
  504.5 3.3 copy-start.14
  504.5 3.3 copy-start.15
  507.7 3.3 copy-start.6
  507.7 6.3 %copy-start.21 = (f32[4,1024]{1,0:T(4,128)S(1)}, f32[4,1024]{1,0:T(4,128)}, u32[]{:S(2)}) copy-start(f32[4,1024]{1,0:T(4,128)} %refs_2_.1) | copy-start | bytes 49156
  507.8 6.3 %copy-start.22 = (f32[4,1024]{1,0:T(4,128)S(1)}, f32[4,1024]{1,0:T(4,128)}, u32[]{:S(2)}) copy-start(f32[4,1024]{1,0:T(4,128)} %get-tuple-element.268) | copy-start | bytes 49156
  507.8 6.3 %copy-start.23 = (f32[4,1024]{1,0:T(4,128)S(1)}, f32[4,1024]{1,0:T(4,128)}, u32[]{:S(2)}) copy-start(f32[4,1024]{1,0:T(4,128)} %param.27) | copy-start | bytes 49156
  507.8 6.3 %copy-start.24 = (f32[4,1024]{1,0:T(4,128)S(1)}, f32[4,1024]{1,0:T(4,128)}, u32[]{:S(2)}) copy-start(f32[4,1024]{1,0:T(4,128)} %param.28) | copy-start | bytes 49156
  507.8 6.9 %copy-start.8 = (bf16[128,1024]{1,0:T(8,128)(2,1)S(1)}, bf16[128,1024]{1,0:T(8,128)(2,1)}, u32[]{:S(2)}) copy-start(bf16[128,1024]{1,0:T(8,128)(2,1)} %get-tuple-element.222.refs_1_) | copy-start | bytes 786436
  507.8 6.9 %copy-start.9 = (bf16[128,1024]{1,0:T(8,128)(2,1)S(1)}, bf16[128,1024]{1,0:T(8,128)(2,1)}, u32[]{:S(2)}) copy-start(bf16[128,1024]{1,0:T(8,128)(2,1)} %get-tuple-element.223.refs_2_) | copy-start | bytes 786436
  511.2 10.1 %collective-permute-start.2 = (bf16[128,1024]{1,0:T(8,128)(2,1)S(1)}, bf16[128,1024]{1,0:T(8,128)(2,1)S(1)}, u32[]{:S(2)}, u32[]{:S(2)}) collective-permute-start(bf16[128,1024]{1,0:T(8,128)(2,1)S(1)} %get-tuple-element.239), channel_id=1, source_target_pairs={{0,16},{4,20},{8,24},{12,28},{16,0},{20,4},{24,8},{28,12},{1,17},{... | collective-permute-start | bytes 786440 | tf_op jit(solution)/shard_map/ppermute | solution.py:2201
  514.7 3.2 copy-start.7

commit v7 on v6

--- a/solution.py
+++ b/solution.py
@@ -2154,7 +2154,7 @@
     new_ema_ref[0] = ema_decay * ema_ref[0] + (1.0 - ema_decay) * new_master
 
 
-def adam(line, layer, third, pieces, left, right, master, first, second, ema, before, tile=512):
+def adam(line, layer, third, pieces, left, right, master, first, second, ema, before, tile=1024):
     owned, columns = pieces[0].shape
     steps = columns // tile
     first_step = third * steps

time: 535 us -> 533 us (level)
  no operation moved by 1% of the time
where the time goes in v7:
time: 533 us; the launch traced here: 523 us
  Pallas kernels  499 us (94%)
  local copies, waits for them, and re-layouts  11.4 us (2%)
  starting transfers between devices  6.46 us (1%)
    pallas_call x16, Pallas kernels, run(): pl.pallas_call(inner, in_specs=[IN_HBM] * lead + list(in_specs) + [IN_HBM...  499 us
    unnamed x51, local copies, waits for them, and re-layouts  11.4 us
  transfers between devices with their start and end apart: 3, of which 1 were waited for; matrix products, arithmetic and copies ran while one was open for 0% of the time, Pallas kernels for 3%

profile of v7, /device:TPU:0, one launch (start us, length us, event | category | flops | bytes accessed | tf_op | source)
XLA Modules:
  0.0 523.0 jit_solution(6212781867571137795)
XLA Ops:
  1.3 0.7 pad_add_fusion.refs_1_
  1.9 0.7 broadcast_xor_fusion
  2.6 1.3 select_reduce_fusion.refs_0_.refs_1_
  4.0 3.7 prep_rows.1
  7.6 4.6 seed_grads.1
  12.3 206.4 %forward_global.1 = (bf16[1024,1024]{1,0:T(8,128)(2,1)}, bf16[1024,1024]{1,0:T(8,128)(2,1)}, bf16[1024,1024]{1,0:T(8,128)(2,1)}, bf16[4,1024,1024]{2,1,0:T(8,128...) custom-call(f32[8,128]{1,0:T(8,128)} %get-tuple-element.132.refs_0_,, ...), custom_call_target="tpu_custom_call" | custom-call | flops 33999998976 | bytes 1000 | tf_op jit(solution)/shard_map/forward_global/pallas_call | solution.py:632
  218.7 0.0 copy-done.16
  218.7 0.0 copy-start.18
  218.7 1.2 copy-done.18
  219.9 0.7 copy-done.19
  220.6 17.8 %local_heads.1 = (bf16[4,768,768]{2,1,0:T(8,128)(2,1)}, bf16[4,768,256]{2,1,0:T(8,128)(2,1)}, f32[768,1024]{1,0:T(8,128)}, bf16[768,1024]{1,0:T(8,128)(2,1)}, bf...) custom-call(f32[8,128]{1,0:T(8,128)S(1)} %copy-done.19, f32[256,1024]{1,0:T(8,128)S(1)} %copy-done.18, ...), custom_call_target="tpu_custom_call" | custom-call | flops 3600000000 | bytes 1000 | tf_op jit(solution)/shard_map/local_heads/pallas_call | solution.py:632
  238.4 0.0 copy-start.20
  238.4 0.6 copy-done.20
  239.0 28.8 %local_ff.1 = (bf16[4,768,1024]{2,1,0:T(8,128)(2,1)}, bf16[4,768,1024]{2,1,0:T(8,128)(2,1)}, bf16[3,256,1024]{2,1,0:T(8,128)(2,1)}, bf16[1024,768]{1,0:T(8,128)(2,1)}, f32[8,128]{1,0:T(8,128)}) custom-call(f32[8,128]{1,0:T(8,128)} %copy-done.20, s32[8]{0:T(128)} %select_reduce_fusion.refs_0_.refs_1_, bf16[768,1024]{1,0:T(8,128)(2,1)} %get-tuple-element.147.refs_2_, ...), custom_call_target="tpu_custom_call" | custom-call | flops 6800000000 | bytes 1000 | tf_op jit(solution)/shard_map/local_ff/pallas_call | solution.py:632
  267.8 74.5 %local_back.1 = (f32[256,1024]{1,0:T(8,128)}, bf16[256,1024]{1,0:T(8,128)(2,1)}, f32[1,1024]{1,0:T(1,128)}, f32[1,1024]{1,0:T(1,128)}, bf16[512,1024]{1,0:T(8,12...) custom-call(f32[8,128]{1,0:T(8,128)} %get-tuple-element.152.refs_0_,, ...), custom_call_target="tpu_custom_call" | custom-call | flops 16199999488 | bytes 1000 | tf_op jit(solution)/shard_map/local_back/pallas_call | solution.py:632
  342.3 88.1 %backward_global.1 = (f32[256,1024]{1,0:T(8,128)}, f32[256,1024]{1,0:T(8,128)}, f32[1,1024]{1,0:T(1,128)}, bf16[512,1024]{1,0:T(8,128)(2,1)}, bf16[512,1024]{1,0...) custom-call(f32[8,128]{1,0:T(8,128)} %get-tuple-element.161.refs_0_,, ...), custom_call_target="tpu_custom_call" | custom-call | flops 17999998976 | bytes 1000 | tf_op jit(solution)/shard_map/backward_global/pallas_call | solution.py:632
  430.4 3.3 input_grad.1
  433.8 0.0 copy-start.12
  433.8 55.7 %last_transfers.1 = (f32[4,1024]{1,0:T(4,128)}, bf16[128,1024]{1,0:T(8,128)(2,1)}, bf16[128,1024]{1,0:T(8,128)(2,1)}, bf16[128,1024]{1,0:T(8,128)(2,1)}, bf16[12...) custom-call(f32[8,128]{1,0:T(8,128)} %get-tuple-element.187.refs_0_,, ...), custom_call_target="tpu_custom_call" | custom-call | flops 12000000000 | bytes 1000 | tf_op jit(solution)/shard_map/last_transfers/pallas_call | solution.py:632
  489.4 3.5 collective-permute-start
  492.9 0.0 collective-permute-start.1
  493.0 0.0 copy-start.1
  493.0 1.9 copy-done.1
  494.9 1.9 copy-done.2
  496.7 1.9 copy-done.3
  498.6 1.9 copy-done.4
  500.5 0.7 copy-done.17
  501.2 2.6 adam_update.6
  503.8 0.0 copy-done.11
  503.8 2.6 adam_update.7
  506.4 0.0 copy-start.21
  506.4 0.0 copy-start.22
  506.5 0.0 copy-start.23
  506.5 0.0 copy-start.24
  506.5 2.6 adam_update.8
  509.1 0.0 collective-permute-done.refs_2_
  509.1 0.1 sum_pieces.1
  509.2 3.0 collective-permute-start.2
  512.2 0.0 copy-done.22
  512.2 0.6 divide_subtract_fusion
  512.8 0.0 copy-done.8
  512.8 2.6 adam_update.9
  515.4 0.0 collective-permute-done.1.refs_2_
  515.4 0.0 copy-done.7
  515.4 2.6 adam_update.10
  518.0 1.3 collective-permute-done.2.refs_2_
  519.4 2.6 adam_update.11
  522.0 0.6 copy.78
  (29 shorter events, 0.1 us)
Async XLA Ops:
  12.3 206.4 %copy-start.16 = (f32[4,1024]{1,0:T(4,128)S(1)}, f32[4,1024]{1,0:T(4,128)}, u32[]{:S(2)}) copy-start(f32[4,1024]{1,0:T(4,128)} %get-tuple-element.135.refs_4_.refs_3_.refs_12_.refs_5_) | copy-start | bytes 49156
  218.7 1.2 copy-start.18
  219.9 0.7 copy-start.19
  238.4 0.6 copy-start.20
  433.7 59.2 %copy-start = (f32[2,128,3072]{2,1,0:T(8,128)S(1)}, f32[2,128,3072]{2,1,0:T(8,128)}, u32[]{:S(2)}) copy-start(f32[2,128,3072]{2,1,0:T(8,128)} %refs_5_.13) | copy-start | bytes 9437188
  433.7 59.2 %copy-start.5 = (f32[2,128,128]{2,1,0:T(8,128)S(1)}, f32[2,128,128]{2,1,0:T(8,128)}, u32[]{:S(2)}) copy-start(f32[2,128,128]{2,1,0:T(8,128)} %refs_3_.13) | copy-start | bytes 393220
  433.8 59.2 %copy-start.12 = (bf16[128,1024]{1,0:T(8,128)(2,1)S(1)}, bf16[128,1024]{1,0:T(8,128)(2,1)}, u32[]{:S(2)}) copy-start(bf16[128,1024]{1,0:T(8,128)(2,1)} %get-tuple-element.200.refs_1_) | copy-start | bytes 786436
  433.8 59.2 %copy-start.13 = (bf16[128,1024]{1,0:T(8,128)(2,1)S(1)}, bf16[128,1024]{1,0:T(8,128)(2,1)}, u32[]{:S(2)}) copy-start(bf16[128,1024]{1,0:T(8,128)(2,1)} %get-tuple-element.201.refs_2_) | copy-start | bytes 786436
  489.4 19.6 %collective-permute-start = (bf16[256,1024]{1,0:T(8,128)(2,1)}, bf16[256,1024]{1,0:T(8,128)(2,1)S(1)}, u32[]{:S(2)}, u32[]{:S(2)}) collective-permute-start(bf16[256,1024]{1,0:T(8,128)(2,1)} %get-tuple-element.220), channel_id=1, source_target_pairs={{0,8},{4,12},{8,0},{12,4},{16,24},{20,28},{24,16},{28,20},{1,9},{5... | collective-permute-start | bytes 1572872 | tf_op jit(solution)/shard_map/ppermute | solution.py:2201
  492.9 22.5 %collective-permute-start.1 = (bf16[128,1024]{1,0:T(8,128)(2,1)}, bf16[128,1024]{1,0:T(8,128)(2,1)S(1)}, u32[]{:S(2)}, u32[]{:S(2)}) collective-permute-start(bf16[128,1024]{1,0:T(8,128)(2,1)} %get-tuple-element.231), channel_id=1, source_target_pairs={{0,16},{4,20},{8,24},{12,28},{16,0},{20,4},{24,8},{28,12},{1,17},{... | collective-permute-start | bytes 786440 | tf_op jit(solution)/shard_map/ppermute | solution.py:2201
  493.0 1.9 copy-start.1
  494.9 1.9 copy-start.2
  496.7 1.9 copy-start.3
  498.6 1.9 copy-start.4
  500.5 0.7 copy-start.17
  501.2 2.6 copy-start.10
  501.2 2.6 copy-start.11
  503.8 2.6 copy-start.14
  503.8 2.6 copy-start.15
  506.4 2.7 copy-start.6
  506.4 5.8 %copy-start.21 = (f32[4,1024]{1,0:T(4,128)S(1)}, f32[4,1024]{1,0:T(4,128)}, u32[]{:S(2)}) copy-start(f32[4,1024]{1,0:T(4,128)} %refs_2_.1) | copy-start | bytes 49156
  506.4 5.8 %copy-start.22 = (f32[4,1024]{1,0:T(4,128)S(1)}, f32[4,1024]{1,0:T(4,128)}, u32[]{:S(2)}) copy-start(f32[4,1024]{1,0:T(4,128)} %get-tuple-element.268) | copy-start | bytes 49156
  506.5 5.7 %copy-start.23 = (f32[4,1024]{1,0:T(4,128)S(1)}, f32[4,1024]{1,0:T(4,128)}, u32[]{:S(2)}) copy-start(f32[4,1024]{1,0:T(4,128)} %param.27) | copy-start | bytes 49156
  506.5 5.7 %copy-start.24 = (f32[4,1024]{1,0:T(4,128)S(1)}, f32[4,1024]{1,0:T(4,128)}, u32[]{:S(2)}) copy-start(f32[4,1024]{1,0:T(4,128)} %param.28) | copy-start | bytes 49156
  506.5 6.4 %copy-start.8 = (bf16[128,1024]{1,0:T(8,128)(2,1)S(1)}, bf16[128,1024]{1,0:T(8,128)(2,1)}, u32[]{:S(2)}) copy-start(bf16[128,1024]{1,0:T(8,128)(2,1)} %get-tuple-element.222.refs_1_) | copy-start | bytes 786436
  506.5 6.4 %copy-start.9 = (bf16[128,1024]{1,0:T(8,128)(2,1)S(1)}, bf16[128,1024]{1,0:T(8,128)(2,1)}, u32[]{:S(2)}) copy-start(bf16[128,1024]{1,0:T(8,128)(2,1)} %get-tuple-element.223.refs_2_) | copy-start | bytes 786436
  509.2 10.1 %collective-permute-start.2 = (bf16[128,1024]{1,0:T(8,128)(2,1)S(1)}, bf16[128,1024]{1,0:T(8,128)(2,1)S(1)}, u32[]{:S(2)}, u32[]{:S(2)}) collective-permute-start(bf16[128,1024]{1,0:T(8,128)(2,1)S(1)} %get-tuple-element.239), channel_id=1, source_target_pairs={{0,16},{4,20},{8,24},{12,28},{16,0},{20,4},{24,8},{28,12},{1,17},{... | collective-permute-start | bytes 786440 | tf_op jit(solution)/shard_map/ppermute | solution.py:2201
  512.8 2.6 copy-start.7
